TPU v7x, 32 devices: a whole 2x2x4 slice. The times are simulated.
32 devices in a mesh: det: 8 (over z, x), exp: 4 (over y, core).
Axes of the slice: x: 2, y: 2, z: 4, core: 2. Of those that a mesh axis runs over, the one named last changes fastest.
Arguments:
- template: bfloat16 [256, 128, 128], P('det'), may hold values from -4 to 4
- template_var: bfloat16 [256, 128, 128], P('det'), may hold values from 2 to 32
- science: bfloat16 [4, 2048, 1024], P('exp', 'det'), may hold values from -10 to 10
- science_var: bfloat16 [4, 2048, 1024], P('exp', 'det'), may hold values from 0.5 to 2
- routes_src: int32 [4, 128], P('exp', 'det'), may hold values from 0 to 7, as said below
- routes_blk: int32 [4, 128], P('exp', 'det'), may hold values from 0 to 31
- stamp_rows: int32 [4, 32], P('exp', 'det'), may hold values from 0 to 128
- stamp_cols: int32 [4, 32], P('exp', 'det'), may hold values from 0 to 896
- basis_col: bfloat16 [40, 21], replicated, may hold values from -1.25 to 1.25
- basis_row: bfloat16 [40, 21], replicated, may hold values from -1.25 to 1.25
- psf_col: float32 [4, 21], P('exp'), may hold values from 0.05 to 0.5
- psf_row: float32 [4, 21], P('exp'), may hold values from 0.05 to 0.5
Outputs:
- significance: float32 [256, 128, 128], P('det')
- psf_score: float32 [4, 2048, 1024], P('exp', 'det')
- coefficients: float32 [4, 328], P('exp', 'det')
Inputs may be any that keep to these rules, and one draw needn't show every extreme that they name: `routes_src`: within the 16 blocks of one device, at most 2 take their template from one owner, and on every device some owner supplies exactly 2 of them.
All inputs are finite; a program needn't handle non-finite values.
Results may differ from a plain program's by a relative error of at most 0.0085.
Values may be sent and summed in bfloat16 or wider, within the bound.
No kernel may reach another device: no remote copies, remote signals or barrier semaphores. Data moves between devices by JAX's collectives and lax.ppermute only.
A program may use at most 128 MiB of HBM per device.

v0:
```python
import functools

import jax
import jax.numpy as jnp
from jax import lax
from jax.experimental import pallas as pl
from jax.experimental.pallas import tpu as pltpu
from jax.sharding import PartitionSpec as P

ridge_term = 0.01
bf16 = jnp.bfloat16
f32 = jnp.float32
vmem = functools.partial(pl.BlockSpec, memory_space=pltpu.VMEM)
smem = functools.partial(pl.BlockSpec, memory_space=pltpu.SMEM)
mib = 1024 * 1024
trailer_rows = 8


def up(value, step):
    return -(-value // step) * step


def cost(flops, moved):
    return pl.CostEstimate(flops=flops, bytes_accessed=moved, transcendentals=0)


def route_body(src, blk, slot_of, sender, request, count, *, peers, capacity):
    def clear_count(p, carry):
        count[p] = 0
        return carry

    def clear_slot(s, carry):
        sender[s] = 0
        request[s // capacity, 0, s % capacity] = 0
        return carry

    lax.fori_loop(0, peers, clear_count, 0, unroll=peers <= 16)
    lax.fori_loop(0, peers * capacity, clear_slot, 0, unroll=peers <= 16)
    for b in range(src.shape[1]):
        owner = src[0, b]
        place = count[owner]
        count[owner] = place + 1
        slot_of[b] = owner * capacity + place
        sender[owner * capacity + place] = b
        request[owner, 0, place] = blk[0, b] + 1


def route_tables(routes_src, routes_blk, peers, capacity):
    return pl.pallas_call(
        functools.partial(route_body, peers=peers, capacity=capacity),
        out_shape=(
            jax.ShapeDtypeStruct((routes_src.shape[1],), jnp.int32),
            jax.ShapeDtypeStruct((peers * capacity,), jnp.int32),
            jax.ShapeDtypeStruct((peers, 1, capacity), jnp.int32),
        ),
        in_specs=[smem()] * 2,
        out_specs=(smem(),) * 3,
        scratch_shapes=[pltpu.SMEM((peers,), jnp.int32)],
        name="route_tables",
    )(routes_src, routes_blk)


def pick_body(asked, template, out, sems, *, capacity):
    copies = []
    for s in range(out.shape[0]):
        block = jnp.maximum(asked[s // capacity, 0, s % capacity] - 1, 0)
        copies.append(pltpu.make_async_copy(template.at[block], out.at[s], sems.at[s]))
        copies[-1].start()
    for copy in copies:
        copy.wait()


def pick_blocks(asked, template, slots, capacity):
    return pl.pallas_call(
        functools.partial(pick_body, capacity=capacity),
        out_shape=jax.ShapeDtypeStruct((slots,) + template.shape[1:], template.dtype),
        in_specs=[smem(), pl.BlockSpec(memory_space=pl.ANY)],
        out_specs=vmem(),
        scratch_shapes=[pltpu.SemaphoreType.DMA((slots,))],
        compiler_params=pltpu.CompilerParams(vmem_limit_bytes=60 * mib),
        name="pick_blocks",
    )(asked, template)


def store_parts(sender, image, out, side, exps, capacity, across_blocks):
    part = side // exps
    slots = sender.shape[0]

    def one(s, carry):
        b = sender[s]
        top = pl.multiple_of((b // across_blocks) * side, side)
        left = pl.multiple_of((b % across_blocks) * side, side)
        block = image[pl.ds(top, side), pl.ds(left, side)].astype(bf16)
        row = pl.multiple_of((s % capacity) * part, part)
        for q in range(exps):
            out[(s // capacity) * exps + q, pl.ds(row, part), :] = block[q * part : (q + 1) * part]
        return carry

    lax.fori_loop(0, slots, one, 0, unroll=True if slots <= 32 else 4)


def store_requests(request, out, side, exps, capacity):
    lane = lax.broadcasted_iota(jnp.int32, (trailer_rows, side), 1)

    def put(p, carry):
        line = jnp.zeros((trailer_rows, side), f32)
        for c in range(capacity):
            line = jnp.where(lane == c, request[p, 0, c].astype(f32), line)
        for q in range(exps):
            out[p * exps + q, out.shape[1] - trailer_rows :, :] = line.astype(bf16)
        return carry

    lax.fori_loop(0, request.shape[0], put, 0)


def cut(ref, top, left, height, side):
    down = pl.multiple_of((top // 8) * 8, 8)
    over = pl.multiple_of((left // side) * side, side)
    tile = ref[pl.ds(down, height), pl.ds(over, 3 * side)]
    tile = pltpu.roll(tile, lax.rem(3 * side - (left - over), 3 * side), 1)[:, : 2 * side]
    return pltpu.roll(tile, lax.rem(height - (top - down), height), 0)


def prepare_body(
    sender,
    request,
    rows_at,
    cols_at,
    science,
    variance,
    parts_out,
    root_out,
    data_out,
    image,
    var,
    *,
    exps,
    capacity,
):
    side = root_out.shape[1]
    high, wide = science.shape
    store_parts(sender, variance, parts_out, side, exps, capacity, wide // side)
    store_requests(request, parts_out, side, exps, capacity)
    image[:, wide:] = jnp.zeros((image.shape[0], image.shape[1] - wide), f32)
    image[high:, :wide] = jnp.zeros((image.shape[0] - high, wide), f32)
    image[:high, :wide] = science[...].astype(f32)
    var[:, wide:] = jnp.ones((var.shape[0], var.shape[1] - wide), f32)
    var[high:, :wide] = jnp.ones((var.shape[0] - high, wide), f32)
    var[:high, :wide] = variance[...].astype(f32)
    for s in range(rows_at.shape[1]):
        top = rows_at[0, s]
        left = cols_at[0, s]
        root = lax.rsqrt(cut(var, top, left, side + 8, side)[:side, :side])
        root_out[s * side : (s + 1) * side, :] = root
        data = cut(image, top, left, side + 8, side)[:side, :side]
        data_out[s * side : (s + 1) * side, :] = data * root


def prepare(sender, request, rows_at, cols_at, science, variance, side, exps, capacity):
    high, wide = science.shape
    stamps = rows_at.shape[1]
    rows = capacity * (side // exps) + trailer_rows
    return pl.pallas_call(
        functools.partial(prepare_body, exps=exps, capacity=capacity),
        out_shape=(
            jax.ShapeDtypeStruct((request.shape[0] * exps, rows, side), bf16),
            jax.ShapeDtypeStruct((stamps * side, side), f32),
            jax.ShapeDtypeStruct((stamps * side, side), f32),
        ),
        in_specs=[smem()] * 4 + [vmem()] * 2,
        out_specs=(vmem(),) * 3,
        scratch_shapes=[pltpu.VMEM((high + 8, wide + 2 * side), f32)] * 2,
        compiler_params=pltpu.CompilerParams(vmem_limit_bytes=24 * mib),
        name="prepare",
    )(sender, request, rows_at, cols_at, science, variance)


def normal_body(
    slot_of,
    rows_at,
    cols_at,
    arrived,
    col,
    row_rev,
    roots,
    data,
    gram_out,
    windows,
    frame,
    vert,
    design,
    *,
    count,
    across_blocks,
    taps,
):
    side = row_rev.shape[1]
    margin = taps // 2
    stamps = rows_at.shape[1]
    span = up(side + taps - 1, 16)
    padded_k = gram_out.shape[1]
    pitch = padded_k + 1
    lines_all = stamps * side
    sub = lax.broadcasted_iota(jnp.int32, (side, side), 0)
    lane = lax.broadcasted_iota(jnp.int32, (side, side), 1)

    frame[...] = jnp.zeros(frame.shape, f32)
    for b in range(slot_of.shape[0]):
        top = margin + (b // across_blocks) * side
        left = margin + (b % across_blocks) * side
        frame[top : top + side, left : left + side] = arrived[slot_of[b]].astype(f32)

    cuts = []
    for s in range(stamps):
        cuts.append(cut(frame, rows_at[0, s], cols_at[0, s], span, side).astype(bf16))
    design[pl.ds(count, lines_all, stride=pitch), :] = roots[...]
    design[pl.ds(count + 1, lines_all, stride=pitch), :] = data[...]
    for extra in range(count + 2, padded_k):
        design[pl.ds(extra, lines_all, stride=pitch), :] = jnp.zeros((lines_all, side), f32)

    group = vert.shape[0]
    for k in range(0, count, group):
        filters = []
        for a in range(group):
            line = jnp.broadcast_to(col[k + a : k + a + 1, :], (side, side))
            line = pltpu.roll(line, 0, 1, stride=1, stride_axis=0)
            first = jnp.where(lane >= sub, line, 0.0).astype(bf16)
            second = jnp.where(lane < sub, line, 0.0).astype(bf16)
            filters.append(jnp.concatenate([first, second[:, : span - side]], axis=1))
        filters = jnp.concatenate(filters, axis=0)
        for s in range(stamps):
            out = jnp.dot(filters, cuts[s], preferred_element_type=f32).astype(bf16)
            for a in range(group):
                vert[a, s * side : (s + 1) * side, :] = out[a * side : (a + 1) * side]
        for a in range(group):
            line = jnp.broadcast_to(row_rev[k + a : k + a + 1, :], (side, side))
            line = pltpu.roll(line, 0, 1, stride=1, stride_axis=0)
            first = jnp.where(lane <= sub, line, 0.0).astype(bf16)
            second = jnp.where(lane > sub, line, 0.0).astype(bf16)
            band = jnp.concatenate([first, second], axis=0)
            out = jnp.dot(vert[a], band, preferred_element_type=f32)
            design[pl.ds(k + a, lines_all, stride=pitch), :] = out * roots[...]

    lines = 16
    sets = 4

    def gram_step(step, total):
        start = pl.multiple_of(step * sets * lines * pitch, 8)
        tops = []
        lows = []
        for g in range(sets):
            top_set = []
            low_set = []
            for j in range(lines):
                line = design[pl.ds(start + (g * lines + j) * pitch, padded_k), :]
                top = line.astype(bf16)
                top_set.append(top)
                low_set.append((line - top.astype(f32)).astype(bf16))
            tops.append(jnp.concatenate(top_set, axis=1))
            lows.append(jnp.concatenate(low_set, axis=1))
        right = jnp.concatenate(tops, axis=0)
        left = jnp.concatenate([right] + lows, axis=0)
        return total + lax.dot_general(
            left, right, (((1,), (1,)), ((), ())), preferred_element_type=f32
        )

    total = lax.fori_loop(
        0,
        lines_all // (lines * sets),
        gram_step,
        jnp.zeros((2 * sets * padded_k, sets * padded_k), f32),
    )
    for h in range(2):
        part = jnp.zeros((padded_k, padded_k), f32)
        for g in range(sets):
            first = (h * sets + g) * padded_k
            part = part + total[first : first + padded_k, g * padded_k : (g + 1) * padded_k]
        gram_out[h * padded_k : (h + 1) * padded_k, :] = part

    step = side - taps + 1
    half = windows.shape[2]
    for c in range(windows.shape[0]):
        stage_rows = frame[:, c * step : c * step + side]
        design[: stage_rows.shape[0], :] = stage_rows
        for parity in range(2):
            windows[c, parity] = design[pl.ds(parity, half, stride=2), :]


def normal_matrix(
    slot_of, rows_at, cols_at, arrived, col, row_rev, roots, data, high, wide, count, taps
):
    side = row_rev.shape[1]
    stamps = rows_at.shape[1]
    padded_k = up(count + 2, 16)
    pairs = (taps + 2) // 2
    tall = up(high - side + 8 + up(side + taps - 1, 16), 16)
    tall = max(tall, up(high + 2 * pairs, 16))
    wins = -(-wide // (side - taps + 1))
    group = next(g for g in (4, 2, 1) if count % g == 0)
    return pl.pallas_call(
        functools.partial(normal_body, count=count, across_blocks=wide // side, taps=taps),
        out_shape=(
            jax.ShapeDtypeStruct((2 * padded_k, padded_k), f32),
            jax.ShapeDtypeStruct((wins, 2, tall // 2, side), f32),
        ),
        in_specs=[smem()] * 3 + [vmem()] * 5,
        out_specs=(vmem(),) * 2,
        scratch_shapes=[
            pltpu.VMEM((tall, wide + 2 * side), f32),
            pltpu.VMEM((group, stamps * side, 2 * side), bf16),
            pltpu.VMEM((stamps * side * (padded_k + 1), side), f32),
        ],
        compiler_params=pltpu.CompilerParams(vmem_limit_bytes=36 * mib),
        cost_estimate=cost(10_000_000_000, 8_000_000),
        name="normal_matrix",
    )(slot_of, rows_at, cols_at, arrived, col, row_rev, roots, data)


def subtract_body(
    sender,
    gram,
    frames,
    science,
    col_t,
    row_rev,
    coef_out,
    payload,
    window,
    image,
    bands,
    total,
    *,
    exps,
    capacity,
    count,
    taps,
    pixels,
):
    side = frames.shape[3]
    high, wide = science.shape
    padded_k = gram.shape[1]
    part = side // exps
    size = count + 1

    square = jnp.concatenate(
        [gram[...], jnp.zeros((2 * padded_k, side - padded_k), f32)], axis=1
    )
    cross = square[padded_k:]
    mirror = jnp.concatenate([cross, jnp.zeros((side - padded_k, side), f32)], axis=0).T
    system = (square[:padded_k] + cross + mirror[:padded_k]) / pixels
    sub = lax.broadcasted_iota(jnp.int32, (padded_k, side), 0)
    lane = lax.broadcasted_iota(jnp.int32, (padded_k, side), 1)
    system = jnp.where((sub < size) & (lane <= size), system, 0.0)
    system = system + jnp.where((sub == lane) & (sub < size), ridge_term, 0.0)

    for k in range(0, size, 4):
        block = range(min(4, size - k))
        cols = [jnp.broadcast_to(system[:, k + j : k + j + 1], system.shape) for j in block]
        rows = [system[k + j : k + j + 1, :] for j in block]
        core = [[cols[j][k + i : k + i + 1, :] for j in block] for i in block]
        for j in block:
            inverse = 1.0 / core[j][j]
            factor = jnp.where(sub == k + j, 0.0, cols[j] * inverse)
            system = system - factor * rows[j]
            for i in block[j + 1 :]:
                scale = core[i][j] * inverse
                rows[i] = rows[i] - scale * rows[j]
                for l in block[j + 1 :]:
                    core[i][l] = core[i][l] - scale * core[j][l]
                cols[i] = cols[i] - factor * core[j][i]
    pivot = jnp.sum(jnp.where(sub == lane, system, 0.0), axis=1, keepdims=True)
    solved = system[:, size : size + 1] / jnp.where(sub[:, :1] < size, pivot, 1.0)
    coef_out[...] = jnp.sum(jnp.where(sub == lane, solved, 0.0), axis=0, keepdims=True)
    background = solved[count : count + 1, :]
    basis_coef = jnp.where(sub[:, :1] < count, solved, 0.0)

    scaled = basis_coef * row_rev[...]
    kernel = jnp.zeros((col_t.shape[0], side), f32)
    for _ in range(3):
        piece = scaled.astype(bf16)
        scaled = scaled - piece.astype(f32)
        kernel = kernel + jnp.dot(col_t[...], piece, preferred_element_type=f32)
    kernel_sum = jnp.sum(jnp.sum(kernel, axis=1, keepdims=True), axis=0, keepdims=True)
    rounded = kernel.astype(bf16).astype(f32)

    zero_band = jnp.zeros((side, side), bf16)

    def band(i):
        if i < 0 or i >= taps:
            return zero_band
        line = jnp.broadcast_to(rounded[i : i + 1, :], (side, side))
        return pltpu.roll(line, 0, 1, stride=1, stride_axis=0).astype(bf16)

    pairs = (taps + 2) // 2
    made = {i: band(i) for i in range(-1, 2 * pairs)}
    for q in range(pairs):
        for a in range(2):
            for b in range(2):
                bands[
                    q * 2 * side + a * side : q * 2 * side + (a + 1) * side,
                    b * side : (b + 1) * side,
                ] = made[2 * q + a - b]

    step = side - taps + 1
    rows_half = high // 2
    wins = frames.shape[0]
    for q in range(pairs):
        lhs = jnp.concatenate(
            [
                jnp.concatenate(
                    [frames[c, a, q : q + rows_half, :].astype(bf16) for a in range(2)], axis=1
                )
                for c in range(wins)
            ],
            axis=0,
        )
        out = jnp.dot(
            lhs, bands[q * 2 * side : (q + 1) * 2 * side, :], preferred_element_type=f32
        )
        if q:
            out = out + total[...]
        if q < pairs - 1:
            total[...] = out
    for c in range(wins):
        rows = out[c * rows_half : (c + 1) * rows_half]
        window[c, pl.ds(0, rows_half, stride=2), :] = rows[:, :side]
        window[c, pl.ds(1, rows_half, stride=2), :] = rows[:, side:]
        keep = min(step, wide - c * step)
        image[:, c * step : c * step + keep] = window[c, :, :keep]
    image[...] = science[...].astype(f32) - image[...] - background

    store_parts(sender, image, payload, side, exps, capacity, wide // side)
    line_at = lax.broadcasted_iota(jnp.int32, (trailer_rows, side), 0)
    trailer = jnp.zeros((trailer_rows, side), f32)
    rest = kernel_sum
    for p in range(3):
        piece = rest.astype(bf16).astype(f32)
        rest = rest - piece
        trailer = jnp.where(line_at == p, piece, trailer)
    trailer = trailer.astype(bf16)

    def put(d, carry):
        payload[d, capacity * part :, :] = trailer
        return carry

    lax.fori_loop(0, payload.shape[0], put, 0, unroll=4)


def subtract(
    sender, gram, frames, science, col_t, row_rev, peers, exps, capacity, count, taps, pixels
):
    wins, _, _, side = frames.shape
    high, wide = science.shape
    part = side // exps
    pairs = (taps + 2) // 2
    body = functools.partial(
        subtract_body, exps=exps, capacity=capacity, count=count, taps=taps, pixels=pixels
    )
    return pl.pallas_call(
        body,
        out_shape=(
            jax.ShapeDtypeStruct((1, side), f32),
            jax.ShapeDtypeStruct(
                (peers * exps, capacity * part + trailer_rows, side), bf16
            ),
        ),
        in_specs=[smem()] + [vmem()] * 5,
        out_specs=(vmem(), vmem()),
        scratch_shapes=[
            pltpu.VMEM((wins, high, side), f32),
            pltpu.VMEM((high, wide), f32),
            pltpu.VMEM((pairs * 2 * side, 2 * side), bf16),
            pltpu.VMEM((wins * high // 2, 2 * side), f32),
        ],
        compiler_params=pltpu.CompilerParams(vmem_limit_bytes=24 * mib),
        cost_estimate=cost(5_000_000_000, 4_000_000),
        name="subtract",
    )(sender, gram, frames, science, col_t, row_rev)


def split2(value):
    top = value.astype(bf16)
    return top, (value - top.astype(f32)).astype(bf16)


def score_body(
    table,
    slot_of,
    payload,
    down,
    over,
    parts,
    out,
    var_out,
    padded,
    sideways,
    var_total,
    *,
    side,
    taps,
    part,
    capacity,
):
    add_variance(table, parts, var_out, var_total, part, capacity)
    high, wide = out.shape
    margin = taps // 2
    span = up(side + taps - 1, 16)
    across_blocks = wide // side
    exps = side // part
    padded[...] = jnp.zeros(padded.shape, f32)
    for b in range(slot_of.shape[0]):
        slot = slot_of[b]
        row = pl.multiple_of((slot % capacity) * part, part)
        left = margin + (b % across_blocks) * side
        for q in range(exps):
            top = (b // across_blocks) * side + q * part
            block = payload[(slot // capacity) * exps + q, pl.ds(row, part), :]
            padded[top : top + part, left : left + side] = block.astype(f32)
    line = jnp.broadcast_to(over[...], (2 * side, 2 * side))
    band = pltpu.roll(line, 0, 1, stride=1, stride_axis=0)[:, :side]
    both = jnp.concatenate(split2(band), axis=1)
    sideways[...] = jnp.zeros(sideways.shape, f32)
    for c in range(wide // side):
        window = padded[:, c * side : (c + 2) * side].astype(bf16)
        got = jnp.dot(window, both, preferred_element_type=f32)
        sideways[margin : margin + high, c * side : (c + 1) * side] = got[:, :side] + got[:, side:]
    line = jnp.broadcast_to(down[...], (side, 2 * side))
    band = pltpu.roll(line, 0, 1, stride=1, stride_axis=0)[:, :span]
    top, low = split2(band)
    for r in range(high // side):
        data_top, data_low = split2(sideways[r * side : r * side + span, :])
        got = jnp.dot(top, data_top, preferred_element_type=f32)
        got = got + jnp.dot(top, data_low, preferred_element_type=f32)
        got = got + jnp.dot(low, data_top, preferred_element_type=f32)
        out[r * side : (r + 1) * side, :] = got


def score(
    table, slot_of, payload, down, over_rev, parts, high, wide, taps, tract, part, capacity
):
    side = payload.shape[2]
    span = up(side + taps - 1, 16)
    return pl.pallas_call(
        functools.partial(score_body, side=side, taps=taps, part=part, capacity=capacity),
        out_shape=(
            jax.ShapeDtypeStruct((high, wide), f32),
            jax.ShapeDtypeStruct((tract, part, side), f32),
        ),
        in_specs=[smem()] * 2 + [vmem()] * 4,
        out_specs=(vmem(),) * 2,
        scratch_shapes=[
            pltpu.VMEM((high, wide + side), f32),
            pltpu.VMEM((high - side + span, wide), f32),
            pltpu.VMEM((tract + 1, part, side), f32),
        ],
        compiler_params=pltpu.CompilerParams(vmem_limit_bytes=24 * mib),
        cost_estimate=cost(2_000_000_000, 2_000_000),
        name="score",
    )(table, slot_of, payload, down, over_rev, parts)


def add_variance(table, parts, out, total, part, capacity):
    total[...] = jnp.zeros(total.shape, f32)
    tract = out.shape[0]

    def one(j, carry):
        block = table[j // capacity, j % capacity] - 1
        block = jnp.where(block < 0, tract, block)
        row = pl.multiple_of((j % capacity) * part, part)
        total[block] += parts[j // capacity, pl.ds(row, part), :].astype(f32)
        return carry

    lax.fori_loop(0, parts.shape[0] * capacity, one, 0, unroll=8)
    out[...] = total[:tract]


def combine_body(table, parts, var_sum, var_template, out, total, gain, *, part, capacity):
    total[...] = jnp.zeros(total.shape, f32)
    gain[...] = jnp.zeros(gain.shape, f32)
    tract = out.shape[0]

    def one(d, carry):
        tail = parts[d, capacity * part :, :].astype(f32)
        kernel_sum = tail[0:1] + tail[1:2] + tail[2:3]
        square = jnp.broadcast_to(kernel_sum * kernel_sum, gain.shape[1:])
        for c in range(capacity):
            block = table[d, c] - 1
            block = jnp.where(block < 0, tract, block)
            total[block] += parts[d, c * part : (c + 1) * part, :].astype(f32)
            gain[block] += square
        return carry

    lax.fori_loop(0, parts.shape[0], one, 0, unroll=4)
    for t in range(tract):
        variance = var_sum[t] + gain[t, 0:1, :] * var_template[t].astype(f32)
        out[t] = (total[t] * lax.rsqrt(jnp.maximum(variance, 1.0))).astype(bf16)


def combine(table, parts, var_sum, var_template, part, capacity):
    tract, _, side = var_sum.shape
    return pl.pallas_call(
        functools.partial(combine_body, part=part, capacity=capacity),
        out_shape=jax.ShapeDtypeStruct((tract, part, side), bf16),
        in_specs=[smem(), vmem(), vmem(), vmem()],
        out_specs=vmem(),
        scratch_shapes=[
            pltpu.VMEM((tract + 1, part, side), f32),
            pltpu.VMEM((tract + 1, 8, side), f32),
        ],
        compiler_params=pltpu.CompilerParams(vmem_limit_bytes=16 * mib),
        name="combine",
    )(table, parts, var_sum, var_template)


def join_body(places, *refs, part, chunk):
    out, held, sems = refs[-3:]
    copies = []
    for i in range(out.shape[0] // chunk):
        blocks = pl.ds(i * chunk, chunk)
        for d, ref in enumerate(refs[:-3]):
            row = pl.multiple_of(places[d] * part, part)
            held[blocks, pl.ds(row, part), :] = ref[blocks].astype(f32)
        copies.append(pltpu.make_async_copy(held.at[blocks], out.at[blocks], sems.at[i]))
        copies[-1].start()
    for copy in copies:
        copy.wait()


def join_parts(places, parts):
    tract, part, side = parts[0].shape
    exps = len(parts)
    chunk = 8 if tract % 8 == 0 else tract
    return pl.pallas_call(
        functools.partial(join_body, part=part, chunk=chunk),
        out_shape=jax.ShapeDtypeStruct((tract, part * exps, side), f32),
        in_specs=[smem()] + [vmem()] * exps,
        out_specs=pl.BlockSpec(memory_space=pl.ANY),
        scratch_shapes=[
            pltpu.VMEM((tract, part * exps, side), f32),
            pltpu.SemaphoreType.DMA((tract // chunk,)),
        ],
        compiler_params=pltpu.CompilerParams(vmem_limit_bytes=16 * mib),
        name="join_parts",
    )(places, *parts)


def local(
    template,
    template_var,
    science,
    science_var,
    routes_src,
    routes_blk,
    stamp_rows,
    stamp_cols,
    basis_col,
    basis_row,
    psf_col,
    psf_row,
):
    peers = lax.axis_size("det")
    exps = lax.axis_size("exp")
    me = lax.axis_index("exp").astype(jnp.int32)
    tract, side, _ = template.shape
    science_img = science[0]
    variance_img = science_var[0]
    blocks_dev = routes_src.shape[1]
    count, taps = basis_col.shape
    capacity = max(2, -(-blocks_dev // peers))
    slots = peers * capacity
    part = side // exps

    slot_of, sender, request = route_tables(routes_src, routes_blk, peers, capacity)
    asked = lax.all_to_all(request, "det", split_axis=0, concat_axis=0, tiled=True)
    picked = pick_blocks(asked, template, slots, capacity)
    arrived = lax.all_to_all(picked, "det", split_axis=0, concat_axis=0, tiled=True)

    padded_k = up(count + 2, 16)
    col_t = jnp.pad(basis_col.T, ((0, up(taps, 16) - taps), (0, padded_k - count)))
    col = jnp.pad(basis_col.astype(f32), ((0, padded_k - count), (0, side - taps)))
    row_rev = jnp.pad(
        basis_row.astype(f32)[:, ::-1], ((0, padded_k - count), (side - taps, 0))
    )
    row_rev = jnp.roll(row_rev, 1, axis=1)
    over_rev = jnp.roll(jnp.pad(psf_row[:, ::-1], ((0, 0), (2 * side - taps, 0))), 1, axis=1)
    down = jnp.pad(psf_col, ((0, 0), (0, 2 * side - taps)))
    var_parts, roots, data = prepare(
        sender, request, stamp_rows, stamp_cols, science_img, variance_img, side, exps, capacity
    )
    var_back = lax.all_to_all(
        var_parts, ("det", "exp"), split_axis=0, concat_axis=0, tiled=True
    )
    table = var_back[:, capacity * part, :capacity].astype(f32).astype(jnp.int32)

    high, wide = science_img.shape
    gram, frames = normal_matrix(
        slot_of,
        stamp_rows,
        stamp_cols,
        arrived,
        col,
        row_rev,
        roots,
        data,
        high,
        wide,
        count,
        taps,
    )
    coef, payload = subtract(
        sender,
        gram,
        frames,
        science_img,
        col_t,
        row_rev,
        peers,
        exps,
        capacity,
        count,
        taps,
        stamp_rows.shape[1] * side * side,
    )
    diff_back = lax.all_to_all(payload, ("det", "exp"), split_axis=0, concat_axis=0, tiled=True)
    scored, var_sum = score(
        table,
        slot_of,
        payload,
        down,
        over_rev,
        var_back,
        high,
        wide,
        taps,
        tract,
        part,
        capacity,
    )
    var_template = lax.dynamic_slice_in_dim(template_var, me * part, part, 1)
    mine = combine(table, diff_back, var_sum, var_template, part, capacity)

    if exps & (exps - 1) == 0:
        held = [mine]
        reach = exps // 2
        gaps = [0]
        while reach:
            pairs = [(e, e ^ reach) for e in range(exps)]
            held = held + [lax.ppermute(h, "exp", pairs) for h in held]
            gaps = gaps + [g ^ reach for g in gaps]
            reach //= 2
        places = jnp.stack([me ^ g for g in gaps])
    else:
        held = [mine]
        for gap in range(1, exps):
            pairs = [(e, (e + gap) % exps) for e in range(exps)]
            held.append(lax.ppermute(mine, "exp", pairs))
        places = jnp.stack([(me - g) % exps for g in range(exps)])
    significance = join_parts(places, held)
    return (significance, scored[None], coef[:, : count + 1])


def solution(mesh):
    placed = (
        P("det", None, None),
        P("det", None, None),
        P("exp", "det", None),
        P("exp", "det", None),
        P("exp", "det"),
        P("exp", "det"),
        P("exp", "det"),
        P("exp", "det"),
        P(),
        P(),
        P("exp", None),
        P("exp", None),
    )
    return jax.shard_map(
        local,
        mesh=mesh,
        in_specs=placed,
        out_specs=(P("det", None, None), P("exp", "det", None), P("exp", "det")),
        check_vma=False,
    )
```

profile of v0, /device:TPU:1, one launch (start us, length us, event | category | flops | bytes accessed | tf_op | source)
XLA Modules:
  0.0 94.4 jit_solution(12600649857933617773)
XLA Ops:
  0.7 1.5 %route_tables.1 = (s32[16]{0:T(128)}, s32[16]{0:T(128)}, s32[8,1,2]{2,1,0:T(1,128)}) custom-call(s32[1,16]{1,0:T(1,128)} %src.1, s32[1,16]{1,0:T(1,128)} %blk.1), custom_call_target="tpu_custom_call" | custom-call | tf_op jit(solution)/shard_map/route_tables/pallas_call | solution.py:49
  2.3 11.7 %all_to_all.20.asked = s32[8,1,2]{2,1,0:T(1,128)} all-to-all(s32[8,1,2]{2,1,0:T(1,128)} %get-tuple-element.16.request), channel_id=1, replica_groups=mesh['det'=8,'exp'=4] {'det'}, dimensions={0} | all-to-all | bytes 128 | tf_op jit(solution)/shard_map/all_to_all | solution.py:674
  14.0 2.7 %pick_blocks.1 = bf16[16,128,128]{2,1,0:T(8,128)(2,1)} custom-call(s32[8,1,2]{2,1,0:T(1,128)} %all_to_all.20.asked, bf16[32,128,128]{2,1,0:T(8,128)(2,1)} %template.1), custom_call_target="tpu_custom_call" | custom-call | tf_op jit(solution)/shard_map/pick_blocks/pallas_call | solution.py:74
  16.7 3.5 %all-to-all-start.2 = ((bf16[16,128,128]{2,1,0:T(8,128)(2,1)}), bf16[16,128,128]{2,1,0:T(8,128)(2,1)S(1)}, u32[]{:S(2)}, u32[]{:S(2)}) async-start(bf16[16,128,128]{2,1,0:T(8,128)(2,1)} %pick_blocks.1), calls=%async_computation.2 | async-start | bytes 1048576 | tf_op jit(solution)/shard_map/all_to_all | solution.py:676
  20.2 0.1 copy.21
  20.5 2.2 %prepare.1 = (bf16[32,72,128]{2,1,0:T(8,128)(2,1)}, f32[512,128]{1,0:T(8,128)S(1)}, f32[512,128]{1,0:T(8,128)S(1)}) custom-call(s32[16]{0:T(128)S(1)} %copy-done.6, s32[8,1,2]{2,1,0:T(1,128)S(1)} %copy-done.3, s32[1,4]{1,0:T(1,128)S(1)} %copy-done.4, s32[1,4]{1,0:T(1,128)S(1)} %copy-done.5, bf16[256,1024]{1,0:T(8,128)(2,1)S(1)} %bitcast.12, ...), custom_call_target="tpu_custom_call" | custom-call | tf_op jit(solution)/shard_map/prepare/pallas_call | solution.py:163
  22.8 0.7 copy-done.7
  23.7 9.7 %all-to-all-done.2.arrived = bf16[16,128,128]{2,1,0:T(8,128)(2,1)S(1)} async-done(((bf16[16,128,128]{2,1,0:T(8,128)(2,1)}), bf16[16,128,128]{2,1,0:T(8,128)(2,1)S(1)}, u32[]{:S(2)}, u32[]{:S(2)}) %all-to-all-start.2) | async-done | bytes 524320 | tf_op jit(solution)/shard_map/all_to_all | solution.py:676
  33.4 5.6 %all-to-all-start = ((bf16[32,72,128]{2,1,0:T(8,128)(2,1)}), bf16[32,72,128]{2,1,0:T(8,128)(2,1)S(1)}, u32[]{:S(2)}, u32[]{:S(2)}) async-start(bf16[32,72,128]{2,1,0:T(8,128)(2,1)} %get-tuple-element.17), calls=%async_computation | async-start | bytes 1179648 | tf_op jit(solution)/shard_map/all_to_all | solution.py:690
  39.0 0.9 copy-done.8
  40.0 13.0 %normal_matrix.1 = (f32[96,48]{1,0:T(8,128)S(1)}, f32[10,2,152,128]{3,2,1,0:T(8,128)S(1)}) custom-call(s32[16]{0:T(128)S(1)} %copy-done.9, s32[1,4]{1,0:T(1,128)S(1)} %copy-done.4, s32[1,4]{1,0:T(1,128)S(1)} %copy-done.5, bf16[16,128,128]{2,1,0:T(8,128)(2,1)S(1)} %all-to-all-done.2.arrived, f32[48,128]{1,0:T(8,128)S(1)} %pad_convert_fusion.col, ...), custom_call_target="tpu_custom_call" | custom-call | flops 10000000000 | bytes 8000000 | tf_op jit(solution)/shard_map/normal_matrix/pallas_call | solution.py:300
  53.0 5.9 %subtract.1 = (f32[1,128]{1,0:T(1,128)}, bf16[32,72,128]{2,1,0:T(8,128)(2,1)}) custom-call(s32[16]{0:T(128)S(1)} %copy-done.6, f32[96,48]{1,0:T(8,128)S(1)} %get-tuple-element.21.gram, f32[10,2,152,128]{3,2,1,0:T(8,128)S(1)} %get-tuple-element.22.frames, bf16[256,1024]{1,0:T(8,128)(2,1)S(1)} %bitcast.13, bf16[32,48]{1,0:T(8,128)(2,1)S(1)} %pad.25.col_t, ...), custom_call_target="tpu_custom_call" | custom-call | flops 5000000000 | bytes 4000000 | tf_op jit(solution)/shard_map/subtract/pallas_call | solution.py:459
  58.9 5.8 %all-to-all-start.3 = ((bf16[32,72,128]{2,1,0:T(8,128)(2,1)}), bf16[32,72,128]{2,1,0:T(8,128)(2,1)S(1)}, u32[]{:S(2)}, u32[]{:S(2)}) async-start(bf16[32,72,128]{2,1,0:T(8,128)(2,1)} %get-tuple-element.23.payload), calls=%async_computation.3 | async-start | bytes 1179648 | tf_op jit(solution)/shard_map/all_to_all | solution.py:724
  64.8 0.1 rev.7
  65.0 0.1 pad_maximum_fusion.1.over
  65.1 3.9 %score.1 = (f32[256,1024]{1,0:T(8,128)}, f32[32,32,128]{2,1,0:T(8,128)S(1)}) custom-call(s32[32,2]{1,0:T(8,128)S(1)} %bitcast.14, s32[16]{0:T(128)S(1)} %copy-done.9, bf16[32,72,128]{2,1,0:T(8,128)(2,1)} %get-tuple-element.23.payload, f32[1,256]{1,0:T(1,128)S(1)} %pad.26.down, f32[1,256]{1,0:T(1,128)S(1)} %pad_maximum_fusion.1.over, ...), custom_call_target="tpu_custom_call" | custom-call | flops 2000000000 | bytes 2000000 | tf_op jit(solution)/shard_map/score/pallas_call | solution.py:543
  69.0 12.2 %all-to-all-done.3.parts = bf16[32,72,128]{2,1,0:T(8,128)(2,1)S(1)} async-done(((bf16[32,72,128]{2,1,0:T(8,128)(2,1)}), bf16[32,72,128]{2,1,0:T(8,128)(2,1)S(1)}, u32[]{:S(2)}, u32[]{:S(2)}) %all-to-all-start.3) | async-done | bytes 589856 | tf_op jit(solution)/shard_map/all_to_all | solution.py:724
  81.2 1.3 %combine.1.refs_0_ = bf16[32,32,128]{2,1,0:T(8,128)(2,1)S(1)} custom-call(s32[32,2]{1,0:T(8,128)S(1)} %bitcast.15, bf16[32,72,128]{2,1,0:T(8,128)(2,1)S(1)} %all-to-all-done.3.parts, f32[32,32,128]{2,1,0:T(8,128)S(1)} %get-tuple-element.24.var_sum, bf16[32,32,128]{2,1,0:T(8,128)(2,1)S(1)} %constant_dynamic-slice_fusion.var_template), custom_call_target="tpu_custom_call" | custom-call | tf_op jit(solution)/shard_map/combine/pallas_call | solution.py:601
  82.5 1.3 %collective-permute-start = (bf16[32,32,128]{2,1,0:T(8,128)(2,1)S(1)}, bf16[32,32,128]{2,1,0:T(8,128)(2,1)S(1)}, u32[]{:S(2)}, u32[]{:S(2)}) collective-permute-start(bf16[32,32,128]{2,1,0:T(8,128)(2,1)S(1)} %combine.1.refs_0_), channel_id=1, source_target_pairs={{0,2},{1,3},{2,0},{3,1},{4,6},{5,7},{6,4},{7,5},{8,10},{9,11},{10,... | collective-permute-start | bytes 786440 | tf_op jit(solution)/shard_map/ppermute | solution.py:748
  83.8 0.4 collective-permute-start.1
  84.3 5.7 %collective-permute-done.refs_1_ = bf16[32,32,128]{2,1,0:T(8,128)(2,1)S(1)} collective-permute-done((bf16[32,32,128]{2,1,0:T(8,128)(2,1)S(1)}, bf16[32,32,128]{2,1,0:T(8,128)(2,1)S(1)}, u32[]{:S(2)}, u32[]{:S(2)}) %collective-permute-start) | collective-permute-done | bytes 262176 | tf_op jit(solution)/shard_map/ppermute | solution.py:748
  89.9 1.4 %collective-permute-start.2 = (bf16[32,32,128]{2,1,0:T(8,128)(2,1)S(1)}, bf16[32,32,128]{2,1,0:T(8,128)(2,1)S(1)}, u32[]{:S(2)}, u32[]{:S(2)}) collective-permute-start(bf16[32,32,128]{2,1,0:T(8,128)(2,1)S(1)} %collective-permute-done.refs_1_), channel_id=1, source_target_pairs={{0,1},{1,0},{2,3},{3,2},{4,5},{5,4},{6,7},{7,6},{8,9},{9,8},{10,11... | collective-permute-start | bytes 786440 | tf_op jit(solution)/shard_map/ppermute | solution.py:748
  91.4 1.1 %collective-permute-done.2.refs_3_ = bf16[32,32,128]{2,1,0:T(8,128)(2,1)S(1)} collective-permute-done((bf16[32,32,128]{2,1,0:T(8,128)(2,1)S(1)}, bf16[32,32,128]{2,1,0:T(8,128)(2,1)S(1)}, u32[]{:S(2)}, u32[]{:S(2)}) %collective-permute-start.2) | collective-permute-done | bytes 262176 | tf_op jit(solution)/shard_map/ppermute | solution.py:748
  92.5 1.9 %join_parts.1 = f32[32,128,128]{2,1,0:T(8,128)} custom-call(s32[4]{0:T(128)S(1)} %pad_add_fusion.places, bf16[32,32,128]{2,1,0:T(8,128)(2,1)S(1)} %combine.1.refs_0_, bf16[32,32,128]{2,1,0:T(8,128)(2,1)S(1)} %collective-permute-done.refs_1_, bf16[32,32,128]{2,1,0:T(8,128)(2,1)S(1)} %collective-permute-done.1.refs_2_, ...), custom_call_target="tpu_custom_call" | custom-call | tf_op jit(solution)/shard_map/join_parts/pallas_call | solution.py:633
  (40 shorter events, 0.7 us)
Async XLA Ops:
  0.6 64.4 %copy-start = (bf16[32,128,128]{2,1,0:T(8,128)(2,1)S(1)}, bf16[32,128,128]{2,1,0:T(8,128)(2,1)}, u32[]{:S(2)}) copy-start(bf16[32,128,128]{2,1,0:T(8,128)(2,1)} %param.13) | copy-start | bytes 3145732
  0.6 19.5 %copy-start.10 = (bf16[40,21]{0,1:T(8,128)(2,1)S(1)}, bf16[40,21]{0,1:T(8,128)(2,1)}, u32[]{:S(2)}) copy-start(bf16[40,21]{0,1:T(8,128)(2,1)} %param.20) | copy-start | bytes 5044
  0.7 19.6 %copy-start.11 = (bf16[40,21]{0,1:T(8,128)(2,1)S(1)}, bf16[40,21]{0,1:T(8,128)(2,1)}, u32[]{:S(2)}) copy-start(bf16[40,21]{0,1:T(8,128)(2,1)} %param.21) | copy-start | bytes 5044
  0.7 19.8 %copy-start.5 = (s32[1,4]{1,0:T(1,128)S(1)}, s32[1,4]{1,0:T(1,128)}, u32[]{:S(2)}) copy-start(s32[1,4]{1,0:T(1,128)} %cols_at.3) | copy-start | bytes 52
  0.7 19.8 %copy-start.4 = (s32[1,4]{1,0:T(1,128)S(1)}, s32[1,4]{1,0:T(1,128)}, u32[]{:S(2)}) copy-start(s32[1,4]{1,0:T(1,128)} %rows_at.3) | copy-start | bytes 52
  0.7 19.8 %copy-start.1 = (bf16[1,256,1024]{2,1,0:T(8,128)(2,1)S(1)}, bf16[1,256,1024]{2,1,0:T(8,128)(2,1)}, u32[]{:S(2)}) copy-start(bf16[1,256,1024]{2,1,0:T(8,128)(2,1)} %param.15) | copy-start | bytes 1572868
  0.7 19.8 %copy-start.2 = (bf16[1,256,1024]{2,1,0:T(8,128)(2,1)S(1)}, bf16[1,256,1024]{2,1,0:T(8,128)(2,1)}, u32[]{:S(2)}) copy-start(bf16[1,256,1024]{2,1,0:T(8,128)(2,1)} %param.14) | copy-start | bytes 1572868
  2.3 18.3 %copy-start.3 = (s32[8,1,2]{2,1,0:T(1,128)S(1)}, s32[8,1,2]{2,1,0:T(1,128)}, u32[]{:S(2)}) copy-start(s32[8,1,2]{2,1,0:T(1,128)} %get-tuple-element.16.request) | copy-start | bytes 196
  2.3 18.3 %copy-start.6 = (s32[16]{0:T(128)S(1)}, s32[16]{0:T(128)}, u32[]{:S(2)}) copy-start(s32[16]{0:T(128)} %get-tuple-element.15.sender) | copy-start | bytes 196
  16.7 22.3 %copy-start.9 = (s32[16]{0:T(128)S(1)}, s32[16]{0:T(128)}, u32[]{:S(2)}) copy-start(s32[16]{0:T(128)} %get-tuple-element.18.slot_of) | copy-start | bytes 196
  16.7 16.7 %all-to-all-start.2 = ((bf16[16,128,128]{2,1,0:T(8,128)(2,1)}), bf16[16,128,128]{2,1,0:T(8,128)(2,1)S(1)}, u32[]{:S(2)}, u32[]{:S(2)}) async-start(bf16[16,128,128]{2,1,0:T(8,128)(2,1)} %pick_blocks.1), calls=%async_computation.2 | async-start | bytes 1048576 | tf_op jit(solution)/shard_map/all_to_all | solution.py:676
  22.7 0.7 copy-start.7
  33.4 25.6 %all-to-all-start = ((bf16[32,72,128]{2,1,0:T(8,128)(2,1)}), bf16[32,72,128]{2,1,0:T(8,128)(2,1)S(1)}, u32[]{:S(2)}, u32[]{:S(2)}) async-start(bf16[32,72,128]{2,1,0:T(8,128)(2,1)} %get-tuple-element.17), calls=%async_computation | async-start | bytes 1179648 | tf_op jit(solution)/shard_map/all_to_all | solution.py:690
  39.0 1.0 %copy-start.8 = (f32[512,128]{1,0:T(8,128)S(1)}, f32[512,128]{1,0:T(8,128)}, u32[]{:S(2)}) copy-start(f32[512,128]{1,0:T(8,128)} %copy-done.7) | copy-start | bytes 786436
  53.0 11.8 %copy-start.12 = (f32[1,21]{1,0:T(1,128)S(1)}, f32[1,21]{1,0:T(1,128)}, u32[]{:S(2)}) copy-start(f32[1,21]{1,0:T(1,128)} %param.23) | copy-start | bytes 256
  53.0 11.9 %copy-start.13 = (f32[1,21]{1,0:T(1,128)S(1)}, f32[1,21]{1,0:T(1,128)}, u32[]{:S(2)}) copy-start(f32[1,21]{1,0:T(1,128)} %param.22) | copy-start | bytes 256
  58.9 22.3 %all-to-all-start.3 = ((bf16[32,72,128]{2,1,0:T(8,128)(2,1)}), bf16[32,72,128]{2,1,0:T(8,128)(2,1)S(1)}, u32[]{:S(2)}, u32[]{:S(2)}) async-start(bf16[32,72,128]{2,1,0:T(8,128)(2,1)} %get-tuple-element.23.payload), calls=%async_computation.3 | async-start | bytes 1179648 | tf_op jit(solution)/shard_map/all_to_all | solution.py:724
  82.5 7.4 %collective-permute-start = (bf16[32,32,128]{2,1,0:T(8,128)(2,1)S(1)}, bf16[32,32,128]{2,1,0:T(8,128)(2,1)S(1)}, u32[]{:S(2)}, u32[]{:S(2)}) collective-permute-start(bf16[32,32,128]{2,1,0:T(8,128)(2,1)S(1)} %combine.1.refs_0_), channel_id=1, source_target_pairs={{0,2},{1,3},{2,0},{3,1},{4,6},{5,7},{6,4},{7,5},{8,10},{9,11},{10,... | collective-permute-start | bytes 786440 | tf_op jit(solution)/shard_map/ppermute | solution.py:748
  83.8 7.6 %collective-permute-start.1 = (bf16[32,32,128]{2,1,0:T(8,128)(2,1)S(1)}, bf16[32,32,128]{2,1,0:T(8,128)(2,1)S(1)}, u32[]{:S(2)}, u32[]{:S(2)}) collective-permute-start(bf16[32,32,128]{2,1,0:T(8,128)(2,1)S(1)} %combine.1.refs_0_), channel_id=1, source_target_pairs={{0,1},{1,0},{2,3},{3,2},{4,5},{5,4},{6,7},{7,6},{8,9},{9,8},{10,11... | collective-permute-start | bytes 786440 | tf_op jit(solution)/shard_map/ppermute | solution.py:748
  89.9 2.5 %collective-permute-start.2 = (bf16[32,32,128]{2,1,0:T(8,128)(2,1)S(1)}, bf16[32,32,128]{2,1,0:T(8,128)(2,1)S(1)}, u32[]{:S(2)}, u32[]{:S(2)}) collective-permute-start(bf16[32,32,128]{2,1,0:T(8,128)(2,1)S(1)} %collective-permute-done.refs_1_), channel_id=1, source_target_pairs={{0,1},{1,0},{2,3},{3,2},{4,5},{5,4},{6,7},{7,6},{8,9},{9,8},{10,11... | collective-permute-start | bytes 786440 | tf_op jit(solution)/shard_map/ppermute | solution.py:748
where the time goes:
time: 95.3 us; the launch traced here: 94.4 us
  Pallas kernels  32.4 us (34%)
  waiting for transfers between devices  28.7 us (30%)
  starting transfers between devices  18.1 us (19%)
  blocking collectives  11.7 us (12%)
  local copies, waits for them, and re-layouts  2.32 us (2%)
    pallas_call x1, Pallas kernels, normal_matrix(): pl.pallas_call(functools.partial(normal_body, count=count, across_blocks=...  13 us
    all_to_all x1, waiting for transfers between devices, local(): lax.all_to_all(payload, ('det', 'exp'), split_axis=0, concat_axis=0, tile...  12.2 us
    all_to_all x1, blocking collectives, local(): lax.all_to_all(request, 'det', split_axis=0, concat_axis=0, tiled=True)  11.7 us
    all_to_all x1, waiting for transfers between devices, local(): lax.all_to_all(picked, 'det', split_axis=0, concat_axis=0, tiled=True)  9.68 us
    ppermute x3, waiting for transfers between devices, local(): held = held + [lax.ppermute(h, 'exp', pairs) for h in held]  6.74 us
    pallas_call x1, Pallas kernels, subtract(): pl.pallas_call(body, out_shape=(jax.ShapeDtypeStruct((1, side), f32), jax...  5.9 us
    all_to_all x1, starting transfers between devices, local(): lax.all_to_all(payload, ('det', 'exp'), split_axis=0, concat_axis=0, tile...  5.83 us
    all_to_all x1, starting transfers between devices, local(): lax.all_to_all(var_parts, ('det', 'exp'), split_axis=0, concat_axis=0, ti...  5.62 us
  transfers between devices with their start and end apart: 6, of which 4 were waited for; matrix products, arithmetic and copies ran while one was open for 1% of the time, Pallas kernels for 27%

commit v1 on v0

--- a/solution.py
+++ b/solution.py
@@ -60,26 +60,26 @@
     )(routes_src, routes_blk)
 
 
-def pick_body(asked, template, out, sems, *, capacity):
-    copies = []
-    for s in range(out.shape[0]):
+def pick_body(asked, template, earlier, out, *, capacity):
+    del earlier
+
+    def one(s, carry):
         block = jnp.maximum(asked[s // capacity, 0, s % capacity] - 1, 0)
-        copies.append(pltpu.make_async_copy(template.at[block], out.at[s], sems.at[s]))
-        copies[-1].start()
-    for copy in copies:
-        copy.wait()
-
-
-def pick_blocks(asked, template, slots, capacity):
+        out[s] = template[block]
+        return carry
+
+    lax.fori_loop(0, out.shape[0], one, 0, unroll=True if out.shape[0] <= 32 else 4)
+
+
+def pick_blocks(asked, template, earlier, slots, capacity):
     return pl.pallas_call(
         functools.partial(pick_body, capacity=capacity),
         out_shape=jax.ShapeDtypeStruct((slots,) + template.shape[1:], template.dtype),
-        in_specs=[smem(), pl.BlockSpec(memory_space=pl.ANY)],
+        in_specs=[smem(), vmem(), pl.BlockSpec(memory_space=pl.ANY)],
         out_specs=vmem(),
-        scratch_shapes=[pltpu.SemaphoreType.DMA((slots,))],
-        compiler_params=pltpu.CompilerParams(vmem_limit_bytes=60 * mib),
+        compiler_params=pltpu.CompilerParams(vmem_limit_bytes=16 * mib),
         name="pick_blocks",
-    )(asked, template)
+    )(asked, template, earlier)
 
 
 def store_parts(sender, image, out, side, exps, capacity, across_blocks):
@@ -121,58 +121,22 @@
     return pltpu.roll(tile, lax.rem(height - (top - down), height), 0)
 
 
-def prepare_body(
-    sender,
-    request,
-    rows_at,
-    cols_at,
-    science,
-    variance,
-    parts_out,
-    root_out,
-    data_out,
-    image,
-    var,
-    *,
-    exps,
-    capacity,
-):
-    side = root_out.shape[1]
-    high, wide = science.shape
-    store_parts(sender, variance, parts_out, side, exps, capacity, wide // side)
-    store_requests(request, parts_out, side, exps, capacity)
-    image[:, wide:] = jnp.zeros((image.shape[0], image.shape[1] - wide), f32)
-    image[high:, :wide] = jnp.zeros((image.shape[0] - high, wide), f32)
-    image[:high, :wide] = science[...].astype(f32)
-    var[:, wide:] = jnp.ones((var.shape[0], var.shape[1] - wide), f32)
-    var[high:, :wide] = jnp.ones((var.shape[0] - high, wide), f32)
-    var[:high, :wide] = variance[...].astype(f32)
-    for s in range(rows_at.shape[1]):
-        top = rows_at[0, s]
-        left = cols_at[0, s]
-        root = lax.rsqrt(cut(var, top, left, side + 8, side)[:side, :side])
-        root_out[s * side : (s + 1) * side, :] = root
-        data = cut(image, top, left, side + 8, side)[:side, :side]
-        data_out[s * side : (s + 1) * side, :] = data * root
-
-
-def prepare(sender, request, rows_at, cols_at, science, variance, side, exps, capacity):
-    high, wide = science.shape
-    stamps = rows_at.shape[1]
+def prepare_body(sender, request, variance, out, *, side, exps, capacity):
+    store_parts(sender, variance, out, side, exps, capacity, variance.shape[1] // side)
+    store_requests(request, out, side, exps, capacity)
+
+
+def prepare(sender, request, variance, side, exps, capacity):
     rows = capacity * (side // exps) + trailer_rows
     return pl.pallas_call(
-        functools.partial(prepare_body, exps=exps, capacity=capacity),
-        out_shape=(
-            jax.ShapeDtypeStruct((request.shape[0] * exps, rows, side), bf16),
-            jax.ShapeDtypeStruct((stamps * side, side), f32),
-            jax.ShapeDtypeStruct((stamps * side, side), f32),
-        ),
-        in_specs=[smem()] * 4 + [vmem()] * 2,
-        out_specs=(vmem(),) * 3,
-        scratch_shapes=[pltpu.VMEM((high + 8, wide + 2 * side), f32)] * 2,
-        compiler_params=pltpu.CompilerParams(vmem_limit_bytes=24 * mib),
+        functools.partial(prepare_body, side=side, exps=exps, capacity=capacity),
+        out_shape=jax.ShapeDtypeStruct((request.shape[0] * exps, rows, side), bf16),
+        in_specs=[smem()] * 2 + [vmem()],
+        out_specs=vmem(),
+        compiler_params=pltpu.CompilerParams(vmem_limit_bytes=16 * mib),
+        cost_estimate=cost(0, 3_000_000),
         name="prepare",
-    )(sender, request, rows_at, cols_at, science, variance)
+    )(sender, request, variance)
 
 
 def normal_body(
@@ -182,13 +146,16 @@
     arrived,
     col,
     row_rev,
-    roots,
-    data,
+    science,
+    variance,
     gram_out,
     windows,
     frame,
     vert,
     design,
+    image,
+    var,
+    roots,
     *,
     count,
     across_blocks,
@@ -213,8 +180,22 @@
     cuts = []
     for s in range(stamps):
         cuts.append(cut(frame, rows_at[0, s], cols_at[0, s], span, side).astype(bf16))
-    design[pl.ds(count, lines_all, stride=pitch), :] = roots[...]
-    design[pl.ds(count + 1, lines_all, stride=pitch), :] = data[...]
+    high, wide = science.shape
+    image[:, wide:] = jnp.zeros((image.shape[0], image.shape[1] - wide), f32)
+    image[high:, :wide] = jnp.zeros((image.shape[0] - high, wide), f32)
+    image[:high, :wide] = science[...].astype(f32)
+    var[:, wide:] = jnp.ones((var.shape[0], var.shape[1] - wide), f32)
+    var[high:, :wide] = jnp.ones((var.shape[0] - high, wide), f32)
+    var[:high, :wide] = variance[...].astype(f32)
+    for s in range(stamps):
+        top = rows_at[0, s]
+        left = cols_at[0, s]
+        root = lax.rsqrt(cut(var, top, left, side + 8, side)[:side, :side])
+        roots[s * side : (s + 1) * side, :] = root
+        place = pl.ds(s * side * pitch + count, side, stride=pitch)
+        design[place, :] = root
+        place = pl.ds(s * side * pitch + count + 1, side, stride=pitch)
+        design[place, :] = root * cut(image, top, left, side + 8, side)[:side, :side]
     for extra in range(count + 2, padded_k):
         design[pl.ds(extra, lines_all, stride=pitch), :] = jnp.zeros((lines_all, side), f32)
 
@@ -246,36 +227,29 @@
 
     def gram_step(step, total):
         start = pl.multiple_of(step * sets * lines * pitch, 8)
-        tops = []
-        lows = []
+        rows = []
         for g in range(sets):
-            top_set = []
-            low_set = []
-            for j in range(lines):
-                line = design[pl.ds(start + (g * lines + j) * pitch, padded_k), :]
-                top = line.astype(bf16)
-                top_set.append(top)
-                low_set.append((line - top.astype(f32)).astype(bf16))
-            tops.append(jnp.concatenate(top_set, axis=1))
-            lows.append(jnp.concatenate(low_set, axis=1))
-        right = jnp.concatenate(tops, axis=0)
-        left = jnp.concatenate([right] + lows, axis=0)
+            row = [
+                design[pl.ds(start + (g * lines + j) * pitch, padded_k), :].astype(bf16)
+                for j in range(lines)
+            ]
+            rows.append(jnp.concatenate(row, axis=1))
+        both = jnp.concatenate(rows, axis=0)
         return total + lax.dot_general(
-            left, right, (((1,), (1,)), ((), ())), preferred_element_type=f32
+            both, both, (((1,), (1,)), ((), ())), preferred_element_type=f32
         )
 
     total = lax.fori_loop(
         0,
         lines_all // (lines * sets),
         gram_step,
-        jnp.zeros((2 * sets * padded_k, sets * padded_k), f32),
-    )
-    for h in range(2):
-        part = jnp.zeros((padded_k, padded_k), f32)
-        for g in range(sets):
-            first = (h * sets + g) * padded_k
-            part = part + total[first : first + padded_k, g * padded_k : (g + 1) * padded_k]
-        gram_out[h * padded_k : (h + 1) * padded_k, :] = part
+        jnp.zeros((sets * padded_k, sets * padded_k), f32),
+    )
+    part = jnp.zeros((padded_k, padded_k), f32)
+    for g in range(sets):
+        rows = slice(g * padded_k, (g + 1) * padded_k)
+        part = part + total[rows, rows]
+    gram_out[...] = part
 
     step = side - taps + 1
     half = windows.shape[2]
@@ -287,8 +261,9 @@
 
 
 def normal_matrix(
-    slot_of, rows_at, cols_at, arrived, col, row_rev, roots, data, high, wide, count, taps
+    slot_of, rows_at, cols_at, arrived, col, row_rev, science, variance, count, taps
 ):
+    high, wide = science.shape
     side = row_rev.shape[1]
     stamps = rows_at.shape[1]
     padded_k = up(count + 2, 16)
@@ -300,7 +275,7 @@
     return pl.pallas_call(
         functools.partial(normal_body, count=count, across_blocks=wide // side, taps=taps),
         out_shape=(
-            jax.ShapeDtypeStruct((2 * padded_k, padded_k), f32),
+            jax.ShapeDtypeStruct((padded_k, padded_k), f32),
             jax.ShapeDtypeStruct((wins, 2, tall // 2, side), f32),
         ),
         in_specs=[smem()] * 3 + [vmem()] * 5,
@@ -309,11 +284,14 @@
             pltpu.VMEM((tall, wide + 2 * side), f32),
             pltpu.VMEM((group, stamps * side, 2 * side), bf16),
             pltpu.VMEM((stamps * side * (padded_k + 1), side), f32),
+            pltpu.VMEM((high + 8, wide + 2 * side), f32),
+            pltpu.VMEM((high + 8, wide + 2 * side), f32),
+            pltpu.VMEM((stamps * side, side), f32),
         ],
         compiler_params=pltpu.CompilerParams(vmem_limit_bytes=36 * mib),
         cost_estimate=cost(10_000_000_000, 8_000_000),
         name="normal_matrix",
-    )(slot_of, rows_at, cols_at, arrived, col, row_rev, roots, data)
+    )(slot_of, rows_at, cols_at, arrived, col, row_rev, science, variance)
 
 
 def subtract_body(
@@ -342,12 +320,9 @@
     part = side // exps
     size = count + 1
 
-    square = jnp.concatenate(
-        [gram[...], jnp.zeros((2 * padded_k, side - padded_k), f32)], axis=1
-    )
-    cross = square[padded_k:]
-    mirror = jnp.concatenate([cross, jnp.zeros((side - padded_k, side), f32)], axis=0).T
-    system = (square[:padded_k] + cross + mirror[:padded_k]) / pixels
+    system = jnp.concatenate(
+        [gram[...], jnp.zeros((padded_k, side - padded_k), f32)], axis=1
+    ) / pixels
     sub = lax.broadcasted_iota(jnp.int32, (padded_k, side), 0)
     lane = lax.broadcasted_iota(jnp.int32, (padded_k, side), 1)
     system = jnp.where((sub < size) & (lane <= size), system, 0.0)
@@ -359,7 +334,9 @@
         rows = [system[k + j : k + j + 1, :] for j in block]
         core = [[cols[j][k + i : k + i + 1, :] for j in block] for i in block]
         for j in block:
-            inverse = 1.0 / core[j][j]
+            inverse = pl.reciprocal(core[j][j], approx=True)
+            for _ in range(2):
+                inverse = inverse * (2.0 - core[j][j] * inverse)
             factor = jnp.where(sub == k + j, 0.0, cols[j] * inverse)
             system = system - factor * rows[j]
             for i in block[j + 1 :]:
@@ -612,36 +589,39 @@
     )(table, parts, var_sum, var_template)
 
 
-def join_body(places, *refs, part, chunk):
+def join_body(places, *refs, part, count, fresh):
     out, held, sems = refs[-3:]
+    ins = refs[:count]
     copies = []
-    for i in range(out.shape[0] // chunk):
-        blocks = pl.ds(i * chunk, chunk)
-        for d, ref in enumerate(refs[:-3]):
-            row = pl.multiple_of(places[d] * part, part)
-            held[blocks, pl.ds(row, part), :] = ref[blocks].astype(f32)
-        copies.append(pltpu.make_async_copy(held.at[blocks], out.at[blocks], sems.at[i]))
+    for d, ref in enumerate(ins):
+        held[d] = ref[...].astype(f32)
+        row = pl.multiple_of(places[d] * part, part)
+        copies.append(
+            pltpu.make_async_copy(held.at[d], out.at[:, pl.ds(row, part), :], sems.at[d])
+        )
         copies[-1].start()
     for copy in copies:
         copy.wait()
 
 
-def join_parts(places, parts):
+def join_parts(places, parts, whole, exps):
     tract, part, side = parts[0].shape
-    exps = len(parts)
-    chunk = 8 if tract % 8 == 0 else tract
+    count = len(parts)
+    fresh = whole is None
+    anywhere = pl.BlockSpec(memory_space=pl.ANY)
     return pl.pallas_call(
-        functools.partial(join_body, part=part, chunk=chunk),
+        functools.partial(join_body, part=part, count=count, fresh=fresh),
         out_shape=jax.ShapeDtypeStruct((tract, part * exps, side), f32),
-        in_specs=[smem()] + [vmem()] * exps,
-        out_specs=pl.BlockSpec(memory_space=pl.ANY),
+        in_specs=[smem()] + [vmem()] * count + ([] if fresh else [anywhere]),
+        out_specs=anywhere,
         scratch_shapes=[
-            pltpu.VMEM((tract, part * exps, side), f32),
-            pltpu.SemaphoreType.DMA((tract // chunk,)),
+            pltpu.VMEM((count, tract, part, side), f32),
+            pltpu.SemaphoreType.DMA((count,)),
         ],
+        input_output_aliases={} if fresh else {count + 1: 0},
         compiler_params=pltpu.CompilerParams(vmem_limit_bytes=16 * mib),
         name="join_parts",
-    )(places, *parts)
+    )(places, *parts, *([] if fresh else [whole]))
 
 
 def local(
@@ -672,7 +652,8 @@
 
     slot_of, sender, request = route_tables(routes_src, routes_blk, peers, capacity)
     asked = lax.all_to_all(request, "det", split_axis=0, concat_axis=0, tiled=True)
-    picked = pick_blocks(asked, template, slots, capacity)
+    var_parts = prepare(sender, request, variance_img, side, exps, capacity)
+    picked = pick_blocks(asked, template, var_parts, slots, capacity)
     arrived = lax.all_to_all(picked, "det", split_axis=0, concat_axis=0, tiled=True)
 
     padded_k = up(count + 2, 16)
@@ -684,11 +665,9 @@
     row_rev = jnp.roll(row_rev, 1, axis=1)
     over_rev = jnp.roll(jnp.pad(psf_row[:, ::-1], ((0, 0), (2 * side - taps, 0))), 1, axis=1)
     down = jnp.pad(psf_col, ((0, 0), (0, 2 * side - taps)))
-    var_parts, roots, data = prepare(
-        sender, request, stamp_rows, stamp_cols, science_img, variance_img, side, exps, capacity
-    )
+    var_late, arrived = lax.optimization_barrier((var_parts, arrived))
     var_back = lax.all_to_all(
-        var_parts, ("det", "exp"), split_axis=0, concat_axis=0, tiled=True
+        var_late, ("det", "exp"), split_axis=0, concat_axis=0, tiled=True
     )
     table = var_back[:, capacity * part, :capacity].astype(f32).astype(jnp.int32)
 
@@ -700,10 +679,8 @@
         arrived,
         col,
         row_rev,
-        roots,
-        data,
-        high,
-        wide,
+        science_img,
+        variance_img,
         count,
         taps,
     )
@@ -740,22 +717,24 @@
     mine = combine(table, diff_back, var_sum, var_template, part, capacity)
 
     if exps & (exps - 1) == 0:
-        held = [mine]
+        held = {0: mine}
         reach = exps // 2
-        gaps = [0]
         while reach:
             pairs = [(e, e ^ reach) for e in range(exps)]
-            held = held + [lax.ppermute(h, "exp", pairs) for h in held]
-            gaps = gaps + [g ^ reach for g in gaps]
+            held.update({g ^ reach: lax.ppermute(h, "exp", pairs) for g, h in held.items()})
             reach //= 2
-        places = jnp.stack([me ^ g for g in gaps])
+        there = {g: me ^ g for g in held}
     else:
-        held = [mine]
+        held = {0: mine}
         for gap in range(1, exps):
             pairs = [(e, (e + gap) % exps) for e in range(exps)]
-            held.append(lax.ppermute(mine, "exp", pairs))
-        places = jnp.stack([(me - g) % exps for g in range(exps)])
-    significance = join_parts(places, held)
+            held[gap] = lax.ppermute(mine, "exp", pairs)
+        there = {g: (me - g) % exps for g in held}
+    first = max(1, exps // 2)
+    significance = None
+    for gaps in [list(range(first))] + [[g] for g in range(first, exps)]:
+        places = jnp.stack([there[g] for g in gaps])
+        significance = join_parts(places, [held[g] for g in gaps], significance, exps)
     return (significance, scored[None], coef[:, : count + 1])
 
 

time: 95.3 us -> 94 us (0.986)
  blocking collectives: 11.7 us -> 0 us
  starting transfers between devices: 18.1 us -> 25.1 us
  waiting for transfers between devices: 28.7 us -> 31.9 us
  local copies, waits for them, and re-layouts: 2.32 us -> 4.24 us
  Pallas kernels: 32.4 us -> 31 us
    all_to_all x1 -> x0, blocking collectives: 11.7 us -> none  [local(): lax.all_to_all(request, 'det', split_axis=0, concat_axis=0, tiled=True)]
    all_to_all x1 -> x2, starting transfers between devices: 5.62 us -> 12 us  [the longest x1 6.37 us: local(): lax.all_to_all(request, 'det', split_axis=0, concat_axis=0, tiled=True)]
    all_to_all x1, waiting for transfers between devices: 9.68 us -> 12.8 us  [local(): lax.all_to_all(picked, 'det', split_axis=0, concat_axis=0, tiled=True)]
    unnamed x29 -> x31, local copies, waits for them, and re-layouts: 1.8 us -> 3.72 us
    all_to_all x1 -> x2, waiting for transfers between devices: 0.01 us -> 1.25 us  [the longest x1 1.25 us: local(): lax.all_to_all(request, 'det', split_axis=0, concat_axis=0, tiled=True)]
    pallas_call x1, Pallas kernels: 13 us -> 11.8 us  [normal_matrix(): pl.pallas_call(functools.partial(normal_body, count=count, across_blocks=...]
    pallas_call x1, Pallas kernels: 2.66 us -> 1.43 us  [pick_blocks(): pl.pallas_call(functools.partial(pick_body, capacity=capacity), out_shape...]
    ppermute x3, waiting for transfers between devices: 6.74 us -> 5.66 us  [local(): lax.ppermute(h, 'exp', pairs)]
  transfers between devices with their start and end apart: 6 -> 7, of which waited for: 4 -> 4; matrix products, arithmetic and copies ran while one was open for 1% -> 1% of each run, Pallas kernels for 27% -> 28%
where the time goes in v1:
time: 94 us; the launch traced here: 93.4 us
  waiting for transfers between devices  31.9 us (34%)
  Pallas kernels  31 us (33%)
  starting transfers between devices  25.1 us (27%)
  local copies, waits for them, and re-layouts  4.24 us (5%)
    all_to_all x1, waiting for transfers between devices, local(): lax.all_to_all(picked, 'det', split_axis=0, concat_axis=0, tiled=True)  12.8 us
    all_to_all x1, waiting for transfers between devices, local(): lax.all_to_all(payload, ('det', 'exp'), split_axis=0, concat_axis=0, tile...  12.2 us
    pallas_call x1, Pallas kernels, normal_matrix(): pl.pallas_call(functools.partial(normal_body, count=count, across_blocks=...  11.8 us
    all_to_all x1, starting transfers between devices, local(): lax.all_to_all(request, 'det', split_axis=0, concat_axis=0, tiled=True)  6.37 us
    pallas_call x1, Pallas kernels, subtract(): pl.pallas_call(body, out_shape=(jax.ShapeDtypeStruct((1, side), f32), jax...  6.2 us
    all_to_all x1, starting transfers between devices, local(): lax.all_to_all(payload, ('det', 'exp'), split_axis=0, concat_axis=0, tile...  5.82 us
    ppermute x3, waiting for transfers between devices, local(): lax.ppermute(h, 'exp', pairs)  5.66 us
    all_to_all x1, starting transfers between devices, local(): lax.all_to_all(var_late, ('det', 'exp'), split_axis=0, concat_axis=0, til...  5.59 us
  transfers between devices with their start and end apart: 7, of which 4 were waited for; matrix products, arithmetic and copies ran while one was open for 1% of the time, Pallas kernels for 28%

profile of v1, /device:TPU:1, one launch (start us, length us, event | category | flops | bytes accessed | tf_op | source)
XLA Modules:
  0.0 93.4 jit_solution(10884460583905534109)
XLA Ops:
  0.6 1.5 %route_tables.1 = (s32[16]{0:T(128)}, s32[16]{0:T(128)}, s32[8,1,2]{2,1,0:T(1,128)}) custom-call(s32[1,16]{1,0:T(1,128)} %src.1, s32[1,16]{1,0:T(1,128)} %blk.1), custom_call_target="tpu_custom_call" | custom-call | tf_op jit(solution)/shard_map/route_tables/pallas_call | solution.py:49
  2.2 6.4 %all-to-all-start = ((s32[8,1,2]{2,1,0:T(1,128)}), s32[8,1,2]{2,1,0:T(1,128)S(1)}, u32[]{:S(2)}, u32[]{:S(2)}) async-start(s32[8,1,2]{2,1,0:T(1,128)} %get-tuple-element.15.request), calls=%async_computation | async-start | bytes 8192 | tf_op jit(solution)/shard_map/all_to_all | solution.py:654
  8.6 1.0 %copy-done.2 = bf16[1,256,1024]{2,1,0:T(8,128)(2,1)S(1)} copy-done((bf16[1,256,1024]{2,1,0:T(8,128)(2,1)S(1)}, bf16[1,256,1024]{2,1,0:T(8,128)(2,1)}, u32[]{:S(2)}) %copy-start.2) | copy-done | bytes 524312
  9.6 0.7 copy-done.4
  10.3 0.6 copy-done.5
  10.9 1.6 %prepare.1.earlier = bf16[32,72,128]{2,1,0:T(8,128)(2,1)} custom-call(s32[16]{0:T(128)S(1)} %copy-done.5, s32[8,1,2]{2,1,0:T(1,128)S(1)} %copy-done.4, bf16[256,1024]{1,0:T(8,128)(2,1)S(1)} %bitcast.11), custom_call_target="tpu_custom_call" | custom-call | bytes 3000000 | tf_op jit(solution)/shard_map/prepare/pallas_call | solution.py:131
  12.5 1.2 %all-to-all-done.asked = s32[8,1,2]{2,1,0:T(1,128)S(1)} async-done(((s32[8,1,2]{2,1,0:T(1,128)}), s32[8,1,2]{2,1,0:T(1,128)S(1)}, u32[]{:S(2)}, u32[]{:S(2)}) %all-to-all-start) | async-done | bytes 96 | tf_op jit(solution)/shard_map/all_to_all | solution.py:654
  13.8 1.2 %copy-done.1 = bf16[32,128,128]{2,1,0:T(8,128)(2,1)S(1)} copy-done((bf16[32,128,128]{2,1,0:T(8,128)(2,1)S(1)}, bf16[32,128,128]{2,1,0:T(8,128)(2,1)}, u32[]{:S(2)}) %copy-start.1) | copy-done | bytes 1048600
  15.0 1.4 %pick_blocks.1 = bf16[16,128,128]{2,1,0:T(8,128)(2,1)} custom-call(s32[8,1,2]{2,1,0:T(1,128)S(1)} %all-to-all-done.asked, bf16[32,128,128]{2,1,0:T(8,128)(2,1)S(1)} %copy-done.1, bf16[32,72,128]{2,1,0:T(8,128)(2,1)} %prepare.1.earlier), custom_call_target="tpu_custom_call" | custom-call | tf_op jit(solution)/shard_map/pick_blocks/pallas_call | solution.py:75
  16.5 4.2 %all-to-all-start.1 = ((bf16[16,128,128]{2,1,0:T(8,128)(2,1)}), bf16[16,128,128]{2,1,0:T(8,128)(2,1)S(1)}, u32[]{:S(2)}, u32[]{:S(2)}) async-start(bf16[16,128,128]{2,1,0:T(8,128)(2,1)} %pick_blocks.1), calls=%async_computation.1 | async-start | bytes 1048576 | tf_op jit(solution)/shard_map/all_to_all | solution.py:657
  21.2 12.8 %all-to-all-done.1.arrived = bf16[16,128,128]{2,1,0:T(8,128)(2,1)S(1)} async-done(((bf16[16,128,128]{2,1,0:T(8,128)(2,1)}), bf16[16,128,128]{2,1,0:T(8,128)(2,1)S(1)}, u32[]{:S(2)}, u32[]{:S(2)}) %all-to-all-start.1) | async-done | bytes 524320 | tf_op jit(solution)/shard_map/all_to_all | solution.py:657
  34.0 5.6 %all-to-all-start.2 = ((bf16[32,72,128]{2,1,0:T(8,128)(2,1)}), bf16[32,72,128]{2,1,0:T(8,128)(2,1)S(1)}, u32[]{:S(2)}, u32[]{:S(2)}) async-start(bf16[32,72,128]{2,1,0:T(8,128)(2,1)} %prepare.1.earlier), calls=%async_computation.2 | async-start | bytes 1179648 | tf_op jit(solution)/shard_map/all_to_all | solution.py:669
  39.7 11.8 %normal_matrix.1 = (f32[48,48]{1,0:T(8,128)S(1)}, f32[10,2,152,128]{3,2,1,0:T(8,128)S(1)}) custom-call(s32[16]{0:T(128)S(1)} %copy-done.10, s32[1,4]{1,0:T(1,128)S(1)} %copy-done.8, s32[1,4]{1,0:T(1,128)S(1)} %copy-done.9, bf16[16,128,128]{2,1,0:T(8,128)(2,1)S(1)} %all-to-all-done.1.arrived, f32[48,128]{1,0:T(8,128)S(1)} %pad_convert_fusion.col, ...), custom_call_target="tpu_custom_call" | custom-call | flops 10000000000 | bytes 8000000 | tf_op jit(solution)/shard_map/normal_matrix/pallas_call | solution.py:275
  51.5 6.2 %subtract.1 = (f32[1,128]{1,0:T(1,128)}, bf16[32,72,128]{2,1,0:T(8,128)(2,1)}) custom-call(s32[16]{0:T(128)S(1)} %copy-done.6, f32[48,48]{1,0:T(8,128)S(1)} %get-tuple-element.19.gram, f32[10,2,152,128]{3,2,1,0:T(8,128)S(1)} %get-tuple-element.20.frames, bf16[256,1024]{1,0:T(8,128)(2,1)S(1)} %bitcast.16, bf16[32,48]{1,0:T(8,128)(2,1)S(1)} %pad.25.col_t, ...), custom_call_target="tpu_custom_call" | custom-call | flops 5000000000 | bytes 4000000 | tf_op jit(solution)/shard_map/subtract/pallas_call | solution.py:436
  57.7 5.8 %all-to-all-start.3 = ((bf16[32,72,128]{2,1,0:T(8,128)(2,1)}), bf16[32,72,128]{2,1,0:T(8,128)(2,1)S(1)}, u32[]{:S(2)}, u32[]{:S(2)}) async-start(bf16[32,72,128]{2,1,0:T(8,128)(2,1)} %get-tuple-element.21.payload), calls=%async_computation.3 | async-start | bytes 1179648 | tf_op jit(solution)/shard_map/all_to_all | solution.py:701
  63.9 3.9 %score.1 = (f32[256,1024]{1,0:T(8,128)}, f32[32,32,128]{2,1,0:T(8,128)S(1)}) custom-call(s32[32,2]{1,0:T(8,128)S(1)} %bitcast.13, s32[16]{0:T(128)S(1)} %copy-done.10, bf16[32,72,128]{2,1,0:T(8,128)(2,1)} %get-tuple-element.21.payload, f32[1,256]{1,0:T(1,128)S(1)} %pad.26.down, f32[1,256]{1,0:T(1,128)S(1)} %pad_maximum_fusion.1.over, ...), custom_call_target="tpu_custom_call" | custom-call | flops 2000000000 | bytes 2000000 | tf_op jit(solution)/shard_map/score/pallas_call | solution.py:520
  67.7 12.2 %all-to-all-done.3.parts = bf16[32,72,128]{2,1,0:T(8,128)(2,1)S(1)} async-done(((bf16[32,72,128]{2,1,0:T(8,128)(2,1)}), bf16[32,72,128]{2,1,0:T(8,128)(2,1)S(1)}, u32[]{:S(2)}, u32[]{:S(2)}) %all-to-all-start.3) | async-done | bytes 589856 | tf_op jit(solution)/shard_map/all_to_all | solution.py:701
  80.0 1.3 %combine.1.refs_0_ = bf16[32,32,128]{2,1,0:T(8,128)(2,1)S(1)} custom-call(s32[32,2]{1,0:T(8,128)S(1)} %bitcast.14, bf16[32,72,128]{2,1,0:T(8,128)(2,1)S(1)} %all-to-all-done.3.parts, f32[32,32,128]{2,1,0:T(8,128)S(1)} %get-tuple-element.22.var_sum, bf16[32,32,128]{2,1,0:T(8,128)(2,1)S(1)} %constant_dynamic-slice_fusion.var_template), custom_call_target="tpu_custom_call" | custom-call | tf_op jit(solution)/shard_map/combine/pallas_call | solution.py:578
  81.3 1.3 %collective-permute-start = (bf16[32,32,128]{2,1,0:T(8,128)(2,1)S(1)}, bf16[32,32,128]{2,1,0:T(8,128)(2,1)S(1)}, u32[]{:S(2)}, u32[]{:S(2)}) collective-permute-start(bf16[32,32,128]{2,1,0:T(8,128)(2,1)S(1)} %combine.1.refs_0_), channel_id=1, source_target_pairs={{0,2},{1,3},{2,0},{3,1},{4,6},{5,7},{6,4},{7,5},{8,10},{9,11},{10,... | collective-permute-start | bytes 786440 | tf_op jit(solution)/shard_map/ppermute | solution.py:724
  83.0 5.7 %collective-permute-done.refs_0_ = bf16[32,32,128]{2,1,0:T(8,128)(2,1)S(1)} collective-permute-done((bf16[32,32,128]{2,1,0:T(8,128)(2,1)S(1)}, bf16[32,32,128]{2,1,0:T(8,128)(2,1)S(1)}, u32[]{:S(2)}, u32[]{:S(2)}) %collective-permute-start) | collective-permute-done | bytes 262176 | tf_op jit(solution)/shard_map/ppermute | solution.py:724
  88.7 1.4 %collective-permute-start.1 = (bf16[32,32,128]{2,1,0:T(8,128)(2,1)S(1)}, bf16[32,32,128]{2,1,0:T(8,128)(2,1)S(1)}, u32[]{:S(2)}, u32[]{:S(2)}) collective-permute-start(bf16[32,32,128]{2,1,0:T(8,128)(2,1)S(1)} %collective-permute-done.refs_0_), channel_id=1, source_target_pairs={{0,1},{1,0},{2,3},{3,2},{4,5},{5,4},{6,7},{7,6},{8,9},{9,8},{10,11... | collective-permute-start | bytes 786440 | tf_op jit(solution)/shard_map/ppermute | solution.py:724
  90.1 1.6 %join_parts.3.refs_1_ = f32[32,128,128]{2,1,0:T(8,128)} custom-call(s32[2]{0:T(128)S(1)} %pad_add_fusion.places, bf16[32,32,128]{2,1,0:T(8,128)(2,1)S(1)} %combine.1.refs_0_, bf16[32,32,128]{2,1,0:T(8,128)(2,1)S(1)} %collective-permute-done.2.refs_1_), custom_call_target="tpu_custom_call" | custom-call | tf_op jit(solution)/shard_map/join_parts/pallas_call | solution.py:612
  91.7 0.8 join_parts.4.refs_1_
  92.6 0.8 join_parts.5
  (45 shorter events, 1.4 us)
Async XLA Ops:
  0.6 63.2 %copy-start = (bf16[32,128,128]{2,1,0:T(8,128)(2,1)S(1)}, bf16[32,128,128]{2,1,0:T(8,128)(2,1)}, u32[]{:S(2)}) copy-start(bf16[32,128,128]{2,1,0:T(8,128)(2,1)} %param.13) | copy-start | bytes 3145732
  2.2 11.6 %all-to-all-start = ((s32[8,1,2]{2,1,0:T(1,128)}), s32[8,1,2]{2,1,0:T(1,128)S(1)}, u32[]{:S(2)}, u32[]{:S(2)}) async-start(s32[8,1,2]{2,1,0:T(1,128)} %get-tuple-element.15.request), calls=%async_computation | async-start | bytes 8192 | tf_op jit(solution)/shard_map/all_to_all | solution.py:654
  8.6 1.0 %copy-start.2 = (bf16[1,256,1024]{2,1,0:T(8,128)(2,1)S(1)}, bf16[1,256,1024]{2,1,0:T(8,128)(2,1)}, u32[]{:S(2)}) copy-start(bf16[1,256,1024]{2,1,0:T(8,128)(2,1)} %param.15) | copy-start | bytes 1572868
  9.6 0.7 copy-start.4
  10.3 0.6 copy-start.5
  10.9 9.8 %copy-start.12 = (bf16[40,21]{0,1:T(8,128)(2,1)S(1)}, bf16[40,21]{0,1:T(8,128)(2,1)}, u32[]{:S(2)}) copy-start(bf16[40,21]{0,1:T(8,128)(2,1)} %param.21) | copy-start | bytes 5044
  10.9 9.9 %copy-start.11 = (bf16[40,21]{0,1:T(8,128)(2,1)S(1)}, bf16[40,21]{0,1:T(8,128)(2,1)}, u32[]{:S(2)}) copy-start(bf16[40,21]{0,1:T(8,128)(2,1)} %param.20) | copy-start | bytes 5044
  13.8 1.2 %copy-start.1 = (bf16[32,128,128]{2,1,0:T(8,128)(2,1)S(1)}, bf16[32,128,128]{2,1,0:T(8,128)(2,1)}, u32[]{:S(2)}) copy-start(bf16[32,128,128]{2,1,0:T(8,128)(2,1)} %template.1) | copy-start | bytes 3145732
  15.0 24.6 %copy-start.3 = (bf16[1,256,1024]{2,1,0:T(8,128)(2,1)S(1)}, bf16[1,256,1024]{2,1,0:T(8,128)(2,1)}, u32[]{:S(2)}) copy-start(bf16[1,256,1024]{2,1,0:T(8,128)(2,1)} %param.15) | copy-start | bytes 1572868
  15.0 24.6 %copy-start.7 = (bf16[1,256,1024]{2,1,0:T(8,128)(2,1)S(1)}, bf16[1,256,1024]{2,1,0:T(8,128)(2,1)}, u32[]{:S(2)}) copy-start(bf16[1,256,1024]{2,1,0:T(8,128)(2,1)} %param.14) | copy-start | bytes 1572868
  15.0 24.6 %copy-start.8 = (s32[1,4]{1,0:T(1,128)S(1)}, s32[1,4]{1,0:T(1,128)}, u32[]{:S(2)}) copy-start(s32[1,4]{1,0:T(1,128)} %rows_at.1) | copy-start | bytes 52
  15.0 24.6 %copy-start.9 = (s32[1,4]{1,0:T(1,128)S(1)}, s32[1,4]{1,0:T(1,128)}, u32[]{:S(2)}) copy-start(s32[1,4]{1,0:T(1,128)} %cols_at.1) | copy-start | bytes 52
  15.0 24.6 %copy-start.10 = (s32[16]{0:T(128)S(1)}, s32[16]{0:T(128)}, u32[]{:S(2)}) copy-start(s32[16]{0:T(128)} %get-tuple-element.17.slot_of) | copy-start | bytes 196
  16.5 17.5 %all-to-all-start.1 = ((bf16[16,128,128]{2,1,0:T(8,128)(2,1)}), bf16[16,128,128]{2,1,0:T(8,128)(2,1)S(1)}, u32[]{:S(2)}, u32[]{:S(2)}) async-start(bf16[16,128,128]{2,1,0:T(8,128)(2,1)} %pick_blocks.1), calls=%async_computation.1 | async-start | bytes 1048576 | tf_op jit(solution)/shard_map/all_to_all | solution.py:657
  34.0 23.7 %all-to-all-start.2 = ((bf16[32,72,128]{2,1,0:T(8,128)(2,1)}), bf16[32,72,128]{2,1,0:T(8,128)(2,1)S(1)}, u32[]{:S(2)}, u32[]{:S(2)}) async-start(bf16[32,72,128]{2,1,0:T(8,128)(2,1)} %prepare.1.earlier), calls=%async_computation.2 | async-start | bytes 1179648 | tf_op jit(solution)/shard_map/all_to_all | solution.py:669
  39.6 11.8 %copy-start.6 = (s32[16]{0:T(128)S(1)}, s32[16]{0:T(128)}, u32[]{:S(2)}) copy-start(s32[16]{0:T(128)} %get-tuple-element.14.sender) | copy-start | bytes 196
  51.5 12.1 %copy-start.13 = (f32[1,21]{1,0:T(1,128)S(1)}, f32[1,21]{1,0:T(1,128)}, u32[]{:S(2)}) copy-start(f32[1,21]{1,0:T(1,128)} %param.23) | copy-start | bytes 256
  51.5 12.2 %copy-start.14 = (f32[1,21]{1,0:T(1,128)S(1)}, f32[1,21]{1,0:T(1,128)}, u32[]{:S(2)}) copy-start(f32[1,21]{1,0:T(1,128)} %param.22) | copy-start | bytes 256
  57.7 22.3 %all-to-all-start.3 = ((bf16[32,72,128]{2,1,0:T(8,128)(2,1)}), bf16[32,72,128]{2,1,0:T(8,128)(2,1)S(1)}, u32[]{:S(2)}, u32[]{:S(2)}) async-start(bf16[32,72,128]{2,1,0:T(8,128)(2,1)} %get-tuple-element.21.payload), calls=%async_computation.3 | async-start | bytes 1179648 | tf_op jit(solution)/shard_map/all_to_all | solution.py:701
  81.3 7.4 %collective-permute-start = (bf16[32,32,128]{2,1,0:T(8,128)(2,1)S(1)}, bf16[32,32,128]{2,1,0:T(8,128)(2,1)S(1)}, u32[]{:S(2)}, u32[]{:S(2)}) collective-permute-start(bf16[32,32,128]{2,1,0:T(8,128)(2,1)S(1)} %combine.1.refs_0_), channel_id=1, source_target_pairs={{0,2},{1,3},{2,0},{3,1},{4,6},{5,7},{6,4},{7,5},{8,10},{9,11},{10,... | collective-permute-start | bytes 786440 | tf_op jit(solution)/shard_map/ppermute | solution.py:724
  82.6 7.6 %collective-permute-start.2 = (bf16[32,32,128]{2,1,0:T(8,128)(2,1)S(1)}, bf16[32,32,128]{2,1,0:T(8,128)(2,1)S(1)}, u32[]{:S(2)}, u32[]{:S(2)}) collective-permute-start(bf16[32,32,128]{2,1,0:T(8,128)(2,1)S(1)} %combine.1.refs_0_), channel_id=1, source_target_pairs={{0,1},{1,0},{2,3},{3,2},{4,5},{5,4},{6,7},{7,6},{8,9},{9,8},{10,11... | collective-permute-start | bytes 786440 | tf_op jit(solution)/shard_map/ppermute | solution.py:724
  88.7 3.9 %collective-permute-start.1 = (bf16[32,32,128]{2,1,0:T(8,128)(2,1)S(1)}, bf16[32,32,128]{2,1,0:T(8,128)(2,1)S(1)}, u32[]{:S(2)}, u32[]{:S(2)}) collective-permute-start(bf16[32,32,128]{2,1,0:T(8,128)(2,1)S(1)} %collective-permute-done.refs_0_), channel_id=1, source_target_pairs={{0,1},{1,0},{2,3},{3,2},{4,5},{5,4},{6,7},{7,6},{8,9},{9,8},{10,11... | collective-permute-start | bytes 786440 | tf_op jit(solution)/shard_map/ppermute | solution.py:724

commit v2 on v1

--- a/solution.py
+++ b/solution.py
@@ -60,9 +60,7 @@
     )(routes_src, routes_blk)
 
 
-def pick_body(asked, template, earlier, out, *, capacity):
-    del earlier
-
+def pick_body(asked, template, out, *, capacity):
     def one(s, carry):
         block = jnp.maximum(asked[s // capacity, 0, s % capacity] - 1, 0)
         out[s] = template[block]
@@ -71,20 +69,21 @@
     lax.fori_loop(0, out.shape[0], one, 0, unroll=True if out.shape[0] <= 32 else 4)
 
 
-def pick_blocks(asked, template, earlier, slots, capacity):
+def pick_blocks(asked, template, slots, capacity):
     return pl.pallas_call(
         functools.partial(pick_body, capacity=capacity),
         out_shape=jax.ShapeDtypeStruct((slots,) + template.shape[1:], template.dtype),
-        in_specs=[smem(), vmem(), pl.BlockSpec(memory_space=pl.ANY)],
+        in_specs=[smem(), vmem()],
         out_specs=vmem(),
         compiler_params=pltpu.CompilerParams(vmem_limit_bytes=16 * mib),
         name="pick_blocks",
-    )(asked, template, earlier)
+    )(asked, template)
 
 
 def store_parts(sender, image, out, side, exps, capacity, across_blocks):
     part = side // exps
     slots = sender.shape[0]
+    peers = slots // capacity
 
     def one(s, carry):
         b = sender[s]
@@ -93,7 +92,7 @@
         block = image[pl.ds(top, side), pl.ds(left, side)].astype(bf16)
         row = pl.multiple_of((s % capacity) * part, part)
         for q in range(exps):
-            out[(s // capacity) * exps + q, pl.ds(row, part), :] = block[q * part : (q + 1) * part]
+            out[q * peers + s // capacity, pl.ds(row, part), :] = block[q * part : (q + 1) * part]
         return carry
 
     lax.fori_loop(0, slots, one, 0, unroll=True if slots <= 32 else 4)
@@ -107,7 +106,7 @@
         for c in range(capacity):
             line = jnp.where(lane == c, request[p, 0, c].astype(f32), line)
         for q in range(exps):
-            out[p * exps + q, out.shape[1] - trailer_rows :, :] = line.astype(bf16)
+            out[q * request.shape[0] + p, out.shape[1] - trailer_rows :, :] = line.astype(bf16)
         return carry
 
     lax.fori_loop(0, request.shape[0], put, 0)
@@ -121,22 +120,29 @@
     return pltpu.roll(tile, lax.rem(height - (top - down), height), 0)
 
 
-def prepare_body(sender, request, variance, out, *, side, exps, capacity):
+def prepare_body(sender, request, variance, template, out, near, sem, *, side, exps, capacity):
+    copy = pltpu.make_async_copy(template, near, sem)
+    copy.start()
     store_parts(sender, variance, out, side, exps, capacity, variance.shape[1] // side)
     store_requests(request, out, side, exps, capacity)
-
-
-def prepare(sender, request, variance, side, exps, capacity):
+    copy.wait()
+
+
+def prepare(sender, request, variance, template, side, exps, capacity):
     rows = capacity * (side // exps) + trailer_rows
     return pl.pallas_call(
         functools.partial(prepare_body, side=side, exps=exps, capacity=capacity),
-        out_shape=jax.ShapeDtypeStruct((request.shape[0] * exps, rows, side), bf16),
-        in_specs=[smem()] * 2 + [vmem()],
-        out_specs=vmem(),
+        out_shape=(
+            jax.ShapeDtypeStruct((request.shape[0] * exps, rows, side), bf16),
+            jax.ShapeDtypeStruct(template.shape, template.dtype),
+        ),
+        in_specs=[smem()] * 2 + [vmem(), pl.BlockSpec(memory_space=pl.ANY)],
+        out_specs=(vmem(), vmem()),
+        scratch_shapes=[pltpu.SemaphoreType.DMA(())],
         compiler_params=pltpu.CompilerParams(vmem_limit_bytes=16 * mib),
-        cost_estimate=cost(0, 3_000_000),
+        cost_estimate=cost(0, 6_000_000),
         name="prepare",
-    )(sender, request, variance)
+    )(sender, request, variance, template)
 
 
 def normal_body(
@@ -156,6 +162,7 @@
     image,
     var,
     roots,
+    window,
     *,
     count,
     across_blocks,
@@ -200,7 +207,14 @@
         design[pl.ds(extra, lines_all, stride=pitch), :] = jnp.zeros((lines_all, side), f32)
 
     group = vert.shape[0]
-    for k in range(0, count, group):
+    step = side - taps + 1
+    starts = list(range(0, count, group))
+    for turn, k in enumerate(starts):
+        for c in range(turn, windows.shape[0], len(starts)):
+            window[...] = frame[:, c * step : c * step + side]
+            for parity in range(2):
+                place = pl.ds(parity, windows.shape[2], stride=2)
+                windows[c, parity] = window[place, :]
         filters = []
         for a in range(group):
             line = jnp.broadcast_to(col[k + a : k + a + 1, :], (side, side))
@@ -250,14 +264,6 @@
         rows = slice(g * padded_k, (g + 1) * padded_k)
         part = part + total[rows, rows]
     gram_out[...] = part
-
-    step = side - taps + 1
-    half = windows.shape[2]
-    for c in range(windows.shape[0]):
-        stage_rows = frame[:, c * step : c * step + side]
-        design[: stage_rows.shape[0], :] = stage_rows
-        for parity in range(2):
-            windows[c, parity] = design[pl.ds(parity, half, stride=2), :]
 
 
 def normal_matrix(
@@ -287,6 +293,7 @@
             pltpu.VMEM((high + 8, wide + 2 * side), f32),
             pltpu.VMEM((high + 8, wide + 2 * side), f32),
             pltpu.VMEM((stamps * side, side), f32),
+            pltpu.VMEM((tall, side), f32),
         ],
         compiler_params=pltpu.CompilerParams(vmem_limit_bytes=36 * mib),
         cost_estimate=cost(10_000_000_000, 8_000_000),
@@ -307,6 +314,7 @@
     image,
     bands,
     total,
+    stacked,
     *,
     exps,
     capacity,
@@ -328,15 +336,27 @@
     system = jnp.where((sub < size) & (lane <= size), system, 0.0)
     system = system + jnp.where((sub == lane) & (sub < size), ridge_term, 0.0)
 
-    for k in range(0, size, 4):
+    pairs = (taps + 2) // 2
+    rows_half = high // 2
+    wins = frames.shape[0]
+
+    def stack_rows(q):
+        for c in range(wins):
+            for a in range(2):
+                stacked[q, c * rows_half : (c + 1) * rows_half, a * side : (a + 1) * side] = (
+                    frames[c, a, q : q + rows_half, :].astype(bf16)
+                )
+
+    starts = list(range(0, size, 4))
+    for step, k in enumerate(starts):
+        for q in range(step, pairs, len(starts)):
+            stack_rows(q)
         block = range(min(4, size - k))
         cols = [jnp.broadcast_to(system[:, k + j : k + j + 1], system.shape) for j in block]
         rows = [system[k + j : k + j + 1, :] for j in block]
         core = [[cols[j][k + i : k + i + 1, :] for j in block] for i in block]
         for j in block:
-            inverse = pl.reciprocal(core[j][j], approx=True)
-            for _ in range(2):
-                inverse = inverse * (2.0 - core[j][j] * inverse)
+            inverse = 1.0 / core[j][j]
             factor = jnp.where(sub == k + j, 0.0, cols[j] * inverse)
             system = system - factor * rows[j]
             for i in block[j + 1 :]:
@@ -368,7 +388,6 @@
         line = jnp.broadcast_to(rounded[i : i + 1, :], (side, side))
         return pltpu.roll(line, 0, 1, stride=1, stride_axis=0).astype(bf16)
 
-    pairs = (taps + 2) // 2
     made = {i: band(i) for i in range(-1, 2 * pairs)}
     for q in range(pairs):
         for a in range(2):
@@ -379,20 +398,9 @@
                 ] = made[2 * q + a - b]
 
     step = side - taps + 1
-    rows_half = high // 2
-    wins = frames.shape[0]
     for q in range(pairs):
-        lhs = jnp.concatenate(
-            [
-                jnp.concatenate(
-                    [frames[c, a, q : q + rows_half, :].astype(bf16) for a in range(2)], axis=1
-                )
-                for c in range(wins)
-            ],
-            axis=0,
-        )
         out = jnp.dot(
-            lhs, bands[q * 2 * side : (q + 1) * 2 * side, :], preferred_element_type=f32
+            stacked[q], bands[q * 2 * side : (q + 1) * 2 * side, :], preferred_element_type=f32
         )
         if q:
             out = out + total[...]
@@ -448,8 +456,9 @@
             pltpu.VMEM((high, wide), f32),
             pltpu.VMEM((pairs * 2 * side, 2 * side), bf16),
             pltpu.VMEM((wins * high // 2, 2 * side), f32),
+            pltpu.VMEM((pairs, wins * high // 2, 2 * side), bf16),
         ],
-        compiler_params=pltpu.CompilerParams(vmem_limit_bytes=24 * mib),
+        compiler_params=pltpu.CompilerParams(vmem_limit_bytes=32 * mib),
         cost_estimate=cost(5_000_000_000, 4_000_000),
         name="subtract",
     )(sender, gram, frames, science, col_t, row_rev)
@@ -484,6 +493,7 @@
     span = up(side + taps - 1, 16)
     across_blocks = wide // side
     exps = side // part
+    peers = payload.shape[0] // exps
     padded[...] = jnp.zeros(padded.shape, f32)
     for b in range(slot_of.shape[0]):
         slot = slot_of[b]
@@ -491,7 +501,7 @@
         left = margin + (b % across_blocks) * side
         for q in range(exps):
             top = (b // across_blocks) * side + q * part
-            block = payload[(slot // capacity) * exps + q, pl.ds(row, part), :]
+            block = payload[q * peers + slot // capacity, pl.ds(row, part), :]
             padded[top : top + part, left : left + side] = block.astype(f32)
     line = jnp.broadcast_to(over[...], (2 * side, 2 * side))
     band = pltpu.roll(line, 0, 1, stride=1, stride_axis=0)[:, :side]
@@ -620,6 +630,7 @@
         ],
         input_output_aliases={} if fresh else {count + 1: 0},
         compiler_params=pltpu.CompilerParams(vmem_limit_bytes=16 * mib),
+        cost_estimate=cost(0, 3_000_000 * count),
         name="join_parts",
     )(places, *parts, *([] if fresh else [whole]))
 
@@ -652,8 +663,8 @@
 
     slot_of, sender, request = route_tables(routes_src, routes_blk, peers, capacity)
     asked = lax.all_to_all(request, "det", split_axis=0, concat_axis=0, tiled=True)
-    var_parts = prepare(sender, request, variance_img, side, exps, capacity)
-    picked = pick_blocks(asked, template, var_parts, slots, capacity)
+    var_parts, near = prepare(sender, request, variance_img, template, side, exps, capacity)
+    picked = pick_blocks(asked, near, slots, capacity)
     arrived = lax.all_to_all(picked, "det", split_axis=0, concat_axis=0, tiled=True)
 
     padded_k = up(count + 2, 16)
@@ -667,7 +678,7 @@
     down = jnp.pad(psf_col, ((0, 0), (0, 2 * side - taps)))
     var_late, arrived = lax.optimization_barrier((var_parts, arrived))
     var_back = lax.all_to_all(
-        var_late, ("det", "exp"), split_axis=0, concat_axis=0, tiled=True
+        var_late, ("exp", "det"), split_axis=0, concat_axis=0, tiled=True
     )
     table = var_back[:, capacity * part, :capacity].astype(f32).astype(jnp.int32)
 
@@ -698,7 +709,7 @@
         taps,
         stamp_rows.shape[1] * side * side,
     )
-    diff_back = lax.all_to_all(payload, ("det", "exp"), split_axis=0, concat_axis=0, tiled=True)
+    diff_back = lax.all_to_all(payload, ("exp", "det"), split_axis=0, concat_axis=0, tiled=True)
     scored, var_sum = score(
         table,
         slot_of,

time: 94 us -> 94.6 us (level)
  starting transfers between devices: 25.1 us -> 26.9 us
  waiting for transfers between devices: 31.9 us -> 30.6 us
  local copies, waits for them, and re-layouts: 4.24 us -> 5.3 us
  Pallas kernels: 31 us -> 30 us
    all_to_all x1, waiting for transfers between devices: 1.25 us -> 0.01 us  [local(): lax.all_to_all(request, 'det', split_axis=0, concat_axis=0, tiled=True)]
    all_to_all x1, starting transfers between devices: 4.19 us -> 5.44 us  [local(): lax.all_to_all(picked, 'det', split_axis=0, concat_axis=0, tiled=True)]
    unnamed x31, local copies, waits for them, and re-layouts: 3.72 us -> 4.78 us
  transfers between devices with their start and end apart: 7 -> 7, of which waited for: 4 -> 3; matrix products, arithmetic and copies ran while one was open for 1% -> 1% of each run, Pallas kernels for 28% -> 27%
where the time goes in v2:
time: 94.6 us; the launch traced here: 93.9 us
  waiting for transfers between devices  30.6 us (32%)
  Pallas kernels  30 us (32%)
  starting transfers between devices  26.9 us (28%)
  local copies, waits for them, and re-layouts  5.3 us (6%)
    all_to_all x1, waiting for transfers between devices, local(): lax.all_to_all(picked, 'det', split_axis=0, concat_axis=0, tiled=True)  12.8 us
    all_to_all x1, waiting for transfers between devices, local(): lax.all_to_all(payload, ('exp', 'det'), split_axis=0, concat_axis=0, tile...  12.7 us
    pallas_call x1, Pallas kernels, normal_matrix(): pl.pallas_call(functools.partial(normal_body, count=count, across_blocks=...  11 us
    all_to_all x1, starting transfers between devices, local(): lax.all_to_all(request, 'det', split_axis=0, concat_axis=0, tiled=True)  6.37 us
    pallas_call x1, Pallas kernels, subtract(): pl.pallas_call(body, out_shape=(jax.ShapeDtypeStruct((1, side), f32), jax...  5.9 us
    all_to_all x1, starting transfers between devices, local(): lax.all_to_all(payload, ('exp', 'det'), split_axis=0, concat_axis=0, tile...  5.84 us
    all_to_all x1, starting transfers between devices, local(): lax.all_to_all(var_late, ('exp', 'det'), split_axis=0, concat_axis=0, til...  5.59 us
    all_to_all x1, starting transfers between devices, local(): lax.all_to_all(picked, 'det', split_axis=0, concat_axis=0, tiled=True)  5.44 us
  transfers between devices with their start and end apart: 7, of which 3 were waited for; matrix products, arithmetic and copies ran while one was open for 1% of the time, Pallas kernels for 27%

profile of v2, /device:TPU:1, one launch (start us, length us, event | category | flops | bytes accessed | tf_op | source)
XLA Modules:
  0.0 93.9 jit_solution(9337197945263155806)
XLA Ops:
  0.6 1.5 %route_tables.1 = (s32[16]{0:T(128)}, s32[16]{0:T(128)}, s32[8,1,2]{2,1,0:T(1,128)}) custom-call(s32[1,16]{1,0:T(1,128)} %src.1, s32[1,16]{1,0:T(1,128)} %blk.1), custom_call_target="tpu_custom_call" | custom-call | tf_op jit(solution)/shard_map/route_tables/pallas_call | solution.py:49
  2.2 6.4 %all-to-all-start = ((s32[8,1,2]{2,1,0:T(1,128)}), s32[8,1,2]{2,1,0:T(1,128)S(1)}, u32[]{:S(2)}, u32[]{:S(2)}) async-start(s32[8,1,2]{2,1,0:T(1,128)} %get-tuple-element.17.request), calls=%async_computation | async-start | bytes 8192 | tf_op jit(solution)/shard_map/all_to_all | solution.py:665
  8.6 1.2 %copy-done.1 = bf16[32,128,128]{2,1,0:T(8,128)(2,1)S(1)} copy-done((bf16[32,128,128]{2,1,0:T(8,128)(2,1)S(1)}, bf16[32,128,128]{2,1,0:T(8,128)(2,1)}, u32[]{:S(2)}) %copy-start.1) | copy-done | bytes 1048600
  9.8 1.0 %copy-done.2 = bf16[1,256,1024]{2,1,0:T(8,128)(2,1)S(1)} copy-done((bf16[1,256,1024]{2,1,0:T(8,128)(2,1)S(1)}, bf16[1,256,1024]{2,1,0:T(8,128)(2,1)}, u32[]{:S(2)}) %copy-start.2) | copy-done | bytes 524312
  10.8 0.7 copy-done.4
  11.5 0.6 copy-done.5
  12.2 1.7 %prepare.1 = (bf16[32,72,128]{2,1,0:T(8,128)(2,1)}, bf16[32,128,128]{2,1,0:T(8,128)(2,1)S(1)}) custom-call(s32[16]{0:T(128)S(1)} %copy-done.5, s32[8,1,2]{2,1,0:T(1,128)S(1)} %copy-done.4, bf16[256,1024]{1,0:T(8,128)(2,1)S(1)} %bitcast.11, bf16[32,128,128]{2,1,0:T(8,128)(2,1)S(1)} %copy-done.1), custom_call_target="tpu_custom_call" | custom-call | bytes 6000000 | tf_op jit(solution)/shard_map/prepare/pallas_call | solution.py:133
  13.9 1.4 %pick_blocks.1 = bf16[16,128,128]{2,1,0:T(8,128)(2,1)} custom-call(s32[8,1,2]{2,1,0:T(1,128)S(1)} %all-to-all-done.asked, bf16[32,128,128]{2,1,0:T(8,128)(2,1)S(1)} %get-tuple-element.19.template), custom_call_target="tpu_custom_call" | custom-call | tf_op jit(solution)/shard_map/pick_blocks/pallas_call | solution.py:73
  15.4 5.4 %all-to-all-start.1 = ((bf16[16,128,128]{2,1,0:T(8,128)(2,1)}), bf16[16,128,128]{2,1,0:T(8,128)(2,1)S(1)}, u32[]{:S(2)}, u32[]{:S(2)}) async-start(bf16[16,128,128]{2,1,0:T(8,128)(2,1)} %pick_blocks.1), calls=%async_computation.1 | async-start | bytes 1048576 | tf_op jit(solution)/shard_map/all_to_all | solution.py:668
  21.3 12.8 %all-to-all-done.1.arrived = bf16[16,128,128]{2,1,0:T(8,128)(2,1)S(1)} async-done(((bf16[16,128,128]{2,1,0:T(8,128)(2,1)}), bf16[16,128,128]{2,1,0:T(8,128)(2,1)S(1)}, u32[]{:S(2)}, u32[]{:S(2)}) %all-to-all-start.1) | async-done | bytes 524320 | tf_op jit(solution)/shard_map/all_to_all | solution.py:668
  34.1 5.6 %all-to-all-start.2 = ((bf16[32,72,128]{2,1,0:T(8,128)(2,1)}), bf16[32,72,128]{2,1,0:T(8,128)(2,1)S(1)}, u32[]{:S(2)}, u32[]{:S(2)}) async-start(bf16[32,72,128]{2,1,0:T(8,128)(2,1)} %get-tuple-element.20), calls=%async_computation.2 | async-start | bytes 1179648 | tf_op jit(solution)/shard_map/all_to_all | solution.py:680
  39.8 1.0 %copy-done.7 = bf16[1,256,1024]{2,1,0:T(8,128)(2,1)S(1)} copy-done((bf16[1,256,1024]{2,1,0:T(8,128)(2,1)S(1)}, bf16[1,256,1024]{2,1,0:T(8,128)(2,1)}, u32[]{:S(2)}) %copy-start.7) | copy-done | bytes 524312
  40.8 11.0 %normal_matrix.1 = (f32[48,48]{1,0:T(8,128)S(1)}, f32[10,2,152,128]{3,2,1,0:T(8,128)S(1)}) custom-call(s32[16]{0:T(128)S(1)} %copy-done.10, s32[1,4]{1,0:T(1,128)S(1)} %copy-done.8, s32[1,4]{1,0:T(1,128)S(1)} %copy-done.9, bf16[16,128,128]{2,1,0:T(8,128)(2,1)S(1)} %all-to-all-done.1.arrived, f32[48,128]{1,0:T(8,128)S(1)} %pad_convert_fusion.col, ...), custom_call_target="tpu_custom_call" | custom-call | flops 10000000000 | bytes 8000000 | tf_op jit(solution)/shard_map/normal_matrix/pallas_call | solution.py:281
  51.9 5.9 %subtract.1 = (f32[1,128]{1,0:T(1,128)}, bf16[32,72,128]{2,1,0:T(8,128)(2,1)}) custom-call(s32[16]{0:T(128)S(1)} %copy-done.6, f32[48,48]{1,0:T(8,128)S(1)} %get-tuple-element.23.gram, f32[10,2,152,128]{3,2,1,0:T(8,128)S(1)} %get-tuple-element.24.frames, bf16[256,1024]{1,0:T(8,128)(2,1)S(1)} %bitcast.16, bf16[32,48]{1,0:T(8,128)(2,1)S(1)} %pad.25.col_t, ...), custom_call_target="tpu_custom_call" | custom-call | flops 5000000000 | bytes 4000000 | tf_op jit(solution)/shard_map/subtract/pallas_call | solution.py:444
  57.8 5.8 %all-to-all-start.3 = ((bf16[32,72,128]{2,1,0:T(8,128)(2,1)}), bf16[32,72,128]{2,1,0:T(8,128)(2,1)S(1)}, u32[]{:S(2)}, u32[]{:S(2)}) async-start(bf16[32,72,128]{2,1,0:T(8,128)(2,1)} %get-tuple-element.25.payload), calls=%async_computation.3 | async-start | bytes 1179648 | tf_op jit(solution)/shard_map/all_to_all | solution.py:712
  64.0 3.8 %score.1 = (f32[256,1024]{1,0:T(8,128)}, f32[32,32,128]{2,1,0:T(8,128)S(1)}) custom-call(s32[32,2]{1,0:T(8,128)S(1)} %bitcast.13, s32[16]{0:T(128)S(1)} %copy-done.10, bf16[32,72,128]{2,1,0:T(8,128)(2,1)} %get-tuple-element.25.payload, f32[1,256]{1,0:T(1,128)S(1)} %pad.26.down, f32[1,256]{1,0:T(1,128)S(1)} %pad_maximum_fusion.1.over, ...), custom_call_target="tpu_custom_call" | custom-call | flops 2000000000 | bytes 2000000 | tf_op jit(solution)/shard_map/score/pallas_call | solution.py:530
  67.8 12.7 %all-to-all-done.3.parts = bf16[32,72,128]{2,1,0:T(8,128)(2,1)S(1)} async-done(((bf16[32,72,128]{2,1,0:T(8,128)(2,1)}), bf16[32,72,128]{2,1,0:T(8,128)(2,1)S(1)}, u32[]{:S(2)}, u32[]{:S(2)}) %all-to-all-start.3) | async-done | bytes 589856 | tf_op jit(solution)/shard_map/all_to_all | solution.py:712
  80.5 1.3 %combine.1.refs_0_ = bf16[32,32,128]{2,1,0:T(8,128)(2,1)S(1)} custom-call(s32[32,2]{1,0:T(8,128)S(1)} %bitcast.14, bf16[32,72,128]{2,1,0:T(8,128)(2,1)S(1)} %all-to-all-done.3.parts, f32[32,32,128]{2,1,0:T(8,128)S(1)} %get-tuple-element.26.var_sum, bf16[32,32,128]{2,1,0:T(8,128)(2,1)S(1)} %constant_dynamic-slice_fusion.var_template), custom_call_target="tpu_custom_call" | custom-call | tf_op jit(solution)/shard_map/combine/pallas_call | solution.py:588
  81.8 1.3 %collective-permute-start = (bf16[32,32,128]{2,1,0:T(8,128)(2,1)S(1)}, bf16[32,32,128]{2,1,0:T(8,128)(2,1)S(1)}, u32[]{:S(2)}, u32[]{:S(2)}) collective-permute-start(bf16[32,32,128]{2,1,0:T(8,128)(2,1)S(1)} %combine.1.refs_0_), channel_id=1, source_target_pairs={{0,2},{1,3},{2,0},{3,1},{4,6},{5,7},{6,4},{7,5},{8,10},{9,11},{10,... | collective-permute-start | bytes 786440 | tf_op jit(solution)/shard_map/ppermute | solution.py:735
  83.5 5.1 %collective-permute-done.refs_0_ = bf16[32,32,128]{2,1,0:T(8,128)(2,1)S(1)} collective-permute-done((bf16[32,32,128]{2,1,0:T(8,128)(2,1)S(1)}, bf16[32,32,128]{2,1,0:T(8,128)(2,1)S(1)}, u32[]{:S(2)}, u32[]{:S(2)}) %collective-permute-start) | collective-permute-done | bytes 262176 | tf_op jit(solution)/shard_map/ppermute | solution.py:735
  88.6 2.0 %collective-permute-start.1 = (bf16[32,32,128]{2,1,0:T(8,128)(2,1)S(1)}, bf16[32,32,128]{2,1,0:T(8,128)(2,1)S(1)}, u32[]{:S(2)}, u32[]{:S(2)}) collective-permute-start(bf16[32,32,128]{2,1,0:T(8,128)(2,1)S(1)} %collective-permute-done.refs_0_), channel_id=1, source_target_pairs={{0,1},{1,0},{2,3},{3,2},{4,5},{5,4},{6,7},{7,6},{8,9},{9,8},{10,11... | collective-permute-start | bytes 786440 | tf_op jit(solution)/shard_map/ppermute | solution.py:735
  90.7 1.6 %join_parts.3.refs_1_ = f32[32,128,128]{2,1,0:T(8,128)} custom-call(s32[2]{0:T(128)S(1)} %pad_add_fusion.places, bf16[32,32,128]{2,1,0:T(8,128)(2,1)S(1)} %combine.1.refs_0_, bf16[32,32,128]{2,1,0:T(8,128)(2,1)S(1)} %collective-permute-done.2.refs_1_), custom_call_target="tpu_custom_call" | custom-call | bytes 6000000 | tf_op jit(solution)/shard_map/join_parts/pallas_call | solution.py:622
  92.2 0.8 join_parts.4.refs_1_
  93.1 0.8 join_parts.5
  (45 shorter events, 1.4 us)
Async XLA Ops:
  0.6 63.3 %copy-start = (bf16[32,128,128]{2,1,0:T(8,128)(2,1)S(1)}, bf16[32,128,128]{2,1,0:T(8,128)(2,1)}, u32[]{:S(2)}) copy-start(bf16[32,128,128]{2,1,0:T(8,128)(2,1)} %param.13) | copy-start | bytes 3145732
  2.2 11.7 %all-to-all-start = ((s32[8,1,2]{2,1,0:T(1,128)}), s32[8,1,2]{2,1,0:T(1,128)S(1)}, u32[]{:S(2)}, u32[]{:S(2)}) async-start(s32[8,1,2]{2,1,0:T(1,128)} %get-tuple-element.17.request), calls=%async_computation | async-start | bytes 8192 | tf_op jit(solution)/shard_map/all_to_all | solution.py:665
  8.6 1.2 %copy-start.1 = (bf16[32,128,128]{2,1,0:T(8,128)(2,1)S(1)}, bf16[32,128,128]{2,1,0:T(8,128)(2,1)}, u32[]{:S(2)}) copy-start(bf16[32,128,128]{2,1,0:T(8,128)(2,1)} %template.1) | copy-start | bytes 3145732
  9.8 1.0 %copy-start.2 = (bf16[1,256,1024]{2,1,0:T(8,128)(2,1)S(1)}, bf16[1,256,1024]{2,1,0:T(8,128)(2,1)}, u32[]{:S(2)}) copy-start(bf16[1,256,1024]{2,1,0:T(8,128)(2,1)} %param.15) | copy-start | bytes 1572868
  10.8 0.7 copy-start.4
  11.5 0.6 copy-start.5
  12.2 8.7 %copy-start.12 = (bf16[40,21]{0,1:T(8,128)(2,1)S(1)}, bf16[40,21]{0,1:T(8,128)(2,1)}, u32[]{:S(2)}) copy-start(bf16[40,21]{0,1:T(8,128)(2,1)} %param.21) | copy-start | bytes 5044
  12.2 8.8 %copy-start.11 = (bf16[40,21]{0,1:T(8,128)(2,1)S(1)}, bf16[40,21]{0,1:T(8,128)(2,1)}, u32[]{:S(2)}) copy-start(bf16[40,21]{0,1:T(8,128)(2,1)} %param.20) | copy-start | bytes 5044
  13.9 25.9 %copy-start.3 = (bf16[1,256,1024]{2,1,0:T(8,128)(2,1)S(1)}, bf16[1,256,1024]{2,1,0:T(8,128)(2,1)}, u32[]{:S(2)}) copy-start(bf16[1,256,1024]{2,1,0:T(8,128)(2,1)} %param.15) | copy-start | bytes 1572868
  13.9 25.8 %copy-start.8 = (s32[1,4]{1,0:T(1,128)S(1)}, s32[1,4]{1,0:T(1,128)}, u32[]{:S(2)}) copy-start(s32[1,4]{1,0:T(1,128)} %rows_at.1) | copy-start | bytes 52
  13.9 25.8 %copy-start.9 = (s32[1,4]{1,0:T(1,128)S(1)}, s32[1,4]{1,0:T(1,128)}, u32[]{:S(2)}) copy-start(s32[1,4]{1,0:T(1,128)} %cols_at.1) | copy-start | bytes 52
  13.9 25.8 %copy-start.10 = (s32[16]{0:T(128)S(1)}, s32[16]{0:T(128)}, u32[]{:S(2)}) copy-start(s32[16]{0:T(128)} %get-tuple-element.21.slot_of) | copy-start | bytes 196
  15.4 18.8 %all-to-all-start.1 = ((bf16[16,128,128]{2,1,0:T(8,128)(2,1)}), bf16[16,128,128]{2,1,0:T(8,128)(2,1)S(1)}, u32[]{:S(2)}, u32[]{:S(2)}) async-start(bf16[16,128,128]{2,1,0:T(8,128)(2,1)} %pick_blocks.1), calls=%async_computation.1 | async-start | bytes 1048576 | tf_op jit(solution)/shard_map/all_to_all | solution.py:668
  34.1 23.7 %all-to-all-start.2 = ((bf16[32,72,128]{2,1,0:T(8,128)(2,1)}), bf16[32,72,128]{2,1,0:T(8,128)(2,1)S(1)}, u32[]{:S(2)}, u32[]{:S(2)}) async-start(bf16[32,72,128]{2,1,0:T(8,128)(2,1)} %get-tuple-element.20), calls=%async_computation.2 | async-start | bytes 1179648 | tf_op jit(solution)/shard_map/all_to_all | solution.py:680
  39.8 1.0 %copy-start.7 = (bf16[1,256,1024]{2,1,0:T(8,128)(2,1)S(1)}, bf16[1,256,1024]{2,1,0:T(8,128)(2,1)}, u32[]{:S(2)}) copy-start(bf16[1,256,1024]{2,1,0:T(8,128)(2,1)} %param.14) | copy-start | bytes 1572868
  40.8 11.0 %copy-start.6 = (s32[16]{0:T(128)S(1)}, s32[16]{0:T(128)}, u32[]{:S(2)}) copy-start(s32[16]{0:T(128)} %get-tuple-element.16.sender) | copy-start | bytes 196
  51.9 11.8 %copy-start.13 = (f32[1,21]{1,0:T(1,128)S(1)}, f32[1,21]{1,0:T(1,128)}, u32[]{:S(2)}) copy-start(f32[1,21]{1,0:T(1,128)} %param.23) | copy-start | bytes 256
  51.9 11.9 %copy-start.14 = (f32[1,21]{1,0:T(1,128)S(1)}, f32[1,21]{1,0:T(1,128)}, u32[]{:S(2)}) copy-start(f32[1,21]{1,0:T(1,128)} %param.22) | copy-start | bytes 256
  57.8 22.7 %all-to-all-start.3 = ((bf16[32,72,128]{2,1,0:T(8,128)(2,1)}), bf16[32,72,128]{2,1,0:T(8,128)(2,1)S(1)}, u32[]{:S(2)}, u32[]{:S(2)}) async-start(bf16[32,72,128]{2,1,0:T(8,128)(2,1)} %get-tuple-element.25.payload), calls=%async_computation.3 | async-start | bytes 1179648 | tf_op jit(solution)/shard_map/all_to_all | solution.py:712
  81.8 6.8 %collective-permute-start = (bf16[32,32,128]{2,1,0:T(8,128)(2,1)S(1)}, bf16[32,32,128]{2,1,0:T(8,128)(2,1)S(1)}, u32[]{:S(2)}, u32[]{:S(2)}) collective-permute-start(bf16[32,32,128]{2,1,0:T(8,128)(2,1)S(1)} %combine.1.refs_0_), channel_id=1, source_target_pairs={{0,2},{1,3},{2,0},{3,1},{4,6},{5,7},{6,4},{7,5},{8,10},{9,11},{10,... | collective-permute-start | bytes 786440 | tf_op jit(solution)/shard_map/ppermute | solution.py:735
  83.1 7.6 %collective-permute-start.2 = (bf16[32,32,128]{2,1,0:T(8,128)(2,1)S(1)}, bf16[32,32,128]{2,1,0:T(8,128)(2,1)S(1)}, u32[]{:S(2)}, u32[]{:S(2)}) collective-permute-start(bf16[32,32,128]{2,1,0:T(8,128)(2,1)S(1)} %combine.1.refs_0_), channel_id=1, source_target_pairs={{0,1},{1,0},{2,3},{3,2},{4,5},{5,4},{6,7},{7,6},{8,9},{9,8},{10,11... | collective-permute-start | bytes 786440 | tf_op jit(solution)/shard_map/ppermute | solution.py:735
  88.6 4.5 %collective-permute-start.1 = (bf16[32,32,128]{2,1,0:T(8,128)(2,1)S(1)}, bf16[32,32,128]{2,1,0:T(8,128)(2,1)S(1)}, u32[]{:S(2)}, u32[]{:S(2)}) collective-permute-start(bf16[32,32,128]{2,1,0:T(8,128)(2,1)S(1)} %collective-permute-done.refs_0_), channel_id=1, source_target_pairs={{0,1},{1,0},{2,3},{3,2},{4,5},{5,4},{6,7},{7,6},{8,9},{9,8},{10,11... | collective-permute-start | bytes 786440 | tf_op jit(solution)/shard_map/ppermute | solution.py:735

commit v3 on v2

--- a/solution.py
+++ b/solution.py
@@ -60,7 +60,25 @@
     )(routes_src, routes_blk)
 
 
-def pick_body(asked, template, out, *, capacity):
+def touch_body(template, out):
+    out[...] = template[0, : out.shape[0], : out.shape[1]]
+
+
+def touch(template):
+    return pl.pallas_call(
+        touch_body,
+        out_shape=jax.ShapeDtypeStruct((16, 128), template.dtype),
+        in_specs=[vmem()],
+        out_specs=vmem(),
+        compiler_params=pltpu.CompilerParams(vmem_limit_bytes=16 * mib),
+        cost_estimate=cost(0, 4_000_000),
+        name="touch",
+    )(template)
+
+
+def pick_body(asked, template, earlier, out, *, capacity):
+    del earlier
+
     def one(s, carry):
         block = jnp.maximum(asked[s // capacity, 0, s % capacity] - 1, 0)
         out[s] = template[block]
@@ -69,21 +87,20 @@
     lax.fori_loop(0, out.shape[0], one, 0, unroll=True if out.shape[0] <= 32 else 4)
 
 
-def pick_blocks(asked, template, slots, capacity):
+def pick_blocks(asked, template, earlier, slots, capacity):
     return pl.pallas_call(
         functools.partial(pick_body, capacity=capacity),
         out_shape=jax.ShapeDtypeStruct((slots,) + template.shape[1:], template.dtype),
-        in_specs=[smem(), vmem()],
+        in_specs=[smem(), vmem(), pl.BlockSpec(memory_space=pl.ANY)],
         out_specs=vmem(),
         compiler_params=pltpu.CompilerParams(vmem_limit_bytes=16 * mib),
         name="pick_blocks",
-    )(asked, template)
+    )(asked, template, earlier)
 
 
 def store_parts(sender, image, out, side, exps, capacity, across_blocks):
     part = side // exps
     slots = sender.shape[0]
-    peers = slots // capacity
 
     def one(s, carry):
         b = sender[s]
@@ -92,7 +109,7 @@
         block = image[pl.ds(top, side), pl.ds(left, side)].astype(bf16)
         row = pl.multiple_of((s % capacity) * part, part)
         for q in range(exps):
-            out[q * peers + s // capacity, pl.ds(row, part), :] = block[q * part : (q + 1) * part]
+            out[(s // capacity) * exps + q, pl.ds(row, part), :] = block[q * part : (q + 1) * part]
         return carry
 
     lax.fori_loop(0, slots, one, 0, unroll=True if slots <= 32 else 4)
@@ -106,7 +123,7 @@
         for c in range(capacity):
             line = jnp.where(lane == c, request[p, 0, c].astype(f32), line)
         for q in range(exps):
-            out[q * request.shape[0] + p, out.shape[1] - trailer_rows :, :] = line.astype(bf16)
+            out[p * exps + q, out.shape[1] - trailer_rows :, :] = line.astype(bf16)
         return carry
 
     lax.fori_loop(0, request.shape[0], put, 0)
@@ -120,29 +137,23 @@
     return pltpu.roll(tile, lax.rem(height - (top - down), height), 0)
 
 
-def prepare_body(sender, request, variance, template, out, near, sem, *, side, exps, capacity):
-    copy = pltpu.make_async_copy(template, near, sem)
-    copy.start()
+def prepare_body(sender, request, variance, earlier, out, *, side, exps, capacity):
+    del earlier
     store_parts(sender, variance, out, side, exps, capacity, variance.shape[1] // side)
     store_requests(request, out, side, exps, capacity)
-    copy.wait()
-
-
-def prepare(sender, request, variance, template, side, exps, capacity):
+
+
+def prepare(sender, request, variance, earlier, side, exps, capacity):
     rows = capacity * (side // exps) + trailer_rows
     return pl.pallas_call(
         functools.partial(prepare_body, side=side, exps=exps, capacity=capacity),
-        out_shape=(
-            jax.ShapeDtypeStruct((request.shape[0] * exps, rows, side), bf16),
-            jax.ShapeDtypeStruct(template.shape, template.dtype),
-        ),
+        out_shape=jax.ShapeDtypeStruct((request.shape[0] * exps, rows, side), bf16),
         in_specs=[smem()] * 2 + [vmem(), pl.BlockSpec(memory_space=pl.ANY)],
-        out_specs=(vmem(), vmem()),
-        scratch_shapes=[pltpu.SemaphoreType.DMA(())],
+        out_specs=vmem(),
         compiler_params=pltpu.CompilerParams(vmem_limit_bytes=16 * mib),
         cost_estimate=cost(0, 6_000_000),
         name="prepare",
-    )(sender, request, variance, template)
+    )(sender, request, variance, earlier)
 
 
 def normal_body(
@@ -295,7 +306,7 @@
             pltpu.VMEM((stamps * side, side), f32),
             pltpu.VMEM((tall, side), f32),
         ],
-        compiler_params=pltpu.CompilerParams(vmem_limit_bytes=36 * mib),
+        compiler_params=pltpu.CompilerParams(vmem_limit_bytes=28 * mib),
         cost_estimate=cost(10_000_000_000, 8_000_000),
         name="normal_matrix",
     )(slot_of, rows_at, cols_at, arrived, col, row_rev, science, variance)
@@ -458,7 +469,7 @@
             pltpu.VMEM((wins * high // 2, 2 * side), f32),
             pltpu.VMEM((pairs, wins * high // 2, 2 * side), bf16),
         ],
-        compiler_params=pltpu.CompilerParams(vmem_limit_bytes=32 * mib),
+        compiler_params=pltpu.CompilerParams(vmem_limit_bytes=24 * mib),
         cost_estimate=cost(5_000_000_000, 4_000_000),
         name="subtract",
     )(sender, gram, frames, science, col_t, row_rev)
@@ -493,7 +504,6 @@
     span = up(side + taps - 1, 16)
     across_blocks = wide // side
     exps = side // part
-    peers = payload.shape[0] // exps
     padded[...] = jnp.zeros(padded.shape, f32)
     for b in range(slot_of.shape[0]):
         slot = slot_of[b]
@@ -501,7 +511,7 @@
         left = margin + (b % across_blocks) * side
         for q in range(exps):
             top = (b // across_blocks) * side + q * part
-            block = payload[q * peers + slot // capacity, pl.ds(row, part), :]
+            block = payload[(slot // capacity) * exps + q, pl.ds(row, part), :]
             padded[top : top + part, left : left + side] = block.astype(f32)
     line = jnp.broadcast_to(over[...], (2 * side, 2 * side))
     band = pltpu.roll(line, 0, 1, stride=1, stride_axis=0)[:, :side]
@@ -599,9 +609,9 @@
     )(table, parts, var_sum, var_template)
 
 
-def join_body(places, *refs, part, count, fresh):
+def join_body(places, *refs, part, count):
+    ins = refs[:count]
     out, held, sems = refs[-3:]
-    ins = refs[:count]
     copies = []
     for d, ref in enumerate(ins):
         held[d] = ref[...].astype(f32)
@@ -620,7 +630,7 @@
     fresh = whole is None
     anywhere = pl.BlockSpec(memory_space=pl.ANY)
     return pl.pallas_call(
-        functools.partial(join_body, part=part, count=count, fresh=fresh),
+        functools.partial(join_body, part=part, count=count),
         out_shape=jax.ShapeDtypeStruct((tract, part * exps, side), f32),
         in_specs=[smem()] + [vmem()] * count + ([] if fresh else [anywhere]),
         out_specs=anywhere,
@@ -663,8 +673,8 @@
 
     slot_of, sender, request = route_tables(routes_src, routes_blk, peers, capacity)
     asked = lax.all_to_all(request, "det", split_axis=0, concat_axis=0, tiled=True)
-    var_parts, near = prepare(sender, request, variance_img, template, side, exps, capacity)
-    picked = pick_blocks(asked, near, slots, capacity)
+    picked = pick_blocks(asked, template, touch(template), slots, capacity)
+    var_parts = prepare(sender, request, variance_img, picked, side, exps, capacity)
     arrived = lax.all_to_all(picked, "det", split_axis=0, concat_axis=0, tiled=True)
 
     padded_k = up(count + 2, 16)
@@ -678,7 +688,7 @@
     down = jnp.pad(psf_col, ((0, 0), (0, 2 * side - taps)))
     var_late, arrived = lax.optimization_barrier((var_parts, arrived))
     var_back = lax.all_to_all(
-        var_late, ("exp", "det"), split_axis=0, concat_axis=0, tiled=True
+        var_late, ("det", "exp"), split_axis=0, concat_axis=0, tiled=True
     )
     table = var_back[:, capacity * part, :capacity].astype(f32).astype(jnp.int32)
 
@@ -709,7 +719,7 @@
         taps,
         stamp_rows.shape[1] * side * side,
     )
-    diff_back = lax.all_to_all(payload, ("exp", "det"), split_axis=0, concat_axis=0, tiled=True)
+    diff_back = lax.all_to_all(payload, ("det", "exp"), split_axis=0, concat_axis=0, tiled=True)
     scored, var_sum = score(
         table,
         slot_of,
@@ -727,25 +737,25 @@
     var_template = lax.dynamic_slice_in_dim(template_var, me * part, part, 1)
     mine = combine(table, diff_back, var_sum, var_template, part, capacity)
 
-    if exps & (exps - 1) == 0:
-        held = {0: mine}
-        reach = exps // 2
-        while reach:
-            pairs = [(e, e ^ reach) for e in range(exps)]
-            held.update({g ^ reach: lax.ppermute(h, "exp", pairs) for g, h in held.items()})
-            reach //= 2
-        there = {g: me ^ g for g in held}
+    def swap(value, distance):
+        return lax.ppermute(value, "exp", [(e, e ^ distance) for e in range(exps)])
+
+    def put(parts, whole):
+        places = jnp.stack([there for there, _ in parts])
+        return join_parts(places, [held for _, held in parts], whole, exps)
+
+    if exps == 4:
+        far = swap(mine, 2)
+        near = swap(mine, 1)
+        last = swap(far, 1)
+        whole = put([(me, mine), (me ^ 1, near), (me ^ 2, far)], None)
+        significance = put([(me ^ 3, last)], whole)
     else:
-        held = {0: mine}
+        parts = [(me, mine)]
         for gap in range(1, exps):
             pairs = [(e, (e + gap) % exps) for e in range(exps)]
-            held[gap] = lax.ppermute(mine, "exp", pairs)
-        there = {g: (me - g) % exps for g in held}
-    first = max(1, exps // 2)
-    significance = None
-    for gaps in [list(range(first))] + [[g] for g in range(first, exps)]:
-        places = jnp.stack([there[g] for g in gaps])
-        significance = join_parts(places, [held[g] for g in gaps], significance, exps)
+            parts.append(((me - gap) % exps, lax.ppermute(mine, "exp", pairs)))
+        significance = put(parts, None)
     return (significance, scored[None], coef[:, : count + 1])
 
 

time: 94.6 us -> 91.6 us (0.968)
  local copies, waits for them, and re-layouts: 5.3 us -> 3.12 us
    all_to_all x1, waiting for transfers between devices: 12.8 us -> 8.74 us  [local(): lax.all_to_all(picked, 'det', split_axis=0, concat_axis=0, tiled=True)]
    all_to_all x1, waiting for transfers between devices: 0.01 us -> 4.01 us  [local(): lax.all_to_all(request, 'det', split_axis=0, concat_axis=0, tiled=True)]
    all_to_all x2, starting transfers between devices: 11.4 us -> 13.7 us  [the longest x1 7.88 us: local(): lax.all_to_all(var_late, ('det', 'exp'), split_axis=0, concat_axis=0, til...]
    unnamed x31 -> x29, local copies, waits for them, and re-layouts: 4.78 us -> 2.61 us
    all_to_all x1, starting transfers between devices: 5.44 us -> 3.64 us  [local(): lax.all_to_all(picked, 'det', split_axis=0, concat_axis=0, tiled=True)]
  transfers between devices with their start and end apart: 7 -> 7, of which waited for: 3 -> 4; matrix products, arithmetic and copies ran while one was open for 1% -> 1% of each run, Pallas kernels for 27% -> 27%
where the time goes in v3:
time: 91.6 us; the launch traced here: 91 us
  waiting for transfers between devices  30.7 us (34%)
  Pallas kernels  29.3 us (32%)
  starting transfers between devices  26.8 us (29%)
  local copies, waits for them, and re-layouts  3.12 us (3%)
    all_to_all x1, waiting for transfers between devices, local(): lax.all_to_all(payload, ('det', 'exp'), split_axis=0, concat_axis=0, tile...  12.3 us
    pallas_call x1, Pallas kernels, normal_matrix(): pl.pallas_call(functools.partial(normal_body, count=count, across_blocks=...  11 us
    all_to_all x1, waiting for transfers between devices, local(): lax.all_to_all(picked, 'det', split_axis=0, concat_axis=0, tiled=True)  8.74 us
    all_to_all x1, starting transfers between devices, local(): lax.all_to_all(var_late, ('det', 'exp'), split_axis=0, concat_axis=0, til...  7.88 us
    all_to_all x1, starting transfers between devices, local(): lax.all_to_all(request, 'det', split_axis=0, concat_axis=0, tiled=True)  6.37 us
    pallas_call x1, Pallas kernels, subtract(): pl.pallas_call(body, out_shape=(jax.ShapeDtypeStruct((1, side), f32), jax...  5.9 us
    all_to_all x1, starting transfers between devices, local(): lax.all_to_all(payload, ('det', 'exp'), split_axis=0, concat_axis=0, tile...  5.83 us
    ppermute x3, waiting for transfers between devices, swap(): return lax.ppermute(value, 'exp', [(e, e ^ distance) for e in range(exps)])  5.66 us
  transfers between devices with their start and end apart: 7, of which 4 were waited for; matrix products, arithmetic and copies ran while one was open for 1% of the time, Pallas kernels for 27%

profile of v3, /device:TPU:1, one launch (start us, length us, event | category | flops | bytes accessed | tf_op | source)
XLA Modules:
  0.0 91.0 jit_solution(12491552063169344855)
XLA Ops:
  0.7 1.5 %route_tables.1 = (s32[16]{0:T(128)}, s32[16]{0:T(128)}, s32[8,1,2]{2,1,0:T(1,128)}) custom-call(s32[1,16]{1,0:T(1,128)} %src.1, s32[1,16]{1,0:T(1,128)} %blk.1), custom_call_target="tpu_custom_call" | custom-call | tf_op jit(solution)/shard_map/route_tables/pallas_call | solution.py:49
  2.2 6.4 %all-to-all-start = ((s32[8,1,2]{2,1,0:T(1,128)}), s32[8,1,2]{2,1,0:T(1,128)S(1)}, u32[]{:S(2)}, u32[]{:S(2)}) async-start(s32[8,1,2]{2,1,0:T(1,128)} %get-tuple-element.15.request), calls=%async_computation | async-start | bytes 8192 | tf_op jit(solution)/shard_map/all_to_all | solution.py:675
  8.6 1.2 %copy-done.1 = bf16[32,128,128]{2,1,0:T(8,128)(2,1)S(1)} copy-done((bf16[32,128,128]{2,1,0:T(8,128)(2,1)S(1)}, bf16[32,128,128]{2,1,0:T(8,128)(2,1)}, u32[]{:S(2)}) %copy-start.1) | copy-done | bytes 1048600
  9.8 4.0 %all-to-all-done.asked = s32[8,1,2]{2,1,0:T(1,128)S(1)} async-done(((s32[8,1,2]{2,1,0:T(1,128)}), s32[8,1,2]{2,1,0:T(1,128)S(1)}, u32[]{:S(2)}, u32[]{:S(2)}) %all-to-all-start) | async-done | bytes 96 | tf_op jit(solution)/shard_map/all_to_all | solution.py:675
  13.8 1.2 %copy-done.2 = bf16[32,128,128]{2,1,0:T(8,128)(2,1)S(1)} copy-done((bf16[32,128,128]{2,1,0:T(8,128)(2,1)S(1)}, bf16[32,128,128]{2,1,0:T(8,128)(2,1)}, u32[]{:S(2)}) %copy-start.2) | copy-done | bytes 1048600
  15.1 1.4 %pick_blocks.1.earlier = bf16[16,128,128]{2,1,0:T(8,128)(2,1)} custom-call(s32[8,1,2]{2,1,0:T(1,128)S(1)} %all-to-all-done.asked, bf16[32,128,128]{2,1,0:T(8,128)(2,1)S(1)} %copy-done.2, bf16[16,128]{1,0:T(8,128)(2,1)S(1)} %touch.1.earlier), custom_call_target="tpu_custom_call" | custom-call | tf_op jit(solution)/shard_map/pick_blocks/pallas_call | solution.py:91
  16.5 3.6 %all-to-all-start.1 = ((bf16[16,128,128]{2,1,0:T(8,128)(2,1)}), bf16[16,128,128]{2,1,0:T(8,128)(2,1)S(1)}, u32[]{:S(2)}, u32[]{:S(2)}) async-start(bf16[16,128,128]{2,1,0:T(8,128)(2,1)} %pick_blocks.1.earlier), calls=%async_computation.1 | async-start | bytes 1048576 | tf_op jit(solution)/shard_map/all_to_all | solution.py:678
  20.2 0.1 copy.22
  20.7 1.6 %prepare.1 = bf16[32,72,128]{2,1,0:T(8,128)(2,1)} custom-call(s32[16]{0:T(128)S(1)} %copy-done.5, s32[8,1,2]{2,1,0:T(1,128)S(1)} %copy-done.4, bf16[256,1024]{1,0:T(8,128)(2,1)S(1)} %bitcast.11, bf16[16,128,128]{2,1,0:T(8,128)(2,1)} %pick_blocks.1.earlier), custom_call_target="tpu_custom_call" | custom-call | bytes 6000000 | tf_op jit(solution)/shard_map/prepare/pallas_call | solution.py:148
  22.3 8.7 %all-to-all-done.1.arrived = bf16[16,128,128]{2,1,0:T(8,128)(2,1)S(1)} async-done(((bf16[16,128,128]{2,1,0:T(8,128)(2,1)}), bf16[16,128,128]{2,1,0:T(8,128)(2,1)S(1)}, u32[]{:S(2)}, u32[]{:S(2)}) %all-to-all-start.1) | async-done | bytes 524320 | tf_op jit(solution)/shard_map/all_to_all | solution.py:678
  31.1 7.9 %all-to-all-start.2 = ((bf16[32,72,128]{2,1,0:T(8,128)(2,1)}), bf16[32,72,128]{2,1,0:T(8,128)(2,1)S(1)}, u32[]{:S(2)}, u32[]{:S(2)}) async-start(bf16[32,72,128]{2,1,0:T(8,128)(2,1)} %prepare.1), calls=%async_computation.2 | async-start | bytes 1179648 | tf_op jit(solution)/shard_map/all_to_all | solution.py:690
  39.0 11.0 %normal_matrix.1 = (f32[48,48]{1,0:T(8,128)S(1)}, f32[10,2,152,128]{3,2,1,0:T(8,128)S(1)}) custom-call(s32[16]{0:T(128)S(1)} %copy-done.9, s32[1,4]{1,0:T(1,128)S(1)} %copy-done.7, s32[1,4]{1,0:T(1,128)S(1)} %copy-done.8, bf16[16,128,128]{2,1,0:T(8,128)(2,1)S(1)} %all-to-all-done.1.arrived, f32[48,128]{1,0:T(8,128)S(1)} %pad_convert_fusion.col, ...), custom_call_target="tpu_custom_call" | custom-call | flops 10000000000 | bytes 8000000 | tf_op jit(solution)/shard_map/normal_matrix/pallas_call | solution.py:292
  50.1 5.9 %subtract.1 = (f32[1,128]{1,0:T(1,128)}, bf16[32,72,128]{2,1,0:T(8,128)(2,1)}) custom-call(s32[16]{0:T(128)S(1)} %copy-done.5, f32[48,48]{1,0:T(8,128)S(1)} %get-tuple-element.19.gram, f32[10,2,152,128]{3,2,1,0:T(8,128)S(1)} %get-tuple-element.20.frames, bf16[256,1024]{1,0:T(8,128)(2,1)S(1)} %bitcast.16, bf16[32,48]{1,0:T(8,128)(2,1)S(1)} %pad.25.col_t, ...), custom_call_target="tpu_custom_call" | custom-call | flops 5000000000 | bytes 4000000 | tf_op jit(solution)/shard_map/subtract/pallas_call | solution.py:455
  56.0 5.8 %all-to-all-start.3 = ((bf16[32,72,128]{2,1,0:T(8,128)(2,1)}), bf16[32,72,128]{2,1,0:T(8,128)(2,1)S(1)}, u32[]{:S(2)}, u32[]{:S(2)}) async-start(bf16[32,72,128]{2,1,0:T(8,128)(2,1)} %get-tuple-element.21.payload), calls=%async_computation.3 | async-start | bytes 1179648 | tf_op jit(solution)/shard_map/all_to_all | solution.py:722
  62.0 0.1 pad_maximum_fusion.1.over
  62.2 3.9 %score.1 = (f32[256,1024]{1,0:T(8,128)}, f32[32,32,128]{2,1,0:T(8,128)S(1)}) custom-call(s32[32,2]{1,0:T(8,128)S(1)} %bitcast.13, s32[16]{0:T(128)S(1)} %copy-done.9, bf16[32,72,128]{2,1,0:T(8,128)(2,1)} %get-tuple-element.21.payload, f32[1,256]{1,0:T(1,128)S(1)} %pad.26.down, f32[1,256]{1,0:T(1,128)S(1)} %pad_maximum_fusion.1.over, ...), custom_call_target="tpu_custom_call" | custom-call | flops 2000000000 | bytes 2000000 | tf_op jit(solution)/shard_map/score/pallas_call | solution.py:540
  66.0 12.3 %all-to-all-done.3.parts = bf16[32,72,128]{2,1,0:T(8,128)(2,1)S(1)} async-done(((bf16[32,72,128]{2,1,0:T(8,128)(2,1)}), bf16[32,72,128]{2,1,0:T(8,128)(2,1)S(1)}, u32[]{:S(2)}, u32[]{:S(2)}) %all-to-all-start.3) | async-done | bytes 589856 | tf_op jit(solution)/shard_map/all_to_all | solution.py:722
  78.3 1.3 %combine.1.refs_0_ = bf16[32,32,128]{2,1,0:T(8,128)(2,1)S(1)} custom-call(s32[32,2]{1,0:T(8,128)S(1)} %bitcast.14, bf16[32,72,128]{2,1,0:T(8,128)(2,1)S(1)} %all-to-all-done.3.parts, f32[32,32,128]{2,1,0:T(8,128)S(1)} %get-tuple-element.22.var_sum, bf16[32,32,128]{2,1,0:T(8,128)(2,1)S(1)} %constant_dynamic-slice_fusion.var_template), custom_call_target="tpu_custom_call" | custom-call | tf_op jit(solution)/shard_map/combine/pallas_call | solution.py:598
  79.6 1.3 %collective-permute-start = (bf16[32,32,128]{2,1,0:T(8,128)(2,1)S(1)}, bf16[32,32,128]{2,1,0:T(8,128)(2,1)S(1)}, u32[]{:S(2)}, u32[]{:S(2)}) collective-permute-start(bf16[32,32,128]{2,1,0:T(8,128)(2,1)S(1)} %combine.1.refs_0_), channel_id=1, source_target_pairs={{0,2},{1,3},{2,0},{3,1},{4,6},{5,7},{6,4},{7,5},{8,10},{9,11},{10,... | collective-permute-start | bytes 786440 | tf_op jit(solution)/shard_map/ppermute | solution.py:741
  80.9 0.4 collective-permute-start.2
  81.3 5.7 %collective-permute-done.refs_2_ = bf16[32,32,128]{2,1,0:T(8,128)(2,1)S(1)} collective-permute-done((bf16[32,32,128]{2,1,0:T(8,128)(2,1)S(1)}, bf16[32,32,128]{2,1,0:T(8,128)(2,1)S(1)}, u32[]{:S(2)}, u32[]{:S(2)}) %collective-permute-start) | collective-permute-done | bytes 262176 | tf_op jit(solution)/shard_map/ppermute | solution.py:741
  87.0 1.4 %collective-permute-start.1 = (bf16[32,32,128]{2,1,0:T(8,128)(2,1)S(1)}, bf16[32,32,128]{2,1,0:T(8,128)(2,1)S(1)}, u32[]{:S(2)}, u32[]{:S(2)}) collective-permute-start(bf16[32,32,128]{2,1,0:T(8,128)(2,1)S(1)} %collective-permute-done.refs_2_), channel_id=1, source_target_pairs={{0,1},{1,0},{2,3},{3,2},{4,5},{5,4},{6,7},{7,6},{8,9},{9,8},{10,11... | collective-permute-start | bytes 786440 | tf_op jit(solution)/shard_map/ppermute | solution.py:741
  88.4 1.7 %join_parts.2.refs_1_ = f32[32,128,128]{2,1,0:T(8,128)} custom-call(s32[3]{0:T(128)S(1)} %pad_add_fusion.places, bf16[32,32,128]{2,1,0:T(8,128)(2,1)S(1)} %combine.1.refs_0_, bf16[32,32,128]{2,1,0:T(8,128)(2,1)S(1)} %collective-permute-done.2.refs_1_, bf16[32,32,128]{2,1,0:T(8,128)(2,1)S(1)} %collective-permute-done.refs_2_), custom_call_target="tpu_custom_call" | custom-call | bytes 9000000 | tf_op jit(solution)/shard_map/join_parts/pallas_call | solution.py:632
  90.2 0.8 join_parts.3
  (43 shorter events, 0.8 us)
Async XLA Ops:
  0.6 61.5 %copy-start = (bf16[32,128,128]{2,1,0:T(8,128)(2,1)S(1)}, bf16[32,128,128]{2,1,0:T(8,128)(2,1)}, u32[]{:S(2)}) copy-start(bf16[32,128,128]{2,1,0:T(8,128)(2,1)} %param.13) | copy-start | bytes 3145732
  0.6 19.5 %copy-start.10 = (bf16[40,21]{0,1:T(8,128)(2,1)S(1)}, bf16[40,21]{0,1:T(8,128)(2,1)}, u32[]{:S(2)}) copy-start(bf16[40,21]{0,1:T(8,128)(2,1)} %param.20) | copy-start | bytes 5044
  2.2 18.5 %copy-start.4 = (s32[8,1,2]{2,1,0:T(1,128)S(1)}, s32[8,1,2]{2,1,0:T(1,128)}, u32[]{:S(2)}) copy-start(s32[8,1,2]{2,1,0:T(1,128)} %get-tuple-element.15.request) | copy-start | bytes 196
  2.2 18.5 %copy-start.5 = (s32[16]{0:T(128)S(1)}, s32[16]{0:T(128)}, u32[]{:S(2)}) copy-start(s32[16]{0:T(128)} %get-tuple-element.14.sender) | copy-start | bytes 196
  2.2 11.6 %all-to-all-start = ((s32[8,1,2]{2,1,0:T(1,128)}), s32[8,1,2]{2,1,0:T(1,128)S(1)}, u32[]{:S(2)}, u32[]{:S(2)}) async-start(s32[8,1,2]{2,1,0:T(1,128)} %get-tuple-element.15.request), calls=%async_computation | async-start | bytes 8192 | tf_op jit(solution)/shard_map/all_to_all | solution.py:675
  8.6 1.2 %copy-start.1 = (bf16[32,128,128]{2,1,0:T(8,128)(2,1)S(1)}, bf16[32,128,128]{2,1,0:T(8,128)(2,1)}, u32[]{:S(2)}) copy-start(bf16[32,128,128]{2,1,0:T(8,128)(2,1)} %template.3) | copy-start | bytes 3145732
  9.8 10.4 %copy-start.11 = (bf16[40,21]{0,1:T(8,128)(2,1)S(1)}, bf16[40,21]{0,1:T(8,128)(2,1)}, u32[]{:S(2)}) copy-start(bf16[40,21]{0,1:T(8,128)(2,1)} %param.21) | copy-start | bytes 5044
  9.8 10.9 %copy-start.3 = (bf16[1,256,1024]{2,1,0:T(8,128)(2,1)S(1)}, bf16[1,256,1024]{2,1,0:T(8,128)(2,1)}, u32[]{:S(2)}) copy-start(bf16[1,256,1024]{2,1,0:T(8,128)(2,1)} %param.15) | copy-start | bytes 1572868
  13.8 1.2 %copy-start.2 = (bf16[32,128,128]{2,1,0:T(8,128)(2,1)S(1)}, bf16[32,128,128]{2,1,0:T(8,128)(2,1)}, u32[]{:S(2)}) copy-start(bf16[32,128,128]{2,1,0:T(8,128)(2,1)} %template.3) | copy-start | bytes 3145732
  16.5 22.5 %copy-start.6 = (bf16[1,256,1024]{2,1,0:T(8,128)(2,1)S(1)}, bf16[1,256,1024]{2,1,0:T(8,128)(2,1)}, u32[]{:S(2)}) copy-start(bf16[1,256,1024]{2,1,0:T(8,128)(2,1)} %param.14) | copy-start | bytes 1572868
  16.5 22.5 %copy-start.7 = (s32[1,4]{1,0:T(1,128)S(1)}, s32[1,4]{1,0:T(1,128)}, u32[]{:S(2)}) copy-start(s32[1,4]{1,0:T(1,128)} %rows_at.1) | copy-start | bytes 52
  16.5 22.5 %copy-start.8 = (s32[1,4]{1,0:T(1,128)S(1)}, s32[1,4]{1,0:T(1,128)}, u32[]{:S(2)}) copy-start(s32[1,4]{1,0:T(1,128)} %cols_at.1) | copy-start | bytes 52
  16.5 22.5 %copy-start.9 = (s32[16]{0:T(128)S(1)}, s32[16]{0:T(128)}, u32[]{:S(2)}) copy-start(s32[16]{0:T(128)} %get-tuple-element.17.slot_of) | copy-start | bytes 196
  16.5 14.6 %all-to-all-start.1 = ((bf16[16,128,128]{2,1,0:T(8,128)(2,1)}), bf16[16,128,128]{2,1,0:T(8,128)(2,1)S(1)}, u32[]{:S(2)}, u32[]{:S(2)}) async-start(bf16[16,128,128]{2,1,0:T(8,128)(2,1)} %pick_blocks.1.earlier), calls=%async_computation.1 | async-start | bytes 1048576 | tf_op jit(solution)/shard_map/all_to_all | solution.py:678
  31.1 24.9 %all-to-all-start.2 = ((bf16[32,72,128]{2,1,0:T(8,128)(2,1)}), bf16[32,72,128]{2,1,0:T(8,128)(2,1)S(1)}, u32[]{:S(2)}, u32[]{:S(2)}) async-start(bf16[32,72,128]{2,1,0:T(8,128)(2,1)} %prepare.1), calls=%async_computation.2 | async-start | bytes 1179648 | tf_op jit(solution)/shard_map/all_to_all | solution.py:690
  50.0 11.8 %copy-start.12 = (f32[1,21]{1,0:T(1,128)S(1)}, f32[1,21]{1,0:T(1,128)}, u32[]{:S(2)}) copy-start(f32[1,21]{1,0:T(1,128)} %param.23) | copy-start | bytes 256
  50.1 11.9 %copy-start.13 = (f32[1,21]{1,0:T(1,128)S(1)}, f32[1,21]{1,0:T(1,128)}, u32[]{:S(2)}) copy-start(f32[1,21]{1,0:T(1,128)} %param.22) | copy-start | bytes 256
  56.0 22.3 %all-to-all-start.3 = ((bf16[32,72,128]{2,1,0:T(8,128)(2,1)}), bf16[32,72,128]{2,1,0:T(8,128)(2,1)S(1)}, u32[]{:S(2)}, u32[]{:S(2)}) async-start(bf16[32,72,128]{2,1,0:T(8,128)(2,1)} %get-tuple-element.21.payload), calls=%async_computation.3 | async-start | bytes 1179648 | tf_op jit(solution)/shard_map/all_to_all | solution.py:722
  79.6 7.4 %collective-permute-start = (bf16[32,32,128]{2,1,0:T(8,128)(2,1)S(1)}, bf16[32,32,128]{2,1,0:T(8,128)(2,1)S(1)}, u32[]{:S(2)}, u32[]{:S(2)}) collective-permute-start(bf16[32,32,128]{2,1,0:T(8,128)(2,1)S(1)} %combine.1.refs_0_), channel_id=1, source_target_pairs={{0,2},{1,3},{2,0},{3,1},{4,6},{5,7},{6,4},{7,5},{8,10},{9,11},{10,... | collective-permute-start | bytes 786440 | tf_op jit(solution)/shard_map/ppermute | solution.py:741
  80.9 7.6 %collective-permute-start.2 = (bf16[32,32,128]{2,1,0:T(8,128)(2,1)S(1)}, bf16[32,32,128]{2,1,0:T(8,128)(2,1)S(1)}, u32[]{:S(2)}, u32[]{:S(2)}) collective-permute-start(bf16[32,32,128]{2,1,0:T(8,128)(2,1)S(1)} %combine.1.refs_0_), channel_id=1, source_target_pairs={{0,1},{1,0},{2,3},{3,2},{4,5},{5,4},{6,7},{7,6},{8,9},{9,8},{10,11... | collective-permute-start | bytes 786440 | tf_op jit(solution)/shard_map/ppermute | solution.py:741
  87.0 3.2 %collective-permute-start.1 = (bf16[32,32,128]{2,1,0:T(8,128)(2,1)S(1)}, bf16[32,32,128]{2,1,0:T(8,128)(2,1)S(1)}, u32[]{:S(2)}, u32[]{:S(2)}) collective-permute-start(bf16[32,32,128]{2,1,0:T(8,128)(2,1)S(1)} %collective-permute-done.refs_2_), channel_id=1, source_target_pairs={{0,1},{1,0},{2,3},{3,2},{4,5},{5,4},{6,7},{7,6},{8,9},{9,8},{10,11... | collective-permute-start | bytes 786440 | tf_op jit(solution)/shard_map/ppermute | solution.py:741

commit v4 on v3

--- a/solution.py
+++ b/solution.py
@@ -60,25 +60,26 @@
     )(routes_src, routes_blk)
 
 
-def touch_body(template, out):
-    out[...] = template[0, : out.shape[0], : out.shape[1]]
-
-
-def touch(template):
-    return pl.pallas_call(
-        touch_body,
-        out_shape=jax.ShapeDtypeStruct((16, 128), template.dtype),
-        in_specs=[vmem()],
+def fetch_body(template, near, sem):
+    copy = pltpu.make_async_copy(template, near, sem)
+    copy.start()
+    copy.wait()
+
+
+def fetch(template):
+    return pl.pallas_call(
+        fetch_body,
+        out_shape=jax.ShapeDtypeStruct(template.shape, template.dtype),
+        in_specs=[pl.BlockSpec(memory_space=pl.ANY)],
         out_specs=vmem(),
+        scratch_shapes=[pltpu.SemaphoreType.DMA(())],
         compiler_params=pltpu.CompilerParams(vmem_limit_bytes=16 * mib),
         cost_estimate=cost(0, 4_000_000),
-        name="touch",
+        name="fetch",
     )(template)
 
 
-def pick_body(asked, template, earlier, out, *, capacity):
-    del earlier
-
+def pick_body(asked, template, out, *, capacity):
     def one(s, carry):
         block = jnp.maximum(asked[s // capacity, 0, s % capacity] - 1, 0)
         out[s] = template[block]
@@ -87,15 +88,15 @@
     lax.fori_loop(0, out.shape[0], one, 0, unroll=True if out.shape[0] <= 32 else 4)
 
 
-def pick_blocks(asked, template, earlier, slots, capacity):
+def pick_blocks(asked, template, slots, capacity):
     return pl.pallas_call(
         functools.partial(pick_body, capacity=capacity),
         out_shape=jax.ShapeDtypeStruct((slots,) + template.shape[1:], template.dtype),
-        in_specs=[smem(), vmem(), pl.BlockSpec(memory_space=pl.ANY)],
+        in_specs=[smem(), vmem()],
         out_specs=vmem(),
         compiler_params=pltpu.CompilerParams(vmem_limit_bytes=16 * mib),
         name="pick_blocks",
-    )(asked, template, earlier)
+    )(asked, template)
 
 
 def store_parts(sender, image, out, side, exps, capacity, across_blocks):
@@ -168,10 +169,9 @@
     gram_out,
     windows,
     frame,
-    vert,
+    cuts,
+    across,
     design,
-    image,
-    var,
     roots,
     window,
     *,
@@ -189,63 +189,79 @@
     sub = lax.broadcasted_iota(jnp.int32, (side, side), 0)
     lane = lax.broadcasted_iota(jnp.int32, (side, side), 1)
 
-    frame[...] = jnp.zeros(frame.shape, f32)
+    high, wide = science.shape
+    rows_off = up(margin, 8)
+    frame[:rows_off, :] = jnp.zeros((rows_off, frame.shape[1]), f32)
+    below = rows_off + high
+    frame[below:, :] = jnp.zeros((frame.shape[0] - below, frame.shape[1]), f32)
+    frame[rows_off:below, :side] = jnp.zeros((high, side), f32)
+    after = side + wide
+    frame[rows_off:below, after:] = jnp.zeros((high, frame.shape[1] - after), f32)
     for b in range(slot_of.shape[0]):
-        top = margin + (b // across_blocks) * side
-        left = margin + (b % across_blocks) * side
+        top = rows_off + (b // across_blocks) * side
+        left = side + (b % across_blocks) * side
         frame[top : top + side, left : left + side] = arrived[slot_of[b]].astype(f32)
-
-    cuts = []
-    for s in range(stamps):
-        cuts.append(cut(frame, rows_at[0, s], cols_at[0, s], span, side).astype(bf16))
-    high, wide = science.shape
-    image[:, wide:] = jnp.zeros((image.shape[0], image.shape[1] - wide), f32)
-    image[high:, :wide] = jnp.zeros((image.shape[0] - high, wide), f32)
-    image[:high, :wide] = science[...].astype(f32)
-    var[:, wide:] = jnp.ones((var.shape[0], var.shape[1] - wide), f32)
-    var[high:, :wide] = jnp.ones((var.shape[0] - high, wide), f32)
-    var[:high, :wide] = variance[...].astype(f32)
+    first_row = rows_off - margin
+    first_col = side - margin
+
+    def cut_image(ref, top, left):
+        tall = min(high, side + 16)
+        down = pl.multiple_of(jnp.minimum((top // 16) * 16, high - tall), 16)
+        over = pl.multiple_of(jnp.minimum((left // side) * side, wide - 2 * side), side)
+        tile = ref[pl.ds(down, tall), pl.ds(over, 2 * side)].astype(f32)
+        tile = pltpu.roll(tile, lax.rem(2 * side - (left - over), 2 * side), 1)[:, :side]
+        return pltpu.roll(tile, lax.rem(tall - (top - down), tall), 0)[:side]
+
     for s in range(stamps):
         top = rows_at[0, s]
         left = cols_at[0, s]
-        root = lax.rsqrt(cut(var, top, left, side + 8, side)[:side, :side])
+        tile = cut(frame, top + first_row, left + first_col, span, side)
+        cuts[s * span : (s + 1) * span, :] = tile.astype(bf16)
+        root = lax.rsqrt(cut_image(variance, top, left))
         roots[s * side : (s + 1) * side, :] = root
         place = pl.ds(s * side * pitch + count, side, stride=pitch)
         design[place, :] = root
         place = pl.ds(s * side * pitch + count + 1, side, stride=pitch)
-        design[place, :] = root * cut(image, top, left, side + 8, side)[:side, :side]
+        design[place, :] = root * cut_image(science, top, left)
     for extra in range(count + 2, padded_k):
         design[pl.ds(extra, lines_all, stride=pitch), :] = jnp.zeros((lines_all, side), f32)
 
-    group = vert.shape[0]
+    group = across.shape[1] // side
     step = side - taps + 1
     starts = list(range(0, count, group))
     for turn, k in enumerate(starts):
         for c in range(turn, windows.shape[0], len(starts)):
-            window[...] = frame[:, c * step : c * step + side]
+            left = first_col + c * step
+            window[...] = frame[first_row : first_row + window.shape[0], left : left + side]
             for parity in range(2):
                 place = pl.ds(parity, windows.shape[2], stride=2)
                 windows[c, parity] = window[place, :]
-        filters = []
+        bands = []
+        for a in range(group):
+            line = jnp.broadcast_to(row_rev[k + a : k + a + 1, :], (side, side))
+            line = pltpu.roll(line, 0, 1, stride=1, stride_axis=0)
+            first = jnp.where(lane <= sub, line, 0.0).astype(bf16)
+            second = jnp.where(lane > sub, line, 0.0).astype(bf16)
+            bands.append(jnp.concatenate([first, second], axis=0))
+        out = jnp.dot(cuts[...], jnp.concatenate(bands, axis=1), preferred_element_type=f32)
+        across[...] = out.astype(bf16)
         for a in range(group):
             line = jnp.broadcast_to(col[k + a : k + a + 1, :], (side, side))
             line = pltpu.roll(line, 0, 1, stride=1, stride_axis=0)
             first = jnp.where(lane >= sub, line, 0.0).astype(bf16)
             second = jnp.where(lane < sub, line, 0.0).astype(bf16)
-            filters.append(jnp.concatenate([first, second[:, : span - side]], axis=1))
-        filters = jnp.concatenate(filters, axis=0)
-        for s in range(stamps):
-            out = jnp.dot(filters, cuts[s], preferred_element_type=f32).astype(bf16)
-            for a in range(group):
-                vert[a, s * side : (s + 1) * side, :] = out[a * side : (a + 1) * side]
-        for a in range(group):
-            line = jnp.broadcast_to(row_rev[k + a : k + a + 1, :], (side, side))
-            line = pltpu.roll(line, 0, 1, stride=1, stride_axis=0)
-            first = jnp.where(lane <= sub, line, 0.0).astype(bf16)
-            second = jnp.where(lane > sub, line, 0.0).astype(bf16)
-            band = jnp.concatenate([first, second], axis=0)
-            out = jnp.dot(vert[a], band, preferred_element_type=f32)
-            design[pl.ds(k + a, lines_all, stride=pitch), :] = out * roots[...]
+            band = jnp.concatenate([first, second[:, : span - side]], axis=1)
+            for s in range(0, stamps, 2):
+                members = range(s, min(s + 2, stamps))
+                data = [
+                    across[m * span : (m + 1) * span, a * side : (a + 1) * side] for m in members
+                ]
+                out = jnp.dot(band, jnp.concatenate(data, axis=1), preferred_element_type=f32)
+                for h, m in enumerate(members):
+                    place = pl.ds(m * side * pitch + k + a, side, stride=pitch)
+                    design[place, :] = (
+                        out[:, h * side : (h + 1) * side] * roots[m * side : (m + 1) * side, :]
+                    )
 
     lines = 16
     sets = 4
@@ -285,26 +301,26 @@
     stamps = rows_at.shape[1]
     padded_k = up(count + 2, 16)
     pairs = (taps + 2) // 2
-    tall = up(high - side + 8 + up(side + taps - 1, 16), 16)
-    tall = max(tall, up(high + 2 * pairs, 16))
+    span = up(side + taps - 1, 16)
+    half = up(high // 2 + pairs, 8)
+    tall = up(taps // 2, 8) + max(high - side + span, 2 * half)
     wins = -(-wide // (side - taps + 1))
-    group = next(g for g in (4, 2, 1) if count % g == 0)
+    group = 2 if count % 2 == 0 else 1
     return pl.pallas_call(
         functools.partial(normal_body, count=count, across_blocks=wide // side, taps=taps),
         out_shape=(
             jax.ShapeDtypeStruct((padded_k, padded_k), f32),
-            jax.ShapeDtypeStruct((wins, 2, tall // 2, side), f32),
+            jax.ShapeDtypeStruct((wins, 2, half, side), f32),
         ),
         in_specs=[smem()] * 3 + [vmem()] * 5,
         out_specs=(vmem(),) * 2,
         scratch_shapes=[
             pltpu.VMEM((tall, wide + 2 * side), f32),
-            pltpu.VMEM((group, stamps * side, 2 * side), bf16),
+            pltpu.VMEM((stamps * span, 2 * side), bf16),
+            pltpu.VMEM((stamps * span, group * side), bf16),
             pltpu.VMEM((stamps * side * (padded_k + 1), side), f32),
-            pltpu.VMEM((high + 8, wide + 2 * side), f32),
-            pltpu.VMEM((high + 8, wide + 2 * side), f32),
             pltpu.VMEM((stamps * side, side), f32),
-            pltpu.VMEM((tall, side), f32),
+            pltpu.VMEM((2 * half, side), f32),
         ],
         compiler_params=pltpu.CompilerParams(vmem_limit_bytes=28 * mib),
         cost_estimate=cost(10_000_000_000, 8_000_000),
@@ -673,7 +689,7 @@
 
     slot_of, sender, request = route_tables(routes_src, routes_blk, peers, capacity)
     asked = lax.all_to_all(request, "det", split_axis=0, concat_axis=0, tiled=True)
-    picked = pick_blocks(asked, template, touch(template), slots, capacity)
+    picked = pick_blocks(asked, fetch(template), slots, capacity)
     var_parts = prepare(sender, request, variance_img, picked, side, exps, capacity)
     arrived = lax.all_to_all(picked, "det", split_axis=0, concat_axis=0, tiled=True)
 

time: 91.6 us -> 93.4 us (1.020)
  Pallas kernels: 29.3 us -> 31.4 us
    pallas_call x1, Pallas kernels: 11 us -> 13.1 us  [normal_matrix(): pl.pallas_call(functools.partial(normal_body, count=count, across_blocks=...]
    unnamed x29 -> x27, local copies, waits for them, and re-layouts: 2.61 us -> 2.41 us
  transfers between devices with their start and end apart: 7 -> 7, of which waited for: 4 -> 4; matrix products, arithmetic and copies ran while one was open for 1% -> 1% of each run, Pallas kernels for 27% -> 28%
where the time goes in v4:
time: 93.4 us; the launch traced here: 92.8 us
  Pallas kernels  31.4 us (34%)
  waiting for transfers between devices  30.6 us (33%)
  starting transfers between devices  26.8 us (29%)
  local copies, waits for them, and re-layouts  2.93 us (3%)
    pallas_call x1, Pallas kernels, normal_matrix(): pl.pallas_call(functools.partial(normal_body, count=count, across_blocks=...  13.1 us
    all_to_all x1, waiting for transfers between devices, local(): lax.all_to_all(payload, ('det', 'exp'), split_axis=0, concat_axis=0, tile...  12.3 us
    all_to_all x1, waiting for transfers between devices, local(): lax.all_to_all(picked, 'det', split_axis=0, concat_axis=0, tiled=True)  8.74 us
    all_to_all x1, starting transfers between devices, local(): lax.all_to_all(var_late, ('det', 'exp'), split_axis=0, concat_axis=0, til...  7.88 us
    all_to_all x1, starting transfers between devices, local(): lax.all_to_all(request, 'det', split_axis=0, concat_axis=0, tiled=True)  6.37 us
    pallas_call x1, Pallas kernels, subtract(): pl.pallas_call(body, out_shape=(jax.ShapeDtypeStruct((1, side), f32), jax...  5.9 us
    all_to_all x1, starting transfers between devices, local(): lax.all_to_all(payload, ('det', 'exp'), split_axis=0, concat_axis=0, tile...  5.84 us
    ppermute x3, waiting for transfers between devices, swap(): return lax.ppermute(value, 'exp', [(e, e ^ distance) for e in range(exps)])  5.66 us
  transfers between devices with their start and end apart: 7, of which 4 were waited for; matrix products, arithmetic and copies ran while one was open for 1% of the time, Pallas kernels for 28%

profile of v4, /device:TPU:1, one launch (start us, length us, event | category | flops | bytes accessed | tf_op | source)
XLA Modules:
  0.0 92.8 jit_solution(9131210864368587152)
XLA Ops:
  0.6 1.5 %route_tables.1 = (s32[16]{0:T(128)}, s32[16]{0:T(128)}, s32[8,1,2]{2,1,0:T(1,128)}) custom-call(s32[1,16]{1,0:T(1,128)} %src.1, s32[1,16]{1,0:T(1,128)} %blk.1), custom_call_target="tpu_custom_call" | custom-call | tf_op jit(solution)/shard_map/route_tables/pallas_call | solution.py:49
  2.2 6.4 %all-to-all-start = ((s32[8,1,2]{2,1,0:T(1,128)}), s32[8,1,2]{2,1,0:T(1,128)S(1)}, u32[]{:S(2)}, u32[]{:S(2)}) async-start(s32[8,1,2]{2,1,0:T(1,128)} %get-tuple-element.15.request), calls=%async_computation | async-start | bytes 8192 | tf_op jit(solution)/shard_map/all_to_all | solution.py:691
  8.6 1.2 %copy-done.1 = bf16[32,128,128]{2,1,0:T(8,128)(2,1)S(1)} copy-done((bf16[32,128,128]{2,1,0:T(8,128)(2,1)S(1)}, bf16[32,128,128]{2,1,0:T(8,128)(2,1)}, u32[]{:S(2)}) %copy-start.1) | copy-done | bytes 1048600
  9.9 3.9 %all-to-all-done.asked = s32[8,1,2]{2,1,0:T(1,128)S(1)} async-done(((s32[8,1,2]{2,1,0:T(1,128)}), s32[8,1,2]{2,1,0:T(1,128)S(1)}, u32[]{:S(2)}, u32[]{:S(2)}) %all-to-all-start) | async-done | bytes 96 | tf_op jit(solution)/shard_map/all_to_all | solution.py:691
  13.8 1.4 %pick_blocks.1.earlier = bf16[16,128,128]{2,1,0:T(8,128)(2,1)} custom-call(s32[8,1,2]{2,1,0:T(1,128)S(1)} %all-to-all-done.asked, bf16[32,128,128]{2,1,0:T(8,128)(2,1)S(1)} %fetch.1.template), custom_call_target="tpu_custom_call" | custom-call | tf_op jit(solution)/shard_map/pick_blocks/pallas_call | solution.py:92
  15.2 3.6 %all-to-all-start.1 = ((bf16[16,128,128]{2,1,0:T(8,128)(2,1)}), bf16[16,128,128]{2,1,0:T(8,128)(2,1)S(1)}, u32[]{:S(2)}, u32[]{:S(2)}) async-start(bf16[16,128,128]{2,1,0:T(8,128)(2,1)} %pick_blocks.1.earlier), calls=%async_computation.1 | async-start | bytes 1048576 | tf_op jit(solution)/shard_map/all_to_all | solution.py:694
  18.9 0.1 copy.22
  19.4 1.6 %prepare.1 = bf16[32,72,128]{2,1,0:T(8,128)(2,1)} custom-call(s32[16]{0:T(128)S(1)} %copy-done.4, s32[8,1,2]{2,1,0:T(1,128)S(1)} %copy-done.3, bf16[256,1024]{1,0:T(8,128)(2,1)S(1)} %bitcast.11, bf16[16,128,128]{2,1,0:T(8,128)(2,1)} %pick_blocks.1.earlier), custom_call_target="tpu_custom_call" | custom-call | bytes 6000000 | tf_op jit(solution)/shard_map/prepare/pallas_call | solution.py:149
  21.1 8.7 %all-to-all-done.1.arrived = bf16[16,128,128]{2,1,0:T(8,128)(2,1)S(1)} async-done(((bf16[16,128,128]{2,1,0:T(8,128)(2,1)}), bf16[16,128,128]{2,1,0:T(8,128)(2,1)S(1)}, u32[]{:S(2)}, u32[]{:S(2)}) %all-to-all-start.1) | async-done | bytes 524320 | tf_op jit(solution)/shard_map/all_to_all | solution.py:694
  29.8 7.9 %all-to-all-start.2 = ((bf16[32,72,128]{2,1,0:T(8,128)(2,1)}), bf16[32,72,128]{2,1,0:T(8,128)(2,1)S(1)}, u32[]{:S(2)}, u32[]{:S(2)}) async-start(bf16[32,72,128]{2,1,0:T(8,128)(2,1)} %prepare.1), calls=%async_computation.2 | async-start | bytes 1179648 | tf_op jit(solution)/shard_map/all_to_all | solution.py:706
  37.7 1.0 %copy-done.5 = bf16[1,256,1024]{2,1,0:T(8,128)(2,1)S(1)} copy-done((bf16[1,256,1024]{2,1,0:T(8,128)(2,1)S(1)}, bf16[1,256,1024]{2,1,0:T(8,128)(2,1)}, u32[]{:S(2)}) %copy-start.5) | copy-done | bytes 524312
  38.8 13.1 %normal_matrix.1 = (f32[48,48]{1,0:T(8,128)S(1)}, f32[10,2,144,128]{3,2,1,0:T(8,128)S(1)}) custom-call(s32[16]{0:T(128)S(1)} %copy-done.8, s32[1,4]{1,0:T(1,128)S(1)} %copy-done.6, s32[1,4]{1,0:T(1,128)S(1)} %copy-done.7, bf16[16,128,128]{2,1,0:T(8,128)(2,1)S(1)} %all-to-all-done.1.arrived, f32[48,128]{1,0:T(8,128)S(1)} %pad_convert_fusion.col, ...), custom_call_target="tpu_custom_call" | custom-call | flops 10000000000 | bytes 8000000 | tf_op jit(solution)/shard_map/normal_matrix/pallas_call | solution.py:309
  51.9 5.9 %subtract.1 = (f32[1,128]{1,0:T(1,128)}, bf16[32,72,128]{2,1,0:T(8,128)(2,1)}) custom-call(s32[16]{0:T(128)S(1)} %copy-done.4, f32[48,48]{1,0:T(8,128)S(1)} %get-tuple-element.19.gram, f32[10,2,144,128]{3,2,1,0:T(8,128)S(1)} %get-tuple-element.20.frames, bf16[256,1024]{1,0:T(8,128)(2,1)S(1)} %bitcast.16, bf16[32,48]{1,0:T(8,128)(2,1)S(1)} %pad.25.col_t, ...), custom_call_target="tpu_custom_call" | custom-call | flops 5000000000 | bytes 4000000 | tf_op jit(solution)/shard_map/subtract/pallas_call | solution.py:471
  57.8 5.8 %all-to-all-start.3 = ((bf16[32,72,128]{2,1,0:T(8,128)(2,1)}), bf16[32,72,128]{2,1,0:T(8,128)(2,1)S(1)}, u32[]{:S(2)}, u32[]{:S(2)}) async-start(bf16[32,72,128]{2,1,0:T(8,128)(2,1)} %get-tuple-element.21.payload), calls=%async_computation.3 | async-start | bytes 1179648 | tf_op jit(solution)/shard_map/all_to_all | solution.py:738
  63.8 0.1 pad_maximum_fusion.1.over
  64.0 3.8 %score.1 = (f32[256,1024]{1,0:T(8,128)}, f32[32,32,128]{2,1,0:T(8,128)S(1)}) custom-call(s32[32,2]{1,0:T(8,128)S(1)} %bitcast.13, s32[16]{0:T(128)S(1)} %copy-done.8, bf16[32,72,128]{2,1,0:T(8,128)(2,1)} %get-tuple-element.21.payload, f32[1,256]{1,0:T(1,128)S(1)} %pad.26.down, f32[1,256]{1,0:T(1,128)S(1)} %pad_maximum_fusion.1.over, ...), custom_call_target="tpu_custom_call" | custom-call | flops 2000000000 | bytes 2000000 | tf_op jit(solution)/shard_map/score/pallas_call | solution.py:556
  67.8 12.3 %all-to-all-done.3.parts = bf16[32,72,128]{2,1,0:T(8,128)(2,1)S(1)} async-done(((bf16[32,72,128]{2,1,0:T(8,128)(2,1)}), bf16[32,72,128]{2,1,0:T(8,128)(2,1)S(1)}, u32[]{:S(2)}, u32[]{:S(2)}) %all-to-all-start.3) | async-done | bytes 589856 | tf_op jit(solution)/shard_map/all_to_all | solution.py:738
  80.1 1.3 %combine.1.refs_0_ = bf16[32,32,128]{2,1,0:T(8,128)(2,1)S(1)} custom-call(s32[32,2]{1,0:T(8,128)S(1)} %bitcast.14, bf16[32,72,128]{2,1,0:T(8,128)(2,1)S(1)} %all-to-all-done.3.parts, f32[32,32,128]{2,1,0:T(8,128)S(1)} %get-tuple-element.22.var_sum, bf16[32,32,128]{2,1,0:T(8,128)(2,1)S(1)} %constant_dynamic-slice_fusion.var_template), custom_call_target="tpu_custom_call" | custom-call | tf_op jit(solution)/shard_map/combine/pallas_call | solution.py:614
  81.4 1.3 %collective-permute-start = (bf16[32,32,128]{2,1,0:T(8,128)(2,1)S(1)}, bf16[32,32,128]{2,1,0:T(8,128)(2,1)S(1)}, u32[]{:S(2)}, u32[]{:S(2)}) collective-permute-start(bf16[32,32,128]{2,1,0:T(8,128)(2,1)S(1)} %combine.1.refs_0_), channel_id=1, source_target_pairs={{0,2},{1,3},{2,0},{3,1},{4,6},{5,7},{6,4},{7,5},{8,10},{9,11},{10,... | collective-permute-start | bytes 786440 | tf_op jit(solution)/shard_map/ppermute | solution.py:757
  82.7 0.4 collective-permute-start.2
  83.1 5.7 %collective-permute-done.refs_2_ = bf16[32,32,128]{2,1,0:T(8,128)(2,1)S(1)} collective-permute-done((bf16[32,32,128]{2,1,0:T(8,128)(2,1)S(1)}, bf16[32,32,128]{2,1,0:T(8,128)(2,1)S(1)}, u32[]{:S(2)}, u32[]{:S(2)}) %collective-permute-start) | collective-permute-done | bytes 262176 | tf_op jit(solution)/shard_map/ppermute | solution.py:757
  88.8 1.4 %collective-permute-start.1 = (bf16[32,32,128]{2,1,0:T(8,128)(2,1)S(1)}, bf16[32,32,128]{2,1,0:T(8,128)(2,1)S(1)}, u32[]{:S(2)}, u32[]{:S(2)}) collective-permute-start(bf16[32,32,128]{2,1,0:T(8,128)(2,1)S(1)} %collective-permute-done.refs_2_), channel_id=1, source_target_pairs={{0,1},{1,0},{2,3},{3,2},{4,5},{5,4},{6,7},{7,6},{8,9},{9,8},{10,11... | collective-permute-start | bytes 786440 | tf_op jit(solution)/shard_map/ppermute | solution.py:757
  90.2 1.7 %join_parts.2.refs_1_ = f32[32,128,128]{2,1,0:T(8,128)} custom-call(s32[3]{0:T(128)S(1)} %pad_add_fusion.places, bf16[32,32,128]{2,1,0:T(8,128)(2,1)S(1)} %combine.1.refs_0_, bf16[32,32,128]{2,1,0:T(8,128)(2,1)S(1)} %collective-permute-done.2.refs_1_, bf16[32,32,128]{2,1,0:T(8,128)(2,1)S(1)} %collective-permute-done.refs_2_), custom_call_target="tpu_custom_call" | custom-call | bytes 9000000 | tf_op jit(solution)/shard_map/join_parts/pallas_call | solution.py:648
  92.0 0.8 join_parts.3
  (41 shorter events, 0.8 us)
Async XLA Ops:
  0.6 63.3 %copy-start = (bf16[32,128,128]{2,1,0:T(8,128)(2,1)S(1)}, bf16[32,128,128]{2,1,0:T(8,128)(2,1)}, u32[]{:S(2)}) copy-start(bf16[32,128,128]{2,1,0:T(8,128)(2,1)} %param.13) | copy-start | bytes 3145732
  2.2 11.6 %all-to-all-start = ((s32[8,1,2]{2,1,0:T(1,128)}), s32[8,1,2]{2,1,0:T(1,128)S(1)}, u32[]{:S(2)}, u32[]{:S(2)}) async-start(s32[8,1,2]{2,1,0:T(1,128)} %get-tuple-element.15.request), calls=%async_computation | async-start | bytes 8192 | tf_op jit(solution)/shard_map/all_to_all | solution.py:691
  8.6 1.2 %copy-start.1 = (bf16[32,128,128]{2,1,0:T(8,128)(2,1)S(1)}, bf16[32,128,128]{2,1,0:T(8,128)(2,1)}, u32[]{:S(2)}) copy-start(bf16[32,128,128]{2,1,0:T(8,128)(2,1)} %template.1) | copy-start | bytes 3145732
  9.8 9.1 %copy-start.9 = (bf16[40,21]{0,1:T(8,128)(2,1)S(1)}, bf16[40,21]{0,1:T(8,128)(2,1)}, u32[]{:S(2)}) copy-start(bf16[40,21]{0,1:T(8,128)(2,1)} %param.20) | copy-start | bytes 5044
  9.8 9.2 %copy-start.10 = (bf16[40,21]{0,1:T(8,128)(2,1)S(1)}, bf16[40,21]{0,1:T(8,128)(2,1)}, u32[]{:S(2)}) copy-start(bf16[40,21]{0,1:T(8,128)(2,1)} %param.21) | copy-start | bytes 5044
  9.8 9.6 %copy-start.2 = (bf16[1,256,1024]{2,1,0:T(8,128)(2,1)S(1)}, bf16[1,256,1024]{2,1,0:T(8,128)(2,1)}, u32[]{:S(2)}) copy-start(bf16[1,256,1024]{2,1,0:T(8,128)(2,1)} %param.15) | copy-start | bytes 1572868
  9.8 9.6 %copy-start.3 = (s32[8,1,2]{2,1,0:T(1,128)S(1)}, s32[8,1,2]{2,1,0:T(1,128)}, u32[]{:S(2)}) copy-start(s32[8,1,2]{2,1,0:T(1,128)} %get-tuple-element.15.request) | copy-start | bytes 196
  9.8 9.6 %copy-start.4 = (s32[16]{0:T(128)S(1)}, s32[16]{0:T(128)}, u32[]{:S(2)}) copy-start(s32[16]{0:T(128)} %get-tuple-element.14.sender) | copy-start | bytes 196
  15.2 22.5 %copy-start.6 = (s32[1,4]{1,0:T(1,128)S(1)}, s32[1,4]{1,0:T(1,128)}, u32[]{:S(2)}) copy-start(s32[1,4]{1,0:T(1,128)} %rows_at.1) | copy-start | bytes 52
  15.2 22.5 %copy-start.7 = (s32[1,4]{1,0:T(1,128)S(1)}, s32[1,4]{1,0:T(1,128)}, u32[]{:S(2)}) copy-start(s32[1,4]{1,0:T(1,128)} %cols_at.1) | copy-start | bytes 52
  15.2 22.5 %copy-start.8 = (s32[16]{0:T(128)S(1)}, s32[16]{0:T(128)}, u32[]{:S(2)}) copy-start(s32[16]{0:T(128)} %get-tuple-element.17.slot_of) | copy-start | bytes 196
  15.2 14.6 %all-to-all-start.1 = ((bf16[16,128,128]{2,1,0:T(8,128)(2,1)}), bf16[16,128,128]{2,1,0:T(8,128)(2,1)S(1)}, u32[]{:S(2)}, u32[]{:S(2)}) async-start(bf16[16,128,128]{2,1,0:T(8,128)(2,1)} %pick_blocks.1.earlier), calls=%async_computation.1 | async-start | bytes 1048576 | tf_op jit(solution)/shard_map/all_to_all | solution.py:694
  29.8 28.0 %all-to-all-start.2 = ((bf16[32,72,128]{2,1,0:T(8,128)(2,1)}), bf16[32,72,128]{2,1,0:T(8,128)(2,1)S(1)}, u32[]{:S(2)}, u32[]{:S(2)}) async-start(bf16[32,72,128]{2,1,0:T(8,128)(2,1)} %prepare.1), calls=%async_computation.2 | async-start | bytes 1179648 | tf_op jit(solution)/shard_map/all_to_all | solution.py:706
  37.7 1.0 %copy-start.5 = (bf16[1,256,1024]{2,1,0:T(8,128)(2,1)S(1)}, bf16[1,256,1024]{2,1,0:T(8,128)(2,1)}, u32[]{:S(2)}) copy-start(bf16[1,256,1024]{2,1,0:T(8,128)(2,1)} %param.14) | copy-start | bytes 1572868
  51.8 11.8 %copy-start.11 = (f32[1,21]{1,0:T(1,128)S(1)}, f32[1,21]{1,0:T(1,128)}, u32[]{:S(2)}) copy-start(f32[1,21]{1,0:T(1,128)} %param.23) | copy-start | bytes 256
  51.9 11.9 %copy-start.12 = (f32[1,21]{1,0:T(1,128)S(1)}, f32[1,21]{1,0:T(1,128)}, u32[]{:S(2)}) copy-start(f32[1,21]{1,0:T(1,128)} %param.22) | copy-start | bytes 256
  57.8 22.3 %all-to-all-start.3 = ((bf16[32,72,128]{2,1,0:T(8,128)(2,1)}), bf16[32,72,128]{2,1,0:T(8,128)(2,1)S(1)}, u32[]{:S(2)}, u32[]{:S(2)}) async-start(bf16[32,72,128]{2,1,0:T(8,128)(2,1)} %get-tuple-element.21.payload), calls=%async_computation.3 | async-start | bytes 1179648 | tf_op jit(solution)/shard_map/all_to_all | solution.py:738
  81.4 7.4 %collective-permute-start = (bf16[32,32,128]{2,1,0:T(8,128)(2,1)S(1)}, bf16[32,32,128]{2,1,0:T(8,128)(2,1)S(1)}, u32[]{:S(2)}, u32[]{:S(2)}) collective-permute-start(bf16[32,32,128]{2,1,0:T(8,128)(2,1)S(1)} %combine.1.refs_0_), channel_id=1, source_target_pairs={{0,2},{1,3},{2,0},{3,1},{4,6},{5,7},{6,4},{7,5},{8,10},{9,11},{10,... | collective-permute-start | bytes 786440 | tf_op jit(solution)/shard_map/ppermute | solution.py:757
  82.7 7.6 %collective-permute-start.2 = (bf16[32,32,128]{2,1,0:T(8,128)(2,1)S(1)}, bf16[32,32,128]{2,1,0:T(8,128)(2,1)S(1)}, u32[]{:S(2)}, u32[]{:S(2)}) collective-permute-start(bf16[32,32,128]{2,1,0:T(8,128)(2,1)S(1)} %combine.1.refs_0_), channel_id=1, source_target_pairs={{0,1},{1,0},{2,3},{3,2},{4,5},{5,4},{6,7},{7,6},{8,9},{9,8},{10,11... | collective-permute-start | bytes 786440 | tf_op jit(solution)/shard_map/ppermute | solution.py:757
  88.8 3.2 %collective-permute-start.1 = (bf16[32,32,128]{2,1,0:T(8,128)(2,1)S(1)}, bf16[32,32,128]{2,1,0:T(8,128)(2,1)S(1)}, u32[]{:S(2)}, u32[]{:S(2)}) collective-permute-start(bf16[32,32,128]{2,1,0:T(8,128)(2,1)S(1)} %collective-permute-done.refs_2_), channel_id=1, source_target_pairs={{0,1},{1,0},{2,3},{3,2},{4,5},{5,4},{6,7},{7,6},{8,9},{9,8},{10,11... | collective-permute-start | bytes 786440 | tf_op jit(solution)/shard_map/ppermute | solution.py:757

commit v5 on v4

--- a/solution.py
+++ b/solution.py
@@ -138,23 +138,23 @@
     return pltpu.roll(tile, lax.rem(height - (top - down), height), 0)
 
 
-def prepare_body(sender, request, variance, earlier, out, *, side, exps, capacity):
-    del earlier
+def prepare_body(sender, request, variance, science, earlier, out, *, side, exps, capacity):
+    del earlier, science
     store_parts(sender, variance, out, side, exps, capacity, variance.shape[1] // side)
     store_requests(request, out, side, exps, capacity)
 
 
-def prepare(sender, request, variance, earlier, side, exps, capacity):
+def prepare(sender, request, variance, science, earlier, side, exps, capacity):
     rows = capacity * (side // exps) + trailer_rows
     return pl.pallas_call(
         functools.partial(prepare_body, side=side, exps=exps, capacity=capacity),
         out_shape=jax.ShapeDtypeStruct((request.shape[0] * exps, rows, side), bf16),
-        in_specs=[smem()] * 2 + [vmem(), pl.BlockSpec(memory_space=pl.ANY)],
+        in_specs=[smem()] * 2 + [vmem(), vmem(), pl.BlockSpec(memory_space=pl.ANY)],
         out_specs=vmem(),
         compiler_params=pltpu.CompilerParams(vmem_limit_bytes=16 * mib),
         cost_estimate=cost(0, 6_000_000),
         name="prepare",
-    )(sender, request, variance, earlier)
+    )(sender, request, variance, science, earlier)
 
 
 def normal_body(
@@ -170,7 +170,7 @@
     windows,
     frame,
     cuts,
-    across,
+    vert,
     design,
     roots,
     window,
@@ -226,7 +226,7 @@
     for extra in range(count + 2, padded_k):
         design[pl.ds(extra, lines_all, stride=pitch), :] = jnp.zeros((lines_all, side), f32)
 
-    group = across.shape[1] // side
+    group = vert.shape[0]
     step = side - taps + 1
     starts = list(range(0, count, group))
     for turn, k in enumerate(starts):
@@ -236,32 +236,28 @@
             for parity in range(2):
                 place = pl.ds(parity, windows.shape[2], stride=2)
                 windows[c, parity] = window[place, :]
-        bands = []
+        filters = []
+        for a in range(group):
+            line = jnp.broadcast_to(col[k + a : k + a + 1, :], (side, side))
+            line = pltpu.roll(line, 0, 1, stride=1, stride_axis=0)
+            first = jnp.where(lane >= sub, line, 0.0).astype(bf16)
+            second = jnp.where(lane < sub, line, 0.0).astype(bf16)
+            filters.append(jnp.concatenate([first, second[:, : span - side]], axis=1))
+        filters = jnp.concatenate(filters, axis=0)
+        for s in range(stamps):
+            out = jnp.dot(
+                filters, cuts[s * span : (s + 1) * span, :], preferred_element_type=f32
+            ).astype(bf16)
+            for a in range(group):
+                vert[a, s * side : (s + 1) * side, :] = out[a * side : (a + 1) * side]
         for a in range(group):
             line = jnp.broadcast_to(row_rev[k + a : k + a + 1, :], (side, side))
             line = pltpu.roll(line, 0, 1, stride=1, stride_axis=0)
             first = jnp.where(lane <= sub, line, 0.0).astype(bf16)
             second = jnp.where(lane > sub, line, 0.0).astype(bf16)
-            bands.append(jnp.concatenate([first, second], axis=0))
-        out = jnp.dot(cuts[...], jnp.concatenate(bands, axis=1), preferred_element_type=f32)
-        across[...] = out.astype(bf16)
-        for a in range(group):
-            line = jnp.broadcast_to(col[k + a : k + a + 1, :], (side, side))
-            line = pltpu.roll(line, 0, 1, stride=1, stride_axis=0)
-            first = jnp.where(lane >= sub, line, 0.0).astype(bf16)
-            second = jnp.where(lane < sub, line, 0.0).astype(bf16)
-            band = jnp.concatenate([first, second[:, : span - side]], axis=1)
-            for s in range(0, stamps, 2):
-                members = range(s, min(s + 2, stamps))
-                data = [
-                    across[m * span : (m + 1) * span, a * side : (a + 1) * side] for m in members
-                ]
-                out = jnp.dot(band, jnp.concatenate(data, axis=1), preferred_element_type=f32)
-                for h, m in enumerate(members):
-                    place = pl.ds(m * side * pitch + k + a, side, stride=pitch)
-                    design[place, :] = (
-                        out[:, h * side : (h + 1) * side] * roots[m * side : (m + 1) * side, :]
-                    )
+            band = jnp.concatenate([first, second], axis=0)
+            out = jnp.dot(vert[a], band, preferred_element_type=f32)
+            design[pl.ds(k + a, lines_all, stride=pitch), :] = out * roots[...]
 
     lines = 16
     sets = 4
@@ -305,7 +301,7 @@
     half = up(high // 2 + pairs, 8)
     tall = up(taps // 2, 8) + max(high - side + span, 2 * half)
     wins = -(-wide // (side - taps + 1))
-    group = 2 if count % 2 == 0 else 1
+    group = next(g for g in (8, 4, 2, 1) if count % g == 0)
     return pl.pallas_call(
         functools.partial(normal_body, count=count, across_blocks=wide // side, taps=taps),
         out_shape=(
@@ -317,7 +313,7 @@
         scratch_shapes=[
             pltpu.VMEM((tall, wide + 2 * side), f32),
             pltpu.VMEM((stamps * span, 2 * side), bf16),
-            pltpu.VMEM((stamps * span, group * side), bf16),
+            pltpu.VMEM((group, stamps * side, 2 * side), bf16),
             pltpu.VMEM((stamps * side * (padded_k + 1), side), f32),
             pltpu.VMEM((stamps * side, side), f32),
             pltpu.VMEM((2 * half, side), f32),
@@ -374,11 +370,11 @@
                     frames[c, a, q : q + rows_half, :].astype(bf16)
                 )
 
-    starts = list(range(0, size, 4))
+    starts = list(range(0, size, 8))
     for step, k in enumerate(starts):
         for q in range(step, pairs, len(starts)):
             stack_rows(q)
-        block = range(min(4, size - k))
+        block = range(min(8, size - k))
         cols = [jnp.broadcast_to(system[:, k + j : k + j + 1], system.shape) for j in block]
         rows = [system[k + j : k + j + 1, :] for j in block]
         core = [[cols[j][k + i : k + i + 1, :] for j in block] for i in block]
@@ -690,7 +686,9 @@
     slot_of, sender, request = route_tables(routes_src, routes_blk, peers, capacity)
     asked = lax.all_to_all(request, "det", split_axis=0, concat_axis=0, tiled=True)
     picked = pick_blocks(asked, fetch(template), slots, capacity)
-    var_parts = prepare(sender, request, variance_img, picked, side, exps, capacity)
+    var_parts = prepare(
+        sender, request, variance_img, science_img, picked, side, exps, capacity
+    )
     arrived = lax.all_to_all(picked, "det", split_axis=0, concat_axis=0, tiled=True)
 
     padded_k = up(count + 2, 16)

time: 93.4 us -> 89.6 us (0.959)
  Pallas kernels: 31.4 us -> 28.6 us
  local copies, waits for them, and re-layouts: 2.93 us -> 1.9 us
    pallas_call x1, Pallas kernels: 13.1 us -> 10.5 us  [normal_matrix(): pl.pallas_call(functools.partial(normal_body, count=count, across_blocks=...]
    unnamed x27 -> x29, local copies, waits for them, and re-layouts: 2.41 us -> 1.38 us
  transfers between devices with their start and end apart: 7 -> 7, of which waited for: 4 -> 5; matrix products, arithmetic and copies ran while one was open for 1% -> 1% of each run, Pallas kernels for 28% -> 26%
where the time goes in v5:
time: 89.6 us; the launch traced here: 89.1 us
  waiting for transfers between devices  30.7 us (34%)
  Pallas kernels  28.6 us (32%)
  starting transfers between devices  26.7 us (30%)
  local copies, waits for them, and re-layouts  1.9 us (2%)
    all_to_all x1, waiting for transfers between devices, local(): lax.all_to_all(payload, ('det', 'exp'), split_axis=0, concat_axis=0, tile...  12.3 us
    pallas_call x1, Pallas kernels, normal_matrix(): pl.pallas_call(functools.partial(normal_body, count=count, across_blocks=...  10.5 us
    all_to_all x1, waiting for transfers between devices, local(): lax.all_to_all(picked, 'det', split_axis=0, concat_axis=0, tiled=True)  8.73 us
    all_to_all x1, starting transfers between devices, local(): lax.all_to_all(var_late, ('det', 'exp'), split_axis=0, concat_axis=0, til...  7.88 us
    all_to_all x1, starting transfers between devices, local(): lax.all_to_all(request, 'det', split_axis=0, concat_axis=0, tiled=True)  6.37 us
    pallas_call x1, Pallas kernels, subtract(): pl.pallas_call(body, out_shape=(jax.ShapeDtypeStruct((1, side), f32), jax...  5.74 us
    all_to_all x1, starting transfers between devices, local(): lax.all_to_all(payload, ('det', 'exp'), split_axis=0, concat_axis=0, tile...  5.7 us
    ppermute x3, waiting for transfers between devices, swap(): return lax.ppermute(value, 'exp', [(e, e ^ distance) for e in range(exps)])  5.66 us
  transfers between devices with their start and end apart: 7, of which 5 were waited for; matrix products, arithmetic and copies ran while one was open for 1% of the time, Pallas kernels for 26%

profile of v5, /device:TPU:1, one launch (start us, length us, event | category | flops | bytes accessed | tf_op | source)
XLA Modules:
  0.0 89.1 jit_solution(6665802182095320816)
XLA Ops:
  0.6 1.5 %route_tables.1 = (s32[16]{0:T(128)}, s32[16]{0:T(128)}, s32[8,1,2]{2,1,0:T(1,128)}) custom-call(s32[1,16]{1,0:T(1,128)} %src.1, s32[1,16]{1,0:T(1,128)} %blk.1), custom_call_target="tpu_custom_call" | custom-call | tf_op jit(solution)/shard_map/route_tables/pallas_call | solution.py:49
  2.2 6.4 %all-to-all-start = ((s32[8,1,2]{2,1,0:T(1,128)}), s32[8,1,2]{2,1,0:T(1,128)S(1)}, u32[]{:S(2)}, u32[]{:S(2)}) async-start(s32[8,1,2]{2,1,0:T(1,128)} %get-tuple-element.15.request), calls=%async_computation | async-start | bytes 8192 | tf_op jit(solution)/shard_map/all_to_all | solution.py:687
  8.6 1.2 %copy-done.1 = bf16[32,128,128]{2,1,0:T(8,128)(2,1)S(1)} copy-done((bf16[32,128,128]{2,1,0:T(8,128)(2,1)S(1)}, bf16[32,128,128]{2,1,0:T(8,128)(2,1)}, u32[]{:S(2)}) %copy-start.1) | copy-done | bytes 1048600
  9.9 3.9 %all-to-all-done.asked = s32[8,1,2]{2,1,0:T(1,128)S(1)} async-done(((s32[8,1,2]{2,1,0:T(1,128)}), s32[8,1,2]{2,1,0:T(1,128)S(1)}, u32[]{:S(2)}, u32[]{:S(2)}) %all-to-all-start) | async-done | bytes 96 | tf_op jit(solution)/shard_map/all_to_all | solution.py:687
  13.8 1.4 %pick_blocks.1.earlier = bf16[16,128,128]{2,1,0:T(8,128)(2,1)} custom-call(s32[8,1,2]{2,1,0:T(1,128)S(1)} %all-to-all-done.asked, bf16[32,128,128]{2,1,0:T(8,128)(2,1)S(1)} %fetch.1.template), custom_call_target="tpu_custom_call" | custom-call | tf_op jit(solution)/shard_map/pick_blocks/pallas_call | solution.py:92
  15.2 3.6 %all-to-all-start.1 = ((bf16[16,128,128]{2,1,0:T(8,128)(2,1)}), bf16[16,128,128]{2,1,0:T(8,128)(2,1)S(1)}, u32[]{:S(2)}, u32[]{:S(2)}) async-start(bf16[16,128,128]{2,1,0:T(8,128)(2,1)} %pick_blocks.1.earlier), calls=%async_computation.1 | async-start | bytes 1048576 | tf_op jit(solution)/shard_map/all_to_all | solution.py:692
  18.9 0.1 copy.22
  19.4 1.6 %prepare.1 = bf16[32,72,128]{2,1,0:T(8,128)(2,1)} custom-call(s32[16]{0:T(128)S(1)} %copy-done.6, s32[8,1,2]{2,1,0:T(1,128)S(1)} %copy-done.5, bf16[256,1024]{1,0:T(8,128)(2,1)S(1)} %bitcast.11, bf16[256,1024]{1,0:T(8,128)(2,1)S(1)} %bitcast.13, bf16[16,128,128]{2,1,0:T(8,128)(2,1)} %pick_blocks.1.earlier), custom_call_target="tpu_custom_call" | custom-call | bytes 6000000 | tf_op jit(solution)/shard_map/prepare/pallas_call | solution.py:149
  21.1 8.7 %all-to-all-done.1.arrived = bf16[16,128,128]{2,1,0:T(8,128)(2,1)S(1)} async-done(((bf16[16,128,128]{2,1,0:T(8,128)(2,1)}), bf16[16,128,128]{2,1,0:T(8,128)(2,1)S(1)}, u32[]{:S(2)}, u32[]{:S(2)}) %all-to-all-start.1) | async-done | bytes 524320 | tf_op jit(solution)/shard_map/all_to_all | solution.py:692
  29.8 7.9 %all-to-all-start.2 = ((bf16[32,72,128]{2,1,0:T(8,128)(2,1)}), bf16[32,72,128]{2,1,0:T(8,128)(2,1)S(1)}, u32[]{:S(2)}, u32[]{:S(2)}) async-start(bf16[32,72,128]{2,1,0:T(8,128)(2,1)} %prepare.1), calls=%async_computation.2 | async-start | bytes 1179648 | tf_op jit(solution)/shard_map/all_to_all | solution.py:704
  37.7 10.5 %normal_matrix.1 = (f32[48,48]{1,0:T(8,128)S(1)}, f32[10,2,144,128]{3,2,1,0:T(8,128)S(1)}) custom-call(s32[16]{0:T(128)S(1)} %copy-done.9, s32[1,4]{1,0:T(1,128)S(1)} %copy-done.7, s32[1,4]{1,0:T(1,128)S(1)} %copy-done.8, bf16[16,128,128]{2,1,0:T(8,128)(2,1)S(1)} %all-to-all-done.1.arrived, f32[48,128]{1,0:T(8,128)S(1)} %pad_convert_fusion.col, ...), custom_call_target="tpu_custom_call" | custom-call | flops 10000000000 | bytes 8000000 | tf_op jit(solution)/shard_map/normal_matrix/pallas_call | solution.py:305
  48.3 5.7 %subtract.1 = (f32[1,128]{1,0:T(1,128)}, bf16[32,72,128]{2,1,0:T(8,128)(2,1)}) custom-call(s32[16]{0:T(128)S(1)} %copy-done.6, f32[48,48]{1,0:T(8,128)S(1)} %get-tuple-element.19.gram, f32[10,2,144,128]{3,2,1,0:T(8,128)S(1)} %get-tuple-element.20.frames, bf16[256,1024]{1,0:T(8,128)(2,1)S(1)} %bitcast.15, bf16[32,48]{1,0:T(8,128)(2,1)S(1)} %pad.25.col_t, ...), custom_call_target="tpu_custom_call" | custom-call | flops 5000000000 | bytes 4000000 | tf_op jit(solution)/shard_map/subtract/pallas_call | solution.py:467
  54.0 0.2 all-to-all-done.2.parts
  54.2 5.7 %all-to-all-start.3 = ((bf16[32,72,128]{2,1,0:T(8,128)(2,1)}), bf16[32,72,128]{2,1,0:T(8,128)(2,1)S(1)}, u32[]{:S(2)}, u32[]{:S(2)}) async-start(bf16[32,72,128]{2,1,0:T(8,128)(2,1)} %get-tuple-element.21.payload), calls=%async_computation.3 | async-start | bytes 1179648 | tf_op jit(solution)/shard_map/all_to_all | solution.py:736
  60.1 0.1 pad_maximum_fusion.1.over
  60.2 3.8 %score.1 = (f32[256,1024]{1,0:T(8,128)}, f32[32,32,128]{2,1,0:T(8,128)S(1)}) custom-call(s32[32,2]{1,0:T(8,128)S(1)} %bitcast.16, s32[16]{0:T(128)S(1)} %copy-done.9, bf16[32,72,128]{2,1,0:T(8,128)(2,1)} %get-tuple-element.21.payload, f32[1,256]{1,0:T(1,128)S(1)} %pad.26.down, f32[1,256]{1,0:T(1,128)S(1)} %pad_maximum_fusion.1.over, ...), custom_call_target="tpu_custom_call" | custom-call | flops 2000000000 | bytes 2000000 | tf_op jit(solution)/shard_map/score/pallas_call | solution.py:552
  64.1 12.3 %all-to-all-done.3.parts = bf16[32,72,128]{2,1,0:T(8,128)(2,1)S(1)} async-done(((bf16[32,72,128]{2,1,0:T(8,128)(2,1)}), bf16[32,72,128]{2,1,0:T(8,128)(2,1)S(1)}, u32[]{:S(2)}, u32[]{:S(2)}) %all-to-all-start.3) | async-done | bytes 589856 | tf_op jit(solution)/shard_map/all_to_all | solution.py:736
  76.3 1.3 %combine.1.refs_0_ = bf16[32,32,128]{2,1,0:T(8,128)(2,1)S(1)} custom-call(s32[32,2]{1,0:T(8,128)S(1)} %bitcast.17, bf16[32,72,128]{2,1,0:T(8,128)(2,1)S(1)} %all-to-all-done.3.parts, f32[32,32,128]{2,1,0:T(8,128)S(1)} %get-tuple-element.22.var_sum, bf16[32,32,128]{2,1,0:T(8,128)(2,1)S(1)} %constant_dynamic-slice_fusion.var_template), custom_call_target="tpu_custom_call" | custom-call | tf_op jit(solution)/shard_map/combine/pallas_call | solution.py:610
  77.6 1.3 %collective-permute-start = (bf16[32,32,128]{2,1,0:T(8,128)(2,1)S(1)}, bf16[32,32,128]{2,1,0:T(8,128)(2,1)S(1)}, u32[]{:S(2)}, u32[]{:S(2)}) collective-permute-start(bf16[32,32,128]{2,1,0:T(8,128)(2,1)S(1)} %combine.1.refs_0_), channel_id=1, source_target_pairs={{0,2},{1,3},{2,0},{3,1},{4,6},{5,7},{6,4},{7,5},{8,10},{9,11},{10,... | collective-permute-start | bytes 786440 | tf_op jit(solution)/shard_map/ppermute | solution.py:755
  78.9 0.4 collective-permute-start.2
  79.4 5.7 %collective-permute-done.refs_2_ = bf16[32,32,128]{2,1,0:T(8,128)(2,1)S(1)} collective-permute-done((bf16[32,32,128]{2,1,0:T(8,128)(2,1)S(1)}, bf16[32,32,128]{2,1,0:T(8,128)(2,1)S(1)}, u32[]{:S(2)}, u32[]{:S(2)}) %collective-permute-start) | collective-permute-done | bytes 262176 | tf_op jit(solution)/shard_map/ppermute | solution.py:755
  85.0 1.4 %collective-permute-start.1 = (bf16[32,32,128]{2,1,0:T(8,128)(2,1)S(1)}, bf16[32,32,128]{2,1,0:T(8,128)(2,1)S(1)}, u32[]{:S(2)}, u32[]{:S(2)}) collective-permute-start(bf16[32,32,128]{2,1,0:T(8,128)(2,1)S(1)} %collective-permute-done.refs_2_), channel_id=1, source_target_pairs={{0,1},{1,0},{2,3},{3,2},{4,5},{5,4},{6,7},{7,6},{8,9},{9,8},{10,11... | collective-permute-start | bytes 786440 | tf_op jit(solution)/shard_map/ppermute | solution.py:755
  86.5 1.7 %join_parts.2.refs_1_ = f32[32,128,128]{2,1,0:T(8,128)} custom-call(s32[3]{0:T(128)S(1)} %pad_add_fusion.places, bf16[32,32,128]{2,1,0:T(8,128)(2,1)S(1)} %combine.1.refs_0_, bf16[32,32,128]{2,1,0:T(8,128)(2,1)S(1)} %collective-permute-done.2.refs_1_, bf16[32,32,128]{2,1,0:T(8,128)(2,1)S(1)} %collective-permute-done.refs_2_), custom_call_target="tpu_custom_call" | custom-call | bytes 9000000 | tf_op jit(solution)/shard_map/join_parts/pallas_call | solution.py:644
  88.2 0.8 join_parts.3
  (43 shorter events, 0.8 us)
Async XLA Ops:
  0.6 59.5 %copy-start = (bf16[32,128,128]{2,1,0:T(8,128)(2,1)S(1)}, bf16[32,128,128]{2,1,0:T(8,128)(2,1)}, u32[]{:S(2)}) copy-start(bf16[32,128,128]{2,1,0:T(8,128)(2,1)} %param.13) | copy-start | bytes 3145732
  2.2 11.6 %all-to-all-start = ((s32[8,1,2]{2,1,0:T(1,128)}), s32[8,1,2]{2,1,0:T(1,128)S(1)}, u32[]{:S(2)}, u32[]{:S(2)}) async-start(s32[8,1,2]{2,1,0:T(1,128)} %get-tuple-element.15.request), calls=%async_computation | async-start | bytes 8192 | tf_op jit(solution)/shard_map/all_to_all | solution.py:687
  8.6 1.2 %copy-start.1 = (bf16[32,128,128]{2,1,0:T(8,128)(2,1)S(1)}, bf16[32,128,128]{2,1,0:T(8,128)(2,1)}, u32[]{:S(2)}) copy-start(bf16[32,128,128]{2,1,0:T(8,128)(2,1)} %template.1) | copy-start | bytes 3145732
  9.8 9.1 %copy-start.10 = (bf16[40,21]{0,1:T(8,128)(2,1)S(1)}, bf16[40,21]{0,1:T(8,128)(2,1)}, u32[]{:S(2)}) copy-start(bf16[40,21]{0,1:T(8,128)(2,1)} %param.20) | copy-start | bytes 5044
  9.8 9.2 %copy-start.11 = (bf16[40,21]{0,1:T(8,128)(2,1)S(1)}, bf16[40,21]{0,1:T(8,128)(2,1)}, u32[]{:S(2)}) copy-start(bf16[40,21]{0,1:T(8,128)(2,1)} %param.21) | copy-start | bytes 5044
  9.8 9.6 %copy-start.2 = (bf16[1,256,1024]{2,1,0:T(8,128)(2,1)S(1)}, bf16[1,256,1024]{2,1,0:T(8,128)(2,1)}, u32[]{:S(2)}) copy-start(bf16[1,256,1024]{2,1,0:T(8,128)(2,1)} %param.15) | copy-start | bytes 1572868
  9.8 9.6 %copy-start.3 = (bf16[1,256,1024]{2,1,0:T(8,128)(2,1)S(1)}, bf16[1,256,1024]{2,1,0:T(8,128)(2,1)}, u32[]{:S(2)}) copy-start(bf16[1,256,1024]{2,1,0:T(8,128)(2,1)} %param.14) | copy-start | bytes 1572868
  9.8 9.6 %copy-start.5 = (s32[8,1,2]{2,1,0:T(1,128)S(1)}, s32[8,1,2]{2,1,0:T(1,128)}, u32[]{:S(2)}) copy-start(s32[8,1,2]{2,1,0:T(1,128)} %get-tuple-element.15.request) | copy-start | bytes 196
  9.8 9.6 %copy-start.6 = (s32[16]{0:T(128)S(1)}, s32[16]{0:T(128)}, u32[]{:S(2)}) copy-start(s32[16]{0:T(128)} %get-tuple-element.14.sender) | copy-start | bytes 196
  15.2 22.5 %copy-start.4 = (bf16[1,256,1024]{2,1,0:T(8,128)(2,1)S(1)}, bf16[1,256,1024]{2,1,0:T(8,128)(2,1)}, u32[]{:S(2)}) copy-start(bf16[1,256,1024]{2,1,0:T(8,128)(2,1)} %param.14) | copy-start | bytes 1572868
  15.2 22.5 %copy-start.7 = (s32[1,4]{1,0:T(1,128)S(1)}, s32[1,4]{1,0:T(1,128)}, u32[]{:S(2)}) copy-start(s32[1,4]{1,0:T(1,128)} %rows_at.1) | copy-start | bytes 52
  15.2 22.5 %copy-start.8 = (s32[1,4]{1,0:T(1,128)S(1)}, s32[1,4]{1,0:T(1,128)}, u32[]{:S(2)}) copy-start(s32[1,4]{1,0:T(1,128)} %cols_at.1) | copy-start | bytes 52
  15.2 22.5 %copy-start.9 = (s32[16]{0:T(128)S(1)}, s32[16]{0:T(128)}, u32[]{:S(2)}) copy-start(s32[16]{0:T(128)} %get-tuple-element.17.slot_of) | copy-start | bytes 196
  15.2 14.6 %all-to-all-start.1 = ((bf16[16,128,128]{2,1,0:T(8,128)(2,1)}), bf16[16,128,128]{2,1,0:T(8,128)(2,1)S(1)}, u32[]{:S(2)}, u32[]{:S(2)}) async-start(bf16[16,128,128]{2,1,0:T(8,128)(2,1)} %pick_blocks.1.earlier), calls=%async_computation.1 | async-start | bytes 1048576 | tf_op jit(solution)/shard_map/all_to_all | solution.py:692
  29.8 24.3 %all-to-all-start.2 = ((bf16[32,72,128]{2,1,0:T(8,128)(2,1)}), bf16[32,72,128]{2,1,0:T(8,128)(2,1)S(1)}, u32[]{:S(2)}, u32[]{:S(2)}) async-start(bf16[32,72,128]{2,1,0:T(8,128)(2,1)} %prepare.1), calls=%async_computation.2 | async-start | bytes 1179648 | tf_op jit(solution)/shard_map/all_to_all | solution.py:704
  48.2 11.6 %copy-start.12 = (f32[1,21]{1,0:T(1,128)S(1)}, f32[1,21]{1,0:T(1,128)}, u32[]{:S(2)}) copy-start(f32[1,21]{1,0:T(1,128)} %param.23) | copy-start | bytes 256
  48.2 11.7 %copy-start.13 = (f32[1,21]{1,0:T(1,128)S(1)}, f32[1,21]{1,0:T(1,128)}, u32[]{:S(2)}) copy-start(f32[1,21]{1,0:T(1,128)} %param.22) | copy-start | bytes 256
  54.2 22.2 %all-to-all-start.3 = ((bf16[32,72,128]{2,1,0:T(8,128)(2,1)}), bf16[32,72,128]{2,1,0:T(8,128)(2,1)S(1)}, u32[]{:S(2)}, u32[]{:S(2)}) async-start(bf16[32,72,128]{2,1,0:T(8,128)(2,1)} %get-tuple-element.21.payload), calls=%async_computation.3 | async-start | bytes 1179648 | tf_op jit(solution)/shard_map/all_to_all | solution.py:736
  77.6 7.4 %collective-permute-start = (bf16[32,32,128]{2,1,0:T(8,128)(2,1)S(1)}, bf16[32,32,128]{2,1,0:T(8,128)(2,1)S(1)}, u32[]{:S(2)}, u32[]{:S(2)}) collective-permute-start(bf16[32,32,128]{2,1,0:T(8,128)(2,1)S(1)} %combine.1.refs_0_), channel_id=1, source_target_pairs={{0,2},{1,3},{2,0},{3,1},{4,6},{5,7},{6,4},{7,5},{8,10},{9,11},{10,... | collective-permute-start | bytes 786440 | tf_op jit(solution)/shard_map/ppermute | solution.py:755
  78.9 7.6 %collective-permute-start.2 = (bf16[32,32,128]{2,1,0:T(8,128)(2,1)S(1)}, bf16[32,32,128]{2,1,0:T(8,128)(2,1)S(1)}, u32[]{:S(2)}, u32[]{:S(2)}) collective-permute-start(bf16[32,32,128]{2,1,0:T(8,128)(2,1)S(1)} %combine.1.refs_0_), channel_id=1, source_target_pairs={{0,1},{1,0},{2,3},{3,2},{4,5},{5,4},{6,7},{7,6},{8,9},{9,8},{10,11... | collective-permute-start | bytes 786440 | tf_op jit(solution)/shard_map/ppermute | solution.py:755
  85.0 3.2 %collective-permute-start.1 = (bf16[32,32,128]{2,1,0:T(8,128)(2,1)S(1)}, bf16[32,32,128]{2,1,0:T(8,128)(2,1)S(1)}, u32[]{:S(2)}, u32[]{:S(2)}) collective-permute-start(bf16[32,32,128]{2,1,0:T(8,128)(2,1)S(1)} %collective-permute-done.refs_2_), channel_id=1, source_target_pairs={{0,1},{1,0},{2,3},{3,2},{4,5},{5,4},{6,7},{7,6},{8,9},{9,8},{10,11... | collective-permute-start | bytes 786440 | tf_op jit(solution)/shard_map/ppermute | solution.py:755

commit v6 on v5

--- a/solution.py
+++ b/solution.py
@@ -22,6 +22,20 @@
 
 def cost(flops, moved):
     return pl.CostEstimate(flops=flops, bytes_accessed=moved, transcendentals=0)
+
+
+def distance(here, there, exps):
+    if exps & (exps - 1) == 0:
+        return here ^ there
+    return lax.rem(here - there + exps, exps)
+
+
+def from_exposure(value, gap, exps):
+    if exps & (exps - 1) == 0:
+        pairs = [(e, e ^ gap) for e in range(exps)]
+    else:
+        pairs = [(e, (e + gap) % exps) for e in range(exps)]
+    return lax.ppermute(value, "exp", pairs)
 
 
 def route_body(src, blk, slot_of, sender, request, count, *, peers, capacity):
@@ -116,20 +130,6 @@
     lax.fori_loop(0, slots, one, 0, unroll=True if slots <= 32 else 4)
 
 
-def store_requests(request, out, side, exps, capacity):
-    lane = lax.broadcasted_iota(jnp.int32, (trailer_rows, side), 1)
-
-    def put(p, carry):
-        line = jnp.zeros((trailer_rows, side), f32)
-        for c in range(capacity):
-            line = jnp.where(lane == c, request[p, 0, c].astype(f32), line)
-        for q in range(exps):
-            out[p * exps + q, out.shape[1] - trailer_rows :, :] = line.astype(bf16)
-        return carry
-
-    lax.fori_loop(0, request.shape[0], put, 0)
-
-
 def cut(ref, top, left, height, side):
     down = pl.multiple_of((top // 8) * 8, 8)
     over = pl.multiple_of((left // side) * side, side)
@@ -138,23 +138,29 @@
     return pltpu.roll(tile, lax.rem(height - (top - down), height), 0)
 
 
-def prepare_body(sender, request, variance, science, earlier, out, *, side, exps, capacity):
+def prepare_body(
+    sender, variance, science, asked, earlier, out, asked_out, *, side, exps, capacity
+):
     del earlier, science
     store_parts(sender, variance, out, side, exps, capacity, variance.shape[1] // side)
-    store_requests(request, out, side, exps, capacity)
-
-
-def prepare(sender, request, variance, science, earlier, side, exps, capacity):
-    rows = capacity * (side // exps) + trailer_rows
+    asked_out[...] = asked[...]
+
+
+def prepare(sender, variance, science, asked, earlier, side, exps, capacity):
+    slots = sender.shape[0]
+    part = side // exps
     return pl.pallas_call(
         functools.partial(prepare_body, side=side, exps=exps, capacity=capacity),
-        out_shape=jax.ShapeDtypeStruct((request.shape[0] * exps, rows, side), bf16),
-        in_specs=[smem()] * 2 + [vmem(), vmem(), pl.BlockSpec(memory_space=pl.ANY)],
-        out_specs=vmem(),
+        out_shape=(
+            jax.ShapeDtypeStruct((slots // capacity * exps, capacity * part, side), bf16),
+            jax.ShapeDtypeStruct(asked.shape, asked.dtype),
+        ),
+        in_specs=[smem()] + [vmem()] * 3 + [pl.BlockSpec(memory_space=pl.ANY)],
+        out_specs=(vmem(), vmem()),
         compiler_params=pltpu.CompilerParams(vmem_limit_bytes=16 * mib),
         cost_estimate=cost(0, 6_000_000),
         name="prepare",
-    )(sender, request, variance, science, earlier)
+    )(sender, variance, science, asked, earlier)
 
 
 def normal_body(
@@ -184,7 +190,7 @@
     stamps = rows_at.shape[1]
     span = up(side + taps - 1, 16)
     padded_k = gram_out.shape[1]
-    pitch = padded_k + 1
+    pitch = (count + 2) | 1
     lines_all = stamps * side
     sub = lax.broadcasted_iota(jnp.int32, (side, side), 0)
     lane = lax.broadcasted_iota(jnp.int32, (side, side), 1)
@@ -223,8 +229,7 @@
         design[place, :] = root
         place = pl.ds(s * side * pitch + count + 1, side, stride=pitch)
         design[place, :] = root * cut_image(science, top, left)
-    for extra in range(count + 2, padded_k):
-        design[pl.ds(extra, lines_all, stride=pitch), :] = jnp.zeros((lines_all, side), f32)
+    design[lines_all * pitch :, :] = jnp.zeros((design.shape[0] - lines_all * pitch, side), f32)
 
     group = vert.shape[0]
     step = side - taps + 1
@@ -281,6 +286,7 @@
         lines_all // (lines * sets),
         gram_step,
         jnp.zeros((sets * padded_k, sets * padded_k), f32),
+        unroll=2,
     )
     part = jnp.zeros((padded_k, padded_k), f32)
     for g in range(sets):
@@ -314,7 +320,7 @@
             pltpu.VMEM((tall, wide + 2 * side), f32),
             pltpu.VMEM((stamps * span, 2 * side), bf16),
             pltpu.VMEM((group, stamps * side, 2 * side), bf16),
-            pltpu.VMEM((stamps * side * (padded_k + 1), side), f32),
+            pltpu.VMEM((up(stamps * side * ((count + 2) | 1) + padded_k, 8), side), f32),
             pltpu.VMEM((stamps * side, side), f32),
             pltpu.VMEM((2 * half, side), f32),
         ],
@@ -493,6 +499,7 @@
 
 
 def score_body(
+    me,
     table,
     slot_of,
     payload,
@@ -510,7 +517,7 @@
     part,
     capacity,
 ):
-    add_variance(table, parts, var_out, var_total, part, capacity)
+    add_variance(me, table, parts, var_out, var_total, part, capacity)
     high, wide = out.shape
     margin = taps // 2
     span = up(side + taps - 1, 16)
@@ -545,7 +552,7 @@
 
 
 def score(
-    table, slot_of, payload, down, over_rev, parts, high, wide, taps, tract, part, capacity
+    me, table, slot_of, payload, down, over_rev, parts, high, wide, taps, tract, part, capacity
 ):
     side = payload.shape[2]
     span = up(side + taps - 1, 16)
@@ -555,7 +562,7 @@
             jax.ShapeDtypeStruct((high, wide), f32),
             jax.ShapeDtypeStruct((tract, part, side), f32),
         ),
-        in_specs=[smem()] * 2 + [vmem()] * 4,
+        in_specs=[smem()] * 3 + [vmem()] * 4,
         out_specs=(vmem(),) * 2,
         scratch_shapes=[
             pltpu.VMEM((high, wide + side), f32),
@@ -565,25 +572,32 @@
         compiler_params=pltpu.CompilerParams(vmem_limit_bytes=24 * mib),
         cost_estimate=cost(2_000_000_000, 2_000_000),
         name="score",
-    )(table, slot_of, payload, down, over_rev, parts)
-
-
-def add_variance(table, parts, out, total, part, capacity):
+    )(me, table, slot_of, payload, down, over_rev, parts)
+
+
+def wanted_block(me, table, d, c, tract):
+    exps = table.shape[0]
+    block = table[distance(me[0], lax.rem(d, exps), exps), d // exps, c] - 1
+    return jnp.where(block < 0, tract, block)
+
+
+def add_variance(me, table, parts, out, total, part, capacity):
     total[...] = jnp.zeros(total.shape, f32)
     tract = out.shape[0]
 
-    def one(j, carry):
-        block = table[j // capacity, j % capacity] - 1
-        block = jnp.where(block < 0, tract, block)
-        row = pl.multiple_of((j % capacity) * part, part)
-        total[block] += parts[j // capacity, pl.ds(row, part), :].astype(f32)
+    def one(d, carry):
+        for c in range(capacity):
+            block = wanted_block(me, table, d, c, tract)
+            total[block] += parts[d, c * part : (c + 1) * part, :].astype(f32)
         return carry
 
-    lax.fori_loop(0, parts.shape[0] * capacity, one, 0, unroll=8)
+    lax.fori_loop(0, parts.shape[0], one, 0, unroll=4)
     out[...] = total[:tract]
 
 
-def combine_body(table, parts, var_sum, var_template, out, total, gain, *, part, capacity):
+def combine_body(
+    me, table, parts, var_sum, var_template, out, total, gain, *, part, capacity
+):
     total[...] = jnp.zeros(total.shape, f32)
     gain[...] = jnp.zeros(gain.shape, f32)
     tract = out.shape[0]
@@ -593,8 +607,7 @@
         kernel_sum = tail[0:1] + tail[1:2] + tail[2:3]
         square = jnp.broadcast_to(kernel_sum * kernel_sum, gain.shape[1:])
         for c in range(capacity):
-            block = table[d, c] - 1
-            block = jnp.where(block < 0, tract, block)
+            block = wanted_block(me, table, d, c, tract)
             total[block] += parts[d, c * part : (c + 1) * part, :].astype(f32)
             gain[block] += square
         return carry
@@ -605,12 +618,12 @@
         out[t] = (total[t] * lax.rsqrt(jnp.maximum(variance, 1.0))).astype(bf16)
 
 
-def combine(table, parts, var_sum, var_template, part, capacity):
+def combine(me, table, parts, var_sum, var_template, part, capacity):
     tract, _, side = var_sum.shape
     return pl.pallas_call(
         functools.partial(combine_body, part=part, capacity=capacity),
         out_shape=jax.ShapeDtypeStruct((tract, part, side), bf16),
-        in_specs=[smem(), vmem(), vmem(), vmem()],
+        in_specs=[smem(), smem(), vmem(), vmem(), vmem()],
         out_specs=vmem(),
         scratch_shapes=[
             pltpu.VMEM((tract + 1, part, side), f32),
@@ -618,7 +631,7 @@
         ],
         compiler_params=pltpu.CompilerParams(vmem_limit_bytes=16 * mib),
         name="combine",
-    )(table, parts, var_sum, var_template)
+    )(me, table, parts, var_sum, var_template)
 
 
 def join_body(places, *refs, part, count):
@@ -686,8 +699,8 @@
     slot_of, sender, request = route_tables(routes_src, routes_blk, peers, capacity)
     asked = lax.all_to_all(request, "det", split_axis=0, concat_axis=0, tiled=True)
     picked = pick_blocks(asked, fetch(template), slots, capacity)
-    var_parts = prepare(
-        sender, request, variance_img, science_img, picked, side, exps, capacity
+    var_parts, asked_late = prepare(
+        sender, variance_img, science_img, asked, picked, side, exps, capacity
     )
     arrived = lax.all_to_all(picked, "det", split_axis=0, concat_axis=0, tiled=True)
 
@@ -704,7 +717,8 @@
     var_back = lax.all_to_all(
         var_late, ("det", "exp"), split_axis=0, concat_axis=0, tiled=True
     )
-    table = var_back[:, capacity * part, :capacity].astype(f32).astype(jnp.int32)
+    tables = [asked_late] + [from_exposure(asked_late, g, exps) for g in range(1, exps)]
+    table = jnp.stack(tables).reshape(exps, peers, capacity)
 
     high, wide = science_img.shape
     gram, frames = normal_matrix(
@@ -735,6 +749,7 @@
     )
     diff_back = lax.all_to_all(payload, ("det", "exp"), split_axis=0, concat_axis=0, tiled=True)
     scored, var_sum = score(
+        me[None],
         table,
         slot_of,
         payload,
@@ -749,7 +764,7 @@
         capacity,
     )
     var_template = lax.dynamic_slice_in_dim(template_var, me * part, part, 1)
-    mine = combine(table, diff_back, var_sum, var_template, part, capacity)
+    mine = combine(me[None], table, diff_back, var_sum, var_template, part, capacity)
 
     def swap(value, distance):
         return lax.ppermute(value, "exp", [(e, e ^ distance) for e in range(exps)])

time: 89.6 us -> 89.6 us (level)
  waiting for transfers between devices: 30.7 us -> 27.3 us
  local copies, waits for them, and re-layouts: 1.9 us -> 4.93 us
  starting transfers between devices: 26.7 us -> 29 us
  Pallas kernels: 28.6 us -> 26.7 us
    all_to_all x1, waiting for transfers between devices: 12.3 us -> 6.78 us  [local(): lax.all_to_all(payload, ('det', 'exp'), split_axis=0, concat_axis=0, tile...]
    unnamed x29 -> x31, local copies, waits for them, and re-layouts: 1.38 us -> 3.99 us
    ppermute x0 -> x3, starting transfers between devices: none -> 2.14 us  [from_exposure(): return lax.ppermute(value, 'exp', pairs)]
    ppermute x0 -> x3, waiting for transfers between devices: none -> 2.1 us  [from_exposure(): return lax.ppermute(value, 'exp', pairs)]
    pallas_call x1, Pallas kernels: 1.64 us -> 0.7 us  [prepare(): pl.pallas_call(functools.partial(prepare_body, side=side, exps=exps, capa...]
  transfers between devices with their start and end apart: 7 -> 10, of which waited for: 5 -> 6; matrix products, arithmetic and copies ran while one was open for 1% -> 1% of each run, Pallas kernels for 26% -> 24%
where the time goes in v6:
time: 89.6 us; the launch traced here: 89 us
  starting transfers between devices  29 us (32%)
  waiting for transfers between devices  27.3 us (30%)
  Pallas kernels  26.7 us (30%)
  local copies, waits for them, and re-layouts  4.93 us (6%)
    pallas_call x1, Pallas kernels, normal_matrix(): pl.pallas_call(functools.partial(normal_body, count=count, across_blocks=...  9.61 us
    all_to_all x1, waiting for transfers between devices, local(): lax.all_to_all(picked, 'det', split_axis=0, concat_axis=0, tiled=True)  8.88 us
    all_to_all x1, starting transfers between devices, local(): lax.all_to_all(var_late, ('det', 'exp'), split_axis=0, concat_axis=0, til...  7.88 us
    all_to_all x1, waiting for transfers between devices, local(): lax.all_to_all(payload, ('det', 'exp'), split_axis=0, concat_axis=0, tile...  6.78 us
    all_to_all x1, starting transfers between devices, local(): lax.all_to_all(request, 'det', split_axis=0, concat_axis=0, tiled=True)  6.37 us
    all_to_all x1, starting transfers between devices, local(): lax.all_to_all(payload, ('det', 'exp'), split_axis=0, concat_axis=0, tile...  5.82 us
    pallas_call x1, Pallas kernels, subtract(): pl.pallas_call(body, out_shape=(jax.ShapeDtypeStruct((1, side), f32), jax...  5.74 us
    ppermute x3, waiting for transfers between devices, swap(): return lax.ppermute(value, 'exp', [(e, e ^ distance) for e in range(exps)])  5.66 us
  transfers between devices with their start and end apart: 10, of which 6 were waited for; matrix products, arithmetic and copies ran while one was open for 1% of the time, Pallas kernels for 24%

profile of v6, /device:TPU:1, one launch (start us, length us, event | category | flops | bytes accessed | tf_op | source)
XLA Modules:
  0.0 89.0 jit_solution(9972017097022433682)
XLA Ops:
  0.6 1.5 %route_tables.1 = (s32[16]{0:T(128)}, s32[16]{0:T(128)}, s32[8,1,2]{2,1,0:T(1,128)}) custom-call(s32[1,16]{1,0:T(1,128)} %src.1, s32[1,16]{1,0:T(1,128)} %blk.1), custom_call_target="tpu_custom_call" | custom-call | tf_op jit(solution)/shard_map/route_tables/pallas_call | solution.py:63
  2.2 6.4 %all-to-all-start = ((s32[8,1,2]{2,1,0:T(1,128)}), s32[8,1,2]{2,1,0:T(1,128)S(1)}, u32[]{:S(2)}, u32[]{:S(2)}) async-start(s32[8,1,2]{2,1,0:T(1,128)} %get-tuple-element.17), calls=%async_computation | async-start | bytes 8192 | tf_op jit(solution)/shard_map/all_to_all | solution.py:700
  8.6 1.2 %copy-done.1 = bf16[32,128,128]{2,1,0:T(8,128)(2,1)S(1)} copy-done((bf16[32,128,128]{2,1,0:T(8,128)(2,1)S(1)}, bf16[32,128,128]{2,1,0:T(8,128)(2,1)}, u32[]{:S(2)}) %copy-start.1) | copy-done | bytes 1048600
  9.9 3.9 %all-to-all-done.asked = s32[8,1,2]{2,1,0:T(1,128)S(1)} async-done(((s32[8,1,2]{2,1,0:T(1,128)}), s32[8,1,2]{2,1,0:T(1,128)S(1)}, u32[]{:S(2)}, u32[]{:S(2)}) %all-to-all-start) | async-done | bytes 96 | tf_op jit(solution)/shard_map/all_to_all | solution.py:700
  13.8 1.4 %pick_blocks.1.earlier = bf16[16,128,128]{2,1,0:T(8,128)(2,1)} custom-call(s32[8,1,2]{2,1,0:T(1,128)S(1)} %all-to-all-done.asked, bf16[32,128,128]{2,1,0:T(8,128)(2,1)S(1)} %fetch.1.template), custom_call_target="tpu_custom_call" | custom-call | tf_op jit(solution)/shard_map/pick_blocks/pallas_call | solution.py:106
  15.2 3.6 %all-to-all-start.1 = ((bf16[16,128,128]{2,1,0:T(8,128)(2,1)}), bf16[16,128,128]{2,1,0:T(8,128)(2,1)S(1)}, u32[]{:S(2)}, u32[]{:S(2)}) async-start(bf16[16,128,128]{2,1,0:T(8,128)(2,1)} %pick_blocks.1.earlier), calls=%async_computation.1 | async-start | bytes 1048576 | tf_op jit(solution)/shard_map/all_to_all | solution.py:705
  20.9 8.9 %all-to-all-done.1.arrived = bf16[16,128,128]{2,1,0:T(8,128)(2,1)S(1)} async-done(((bf16[16,128,128]{2,1,0:T(8,128)(2,1)}), bf16[16,128,128]{2,1,0:T(8,128)(2,1)S(1)}, u32[]{:S(2)}, u32[]{:S(2)}) %all-to-all-start.1) | async-done | bytes 524320 | tf_op jit(solution)/shard_map/all_to_all | solution.py:705
  29.8 7.9 %all-to-all-start.3 = ((bf16[32,64,128]{2,1,0:T(8,128)(2,1)}), bf16[32,64,128]{2,1,0:T(8,128)(2,1)S(1)}, u32[]{:S(2)}, u32[]{:S(2)}) async-start(bf16[32,64,128]{2,1,0:T(8,128)(2,1)} %copy-done.6), calls=%async_computation.3 | async-start | bytes 1048576 | tf_op jit(solution)/shard_map/all_to_all | solution.py:717
  37.7 9.6 %normal_matrix.1 = (f32[48,48]{1,0:T(8,128)S(1)}, f32[10,2,144,128]{3,2,1,0:T(8,128)S(1)}) custom-call(s32[16]{0:T(128)S(1)} %copy-done.10, s32[1,4]{1,0:T(1,128)S(1)} %copy-done.8, s32[1,4]{1,0:T(1,128)S(1)} %copy-done.9, bf16[16,128,128]{2,1,0:T(8,128)(2,1)S(1)} %all-to-all-done.1.arrived, f32[48,128]{1,0:T(8,128)S(1)} %pad_convert_fusion.col, ...), custom_call_target="tpu_custom_call" | custom-call | flops 10000000000 | bytes 8000000 | tf_op jit(solution)/shard_map/normal_matrix/pallas_call | solution.py:311
  47.4 5.7 %subtract.1 = (f32[1,128]{1,0:T(1,128)}, bf16[32,72,128]{2,1,0:T(8,128)(2,1)}) custom-call(s32[16]{0:T(128)S(1)} %copy-done.7, f32[48,48]{1,0:T(8,128)S(1)} %get-tuple-element.22.gram, f32[10,2,144,128]{3,2,1,0:T(8,128)S(1)} %get-tuple-element.23.frames, bf16[256,1024]{1,0:T(8,128)(2,1)S(1)} %bitcast.20, bf16[32,48]{1,0:T(8,128)(2,1)S(1)} %pad.25.col_t, ...), custom_call_target="tpu_custom_call" | custom-call | flops 5000000000 | bytes 4000000 | tf_op jit(solution)/shard_map/subtract/pallas_call | solution.py:473
  53.1 0.8 copy-done.4
  53.9 5.8 %all-to-all-start.2 = ((bf16[32,72,128]{2,1,0:T(8,128)(2,1)}), bf16[32,72,128]{2,1,0:T(8,128)(2,1)S(1)}, u32[]{:S(2)}, u32[]{:S(2)}) async-start(bf16[32,72,128]{2,1,0:T(8,128)(2,1)} %get-tuple-element.24.payload), calls=%async_computation.2 | async-start | bytes 1179648 | tf_op jit(solution)/shard_map/all_to_all | solution.py:750
  60.1 1.6 %collective-permute-start.2 = (s32[8,1,2]{2,1,0:T(1,128)S(1)}, s32[8,1,2]{2,1,0:T(1,128)S(1)}, u32[]{:S(2)}, u32[]{:S(2)}) collective-permute-start(s32[8,1,2]{2,1,0:T(1,128)S(1)} %get-tuple-element.18), channel_id=1, source_target_pairs={{0,3},{1,2},{2,1},{3,0},{4,7},{5,6},{6,5},{7,4},{8,11},{9,10},{10,... | collective-permute-start | bytes 200 | tf_op jit(solution)/shard_map/ppermute | solution.py:38
  62.3 1.2 %collective-permute-done.2 = s32[8,1,2]{2,1,0:T(1,128)S(1)} collective-permute-done((s32[8,1,2]{2,1,0:T(1,128)S(1)}, s32[8,1,2]{2,1,0:T(1,128)S(1)}, u32[]{:S(2)}, u32[]{:S(2)}) %collective-permute-start.2) | collective-permute-done | bytes 96 | tf_op jit(solution)/shard_map/ppermute | solution.py:38
  63.5 0.9 %collective-permute-done.1 = s32[8,1,2]{2,1,0:T(1,128)S(1)} collective-permute-done((s32[8,1,2]{2,1,0:T(1,128)S(1)}, s32[8,1,2]{2,1,0:T(1,128)S(1)}, u32[]{:S(2)}, u32[]{:S(2)}) %collective-permute-start.1) | collective-permute-done | bytes 96 | tf_op jit(solution)/shard_map/ppermute | solution.py:38
  64.7 1.0 %copy-done.5 = bf16[32,64,128]{2,1,0:T(8,128)(2,1)S(1)} copy-done((bf16[32,64,128]{2,1,0:T(8,128)(2,1)S(1)}, bf16[32,64,128]{2,1,0:T(8,128)(2,1)}, u32[]{:S(2)}) %copy-start.5) | copy-done | bytes 524312
  65.8 3.6 %score.1 = (f32[256,1024]{1,0:T(8,128)}, f32[32,32,128]{2,1,0:T(8,128)S(1)}) custom-call(s32[1]{0:T(128)} %bitcast.1.me, s32[4,8,2]{2,1,0:T(8,128)S(1)} %copy.33.table, s32[16]{0:T(128)S(1)} %copy-done.10, bf16[32,72,128]{2,1,0:T(8,128)(2,1)} %get-tuple-element.24.payload, f32[1,256]{1,0:T(1,128)S(1)} %pad.26.down, f32[1,256]{1,0:T(1,128)S(1)} %pad_maximum_fusion.1.over, ...), custom_call_target="tpu_custom_call" | custom-call | flops 2000000000 | bytes 2000000 | tf_op jit(solution)/shard_map/score/pallas_call | solution.py:559
  69.4 6.8 %all-to-all-done.2.parts = bf16[32,72,128]{2,1,0:T(8,128)(2,1)S(1)} async-done(((bf16[32,72,128]{2,1,0:T(8,128)(2,1)}), bf16[32,72,128]{2,1,0:T(8,128)(2,1)S(1)}, u32[]{:S(2)}, u32[]{:S(2)}) %all-to-all-start.2) | async-done | bytes 589856 | tf_op jit(solution)/shard_map/all_to_all | solution.py:750
  76.2 1.4 %combine.1.refs_0_ = bf16[32,32,128]{2,1,0:T(8,128)(2,1)S(1)} custom-call(s32[1]{0:T(128)} %bitcast.1.me, s32[4,8,2]{2,1,0:T(8,128)S(1)} %copy.33.table, bf16[32,72,128]{2,1,0:T(8,128)(2,1)S(1)} %all-to-all-done.2.parts, f32[32,32,128]{2,1,0:T(8,128)S(1)} %get-tuple-element.26.var_sum, bf16[32,32,128]{2,1,0:T(8,128)(2,1)S(1)} %constant_dynamic-slice_fusion.var_template), custom_call_target="tpu_custom_call" | custom-call | tf_op jit(solution)/shard_map/combine/pallas_call | solution.py:623
  77.6 1.3 %collective-permute-start.3 = (bf16[32,32,128]{2,1,0:T(8,128)(2,1)S(1)}, bf16[32,32,128]{2,1,0:T(8,128)(2,1)S(1)}, u32[]{:S(2)}, u32[]{:S(2)}) collective-permute-start(bf16[32,32,128]{2,1,0:T(8,128)(2,1)S(1)} %combine.1.refs_0_), channel_id=1, source_target_pairs={{0,2},{1,3},{2,0},{3,1},{4,6},{5,7},{6,4},{7,5},{8,10},{9,11},{10,... | collective-permute-start | bytes 786440 | tf_op jit(solution)/shard_map/ppermute | solution.py:770
  79.3 5.7 %collective-permute-done.3.refs_2_ = bf16[32,32,128]{2,1,0:T(8,128)(2,1)S(1)} collective-permute-done((bf16[32,32,128]{2,1,0:T(8,128)(2,1)S(1)}, bf16[32,32,128]{2,1,0:T(8,128)(2,1)S(1)}, u32[]{:S(2)}, u32[]{:S(2)}) %collective-permute-start.3) | collective-permute-done | bytes 262176 | tf_op jit(solution)/shard_map/ppermute | solution.py:770
  85.0 1.4 %collective-permute-start.4 = (bf16[32,32,128]{2,1,0:T(8,128)(2,1)S(1)}, bf16[32,32,128]{2,1,0:T(8,128)(2,1)S(1)}, u32[]{:S(2)}, u32[]{:S(2)}) collective-permute-start(bf16[32,32,128]{2,1,0:T(8,128)(2,1)S(1)} %collective-permute-done.3.refs_2_), channel_id=1, source_target_pairs={{0,1},{1,0},{2,3},{3,2},{4,5},{5,4},{6,7},{7,6},{8,9},{9,8},{10,11... | collective-permute-start | bytes 786440 | tf_op jit(solution)/shard_map/ppermute | solution.py:770
  86.4 1.7 %join_parts.2.refs_1_ = f32[32,128,128]{2,1,0:T(8,128)} custom-call(s32[3]{0:T(128)S(1)} %pad_add_fusion.places, bf16[32,32,128]{2,1,0:T(8,128)(2,1)S(1)} %combine.1.refs_0_, bf16[32,32,128]{2,1,0:T(8,128)(2,1)S(1)} %collective-permute-done.5.refs_1_, bf16[32,32,128]{2,1,0:T(8,128)(2,1)S(1)} %collective-permute-done.3.refs_2_), custom_call_target="tpu_custom_call" | custom-call | bytes 9000000 | tf_op jit(solution)/shard_map/join_parts/pallas_call | solution.py:657
  88.2 0.8 join_parts.3
  (56 shorter events, 3.9 us)
Async XLA Ops:
  0.6 59.4 %copy-start = (bf16[32,128,128]{2,1,0:T(8,128)(2,1)S(1)}, bf16[32,128,128]{2,1,0:T(8,128)(2,1)}, u32[]{:S(2)}) copy-start(bf16[32,128,128]{2,1,0:T(8,128)(2,1)} %param.13) | copy-start | bytes 3145732
  2.2 11.6 %all-to-all-start = ((s32[8,1,2]{2,1,0:T(1,128)}), s32[8,1,2]{2,1,0:T(1,128)S(1)}, u32[]{:S(2)}, u32[]{:S(2)}) async-start(s32[8,1,2]{2,1,0:T(1,128)} %get-tuple-element.17), calls=%async_computation | async-start | bytes 8192 | tf_op jit(solution)/shard_map/all_to_all | solution.py:700
  8.6 1.2 %copy-start.1 = (bf16[32,128,128]{2,1,0:T(8,128)(2,1)S(1)}, bf16[32,128,128]{2,1,0:T(8,128)(2,1)}, u32[]{:S(2)}) copy-start(bf16[32,128,128]{2,1,0:T(8,128)(2,1)} %template.1) | copy-start | bytes 3145732
  9.8 9.1 %copy-start.11 = (bf16[40,21]{0,1:T(8,128)(2,1)S(1)}, bf16[40,21]{0,1:T(8,128)(2,1)}, u32[]{:S(2)}) copy-start(bf16[40,21]{0,1:T(8,128)(2,1)} %param.20) | copy-start | bytes 5044
  9.8 9.2 %copy-start.12 = (bf16[40,21]{0,1:T(8,128)(2,1)S(1)}, bf16[40,21]{0,1:T(8,128)(2,1)}, u32[]{:S(2)}) copy-start(bf16[40,21]{0,1:T(8,128)(2,1)} %param.21) | copy-start | bytes 5044
  9.8 9.6 %copy-start.2 = (bf16[1,256,1024]{2,1,0:T(8,128)(2,1)S(1)}, bf16[1,256,1024]{2,1,0:T(8,128)(2,1)}, u32[]{:S(2)}) copy-start(bf16[1,256,1024]{2,1,0:T(8,128)(2,1)} %param.15) | copy-start | bytes 1572868
  9.8 9.6 %copy-start.3 = (bf16[1,256,1024]{2,1,0:T(8,128)(2,1)S(1)}, bf16[1,256,1024]{2,1,0:T(8,128)(2,1)}, u32[]{:S(2)}) copy-start(bf16[1,256,1024]{2,1,0:T(8,128)(2,1)} %param.14) | copy-start | bytes 1572868
  9.8 9.6 %copy-start.7 = (s32[16]{0:T(128)S(1)}, s32[16]{0:T(128)}, u32[]{:S(2)}) copy-start(s32[16]{0:T(128)} %get-tuple-element.16.sender) | copy-start | bytes 196
  15.2 22.5 %copy-start.8 = (s32[1,4]{1,0:T(1,128)S(1)}, s32[1,4]{1,0:T(1,128)}, u32[]{:S(2)}) copy-start(s32[1,4]{1,0:T(1,128)} %rows_at.1) | copy-start | bytes 52
  15.2 22.5 %copy-start.9 = (s32[1,4]{1,0:T(1,128)S(1)}, s32[1,4]{1,0:T(1,128)}, u32[]{:S(2)}) copy-start(s32[1,4]{1,0:T(1,128)} %cols_at.1) | copy-start | bytes 52
  15.2 22.5 %copy-start.10 = (s32[16]{0:T(128)S(1)}, s32[16]{0:T(128)}, u32[]{:S(2)}) copy-start(s32[16]{0:T(128)} %get-tuple-element.19.slot_of) | copy-start | bytes 196
  15.2 14.6 %all-to-all-start.1 = ((bf16[16,128,128]{2,1,0:T(8,128)(2,1)}), bf16[16,128,128]{2,1,0:T(8,128)(2,1)S(1)}, u32[]{:S(2)}, u32[]{:S(2)}) async-start(bf16[16,128,128]{2,1,0:T(8,128)(2,1)} %pick_blocks.1.earlier), calls=%async_computation.1 | async-start | bytes 1048576 | tf_op jit(solution)/shard_map/all_to_all | solution.py:705
  29.8 23.3 %all-to-all-start.3 = ((bf16[32,64,128]{2,1,0:T(8,128)(2,1)}), bf16[32,64,128]{2,1,0:T(8,128)(2,1)S(1)}, u32[]{:S(2)}, u32[]{:S(2)}) async-start(bf16[32,64,128]{2,1,0:T(8,128)(2,1)} %copy-done.6), calls=%async_computation.3 | async-start | bytes 1048576 | tf_op jit(solution)/shard_map/all_to_all | solution.py:717
  47.3 12.4 %copy-start.13 = (f32[1,21]{1,0:T(1,128)S(1)}, f32[1,21]{1,0:T(1,128)}, u32[]{:S(2)}) copy-start(f32[1,21]{1,0:T(1,128)} %param.23) | copy-start | bytes 256
  47.3 12.5 %copy-start.14 = (f32[1,21]{1,0:T(1,128)S(1)}, f32[1,21]{1,0:T(1,128)}, u32[]{:S(2)}) copy-start(f32[1,21]{1,0:T(1,128)} %param.22) | copy-start | bytes 256
  53.1 0.8 copy-start.4
  53.9 22.3 %all-to-all-start.2 = ((bf16[32,72,128]{2,1,0:T(8,128)(2,1)}), bf16[32,72,128]{2,1,0:T(8,128)(2,1)S(1)}, u32[]{:S(2)}, u32[]{:S(2)}) async-start(bf16[32,72,128]{2,1,0:T(8,128)(2,1)} %get-tuple-element.24.payload), calls=%async_computation.2 | async-start | bytes 1179648 | tf_op jit(solution)/shard_map/all_to_all | solution.py:750
  60.1 3.3 %collective-permute-start.2 = (s32[8,1,2]{2,1,0:T(1,128)S(1)}, s32[8,1,2]{2,1,0:T(1,128)S(1)}, u32[]{:S(2)}, u32[]{:S(2)}) collective-permute-start(s32[8,1,2]{2,1,0:T(1,128)S(1)} %get-tuple-element.18), channel_id=1, source_target_pairs={{0,3},{1,2},{2,1},{3,0},{4,7},{5,6},{6,5},{7,4},{8,11},{9,10},{10,... | collective-permute-start | bytes 200 | tf_op jit(solution)/shard_map/ppermute | solution.py:38
  61.8 2.7 %collective-permute-start.1 = (s32[8,1,2]{2,1,0:T(1,128)S(1)}, s32[8,1,2]{2,1,0:T(1,128)S(1)}, u32[]{:S(2)}, u32[]{:S(2)}) collective-permute-start(s32[8,1,2]{2,1,0:T(1,128)S(1)} %get-tuple-element.18), channel_id=1, source_target_pairs={{0,2},{1,3},{2,0},{3,1},{4,6},{5,7},{6,4},{7,5},{8,10},{9,11},{10,... | collective-permute-start | bytes 200 | tf_op jit(solution)/shard_map/ppermute | solution.py:38
  61.8 2.8 %collective-permute-start = (s32[8,1,2]{2,1,0:T(1,128)S(1)}, s32[8,1,2]{2,1,0:T(1,128)S(1)}, u32[]{:S(2)}, u32[]{:S(2)}) collective-permute-start(s32[8,1,2]{2,1,0:T(1,128)S(1)} %get-tuple-element.18), channel_id=1, source_target_pairs={{0,1},{1,0},{2,3},{3,2},{4,5},{5,4},{6,7},{7,6},{8,9},{9,8},{10,11... | collective-permute-start | bytes 200 | tf_op jit(solution)/shard_map/ppermute | solution.py:38
  64.7 1.0 %copy-start.5 = (bf16[32,64,128]{2,1,0:T(8,128)(2,1)S(1)}, bf16[32,64,128]{2,1,0:T(8,128)(2,1)}, u32[]{:S(2)}) copy-start(bf16[32,64,128]{2,1,0:T(8,128)(2,1)} %copy-done.4) | copy-start | bytes 1572868
  77.6 7.4 %collective-permute-start.3 = (bf16[32,32,128]{2,1,0:T(8,128)(2,1)S(1)}, bf16[32,32,128]{2,1,0:T(8,128)(2,1)S(1)}, u32[]{:S(2)}, u32[]{:S(2)}) collective-permute-start(bf16[32,32,128]{2,1,0:T(8,128)(2,1)S(1)} %combine.1.refs_0_), channel_id=1, source_target_pairs={{0,2},{1,3},{2,0},{3,1},{4,6},{5,7},{6,4},{7,5},{8,10},{9,11},{10,... | collective-permute-start | bytes 786440 | tf_op jit(solution)/shard_map/ppermute | solution.py:770
  78.9 7.6 %collective-permute-start.5 = (bf16[32,32,128]{2,1,0:T(8,128)(2,1)S(1)}, bf16[32,32,128]{2,1,0:T(8,128)(2,1)S(1)}, u32[]{:S(2)}, u32[]{:S(2)}) collective-permute-start(bf16[32,32,128]{2,1,0:T(8,128)(2,1)S(1)} %combine.1.refs_0_), channel_id=1, source_target_pairs={{0,1},{1,0},{2,3},{3,2},{4,5},{5,4},{6,7},{7,6},{8,9},{9,8},{10,11... | collective-permute-start | bytes 786440 | tf_op jit(solution)/shard_map/ppermute | solution.py:770
  85.0 3.2 %collective-permute-start.4 = (bf16[32,32,128]{2,1,0:T(8,128)(2,1)S(1)}, bf16[32,32,128]{2,1,0:T(8,128)(2,1)S(1)}, u32[]{:S(2)}, u32[]{:S(2)}) collective-permute-start(bf16[32,32,128]{2,1,0:T(8,128)(2,1)S(1)} %collective-permute-done.3.refs_2_), channel_id=1, source_target_pairs={{0,1},{1,0},{2,3},{3,2},{4,5},{5,4},{6,7},{7,6},{8,9},{9,8},{10,11... | collective-permute-start | bytes 786440 | tf_op jit(solution)/shard_map/ppermute | solution.py:770
  (1 other events, 0.8 us)

commit v7 on v6

--- a/solution.py
+++ b/solution.py
@@ -93,13 +93,14 @@
     )(template)
 
 
-def pick_body(asked, template, out, *, capacity):
-    def one(s, carry):
+def pick_body(asked, template, out, sems, *, capacity):
+    copies = []
+    for s in range(out.shape[0]):
         block = jnp.maximum(asked[s // capacity, 0, s % capacity] - 1, 0)
-        out[s] = template[block]
-        return carry
-
-    lax.fori_loop(0, out.shape[0], one, 0, unroll=True if out.shape[0] <= 32 else 4)
+        copies.append(pltpu.make_async_copy(template.at[block], out.at[s], sems.at[s]))
+        copies[-1].start()
+    for copy in copies:
+        copy.wait()
 
 
 def pick_blocks(asked, template, slots, capacity):
@@ -107,7 +108,8 @@
         functools.partial(pick_body, capacity=capacity),
         out_shape=jax.ShapeDtypeStruct((slots,) + template.shape[1:], template.dtype),
         in_specs=[smem(), vmem()],
-        out_specs=vmem(),
+        out_specs=pl.BlockSpec(memory_space=pl.ANY),
+        scratch_shapes=[pltpu.SemaphoreType.DMA((slots,))],
         compiler_params=pltpu.CompilerParams(vmem_limit_bytes=16 * mib),
         name="pick_blocks",
     )(asked, template)
@@ -138,29 +140,39 @@
     return pltpu.roll(tile, lax.rem(height - (top - down), height), 0)
 
 
-def prepare_body(
-    sender, variance, science, asked, earlier, out, asked_out, *, side, exps, capacity
-):
+def hold_body(asked, earlier, out):
+    del earlier
+    out[...] = asked[...]
+
+
+def hold(asked, earlier):
+    return pl.pallas_call(
+        hold_body,
+        out_shape=jax.ShapeDtypeStruct(asked.shape, asked.dtype),
+        in_specs=[vmem(), pl.BlockSpec(memory_space=pl.ANY)],
+        out_specs=vmem(),
+        compiler_params=pltpu.CompilerParams(vmem_limit_bytes=16 * mib),
+        name="hold",
+    )(asked, earlier)
+
+
+def prepare_body(sender, variance, science, earlier, out, *, side, exps, capacity):
     del earlier, science
     store_parts(sender, variance, out, side, exps, capacity, variance.shape[1] // side)
-    asked_out[...] = asked[...]
-
-
-def prepare(sender, variance, science, asked, earlier, side, exps, capacity):
+
+
+def prepare(sender, variance, science, earlier, side, exps, capacity):
     slots = sender.shape[0]
     part = side // exps
     return pl.pallas_call(
         functools.partial(prepare_body, side=side, exps=exps, capacity=capacity),
-        out_shape=(
-            jax.ShapeDtypeStruct((slots // capacity * exps, capacity * part, side), bf16),
-            jax.ShapeDtypeStruct(asked.shape, asked.dtype),
-        ),
-        in_specs=[smem()] + [vmem()] * 3 + [pl.BlockSpec(memory_space=pl.ANY)],
-        out_specs=(vmem(), vmem()),
+        out_shape=jax.ShapeDtypeStruct((slots // capacity * exps, capacity * part, side), bf16),
+        in_specs=[smem()] + [vmem()] * 2 + [pl.BlockSpec(memory_space=pl.ANY)],
+        out_specs=vmem(),
         compiler_params=pltpu.CompilerParams(vmem_limit_bytes=16 * mib),
         cost_estimate=cost(0, 6_000_000),
         name="prepare",
-    )(sender, variance, science, asked, earlier)
+    )(sender, variance, science, earlier)
 
 
 def normal_body(
@@ -295,41 +307,6 @@
     gram_out[...] = part
 
 
-def normal_matrix(
-    slot_of, rows_at, cols_at, arrived, col, row_rev, science, variance, count, taps
-):
-    high, wide = science.shape
-    side = row_rev.shape[1]
-    stamps = rows_at.shape[1]
-    padded_k = up(count + 2, 16)
-    pairs = (taps + 2) // 2
-    span = up(side + taps - 1, 16)
-    half = up(high // 2 + pairs, 8)
-    tall = up(taps // 2, 8) + max(high - side + span, 2 * half)
-    wins = -(-wide // (side - taps + 1))
-    group = next(g for g in (8, 4, 2, 1) if count % g == 0)
-    return pl.pallas_call(
-        functools.partial(normal_body, count=count, across_blocks=wide // side, taps=taps),
-        out_shape=(
-            jax.ShapeDtypeStruct((padded_k, padded_k), f32),
-            jax.ShapeDtypeStruct((wins, 2, half, side), f32),
-        ),
-        in_specs=[smem()] * 3 + [vmem()] * 5,
-        out_specs=(vmem(),) * 2,
-        scratch_shapes=[
-            pltpu.VMEM((tall, wide + 2 * side), f32),
-            pltpu.VMEM((stamps * span, 2 * side), bf16),
-            pltpu.VMEM((group, stamps * side, 2 * side), bf16),
-            pltpu.VMEM((up(stamps * side * ((count + 2) | 1) + padded_k, 8), side), f32),
-            pltpu.VMEM((stamps * side, side), f32),
-            pltpu.VMEM((2 * half, side), f32),
-        ],
-        compiler_params=pltpu.CompilerParams(vmem_limit_bytes=28 * mib),
-        cost_estimate=cost(10_000_000_000, 8_000_000),
-        name="normal_matrix",
-    )(slot_of, rows_at, cols_at, arrived, col, row_rev, science, variance)
-
-
 def subtract_body(
     sender,
     gram,
@@ -460,37 +437,129 @@
     lax.fori_loop(0, payload.shape[0], put, 0, unroll=4)
 
 
-def subtract(
-    sender, gram, frames, science, col_t, row_rev, peers, exps, capacity, count, taps, pixels
+def fit_body(
+    slot_of,
+    sender,
+    rows_at,
+    cols_at,
+    arrived,
+    col,
+    row_rev,
+    science,
+    variance,
+    col_t,
+    coef_out,
+    payload,
+    *scratch,
+    exps,
+    capacity,
+    count,
+    taps,
 ):
-    wins, _, _, side = frames.shape
+    gram, windows = scratch[:2]
+    stamps = rows_at.shape[1]
+    side = row_rev.shape[1]
+    normal_body(
+        slot_of,
+        rows_at,
+        cols_at,
+        arrived,
+        col,
+        row_rev,
+        science,
+        variance,
+        gram,
+        windows,
+        *scratch[2:8],
+        count=count,
+        across_blocks=science.shape[1] // side,
+        taps=taps,
+    )
+    subtract_body(
+        sender,
+        gram,
+        windows,
+        science,
+        col_t,
+        row_rev,
+        coef_out,
+        payload,
+        *scratch[8:],
+        exps=exps,
+        capacity=capacity,
+        count=count,
+        taps=taps,
+        pixels=stamps * side * side,
+    )
+
+
+def fit_and_subtract(
+    slot_of,
+    sender,
+    rows_at,
+    cols_at,
+    arrived,
+    col,
+    row_rev,
+    science,
+    variance,
+    col_t,
+    exps,
+    capacity,
+    count,
+    taps,
+):
     high, wide = science.shape
-    part = side // exps
+    side = row_rev.shape[1]
+    slots = sender.shape[0]
+    stamps = rows_at.shape[1]
+    padded_k = up(count + 2, 16)
     pairs = (taps + 2) // 2
-    body = functools.partial(
-        subtract_body, exps=exps, capacity=capacity, count=count, taps=taps, pixels=pixels
-    )
+    span = up(side + taps - 1, 16)
+    half = up(high // 2 + pairs, 8)
+    tall = up(taps // 2, 8) + max(high - side + span, 2 * half)
+    wins = -(-wide // (side - taps + 1))
+    group = next(g for g in (8, 4, 2, 1) if count % g == 0)
     return pl.pallas_call(
-        body,
+        functools.partial(fit_body, exps=exps, capacity=capacity, count=count, taps=taps),
         out_shape=(
             jax.ShapeDtypeStruct((1, side), f32),
             jax.ShapeDtypeStruct(
-                (peers * exps, capacity * part + trailer_rows, side), bf16
+                (slots // capacity * exps, capacity * side // exps + trailer_rows, side), bf16
             ),
         ),
-        in_specs=[smem()] + [vmem()] * 5,
-        out_specs=(vmem(), vmem()),
+        in_specs=[smem()] * 4 + [vmem()] * 6,
+        out_specs=(vmem(),) * 2,
         scratch_shapes=[
+            pltpu.VMEM((padded_k, padded_k), f32),
+            pltpu.VMEM((wins, 2, half, side), f32),
+            pltpu.VMEM((tall, wide + 2 * side), f32),
+            pltpu.VMEM((stamps * span, 2 * side), bf16),
+            pltpu.VMEM((group, stamps * side, 2 * side), bf16),
+            pltpu.VMEM((up(stamps * side * ((count + 2) | 1) + padded_k, 8), side), f32),
+            pltpu.VMEM((stamps * side, side), f32),
+            pltpu.VMEM((2 * half, side), f32),
             pltpu.VMEM((wins, high, side), f32),
             pltpu.VMEM((high, wide), f32),
             pltpu.VMEM((pairs * 2 * side, 2 * side), bf16),
             pltpu.VMEM((wins * high // 2, 2 * side), f32),
             pltpu.VMEM((pairs, wins * high // 2, 2 * side), bf16),
         ],
-        compiler_params=pltpu.CompilerParams(vmem_limit_bytes=24 * mib),
-        cost_estimate=cost(5_000_000_000, 4_000_000),
-        name="subtract",
-    )(sender, gram, frames, science, col_t, row_rev)
+        compiler_params=pltpu.CompilerParams(vmem_limit_bytes=40 * mib),
+        cost_estimate=cost(15_000_000_000, 8_000_000),
+        name="fit_and_subtract",
+    )(
+        slot_of,
+        sender,
+        rows_at,
+        cols_at,
+        arrived,
+        col,
+        row_rev,
+        science,
+        variance,
+        col_t,
+    )
 
 
 def split2(value):
@@ -699,9 +768,10 @@
     slot_of, sender, request = route_tables(routes_src, routes_blk, peers, capacity)
     asked = lax.all_to_all(request, "det", split_axis=0, concat_axis=0, tiled=True)
     picked = pick_blocks(asked, fetch(template), slots, capacity)
-    var_parts, asked_late = prepare(
-        sender, variance_img, science_img, asked, picked, side, exps, capacity
-    )
+    held = hold(asked, picked)
+    tables = [held] + [from_exposure(held, g, exps) for g in range(1, exps)]
+    table = jnp.stack(tables).reshape(exps, peers, capacity)
+    var_parts = prepare(sender, variance_img, science_img, table, side, exps, capacity)
     arrived = lax.all_to_all(picked, "det", split_axis=0, concat_axis=0, tiled=True)
 
     padded_k = up(count + 2, 16)
@@ -717,12 +787,11 @@
     var_back = lax.all_to_all(
         var_late, ("det", "exp"), split_axis=0, concat_axis=0, tiled=True
     )
-    tables = [asked_late] + [from_exposure(asked_late, g, exps) for g in range(1, exps)]
-    table = jnp.stack(tables).reshape(exps, peers, capacity)
 
     high, wide = science_img.shape
-    gram, frames = normal_matrix(
+    coef, payload = fit_and_subtract(
         slot_of,
+        sender,
         stamp_rows,
         stamp_cols,
         arrived,
@@ -730,22 +799,11 @@
         row_rev,
         science_img,
         variance_img,
-        count,
-        taps,
-    )
-    coef, payload = subtract(
-        sender,
-        gram,
-        frames,
-        science_img,
         col_t,
-        row_rev,
-        peers,
         exps,
         capacity,
         count,
         taps,
-        stamp_rows.shape[1] * side * side,
     )
     diff_back = lax.all_to_all(payload, ("det", "exp"), split_axis=0, concat_axis=0, tiled=True)
     scored, var_sum = score(

time: 89.6 us -> 89.2 us (level)
  starting transfers between devices: 29 us -> 30.3 us
  waiting for transfers between devices: 27.3 us -> 26 us
    all_to_all x1, waiting for transfers between devices: 8.88 us -> 2.6 us  [local(): lax.all_to_all(picked, 'det', split_axis=0, concat_axis=0, tiled=True)]
    all_to_all x1, waiting for transfers between devices: 6.78 us -> 11.5 us  [local(): lax.all_to_all(payload, ('det', 'exp'), split_axis=0, concat_axis=0, tile...]
    ppermute x3, starting transfers between devices: 2.14 us -> 3.7 us  [from_exposure(): return lax.ppermute(value, 'exp', pairs)]
    unnamed x31 -> x29, local copies, waits for them, and re-layouts: 3.99 us -> 3.22 us
  transfers between devices with their start and end apart: 10 -> 10, of which waited for: 6 -> 7; matrix products, arithmetic and copies ran while one was open for 1% -> 1% of each run, Pallas kernels for 24% -> 25%
where the time goes in v7:
time: 89.2 us; the launch traced here: 88.7 us
  starting transfers between devices  30.3 us (34%)
  Pallas kernels  27.1 us (30%)
  waiting for transfers between devices  26 us (29%)
  local copies, waits for them, and re-layouts  4.16 us (5%)
    pallas_call x1, Pallas kernels, fit_and_subtract(): pl.pallas_call(functools.partial(fit_body, exps=exps, capacity=capacity,...  14.9 us
    all_to_all x1, waiting for transfers between devices, local(): lax.all_to_all(payload, ('det', 'exp'), split_axis=0, concat_axis=0, tile...  11.5 us
    all_to_all x1, starting transfers between devices, local(): lax.all_to_all(var_late, ('det', 'exp'), split_axis=0, concat_axis=0, til...  7.88 us
    all_to_all x1, starting transfers between devices, local(): lax.all_to_all(request, 'det', split_axis=0, concat_axis=0, tiled=True)  6.37 us
    ppermute x3, waiting for transfers between devices, swap(): return lax.ppermute(value, 'exp', [(e, e ^ distance) for e in range(exps)])  5.66 us
    all_to_all x1, starting transfers between devices, local(): lax.all_to_all(payload, ('det', 'exp'), split_axis=0, concat_axis=0, tile...  5.54 us
    all_to_all x1, waiting for transfers between devices, local(): lax.all_to_all(request, 'det', split_axis=0, concat_axis=0, tiled=True)  3.89 us
    ppermute x3, starting transfers between devices, from_exposure(): return lax.ppermute(value, 'exp', pairs)  3.7 us
  transfers between devices with their start and end apart: 10, of which 7 were waited for; matrix products, arithmetic and copies ran while one was open for 1% of the time, Pallas kernels for 25%

profile of v7, /device:TPU:1, one launch (start us, length us, event | category | flops | bytes accessed | tf_op | source)
XLA Modules:
  0.0 88.7 jit_solution(9406090091267529577)
XLA Ops:
  0.6 1.5 %route_tables.1 = (s32[16]{0:T(128)}, s32[16]{0:T(128)}, s32[8,1,2]{2,1,0:T(1,128)}) custom-call(s32[1,16]{1,0:T(1,128)} %src.1, s32[1,16]{1,0:T(1,128)} %blk.1), custom_call_target="tpu_custom_call" | custom-call | tf_op jit(solution)/shard_map/route_tables/pallas_call | solution.py:63
  2.2 6.4 %all-to-all-start = ((s32[8,1,2]{2,1,0:T(1,128)}), s32[8,1,2]{2,1,0:T(1,128)S(1)}, u32[]{:S(2)}, u32[]{:S(2)}) async-start(s32[8,1,2]{2,1,0:T(1,128)} %get-tuple-element.12), calls=%async_computation | async-start | bytes 8192 | tf_op jit(solution)/shard_map/all_to_all | solution.py:769
  8.6 1.2 %copy-done.1 = bf16[32,128,128]{2,1,0:T(8,128)(2,1)S(1)} copy-done((bf16[32,128,128]{2,1,0:T(8,128)(2,1)S(1)}, bf16[32,128,128]{2,1,0:T(8,128)(2,1)}, u32[]{:S(2)}) %copy-start.1) | copy-done | bytes 1048600
  9.9 3.9 %all-to-all-done.asked = s32[8,1,2]{2,1,0:T(1,128)S(1)} async-done(((s32[8,1,2]{2,1,0:T(1,128)}), s32[8,1,2]{2,1,0:T(1,128)S(1)}, u32[]{:S(2)}, u32[]{:S(2)}) %all-to-all-start) | async-done | bytes 96 | tf_op jit(solution)/shard_map/all_to_all | solution.py:769
  13.8 1.5 %pick_blocks.1.earlier = bf16[16,128,128]{2,1,0:T(8,128)(2,1)} custom-call(s32[8,1,2]{2,1,0:T(1,128)S(1)} %all-to-all-done.asked, bf16[32,128,128]{2,1,0:T(8,128)(2,1)S(1)} %fetch.1.template), custom_call_target="tpu_custom_call" | custom-call | tf_op jit(solution)/shard_map/pick_blocks/pallas_call | solution.py:107
  15.4 3.6 %all-to-all-start.1 = ((bf16[16,128,128]{2,1,0:T(8,128)(2,1)}), bf16[16,128,128]{2,1,0:T(8,128)(2,1)S(1)}, u32[]{:S(2)}, u32[]{:S(2)}) async-start(bf16[16,128,128]{2,1,0:T(8,128)(2,1)} %pick_blocks.1.earlier), calls=%async_computation.1 | async-start | bytes 1048576 | tf_op jit(solution)/shard_map/all_to_all | solution.py:775
  19.6 3.2 %collective-permute-start.2 = (s32[8,1,2]{2,1,0:T(1,128)S(1)}, s32[8,1,2]{2,1,0:T(1,128)S(1)}, u32[]{:S(2)}, u32[]{:S(2)}) collective-permute-start(s32[8,1,2]{2,1,0:T(1,128)S(1)} %hold.1), channel_id=1, source_target_pairs={{0,3},{1,2},{2,1},{3,0},{4,7},{5,6},{6,5},{7,4},{8,11},{9,10},{10,... | collective-permute-start | bytes 200 | tf_op jit(solution)/shard_map/ppermute | solution.py:38
  23.3 1.1 %collective-permute-done.2 = s32[8,1,2]{2,1,0:T(1,128)S(1)} collective-permute-done((s32[8,1,2]{2,1,0:T(1,128)S(1)}, s32[8,1,2]{2,1,0:T(1,128)S(1)}, u32[]{:S(2)}, u32[]{:S(2)}) %collective-permute-start.2) | collective-permute-done | bytes 96 | tf_op jit(solution)/shard_map/ppermute | solution.py:38
  24.5 1.0 %collective-permute-done.1 = s32[8,1,2]{2,1,0:T(1,128)S(1)} collective-permute-done((s32[8,1,2]{2,1,0:T(1,128)S(1)}, s32[8,1,2]{2,1,0:T(1,128)S(1)}, u32[]{:S(2)}, u32[]{:S(2)}) %collective-permute-start.1) | collective-permute-done | bytes 96 | tf_op jit(solution)/shard_map/ppermute | solution.py:38
  25.8 1.5 %prepare.1 = bf16[32,64,128]{2,1,0:T(8,128)(2,1)} custom-call(s32[16]{0:T(128)S(1)} %copy-done.6, bf16[256,1024]{1,0:T(8,128)(2,1)S(1)} %bitcast.18, bf16[256,1024]{1,0:T(8,128)(2,1)S(1)} %bitcast.16, s32[4,8,2]{2,1,0:T(8,128)S(1)} %copy.35.earlier.table), custom_call_target="tpu_custom_call" | custom-call | bytes 6000000 | tf_op jit(solution)/shard_map/prepare/pallas_call | solution.py:167
  27.3 2.6 %all-to-all-done.1.arrived = bf16[16,128,128]{2,1,0:T(8,128)(2,1)S(1)} async-done(((bf16[16,128,128]{2,1,0:T(8,128)(2,1)}), bf16[16,128,128]{2,1,0:T(8,128)(2,1)S(1)}, u32[]{:S(2)}, u32[]{:S(2)}) %all-to-all-start.1) | async-done | bytes 524320 | tf_op jit(solution)/shard_map/all_to_all | solution.py:775
  29.9 7.9 %all-to-all-start.3 = ((bf16[32,64,128]{2,1,0:T(8,128)(2,1)}), bf16[32,64,128]{2,1,0:T(8,128)(2,1)S(1)}, u32[]{:S(2)}, u32[]{:S(2)}) async-start(bf16[32,64,128]{2,1,0:T(8,128)(2,1)} %prepare.1), calls=%async_computation.3 | async-start | bytes 1048576 | tf_op jit(solution)/shard_map/all_to_all | solution.py:787
  37.9 14.9 %fit_and_subtract.1 = (f32[1,128]{1,0:T(1,128)}, bf16[32,72,128]{2,1,0:T(8,128)(2,1)}) custom-call(s32[16]{0:T(128)S(1)} %copy-done.9, s32[16]{0:T(128)S(1)} %copy-done.6, s32[1,4]{1,0:T(1,128)S(1)} %copy-done.7, s32[1,4]{1,0:T(1,128)S(1)} %copy-done.8, bf16[16,128,128]{2,1,0:T(8,128)(2,1)S(1)} %all-to-all-done.1.arrived, ...), custom_call_target="tpu_custom_call" | custom-call | flops 15000000512 | bytes 8000000 | tf_op jit(solution)/shard_map/fit_and_subtract/pallas_call | solution.py:523
  53.0 0.8 copy-done.4
  53.8 5.5 %all-to-all-start.2 = ((bf16[32,72,128]{2,1,0:T(8,128)(2,1)}), bf16[32,72,128]{2,1,0:T(8,128)(2,1)S(1)}, u32[]{:S(2)}, u32[]{:S(2)}) async-start(bf16[32,72,128]{2,1,0:T(8,128)(2,1)} %get-tuple-element.16.payload), calls=%async_computation.2 | async-start | bytes 1179648 | tf_op jit(solution)/shard_map/all_to_all | solution.py:808
  59.7 1.0 %copy-done.5 = bf16[32,64,128]{2,1,0:T(8,128)(2,1)S(1)} copy-done((bf16[32,64,128]{2,1,0:T(8,128)(2,1)S(1)}, bf16[32,64,128]{2,1,0:T(8,128)(2,1)}, u32[]{:S(2)}) %copy-start.5) | copy-done | bytes 524312
  60.7 3.6 %score.1 = (f32[256,1024]{1,0:T(8,128)}, f32[32,32,128]{2,1,0:T(8,128)S(1)}) custom-call(s32[1]{0:T(128)} %bitcast.1.me, s32[4,8,2]{2,1,0:T(8,128)S(1)} %copy.35.earlier.table, s32[16]{0:T(128)S(1)} %copy-done.9, bf16[32,72,128]{2,1,0:T(8,128)(2,1)} %get-tuple-element.16.payload, f32[1,256]{1,0:T(1,128)S(1)} %pad.26.down, ...), custom_call_target="tpu_custom_call" | custom-call | flops 2000000000 | bytes 2000000 | tf_op jit(solution)/shard_map/score/pallas_call | solution.py:628
  64.3 11.5 %all-to-all-done.2.parts = bf16[32,72,128]{2,1,0:T(8,128)(2,1)S(1)} async-done(((bf16[32,72,128]{2,1,0:T(8,128)(2,1)}), bf16[32,72,128]{2,1,0:T(8,128)(2,1)S(1)}, u32[]{:S(2)}, u32[]{:S(2)}) %all-to-all-start.2) | async-done | bytes 589856 | tf_op jit(solution)/shard_map/all_to_all | solution.py:808
  75.8 1.4 %combine.1.refs_0_ = bf16[32,32,128]{2,1,0:T(8,128)(2,1)S(1)} custom-call(s32[1]{0:T(128)} %bitcast.1.me, s32[4,8,2]{2,1,0:T(8,128)S(1)} %copy.35.earlier.table, bf16[32,72,128]{2,1,0:T(8,128)(2,1)S(1)} %all-to-all-done.2.parts, f32[32,32,128]{2,1,0:T(8,128)S(1)} %get-tuple-element.18.var_sum, bf16[32,32,128]{2,1,0:T(8,128)(2,1)S(1)} %constant_dynamic-slice_fusion.var_template), custom_call_target="tpu_custom_call" | custom-call | tf_op jit(solution)/shard_map/combine/pallas_call | solution.py:692
  77.2 1.3 %collective-permute-start.3 = (bf16[32,32,128]{2,1,0:T(8,128)(2,1)S(1)}, bf16[32,32,128]{2,1,0:T(8,128)(2,1)S(1)}, u32[]{:S(2)}, u32[]{:S(2)}) collective-permute-start(bf16[32,32,128]{2,1,0:T(8,128)(2,1)S(1)} %combine.1.refs_0_), channel_id=1, source_target_pairs={{0,2},{1,3},{2,0},{3,1},{4,6},{5,7},{6,4},{7,5},{8,10},{9,11},{10,... | collective-permute-start | bytes 786440 | tf_op jit(solution)/shard_map/ppermute | solution.py:828
  79.0 5.7 %collective-permute-done.3.refs_2_ = bf16[32,32,128]{2,1,0:T(8,128)(2,1)S(1)} collective-permute-done((bf16[32,32,128]{2,1,0:T(8,128)(2,1)S(1)}, bf16[32,32,128]{2,1,0:T(8,128)(2,1)S(1)}, u32[]{:S(2)}, u32[]{:S(2)}) %collective-permute-start.3) | collective-permute-done | bytes 262176 | tf_op jit(solution)/shard_map/ppermute | solution.py:828
  84.6 1.4 %collective-permute-start.4 = (bf16[32,32,128]{2,1,0:T(8,128)(2,1)S(1)}, bf16[32,32,128]{2,1,0:T(8,128)(2,1)S(1)}, u32[]{:S(2)}, u32[]{:S(2)}) collective-permute-start(bf16[32,32,128]{2,1,0:T(8,128)(2,1)S(1)} %collective-permute-done.3.refs_2_), channel_id=1, source_target_pairs={{0,1},{1,0},{2,3},{3,2},{4,5},{5,4},{6,7},{7,6},{8,9},{9,8},{10,11... | collective-permute-start | bytes 786440 | tf_op jit(solution)/shard_map/ppermute | solution.py:828
  86.1 1.7 %join_parts.2.refs_1_ = f32[32,128,128]{2,1,0:T(8,128)} custom-call(s32[3]{0:T(128)S(1)} %pad_add_fusion.places, bf16[32,32,128]{2,1,0:T(8,128)(2,1)S(1)} %combine.1.refs_0_, bf16[32,32,128]{2,1,0:T(8,128)(2,1)S(1)} %collective-permute-done.5.refs_1_, bf16[32,32,128]{2,1,0:T(8,128)(2,1)S(1)} %collective-permute-done.3.refs_2_), custom_call_target="tpu_custom_call" | custom-call | bytes 9000000 | tf_op jit(solution)/shard_map/join_parts/pallas_call | solution.py:726
  87.8 0.8 join_parts.3
  (54 shorter events, 2.7 us)
Async XLA Ops:
  0.6 59.0 %copy-start = (bf16[32,128,128]{2,1,0:T(8,128)(2,1)S(1)}, bf16[32,128,128]{2,1,0:T(8,128)(2,1)}, u32[]{:S(2)}) copy-start(bf16[32,128,128]{2,1,0:T(8,128)(2,1)} %param.13) | copy-start | bytes 3145732
  2.2 11.6 %all-to-all-start = ((s32[8,1,2]{2,1,0:T(1,128)}), s32[8,1,2]{2,1,0:T(1,128)S(1)}, u32[]{:S(2)}, u32[]{:S(2)}) async-start(s32[8,1,2]{2,1,0:T(1,128)} %get-tuple-element.12), calls=%async_computation | async-start | bytes 8192 | tf_op jit(solution)/shard_map/all_to_all | solution.py:769
  8.6 1.2 %copy-start.1 = (bf16[32,128,128]{2,1,0:T(8,128)(2,1)S(1)}, bf16[32,128,128]{2,1,0:T(8,128)(2,1)}, u32[]{:S(2)}) copy-start(bf16[32,128,128]{2,1,0:T(8,128)(2,1)} %template.1) | copy-start | bytes 3145732
  9.8 9.2 %copy-start.10 = (bf16[40,21]{0,1:T(8,128)(2,1)S(1)}, bf16[40,21]{0,1:T(8,128)(2,1)}, u32[]{:S(2)}) copy-start(bf16[40,21]{0,1:T(8,128)(2,1)} %param.20) | copy-start | bytes 5044
  9.8 9.3 %copy-start.11 = (bf16[40,21]{0,1:T(8,128)(2,1)S(1)}, bf16[40,21]{0,1:T(8,128)(2,1)}, u32[]{:S(2)}) copy-start(bf16[40,21]{0,1:T(8,128)(2,1)} %param.21) | copy-start | bytes 5044
  9.9 15.9 %copy-start.2 = (bf16[1,256,1024]{2,1,0:T(8,128)(2,1)S(1)}, bf16[1,256,1024]{2,1,0:T(8,128)(2,1)}, u32[]{:S(2)}) copy-start(bf16[1,256,1024]{2,1,0:T(8,128)(2,1)} %param.14) | copy-start | bytes 1572868
  9.9 15.9 %copy-start.3 = (bf16[1,256,1024]{2,1,0:T(8,128)(2,1)S(1)}, bf16[1,256,1024]{2,1,0:T(8,128)(2,1)}, u32[]{:S(2)}) copy-start(bf16[1,256,1024]{2,1,0:T(8,128)(2,1)} %param.15) | copy-start | bytes 1572868
  9.9 15.9 %copy-start.6 = (s32[16]{0:T(128)S(1)}, s32[16]{0:T(128)}, u32[]{:S(2)}) copy-start(s32[16]{0:T(128)} %get-tuple-element.14.sender) | copy-start | bytes 196
  15.3 22.5 %copy-start.7 = (s32[1,4]{1,0:T(1,128)S(1)}, s32[1,4]{1,0:T(1,128)}, u32[]{:S(2)}) copy-start(s32[1,4]{1,0:T(1,128)} %rows_at.1) | copy-start | bytes 52
  15.3 22.5 %copy-start.8 = (s32[1,4]{1,0:T(1,128)S(1)}, s32[1,4]{1,0:T(1,128)}, u32[]{:S(2)}) copy-start(s32[1,4]{1,0:T(1,128)} %cols_at.1) | copy-start | bytes 52
  15.3 22.5 %copy-start.9 = (s32[16]{0:T(128)S(1)}, s32[16]{0:T(128)}, u32[]{:S(2)}) copy-start(s32[16]{0:T(128)} %get-tuple-element.13.slot_of) | copy-start | bytes 196
  15.4 14.6 %all-to-all-start.1 = ((bf16[16,128,128]{2,1,0:T(8,128)(2,1)}), bf16[16,128,128]{2,1,0:T(8,128)(2,1)S(1)}, u32[]{:S(2)}, u32[]{:S(2)}) async-start(bf16[16,128,128]{2,1,0:T(8,128)(2,1)} %pick_blocks.1.earlier), calls=%async_computation.1 | async-start | bytes 1048576 | tf_op jit(solution)/shard_map/all_to_all | solution.py:775
  19.6 4.8 %collective-permute-start.2 = (s32[8,1,2]{2,1,0:T(1,128)S(1)}, s32[8,1,2]{2,1,0:T(1,128)S(1)}, u32[]{:S(2)}, u32[]{:S(2)}) collective-permute-start(s32[8,1,2]{2,1,0:T(1,128)S(1)} %hold.1), channel_id=1, source_target_pairs={{0,3},{1,2},{2,1},{3,0},{4,7},{5,6},{6,5},{7,4},{8,11},{9,10},{10,... | collective-permute-start | bytes 200 | tf_op jit(solution)/shard_map/ppermute | solution.py:38
  22.9 2.7 %collective-permute-start.1 = (s32[8,1,2]{2,1,0:T(1,128)S(1)}, s32[8,1,2]{2,1,0:T(1,128)S(1)}, u32[]{:S(2)}, u32[]{:S(2)}) collective-permute-start(s32[8,1,2]{2,1,0:T(1,128)S(1)} %hold.1), channel_id=1, source_target_pairs={{0,2},{1,3},{2,0},{3,1},{4,6},{5,7},{6,4},{7,5},{8,10},{9,11},{10,... | collective-permute-start | bytes 200 | tf_op jit(solution)/shard_map/ppermute | solution.py:38
  23.1 2.5 %collective-permute-start = (s32[8,1,2]{2,1,0:T(1,128)S(1)}, s32[8,1,2]{2,1,0:T(1,128)S(1)}, u32[]{:S(2)}, u32[]{:S(2)}) collective-permute-start(s32[8,1,2]{2,1,0:T(1,128)S(1)} %hold.1), channel_id=1, source_target_pairs={{0,1},{1,0},{2,3},{3,2},{4,5},{5,4},{6,7},{7,6},{8,9},{9,8},{10,11... | collective-permute-start | bytes 200 | tf_op jit(solution)/shard_map/ppermute | solution.py:38
  29.9 23.1 %all-to-all-start.3 = ((bf16[32,64,128]{2,1,0:T(8,128)(2,1)}), bf16[32,64,128]{2,1,0:T(8,128)(2,1)S(1)}, u32[]{:S(2)}, u32[]{:S(2)}) async-start(bf16[32,64,128]{2,1,0:T(8,128)(2,1)} %prepare.1), calls=%async_computation.3 | async-start | bytes 1048576 | tf_op jit(solution)/shard_map/all_to_all | solution.py:787
  37.9 21.5 %copy-start.12 = (f32[1,21]{1,0:T(1,128)S(1)}, f32[1,21]{1,0:T(1,128)}, u32[]{:S(2)}) copy-start(f32[1,21]{1,0:T(1,128)} %param.23) | copy-start | bytes 256
  37.9 21.6 %copy-start.13 = (f32[1,21]{1,0:T(1,128)S(1)}, f32[1,21]{1,0:T(1,128)}, u32[]{:S(2)}) copy-start(f32[1,21]{1,0:T(1,128)} %param.22) | copy-start | bytes 256
  53.0 0.8 copy-start.4
  53.8 22.0 %all-to-all-start.2 = ((bf16[32,72,128]{2,1,0:T(8,128)(2,1)}), bf16[32,72,128]{2,1,0:T(8,128)(2,1)S(1)}, u32[]{:S(2)}, u32[]{:S(2)}) async-start(bf16[32,72,128]{2,1,0:T(8,128)(2,1)} %get-tuple-element.16.payload), calls=%async_computation.2 | async-start | bytes 1179648 | tf_op jit(solution)/shard_map/all_to_all | solution.py:808
  59.7 1.0 %copy-start.5 = (bf16[32,64,128]{2,1,0:T(8,128)(2,1)S(1)}, bf16[32,64,128]{2,1,0:T(8,128)(2,1)}, u32[]{:S(2)}) copy-start(bf16[32,64,128]{2,1,0:T(8,128)(2,1)} %copy-done.4) | copy-start | bytes 1572868
  77.2 7.4 %collective-permute-start.3 = (bf16[32,32,128]{2,1,0:T(8,128)(2,1)S(1)}, bf16[32,32,128]{2,1,0:T(8,128)(2,1)S(1)}, u32[]{:S(2)}, u32[]{:S(2)}) collective-permute-start(bf16[32,32,128]{2,1,0:T(8,128)(2,1)S(1)} %combine.1.refs_0_), channel_id=1, source_target_pairs={{0,2},{1,3},{2,0},{3,1},{4,6},{5,7},{6,4},{7,5},{8,10},{9,11},{10,... | collective-permute-start | bytes 786440 | tf_op jit(solution)/shard_map/ppermute | solution.py:828
  78.5 7.6 %collective-permute-start.5 = (bf16[32,32,128]{2,1,0:T(8,128)(2,1)S(1)}, bf16[32,32,128]{2,1,0:T(8,128)(2,1)S(1)}, u32[]{:S(2)}, u32[]{:S(2)}) collective-permute-start(bf16[32,32,128]{2,1,0:T(8,128)(2,1)S(1)} %combine.1.refs_0_), channel_id=1, source_target_pairs={{0,1},{1,0},{2,3},{3,2},{4,5},{5,4},{6,7},{7,6},{8,9},{9,8},{10,11... | collective-permute-start | bytes 786440 | tf_op jit(solution)/shard_map/ppermute | solution.py:828
  84.6 3.2 %collective-permute-start.4 = (bf16[32,32,128]{2,1,0:T(8,128)(2,1)S(1)}, bf16[32,32,128]{2,1,0:T(8,128)(2,1)S(1)}, u32[]{:S(2)}, u32[]{:S(2)}) collective-permute-start(bf16[32,32,128]{2,1,0:T(8,128)(2,1)S(1)} %collective-permute-done.3.refs_2_), channel_id=1, source_target_pairs={{0,1},{1,0},{2,3},{3,2},{4,5},{5,4},{6,7},{7,6},{8,9},{9,8},{10,11... | collective-permute-start | bytes 786440 | tf_op jit(solution)/shard_map/ppermute | solution.py:828

commit v8 on v7

--- a/solution.py
+++ b/solution.py
@@ -320,7 +320,6 @@
     image,
     bands,
     total,
-    stacked,
     *,
     exps,
     capacity,
@@ -346,17 +345,7 @@
     rows_half = high // 2
     wins = frames.shape[0]
 
-    def stack_rows(q):
-        for c in range(wins):
-            for a in range(2):
-                stacked[q, c * rows_half : (c + 1) * rows_half, a * side : (a + 1) * side] = (
-                    frames[c, a, q : q + rows_half, :].astype(bf16)
-                )
-
-    starts = list(range(0, size, 8))
-    for step, k in enumerate(starts):
-        for q in range(step, pairs, len(starts)):
-            stack_rows(q)
+    for k in range(0, size, 8):
         block = range(min(8, size - k))
         cols = [jnp.broadcast_to(system[:, k + j : k + j + 1], system.shape) for j in block]
         rows = [system[k + j : k + j + 1, :] for j in block]
@@ -405,8 +394,17 @@
 
     step = side - taps + 1
     for q in range(pairs):
+        lhs = jnp.concatenate(
+            [
+                jnp.concatenate(
+                    [frames[c, a, q : q + rows_half, :].astype(bf16) for a in range(2)], axis=1
+                )
+                for c in range(wins)
+            ],
+            axis=0,
+        )
         out = jnp.dot(
-            stacked[q], bands[q * 2 * side : (q + 1) * 2 * side, :], preferred_element_type=f32
+            lhs, bands[q * 2 * side : (q + 1) * 2 * side, :], preferred_element_type=f32
         )
         if q:
             out = out + total[...]
@@ -543,9 +541,8 @@
             pltpu.VMEM((high, wide), f32),
             pltpu.VMEM((pairs * 2 * side, 2 * side), bf16),
             pltpu.VMEM((wins * high // 2, 2 * side), f32),
-            pltpu.VMEM((pairs, wins * high // 2, 2 * side), bf16),
         ],
-        compiler_params=pltpu.CompilerParams(vmem_limit_bytes=40 * mib),
+        compiler_params=pltpu.CompilerParams(vmem_limit_bytes=30 * mib),
         cost_estimate=cost(15_000_000_000, 8_000_000),
         name="fit_and_subtract",
     )(
@@ -575,17 +572,23 @@
     down,
     over,
     parts,
+    template_var,
     out,
     var_out,
+    var_template,
     padded,
     sideways,
     var_total,
+    sem,
     *,
     side,
     taps,
     part,
     capacity,
 ):
+    mine = pl.ds(pl.multiple_of(me[0] * part, part), part)
+    copy = pltpu.make_async_copy(template_var.at[:, mine, :], var_template, sem)
+    copy.start()
     add_variance(me, table, parts, var_out, var_total, part, capacity)
     high, wide = out.shape
     margin = taps // 2
@@ -618,30 +621,34 @@
         got = got + jnp.dot(top, data_low, preferred_element_type=f32)
         got = got + jnp.dot(low, data_top, preferred_element_type=f32)
         out[r * side : (r + 1) * side, :] = got
+    copy.wait()
 
 
 def score(
-    me, table, slot_of, payload, down, over_rev, parts, high, wide, taps, tract, part, capacity
+    me, table, slot_of, payload, down, over_rev, parts, template_var, high, wide, taps, capacity
 ):
-    side = payload.shape[2]
+    tract, side, _ = template_var.shape
+    part = parts.shape[1] // capacity
     span = up(side + taps - 1, 16)
     return pl.pallas_call(
         functools.partial(score_body, side=side, taps=taps, part=part, capacity=capacity),
         out_shape=(
             jax.ShapeDtypeStruct((high, wide), f32),
             jax.ShapeDtypeStruct((tract, part, side), f32),
+            jax.ShapeDtypeStruct((tract, part, side), template_var.dtype),
         ),
-        in_specs=[smem()] * 3 + [vmem()] * 4,
-        out_specs=(vmem(),) * 2,
+        in_specs=[smem()] * 3 + [vmem()] * 4 + [pl.BlockSpec(memory_space=pl.ANY)],
+        out_specs=(vmem(),) * 3,
         scratch_shapes=[
             pltpu.VMEM((high, wide + side), f32),
             pltpu.VMEM((high - side + span, wide), f32),
             pltpu.VMEM((tract + 1, part, side), f32),
+            pltpu.SemaphoreType.DMA(()),
         ],
-        compiler_params=pltpu.CompilerParams(vmem_limit_bytes=24 * mib),
+        compiler_params=pltpu.CompilerParams(vmem_limit_bytes=20 * mib),
         cost_estimate=cost(2_000_000_000, 2_000_000),
         name="score",
-    )(me, table, slot_of, payload, down, over_rev, parts)
+    )(me, table, slot_of, payload, down, over_rev, parts, template_var)
 
 
 def wanted_block(me, table, d, c, tract):
@@ -806,7 +813,7 @@
         taps,
     )
     diff_back = lax.all_to_all(payload, ("det", "exp"), split_axis=0, concat_axis=0, tiled=True)
-    scored, var_sum = score(
+    scored, var_sum, var_template = score(
         me[None],
         table,
         slot_of,
@@ -814,14 +821,12 @@
         down,
         over_rev,
         var_back,
+        template_var,
         high,
         wide,
         taps,
-        tract,
-        part,
         capacity,
     )
-    var_template = lax.dynamic_slice_in_dim(template_var, me * part, part, 1)
     mine = combine(me[None], table, diff_back, var_sum, var_template, part, capacity)
 
     def swap(value, distance):

time: 89.2 us -> 88.2 us (0.989)
    unnamed x29 -> x25, local copies, waits for them, and re-layouts: 3.22 us -> 2.6 us
where the time goes in v8:
time: 88.2 us; the launch traced here: 87.7 us
  starting transfers between devices  30.2 us (34%)
  Pallas kernels  26.9 us (30%)
  waiting for transfers between devices  25.9 us (29%)
  local copies, waits for them, and re-layouts  3.53 us (4%)
    pallas_call x1, Pallas kernels, fit_and_subtract(): pl.pallas_call(functools.partial(fit_body, exps=exps, capacity=capacity,...  14.8 us
    all_to_all x1, waiting for transfers between devices, local(): lax.all_to_all(payload, ('det', 'exp'), split_axis=0, concat_axis=0, tile...  11.3 us
    all_to_all x1, starting transfers between devices, local(): lax.all_to_all(var_late, ('det', 'exp'), split_axis=0, concat_axis=0, til...  7.88 us
    all_to_all x1, starting transfers between devices, local(): lax.all_to_all(request, 'det', split_axis=0, concat_axis=0, tiled=True)  6.37 us
    ppermute x3, waiting for transfers between devices, swap(): return lax.ppermute(value, 'exp', [(e, e ^ distance) for e in range(exps)])  5.66 us
    all_to_all x1, starting transfers between devices, local(): lax.all_to_all(payload, ('det', 'exp'), split_axis=0, concat_axis=0, tile...  5.47 us
    all_to_all x1, waiting for transfers between devices, local(): lax.all_to_all(request, 'det', split_axis=0, concat_axis=0, tiled=True)  3.89 us
    ppermute x3, starting transfers between devices, from_exposure(): return lax.ppermute(value, 'exp', pairs)  3.7 us
  transfers between devices with their start and end apart: 10, of which 7 were waited for; matrix products, arithmetic and copies ran while one was open for 1% of the time, Pallas kernels for 25%

profile of v8, /device:TPU:1, one launch (start us, length us, event | category | flops | bytes accessed | tf_op | source)
XLA Modules:
  0.0 87.7 jit_solution(3636391164678038327)
XLA Ops:
  0.6 1.4 %route_tables.1 = (s32[16]{0:T(128)}, s32[16]{0:T(128)}, s32[8,1,2]{2,1,0:T(1,128)}) custom-call(s32[1,16]{1,0:T(1,128)} %src.1, s32[1,16]{1,0:T(1,128)} %blk.1), custom_call_target="tpu_custom_call" | custom-call | tf_op jit(solution)/shard_map/route_tables/pallas_call | solution.py:63
  2.0 6.4 %all-to-all-start = ((s32[8,1,2]{2,1,0:T(1,128)}), s32[8,1,2]{2,1,0:T(1,128)S(1)}, u32[]{:S(2)}, u32[]{:S(2)}) async-start(s32[8,1,2]{2,1,0:T(1,128)} %get-tuple-element.13), calls=%async_computation | async-start | bytes 8192 | tf_op jit(solution)/shard_map/all_to_all | solution.py:776
  8.4 1.2 %copy-done = bf16[32,128,128]{2,1,0:T(8,128)(2,1)S(1)} copy-done((bf16[32,128,128]{2,1,0:T(8,128)(2,1)S(1)}, bf16[32,128,128]{2,1,0:T(8,128)(2,1)}, u32[]{:S(2)}) %copy-start) | copy-done | bytes 1048600
  9.8 3.9 %all-to-all-done.asked = s32[8,1,2]{2,1,0:T(1,128)S(1)} async-done(((s32[8,1,2]{2,1,0:T(1,128)}), s32[8,1,2]{2,1,0:T(1,128)S(1)}, u32[]{:S(2)}, u32[]{:S(2)}) %all-to-all-start) | async-done | bytes 96 | tf_op jit(solution)/shard_map/all_to_all | solution.py:776
  13.6 1.5 %pick_blocks.1.earlier = bf16[16,128,128]{2,1,0:T(8,128)(2,1)} custom-call(s32[8,1,2]{2,1,0:T(1,128)S(1)} %all-to-all-done.asked, bf16[32,128,128]{2,1,0:T(8,128)(2,1)S(1)} %fetch.1.template), custom_call_target="tpu_custom_call" | custom-call | tf_op jit(solution)/shard_map/pick_blocks/pallas_call | solution.py:107
  15.2 3.6 %all-to-all-start.1 = ((bf16[16,128,128]{2,1,0:T(8,128)(2,1)}), bf16[16,128,128]{2,1,0:T(8,128)(2,1)S(1)}, u32[]{:S(2)}, u32[]{:S(2)}) async-start(bf16[16,128,128]{2,1,0:T(8,128)(2,1)} %pick_blocks.1.earlier), calls=%async_computation.1 | async-start | bytes 1048576 | tf_op jit(solution)/shard_map/all_to_all | solution.py:782
  19.5 3.2 %collective-permute-start.2 = (s32[8,1,2]{2,1,0:T(1,128)S(1)}, s32[8,1,2]{2,1,0:T(1,128)S(1)}, u32[]{:S(2)}, u32[]{:S(2)}) collective-permute-start(s32[8,1,2]{2,1,0:T(1,128)S(1)} %hold.1), channel_id=1, source_target_pairs={{0,3},{1,2},{2,1},{3,0},{4,7},{5,6},{6,5},{7,4},{8,11},{9,10},{10,... | collective-permute-start | bytes 200 | tf_op jit(solution)/shard_map/ppermute | solution.py:38
  23.2 1.1 %collective-permute-done.2 = s32[8,1,2]{2,1,0:T(1,128)S(1)} collective-permute-done((s32[8,1,2]{2,1,0:T(1,128)S(1)}, s32[8,1,2]{2,1,0:T(1,128)S(1)}, u32[]{:S(2)}, u32[]{:S(2)}) %collective-permute-start.2) | collective-permute-done | bytes 96 | tf_op jit(solution)/shard_map/ppermute | solution.py:38
  24.4 1.0 %collective-permute-done.1 = s32[8,1,2]{2,1,0:T(1,128)S(1)} collective-permute-done((s32[8,1,2]{2,1,0:T(1,128)S(1)}, s32[8,1,2]{2,1,0:T(1,128)S(1)}, u32[]{:S(2)}, u32[]{:S(2)}) %collective-permute-start.1) | collective-permute-done | bytes 96 | tf_op jit(solution)/shard_map/ppermute | solution.py:38
  25.7 1.5 %prepare.1 = bf16[32,64,128]{2,1,0:T(8,128)(2,1)} custom-call(s32[16]{0:T(128)S(1)} %copy-done.3, bf16[256,1024]{1,0:T(8,128)(2,1)S(1)} %bitcast.18, bf16[256,1024]{1,0:T(8,128)(2,1)S(1)} %bitcast.16, s32[4,8,2]{2,1,0:T(8,128)S(1)} %copy.35.earlier.table), custom_call_target="tpu_custom_call" | custom-call | bytes 6000000 | tf_op jit(solution)/shard_map/prepare/pallas_call | solution.py:167
  27.2 2.6 %all-to-all-done.1.arrived = bf16[16,128,128]{2,1,0:T(8,128)(2,1)S(1)} async-done(((bf16[16,128,128]{2,1,0:T(8,128)(2,1)}), bf16[16,128,128]{2,1,0:T(8,128)(2,1)S(1)}, u32[]{:S(2)}, u32[]{:S(2)}) %all-to-all-start.1) | async-done | bytes 524320 | tf_op jit(solution)/shard_map/all_to_all | solution.py:782
  29.8 7.9 %all-to-all-start.3 = ((bf16[32,64,128]{2,1,0:T(8,128)(2,1)}), bf16[32,64,128]{2,1,0:T(8,128)(2,1)S(1)}, u32[]{:S(2)}, u32[]{:S(2)}) async-start(bf16[32,64,128]{2,1,0:T(8,128)(2,1)} %prepare.1), calls=%async_computation.3 | async-start | bytes 1048576 | tf_op jit(solution)/shard_map/all_to_all | solution.py:794
  37.7 14.8 %fit_and_subtract.1 = (f32[1,128]{1,0:T(1,128)}, bf16[32,72,128]{2,1,0:T(8,128)(2,1)}) custom-call(s32[16]{0:T(128)S(1)} %copy-done.7, s32[16]{0:T(128)S(1)} %copy-done.3, s32[1,4]{1,0:T(1,128)S(1)} %copy-done.5, s32[1,4]{1,0:T(1,128)S(1)} %copy-done.6, bf16[16,128,128]{2,1,0:T(8,128)(2,1)S(1)} %all-to-all-done.1.arrived, ...), custom_call_target="tpu_custom_call" | custom-call | flops 15000000512 | bytes 8000000 | tf_op jit(solution)/shard_map/fit_and_subtract/pallas_call | solution.py:521
  52.9 5.5 %all-to-all-start.2 = ((bf16[32,72,128]{2,1,0:T(8,128)(2,1)}), bf16[32,72,128]{2,1,0:T(8,128)(2,1)S(1)}, u32[]{:S(2)}, u32[]{:S(2)}) async-start(bf16[32,72,128]{2,1,0:T(8,128)(2,1)} %get-tuple-element.17.payload), calls=%async_computation.2 | async-start | bytes 1179648 | tf_op jit(solution)/shard_map/all_to_all | solution.py:815
  58.6 1.2 %copy-done.4 = bf16[32,128,128]{2,1,0:T(8,128)(2,1)S(1)} copy-done((bf16[32,128,128]{2,1,0:T(8,128)(2,1)S(1)}, bf16[32,128,128]{2,1,0:T(8,128)(2,1)}, u32[]{:S(2)}) %copy-start.4) | copy-done | bytes 1048600
  59.9 3.7 %score.1 = (f32[256,1024]{1,0:T(8,128)}, f32[32,32,128]{2,1,0:T(8,128)S(1)}, bf16[32,32,128]{2,1,0:T(8,128)(2,1)S(1)}) custom-call(s32[1]{0:T(128)} %bitcast.1.me, s32[4,8,2]{2,1,0:T(8,128)S(1)} %copy.35.earlier.table, s32[16]{0:T(128)S(1)} %copy-done.7, bf16[32,72,128]{2,1,0:T(8,128)(2,1)} %get-tuple-element.17.payload, f32[1,256]{1,0:T(1,128)S(1)} %pad.26.down, ...), custom_call_target="tpu_custom_call" | custom-call | flops 2000000000 | bytes 2000000 | tf_op jit(solution)/shard_map/score/pallas_call | solution.py:633
  63.5 11.3 %all-to-all-done.2.parts = bf16[32,72,128]{2,1,0:T(8,128)(2,1)S(1)} async-done(((bf16[32,72,128]{2,1,0:T(8,128)(2,1)}), bf16[32,72,128]{2,1,0:T(8,128)(2,1)S(1)}, u32[]{:S(2)}, u32[]{:S(2)}) %all-to-all-start.2) | async-done | bytes 589856 | tf_op jit(solution)/shard_map/all_to_all | solution.py:815
  74.8 1.4 %combine.1.refs_0_ = bf16[32,32,128]{2,1,0:T(8,128)(2,1)S(1)} custom-call(s32[1]{0:T(128)} %bitcast.1.me, s32[4,8,2]{2,1,0:T(8,128)S(1)} %copy.35.earlier.table, bf16[32,72,128]{2,1,0:T(8,128)(2,1)S(1)} %all-to-all-done.2.parts, f32[32,32,128]{2,1,0:T(8,128)S(1)} %get-tuple-element.19.var_sum, bf16[32,32,128]{2,1,0:T(8,128)(2,1)S(1)} %get-tuple-element.20.var_template), custom_call_target="tpu_custom_call" | custom-call | tf_op jit(solution)/shard_map/combine/pallas_call | solution.py:699
  76.2 1.3 %collective-permute-start.3 = (bf16[32,32,128]{2,1,0:T(8,128)(2,1)S(1)}, bf16[32,32,128]{2,1,0:T(8,128)(2,1)S(1)}, u32[]{:S(2)}, u32[]{:S(2)}) collective-permute-start(bf16[32,32,128]{2,1,0:T(8,128)(2,1)S(1)} %combine.1.refs_0_), channel_id=1, source_target_pairs={{0,2},{1,3},{2,0},{3,1},{4,6},{5,7},{6,4},{7,5},{8,10},{9,11},{10,... | collective-permute-start | bytes 786440 | tf_op jit(solution)/shard_map/ppermute | solution.py:833
  77.5 0.4 collective-permute-start.5
  77.9 5.7 %collective-permute-done.3.refs_2_ = bf16[32,32,128]{2,1,0:T(8,128)(2,1)S(1)} collective-permute-done((bf16[32,32,128]{2,1,0:T(8,128)(2,1)S(1)}, bf16[32,32,128]{2,1,0:T(8,128)(2,1)S(1)}, u32[]{:S(2)}, u32[]{:S(2)}) %collective-permute-start.3) | collective-permute-done | bytes 262176 | tf_op jit(solution)/shard_map/ppermute | solution.py:833
  83.6 1.4 %collective-permute-start.4 = (bf16[32,32,128]{2,1,0:T(8,128)(2,1)S(1)}, bf16[32,32,128]{2,1,0:T(8,128)(2,1)S(1)}, u32[]{:S(2)}, u32[]{:S(2)}) collective-permute-start(bf16[32,32,128]{2,1,0:T(8,128)(2,1)S(1)} %collective-permute-done.3.refs_2_), channel_id=1, source_target_pairs={{0,1},{1,0},{2,3},{3,2},{4,5},{5,4},{6,7},{7,6},{8,9},{9,8},{10,11... | collective-permute-start | bytes 786440 | tf_op jit(solution)/shard_map/ppermute | solution.py:833
  85.1 1.7 %join_parts.2.refs_1_ = f32[32,128,128]{2,1,0:T(8,128)} custom-call(s32[3]{0:T(128)S(1)} %pad_add_fusion.places, bf16[32,32,128]{2,1,0:T(8,128)(2,1)S(1)} %combine.1.refs_0_, bf16[32,32,128]{2,1,0:T(8,128)(2,1)S(1)} %collective-permute-done.5.refs_1_, bf16[32,32,128]{2,1,0:T(8,128)(2,1)S(1)} %collective-permute-done.3.refs_2_), custom_call_target="tpu_custom_call" | custom-call | bytes 9000000 | tf_op jit(solution)/shard_map/join_parts/pallas_call | solution.py:733
  86.8 0.8 join_parts.3
  (49 shorter events, 2.2 us)
Async XLA Ops:
  2.0 11.6 %all-to-all-start = ((s32[8,1,2]{2,1,0:T(1,128)}), s32[8,1,2]{2,1,0:T(1,128)S(1)}, u32[]{:S(2)}, u32[]{:S(2)}) async-start(s32[8,1,2]{2,1,0:T(1,128)} %get-tuple-element.13), calls=%async_computation | async-start | bytes 8192 | tf_op jit(solution)/shard_map/all_to_all | solution.py:776
  8.4 1.2 %copy-start = (bf16[32,128,128]{2,1,0:T(8,128)(2,1)S(1)}, bf16[32,128,128]{2,1,0:T(8,128)(2,1)}, u32[]{:S(2)}) copy-start(bf16[32,128,128]{2,1,0:T(8,128)(2,1)} %template.1) | copy-start | bytes 3145732
  9.6 9.2 %copy-start.8 = (bf16[40,21]{0,1:T(8,128)(2,1)S(1)}, bf16[40,21]{0,1:T(8,128)(2,1)}, u32[]{:S(2)}) copy-start(bf16[40,21]{0,1:T(8,128)(2,1)} %param.20) | copy-start | bytes 5044
  9.6 9.3 %copy-start.9 = (bf16[40,21]{0,1:T(8,128)(2,1)S(1)}, bf16[40,21]{0,1:T(8,128)(2,1)}, u32[]{:S(2)}) copy-start(bf16[40,21]{0,1:T(8,128)(2,1)} %param.21) | copy-start | bytes 5044
  9.7 15.9 %copy-start.1 = (bf16[1,256,1024]{2,1,0:T(8,128)(2,1)S(1)}, bf16[1,256,1024]{2,1,0:T(8,128)(2,1)}, u32[]{:S(2)}) copy-start(bf16[1,256,1024]{2,1,0:T(8,128)(2,1)} %param.14) | copy-start | bytes 1572868
  9.7 15.9 %copy-start.2 = (bf16[1,256,1024]{2,1,0:T(8,128)(2,1)S(1)}, bf16[1,256,1024]{2,1,0:T(8,128)(2,1)}, u32[]{:S(2)}) copy-start(bf16[1,256,1024]{2,1,0:T(8,128)(2,1)} %param.15) | copy-start | bytes 1572868
  9.7 15.9 %copy-start.3 = (s32[16]{0:T(128)S(1)}, s32[16]{0:T(128)}, u32[]{:S(2)}) copy-start(s32[16]{0:T(128)} %get-tuple-element.15.sender) | copy-start | bytes 196
  15.2 22.5 %copy-start.5 = (s32[1,4]{1,0:T(1,128)S(1)}, s32[1,4]{1,0:T(1,128)}, u32[]{:S(2)}) copy-start(s32[1,4]{1,0:T(1,128)} %rows_at.1) | copy-start | bytes 52
  15.2 22.5 %copy-start.6 = (s32[1,4]{1,0:T(1,128)S(1)}, s32[1,4]{1,0:T(1,128)}, u32[]{:S(2)}) copy-start(s32[1,4]{1,0:T(1,128)} %cols_at.1) | copy-start | bytes 52
  15.2 22.5 %copy-start.7 = (s32[16]{0:T(128)S(1)}, s32[16]{0:T(128)}, u32[]{:S(2)}) copy-start(s32[16]{0:T(128)} %get-tuple-element.14.slot_of) | copy-start | bytes 196
  15.2 14.6 %all-to-all-start.1 = ((bf16[16,128,128]{2,1,0:T(8,128)(2,1)}), bf16[16,128,128]{2,1,0:T(8,128)(2,1)S(1)}, u32[]{:S(2)}, u32[]{:S(2)}) async-start(bf16[16,128,128]{2,1,0:T(8,128)(2,1)} %pick_blocks.1.earlier), calls=%async_computation.1 | async-start | bytes 1048576 | tf_op jit(solution)/shard_map/all_to_all | solution.py:782
  19.5 4.8 %collective-permute-start.2 = (s32[8,1,2]{2,1,0:T(1,128)S(1)}, s32[8,1,2]{2,1,0:T(1,128)S(1)}, u32[]{:S(2)}, u32[]{:S(2)}) collective-permute-start(s32[8,1,2]{2,1,0:T(1,128)S(1)} %hold.1), channel_id=1, source_target_pairs={{0,3},{1,2},{2,1},{3,0},{4,7},{5,6},{6,5},{7,4},{8,11},{9,10},{10,... | collective-permute-start | bytes 200 | tf_op jit(solution)/shard_map/ppermute | solution.py:38
  22.7 2.7 %collective-permute-start.1 = (s32[8,1,2]{2,1,0:T(1,128)S(1)}, s32[8,1,2]{2,1,0:T(1,128)S(1)}, u32[]{:S(2)}, u32[]{:S(2)}) collective-permute-start(s32[8,1,2]{2,1,0:T(1,128)S(1)} %hold.1), channel_id=1, source_target_pairs={{0,2},{1,3},{2,0},{3,1},{4,6},{5,7},{6,4},{7,5},{8,10},{9,11},{10,... | collective-permute-start | bytes 200 | tf_op jit(solution)/shard_map/ppermute | solution.py:38
  22.9 2.5 %collective-permute-start = (s32[8,1,2]{2,1,0:T(1,128)S(1)}, s32[8,1,2]{2,1,0:T(1,128)S(1)}, u32[]{:S(2)}, u32[]{:S(2)}) collective-permute-start(s32[8,1,2]{2,1,0:T(1,128)S(1)} %hold.1), channel_id=1, source_target_pairs={{0,1},{1,0},{2,3},{3,2},{4,5},{5,4},{6,7},{7,6},{8,9},{9,8},{10,11... | collective-permute-start | bytes 200 | tf_op jit(solution)/shard_map/ppermute | solution.py:38
  29.8 23.1 %all-to-all-start.3 = ((bf16[32,64,128]{2,1,0:T(8,128)(2,1)}), bf16[32,64,128]{2,1,0:T(8,128)(2,1)S(1)}, u32[]{:S(2)}, u32[]{:S(2)}) async-start(bf16[32,64,128]{2,1,0:T(8,128)(2,1)} %prepare.1), calls=%async_computation.3 | async-start | bytes 1048576 | tf_op jit(solution)/shard_map/all_to_all | solution.py:794
  37.7 20.6 %copy-start.10 = (f32[1,21]{1,0:T(1,128)S(1)}, f32[1,21]{1,0:T(1,128)}, u32[]{:S(2)}) copy-start(f32[1,21]{1,0:T(1,128)} %param.23) | copy-start | bytes 256
  37.7 20.7 %copy-start.11 = (f32[1,21]{1,0:T(1,128)S(1)}, f32[1,21]{1,0:T(1,128)}, u32[]{:S(2)}) copy-start(f32[1,21]{1,0:T(1,128)} %param.22) | copy-start | bytes 256
  52.9 21.9 %all-to-all-start.2 = ((bf16[32,72,128]{2,1,0:T(8,128)(2,1)}), bf16[32,72,128]{2,1,0:T(8,128)(2,1)S(1)}, u32[]{:S(2)}, u32[]{:S(2)}) async-start(bf16[32,72,128]{2,1,0:T(8,128)(2,1)} %get-tuple-element.17.payload), calls=%async_computation.2 | async-start | bytes 1179648 | tf_op jit(solution)/shard_map/all_to_all | solution.py:815
  58.6 1.2 %copy-start.4 = (bf16[32,128,128]{2,1,0:T(8,128)(2,1)S(1)}, bf16[32,128,128]{2,1,0:T(8,128)(2,1)}, u32[]{:S(2)}) copy-start(bf16[32,128,128]{2,1,0:T(8,128)(2,1)} %template_var.1) | copy-start | bytes 3145732
  76.2 7.4 %collective-permute-start.3 = (bf16[32,32,128]{2,1,0:T(8,128)(2,1)S(1)}, bf16[32,32,128]{2,1,0:T(8,128)(2,1)S(1)}, u32[]{:S(2)}, u32[]{:S(2)}) collective-permute-start(bf16[32,32,128]{2,1,0:T(8,128)(2,1)S(1)} %combine.1.refs_0_), channel_id=1, source_target_pairs={{0,2},{1,3},{2,0},{3,1},{4,6},{5,7},{6,4},{7,5},{8,10},{9,11},{10,... | collective-permute-start | bytes 786440 | tf_op jit(solution)/shard_map/ppermute | solution.py:833
  77.5 7.6 %collective-permute-start.5 = (bf16[32,32,128]{2,1,0:T(8,128)(2,1)S(1)}, bf16[32,32,128]{2,1,0:T(8,128)(2,1)S(1)}, u32[]{:S(2)}, u32[]{:S(2)}) collective-permute-start(bf16[32,32,128]{2,1,0:T(8,128)(2,1)S(1)} %combine.1.refs_0_), channel_id=1, source_target_pairs={{0,1},{1,0},{2,3},{3,2},{4,5},{5,4},{6,7},{7,6},{8,9},{9,8},{10,11... | collective-permute-start | bytes 786440 | tf_op jit(solution)/shard_map/ppermute | solution.py:833
  83.6 3.2 %collective-permute-start.4 = (bf16[32,32,128]{2,1,0:T(8,128)(2,1)S(1)}, bf16[32,32,128]{2,1,0:T(8,128)(2,1)S(1)}, u32[]{:S(2)}, u32[]{:S(2)}) collective-permute-start(bf16[32,32,128]{2,1,0:T(8,128)(2,1)S(1)} %collective-permute-done.3.refs_2_), channel_id=1, source_target_pairs={{0,1},{1,0},{2,3},{3,2},{4,5},{5,4},{6,7},{7,6},{8,9},{9,8},{10,11... | collective-permute-start | bytes 786440 | tf_op jit(solution)/shard_map/ppermute | solution.py:833

commit v9 on v8

--- a/solution.py
+++ b/solution.py
@@ -24,6 +24,13 @@
     return pl.CostEstimate(flops=flops, bytes_accessed=moved, transcendentals=0)
 
 
+exposure_axes = ("far", "near")
+
+
+def part_of(exposure, exps, nears):
+    return lax.rem(exposure, nears) * (exps // nears) + exposure // nears
+
+
 def distance(here, there, exps):
     if exps & (exps - 1) == 0:
         return here ^ there
@@ -35,7 +42,7 @@
         pairs = [(e, e ^ gap) for e in range(exps)]
     else:
         pairs = [(e, (e + gap) % exps) for e in range(exps)]
-    return lax.ppermute(value, "exp", pairs)
+    return lax.ppermute(value, exposure_axes, pairs)
 
 
 def route_body(src, blk, slot_of, sender, request, count, *, peers, capacity):
@@ -115,7 +122,8 @@
     )(asked, template)
 
 
-def store_parts(sender, image, out, side, exps, capacity, across_blocks):
+def store_parts(sender, image, out, side, order, capacity, across_blocks):
+    exps = len(order)
     part = side // exps
     slots = sender.shape[0]
 
@@ -125,8 +133,8 @@
         left = pl.multiple_of((b % across_blocks) * side, side)
         block = image[pl.ds(top, side), pl.ds(left, side)].astype(bf16)
         row = pl.multiple_of((s % capacity) * part, part)
-        for q in range(exps):
-            out[(s // capacity) * exps + q, pl.ds(row, part), :] = block[q * part : (q + 1) * part]
+        for e, q in enumerate(order):
+            out[(s // capacity) * exps + e, pl.ds(row, part), :] = block[q * part : (q + 1) * part]
         return carry
 
     lax.fori_loop(0, slots, one, 0, unroll=True if slots <= 32 else 4)
@@ -156,17 +164,17 @@
     )(asked, earlier)
 
 
-def prepare_body(sender, variance, science, earlier, out, *, side, exps, capacity):
+def prepare_body(sender, variance, science, earlier, out, *, side, nears, capacity):
     del earlier, science
-    store_parts(sender, variance, out, side, exps, capacity, variance.shape[1] // side)
-
-
-def prepare(sender, variance, science, earlier, side, exps, capacity):
+    store_parts(sender, variance, out, side, range(nears), capacity, variance.shape[1] // side)
+
+
+def prepare(sender, variance, science, earlier, side, nears, capacity):
     slots = sender.shape[0]
-    part = side // exps
-    return pl.pallas_call(
-        functools.partial(prepare_body, side=side, exps=exps, capacity=capacity),
-        out_shape=jax.ShapeDtypeStruct((slots // capacity * exps, capacity * part, side), bf16),
+    part = side // nears
+    return pl.pallas_call(
+        functools.partial(prepare_body, side=side, nears=nears, capacity=capacity),
+        out_shape=jax.ShapeDtypeStruct((slots // capacity * nears, capacity * part, side), bf16),
         in_specs=[smem()] + [vmem()] * 2 + [pl.BlockSpec(memory_space=pl.ANY)],
         out_specs=vmem(),
         compiler_params=pltpu.CompilerParams(vmem_limit_bytes=16 * mib),
@@ -321,7 +329,7 @@
     bands,
     total,
     *,
-    exps,
+    order,
     capacity,
     count,
     taps,
@@ -330,7 +338,7 @@
     side = frames.shape[3]
     high, wide = science.shape
     padded_k = gram.shape[1]
-    part = side // exps
+    part = side // len(order)
     size = count + 1
 
     system = jnp.concatenate(
@@ -418,7 +426,7 @@
         image[:, c * step : c * step + keep] = window[c, :, :keep]
     image[...] = science[...].astype(f32) - image[...] - background
 
-    store_parts(sender, image, payload, side, exps, capacity, wide // side)
+    store_parts(sender, image, payload, side, order, capacity, wide // side)
     line_at = lax.broadcasted_iota(jnp.int32, (trailer_rows, side), 0)
     trailer = jnp.zeros((trailer_rows, side), f32)
     rest = kernel_sum
@@ -449,7 +457,7 @@
     coef_out,
     payload,
     *scratch,
-    exps,
+    order,
     capacity,
     count,
     taps,
@@ -483,7 +491,7 @@
         coef_out,
         payload,
         *scratch[8:],
-        exps=exps,
+        order=order,
         capacity=capacity,
         count=count,
         taps=taps,
@@ -502,11 +510,12 @@
     science,
     variance,
     col_t,
-    exps,
+    order,
     capacity,
     count,
     taps,
 ):
+    exps = len(order)
     high, wide = science.shape
     side = row_rev.shape[1]
     slots = sender.shape[0]
@@ -519,7 +528,7 @@
     wins = -(-wide // (side - taps + 1))
     group = next(g for g in (8, 4, 2, 1) if count % g == 0)
     return pl.pallas_call(
-        functools.partial(fit_body, exps=exps, capacity=capacity, count=count, taps=taps),
+        functools.partial(fit_body, order=order, capacity=capacity, count=count, taps=taps),
         out_shape=(
             jax.ShapeDtypeStruct((1, side), f32),
             jax.ShapeDtypeStruct(
@@ -564,45 +573,22 @@
     return top, (value - top.astype(f32)).astype(bf16)
 
 
-def score_body(
-    me,
-    table,
-    slot_of,
-    payload,
-    down,
-    over,
-    parts,
-    template_var,
-    out,
-    var_out,
-    var_template,
-    padded,
-    sideways,
-    var_total,
-    sem,
-    *,
-    side,
-    taps,
-    part,
-    capacity,
-):
-    mine = pl.ds(pl.multiple_of(me[0] * part, part), part)
-    copy = pltpu.make_async_copy(template_var.at[:, mine, :], var_template, sem)
-    copy.start()
-    add_variance(me, table, parts, var_out, var_total, part, capacity)
+def score_body(slot_of, payload, down, over, out, padded, sideways, *, order, taps, capacity):
+    side = payload.shape[2]
+    part = side // len(order)
     high, wide = out.shape
     margin = taps // 2
     span = up(side + taps - 1, 16)
     across_blocks = wide // side
-    exps = side // part
+    exps = len(order)
     padded[...] = jnp.zeros(padded.shape, f32)
     for b in range(slot_of.shape[0]):
         slot = slot_of[b]
         row = pl.multiple_of((slot % capacity) * part, part)
         left = margin + (b % across_blocks) * side
-        for q in range(exps):
+        for e, q in enumerate(order):
             top = (b // across_blocks) * side + q * part
-            block = payload[(slot // capacity) * exps + q, pl.ds(row, part), :]
+            block = payload[(slot // capacity) * exps + e, pl.ds(row, part), :]
             padded[top : top + part, left : left + side] = block.astype(f32)
     line = jnp.broadcast_to(over[...], (2 * side, 2 * side))
     band = pltpu.roll(line, 0, 1, stride=1, stride_axis=0)[:, :side]
@@ -621,85 +607,117 @@
         got = got + jnp.dot(top, data_low, preferred_element_type=f32)
         got = got + jnp.dot(low, data_top, preferred_element_type=f32)
         out[r * side : (r + 1) * side, :] = got
-    copy.wait()
-
-
-def score(
-    me, table, slot_of, payload, down, over_rev, parts, template_var, high, wide, taps, capacity
-):
-    tract, side, _ = template_var.shape
-    part = parts.shape[1] // capacity
+
+
+def score(slot_of, payload, down, over_rev, high, wide, taps, order, capacity):
+    side = payload.shape[2]
     span = up(side + taps - 1, 16)
     return pl.pallas_call(
-        functools.partial(score_body, side=side, taps=taps, part=part, capacity=capacity),
-        out_shape=(
-            jax.ShapeDtypeStruct((high, wide), f32),
-            jax.ShapeDtypeStruct((tract, part, side), f32),
-            jax.ShapeDtypeStruct((tract, part, side), template_var.dtype),
-        ),
-        in_specs=[smem()] * 3 + [vmem()] * 4 + [pl.BlockSpec(memory_space=pl.ANY)],
-        out_specs=(vmem(),) * 3,
+        functools.partial(score_body, order=order, taps=taps, capacity=capacity),
+        out_shape=jax.ShapeDtypeStruct((high, wide), f32),
+        in_specs=[smem()] + [vmem()] * 3,
+        out_specs=vmem(),
         scratch_shapes=[
             pltpu.VMEM((high, wide + side), f32),
             pltpu.VMEM((high - side + span, wide), f32),
-            pltpu.VMEM((tract + 1, part, side), f32),
-            pltpu.SemaphoreType.DMA(()),
         ],
         compiler_params=pltpu.CompilerParams(vmem_limit_bytes=20 * mib),
         cost_estimate=cost(2_000_000_000, 2_000_000),
         name="score",
-    )(me, table, slot_of, payload, down, over_rev, parts, template_var)
-
-
-def wanted_block(me, table, d, c, tract):
+    )(slot_of, payload, down, over_rev)
+
+
+def wanted_block(me, exposure, table, d, c, tract):
     exps = table.shape[0]
-    block = table[distance(me[0], lax.rem(d, exps), exps), d // exps, c] - 1
+    block = table[distance(me[0], exposure, exps), d, c] - 1
     return jnp.where(block < 0, tract, block)
 
 
-def add_variance(me, table, parts, out, total, part, capacity):
+def variance_body(
+    me, table, parts, template_var, own_out, other_out, template_out, total, sem, *, nears, capacity
+):
+    exps = table.shape[0]
+    fars = exps // nears
+    tract, part, _ = own_out.shape
+    mine = pl.ds(pl.multiple_of(part_of(me[0], exps, nears) * part, part), part)
+    copy = pltpu.make_async_copy(template_var.at[:, mine, :], template_out, sem)
+    copy.start()
     total[...] = jnp.zeros(total.shape, f32)
-    tract = out.shape[0]
-
-    def one(d, carry):
+    far = me[0] // nears
+    rows = fars * part
+
+    def one(j, carry):
+        exposure = far * nears + lax.rem(j, nears)
         for c in range(capacity):
-            block = wanted_block(me, table, d, c, tract)
-            total[block] += parts[d, c * part : (c + 1) * part, :].astype(f32)
+            block = wanted_block(me, exposure, table, j // nears, c, tract)
+            total[block] += parts[j, c * rows : (c + 1) * rows, :].astype(f32)
         return carry
 
     lax.fori_loop(0, parts.shape[0], one, 0, unroll=4)
-    out[...] = total[:tract]
-
-
-def combine_body(
-    me, table, parts, var_sum, var_template, out, total, gain, *, part, capacity
-):
+    own_out[...] = total[:tract, pl.ds(pl.multiple_of(far * part, part), part), :]
+    for g in range(1, fars):
+        there = lax.rem(far + g, fars)
+        rows_there = pl.ds(pl.multiple_of(there * part, part), part)
+        other_out[g - 1] = total[:tract, rows_there, :].astype(bf16)
+    copy.wait()
+
+
+def sum_variance(me, table, parts, template_var, nears, capacity):
+    tract, side, _ = template_var.shape
+    exps = table.shape[0]
+    fars = exps // nears
+    part = side // exps
+    return pl.pallas_call(
+        functools.partial(variance_body, nears=nears, capacity=capacity),
+        out_shape=(
+            jax.ShapeDtypeStruct((tract, part, side), f32),
+            jax.ShapeDtypeStruct((max(1, fars - 1), tract, part, side), bf16),
+            jax.ShapeDtypeStruct((tract, part, side), template_var.dtype),
+        ),
+        in_specs=[smem()] * 2 + [vmem(), pl.BlockSpec(memory_space=pl.ANY)],
+        out_specs=(vmem(),) * 3,
+        scratch_shapes=[
+            pltpu.VMEM((tract + 1, fars * part, side), f32),
+            pltpu.SemaphoreType.DMA(()),
+        ],
+        compiler_params=pltpu.CompilerParams(vmem_limit_bytes=16 * mib),
+        cost_estimate=cost(0, 4_000_000),
+        name="sum_variance",
+    )(me, table, parts, template_var)
+
+
+def combine_body(me, table, parts, own_var, var_template, *rest, part, capacity):
+    others = rest[:-3]
+    out, total, gain = rest[-3:]
     total[...] = jnp.zeros(total.shape, f32)
     gain[...] = jnp.zeros(gain.shape, f32)
     tract = out.shape[0]
-
-    def one(d, carry):
-        tail = parts[d, capacity * part :, :].astype(f32)
+    exps = table.shape[0]
+
+    def one(j, carry):
+        tail = parts[j, capacity * part :, :].astype(f32)
         kernel_sum = tail[0:1] + tail[1:2] + tail[2:3]
         square = jnp.broadcast_to(kernel_sum * kernel_sum, gain.shape[1:])
         for c in range(capacity):
-            block = wanted_block(me, table, d, c, tract)
-            total[block] += parts[d, c * part : (c + 1) * part, :].astype(f32)
+            block = wanted_block(me, lax.rem(j, exps), table, j // exps, c, tract)
+            total[block] += parts[j, c * part : (c + 1) * part, :].astype(f32)
             gain[block] += square
         return carry
 
     lax.fori_loop(0, parts.shape[0], one, 0, unroll=4)
     for t in range(tract):
-        variance = var_sum[t] + gain[t, 0:1, :] * var_template[t].astype(f32)
+        variance = own_var[t] + gain[t, 0:1, :] * var_template[t].astype(f32)
+        for other in others:
+            variance = variance + other[t].astype(f32)
         out[t] = (total[t] * lax.rsqrt(jnp.maximum(variance, 1.0))).astype(bf16)
 
 
-def combine(me, table, parts, var_sum, var_template, part, capacity):
-    tract, _, side = var_sum.shape
+def combine(me, table, parts, own_var, var_template, others, capacity):
+    tract, part, side = own_var.shape
     return pl.pallas_call(
         functools.partial(combine_body, part=part, capacity=capacity),
         out_shape=jax.ShapeDtypeStruct((tract, part, side), bf16),
-        in_specs=[smem(), smem(), vmem(), vmem(), vmem()],
+        in_specs=[smem(), smem()] + [vmem()] * (3 + len(others)),
         out_specs=vmem(),
         scratch_shapes=[
             pltpu.VMEM((tract + 1, part, side), f32),
@@ -707,7 +725,7 @@
         ],
         compiler_params=pltpu.CompilerParams(vmem_limit_bytes=16 * mib),
         name="combine",
-    )(me, table, parts, var_sum, var_template)
+    )(me, table, parts, own_var, var_template, *others)
 
 
 def join_body(places, *refs, part, count):
@@ -761,8 +779,10 @@
     psf_row,
 ):
     peers = lax.axis_size("det")
-    exps = lax.axis_size("exp")
-    me = lax.axis_index("exp").astype(jnp.int32)
+    nears = lax.axis_size("near")
+    exps = lax.axis_size("far") * nears
+    me = (lax.axis_index("far") * nears + lax.axis_index("near")).astype(jnp.int32)
+    order = tuple((e % nears) * (exps // nears) + e // nears for e in range(exps))
     tract, side, _ = template.shape
     science_img = science[0]
     variance_img = science_var[0]
@@ -778,7 +798,7 @@
     held = hold(asked, picked)
     tables = [held] + [from_exposure(held, g, exps) for g in range(1, exps)]
     table = jnp.stack(tables).reshape(exps, peers, capacity)
-    var_parts = prepare(sender, variance_img, science_img, table, side, exps, capacity)
+    var_parts = prepare(sender, variance_img, science_img, table, side, nears, capacity)
     arrived = lax.all_to_all(picked, "det", split_axis=0, concat_axis=0, tiled=True)
 
     padded_k = up(count + 2, 16)
@@ -792,7 +812,7 @@
     down = jnp.pad(psf_col, ((0, 0), (0, 2 * side - taps)))
     var_late, arrived = lax.optimization_barrier((var_parts, arrived))
     var_back = lax.all_to_all(
-        var_late, ("det", "exp"), split_axis=0, concat_axis=0, tiled=True
+        var_late, ("det", "near"), split_axis=0, concat_axis=0, tiled=True
     )
 
     high, wide = science_img.shape
@@ -807,33 +827,28 @@
         science_img,
         variance_img,
         col_t,
-        exps,
+        order,
         capacity,
         count,
         taps,
     )
-    diff_back = lax.all_to_all(payload, ("det", "exp"), split_axis=0, concat_axis=0, tiled=True)
-    scored, var_sum, var_template = score(
-        me[None],
-        table,
-        slot_of,
-        payload,
-        down,
-        over_rev,
-        var_back,
-        template_var,
-        high,
-        wide,
-        taps,
-        capacity,
-    )
-    mine = combine(me[None], table, diff_back, var_sum, var_template, part, capacity)
+    diff_back = lax.all_to_all(payload, ("det",) + exposure_axes, split_axis=0, concat_axis=0, tiled=True)
+    own_var, other_var, var_template = sum_variance(
+        me[None], table, var_back, template_var, nears, capacity
+    )
+    fars = exps // nears
+    others = []
+    for g in range(1, fars):
+        pairs = [(f, (f + g) % fars) for f in range(fars)]
+        others.append(lax.ppermute(other_var[g - 1], "far", pairs))
+    scored = score(slot_of, payload, down, over_rev, high, wide, taps, order, capacity)
+    mine = combine(me[None], table, diff_back, own_var, var_template, others, capacity)
 
     def swap(value, distance):
-        return lax.ppermute(value, "exp", [(e, e ^ distance) for e in range(exps)])
+        return lax.ppermute(value, exposure_axes, [(e, e ^ distance) for e in range(exps)])
 
     def put(parts, whole):
-        places = jnp.stack([there for there, _ in parts])
+        places = jnp.stack([part_of(there, exps, nears) for there, _ in parts])
         return join_parts(places, [held for _, held in parts], whole, exps)
 
     if exps == 4:
@@ -846,30 +861,39 @@
         parts = [(me, mine)]
         for gap in range(1, exps):
             pairs = [(e, (e + gap) % exps) for e in range(exps)]
-            parts.append(((me - gap) % exps, lax.ppermute(mine, "exp", pairs)))
+            parts.append(((me - gap) % exps, lax.ppermute(mine, exposure_axes, pairs)))
         significance = put(parts, None)
     return (significance, scored[None], coef[:, : count + 1])
 
 
 def solution(mesh):
+    peers, exps = mesh.devices.shape
+    nears = 2 if exps % 2 == 0 else 1
+    split = jax.sharding.Mesh(
+        mesh.devices.reshape(peers, exps // nears, nears), ("det",) + exposure_axes
+    )
     placed = (
         P("det", None, None),
         P("det", None, None),
-        P("exp", "det", None),
-        P("exp", "det", None),
-        P("exp", "det"),
-        P("exp", "det"),
-        P("exp", "det"),
-        P("exp", "det"),
+        P(exposure_axes, "det", None),
+        P(exposure_axes, "det", None),
+        P(exposure_axes, "det"),
+        P(exposure_axes, "det"),
+        P(exposure_axes, "det"),
+        P(exposure_axes, "det"),
         P(),
         P(),
-        P("exp", None),
-        P("exp", None),
+        P(exposure_axes, None),
+        P(exposure_axes, None),
     )
     return jax.shard_map(
         local,
-        mesh=mesh,
+        mesh=split,
         in_specs=placed,
-        out_specs=(P("det", None, None), P("exp", "det", None), P("exp", "det")),
+        out_specs=(
+            P("det", None, None),
+            P(exposure_axes, "det", None),
+            P(exposure_axes, "det"),
+        ),
         check_vma=False,
     )

time: 88.2 us -> 91.5 us (1.037)
  starting transfers between devices: 30.2 us -> 32.4 us
  waiting for transfers between devices: 25.9 us -> 27.6 us
  local copies, waits for them, and re-layouts: 3.53 us -> 2.31 us
    all_to_all x2, waiting for transfers between devices: 11.6 us -> 13.8 us  [the longest x1 13.8 us: local(): lax.all_to_all(payload, ('det',) + exposure_axes, split_axis=0, concat_ax...]
    ppermute x6 -> x7, starting transfers between devices: 6.83 us -> 8.47 us  [the longest x3 3.88 us: from_exposure(): return lax.ppermute(value, exposure_axes, pairs)]
    unnamed x25, local copies, waits for them, and re-layouts: 2.6 us -> 1.38 us
    pallas_call x3 -> x4, Pallas kernels: 19.9 us -> 20.6 us  [the longest x1 14.8 us: fit_and_subtract(): pl.pallas_call(functools.partial(fit_body, order=order, capacity=capacity...]
    ppermute x6 -> x7, waiting for transfers between devices: 7.79 us -> 7.99 us  [the longest x3 5.36 us: swap(): lax.ppermute(value, exposure_axes, [(e, e ^ distance) for e in range(exps)])]
  transfers between devices with their start and end apart: 10 -> 11, of which waited for: 7 -> 6; matrix products, arithmetic and copies ran while one was open for 1% -> 1% of each run, Pallas kernels for 25% -> 25%
where the time goes in v9:
time: 91.5 us; the launch traced here: 91 us
  starting transfers between devices  32.4 us (35%)
  Pallas kernels  27.7 us (30%)
  waiting for transfers between devices  27.6 us (30%)
  local copies, waits for them, and re-layouts  2.31 us (3%)
    pallas_call x1, Pallas kernels, fit_and_subtract(): pl.pallas_call(functools.partial(fit_body, order=order, capacity=capacity...  14.8 us
    all_to_all x1, waiting for transfers between devices, local(): lax.all_to_all(payload, ('det',) + exposure_axes, split_axis=0, concat_ax...  13.8 us
    all_to_all x1, starting transfers between devices, local(): lax.all_to_all(var_late, ('det', 'near'), split_axis=0, concat_axis=0, ti...  8.11 us
    all_to_all x1, starting transfers between devices, local(): lax.all_to_all(request, 'det', split_axis=0, concat_axis=0, tiled=True)  6.37 us
    all_to_all x1, starting transfers between devices, local(): lax.all_to_all(payload, ('det',) + exposure_axes, split_axis=0, concat_ax...  5.78 us
    ppermute x3, waiting for transfers between devices, swap(): lax.ppermute(value, exposure_axes, [(e, e ^ distance) for e in range(exps)])  5.36 us
    all_to_all x1, waiting for transfers between devices, local(): lax.all_to_all(request, 'det', split_axis=0, concat_axis=0, tiled=True)  3.89 us
    ppermute x3, starting transfers between devices, from_exposure(): return lax.ppermute(value, exposure_axes, pairs)  3.88 us
  transfers between devices with their start and end apart: 11, of which 6 were waited for; matrix products, arithmetic and copies ran while one was open for 1% of the time, Pallas kernels for 25%

profile of v9, /device:TPU:1, one launch (start us, length us, event | category | flops | bytes accessed | tf_op | source)
XLA Modules:
  0.0 91.0 jit_solution(17838177726747925516)
XLA Ops:
  0.6 1.4 %route_tables.1 = (s32[16]{0:T(128)}, s32[16]{0:T(128)}, s32[8,1,2]{2,1,0:T(1,128)}) custom-call(s32[1,16]{1,0:T(1,128)} %src.1, s32[1,16]{1,0:T(1,128)} %blk.1), custom_call_target="tpu_custom_call" | custom-call | tf_op jit(solution)/shard_map/route_tables/pallas_call | solution.py:70
  2.0 6.4 %all-to-all-start = ((s32[8,1,2]{2,1,0:T(1,128)}), s32[8,1,2]{2,1,0:T(1,128)S(1)}, u32[]{:S(2)}, u32[]{:S(2)}) async-start(s32[8,1,2]{2,1,0:T(1,128)} %get-tuple-element.13), calls=%async_computation | async-start | bytes 8192 | tf_op jit(solution)/shard_map/all_to_all | solution.py:796
  8.4 1.2 %copy-done = bf16[32,128,128]{2,1,0:T(8,128)(2,1)S(1)} copy-done((bf16[32,128,128]{2,1,0:T(8,128)(2,1)S(1)}, bf16[32,128,128]{2,1,0:T(8,128)(2,1)}, u32[]{:S(2)}) %copy-start) | copy-done | bytes 1048600
  9.8 3.9 %all-to-all-done.asked = s32[8,1,2]{2,1,0:T(1,128)S(1)} async-done(((s32[8,1,2]{2,1,0:T(1,128)}), s32[8,1,2]{2,1,0:T(1,128)S(1)}, u32[]{:S(2)}, u32[]{:S(2)}) %all-to-all-start) | async-done | bytes 96 | tf_op jit(solution)/shard_map/all_to_all | solution.py:796
  13.6 1.5 %pick_blocks.1.earlier = bf16[16,128,128]{2,1,0:T(8,128)(2,1)} custom-call(s32[8,1,2]{2,1,0:T(1,128)S(1)} %all-to-all-done.asked, bf16[32,128,128]{2,1,0:T(8,128)(2,1)S(1)} %fetch.1.template), custom_call_target="tpu_custom_call" | custom-call | tf_op jit(solution)/shard_map/pick_blocks/pallas_call | solution.py:114
  15.2 3.6 %all-to-all-start.1 = ((bf16[16,128,128]{2,1,0:T(8,128)(2,1)}), bf16[16,128,128]{2,1,0:T(8,128)(2,1)S(1)}, u32[]{:S(2)}, u32[]{:S(2)}) async-start(bf16[16,128,128]{2,1,0:T(8,128)(2,1)} %pick_blocks.1.earlier), calls=%async_computation.1 | async-start | bytes 1048576 | tf_op jit(solution)/shard_map/all_to_all | solution.py:802
  19.4 2.2 %collective-permute-start = (s32[8,1,2]{2,1,0:T(1,128)S(1)}, s32[8,1,2]{2,1,0:T(1,128)S(1)}, u32[]{:S(2)}, u32[]{:S(2)}) collective-permute-start(s32[8,1,2]{2,1,0:T(1,128)S(1)} %hold.1), channel_id=1, source_target_pairs={{0,1},{1,0},{2,3},{3,2},{4,5},{5,4},{6,7},{7,6},{8,9},{9,8},{10,11... | collective-permute-start | bytes 200 | tf_op jit(solution)/shard_map/ppermute | solution.py:45
  21.6 1.3 %collective-permute-start.1 = (s32[8,1,2]{2,1,0:T(1,128)S(1)}, s32[8,1,2]{2,1,0:T(1,128)S(1)}, u32[]{:S(2)}, u32[]{:S(2)}) collective-permute-start(s32[8,1,2]{2,1,0:T(1,128)S(1)} %hold.1), channel_id=1, source_target_pairs={{0,2},{1,3},{2,0},{3,1},{4,6},{5,7},{6,4},{7,5},{8,10},{9,11},{10,... | collective-permute-start | bytes 200 | tf_op jit(solution)/shard_map/ppermute | solution.py:45
  23.4 0.9 collective-permute-done.1
  24.4 1.7 %collective-permute-done.2 = s32[8,1,2]{2,1,0:T(1,128)S(1)} collective-permute-done((s32[8,1,2]{2,1,0:T(1,128)S(1)}, s32[8,1,2]{2,1,0:T(1,128)S(1)}, u32[]{:S(2)}, u32[]{:S(2)}) %collective-permute-start.2) | collective-permute-done | bytes 96 | tf_op jit(solution)/shard_map/ppermute | solution.py:45
  26.3 1.5 %prepare.1 = bf16[16,128,128]{2,1,0:T(8,128)(2,1)} custom-call(s32[16]{0:T(128)S(1)} %copy-done.4, bf16[256,1024]{1,0:T(8,128)(2,1)S(1)} %bitcast.20, bf16[256,1024]{1,0:T(8,128)(2,1)S(1)} %bitcast.18, s32[4,8,2]{2,1,0:T(8,128)S(1)} %copy.35.earlier.table), custom_call_target="tpu_custom_call" | custom-call | bytes 6000000 | tf_op jit(solution)/shard_map/prepare/pallas_call | solution.py:175
  27.8 1.9 %all-to-all-done.1.arrived = bf16[16,128,128]{2,1,0:T(8,128)(2,1)S(1)} async-done(((bf16[16,128,128]{2,1,0:T(8,128)(2,1)}), bf16[16,128,128]{2,1,0:T(8,128)(2,1)S(1)}, u32[]{:S(2)}, u32[]{:S(2)}) %all-to-all-start.1) | async-done | bytes 524320 | tf_op jit(solution)/shard_map/all_to_all | solution.py:802
  29.8 8.1 %all-to-all-start.3 = ((bf16[16,128,128]{2,1,0:T(8,128)(2,1)}), bf16[16,128,128]{2,1,0:T(8,128)(2,1)S(1)}, u32[]{:S(2)}, u32[]{:S(2)}) async-start(bf16[16,128,128]{2,1,0:T(8,128)(2,1)} %prepare.1), calls=%async_computation.3 | async-start | bytes 1048576 | tf_op jit(solution)/shard_map/all_to_all | solution.py:814
  37.9 14.8 %fit_and_subtract.1 = (f32[1,128]{1,0:T(1,128)}, bf16[32,72,128]{2,1,0:T(8,128)(2,1)}) custom-call(s32[16]{0:T(128)S(1)} %copy-done.7, s32[16]{0:T(128)S(1)} %copy-done.4, s32[1,4]{1,0:T(1,128)S(1)} %copy-done.5, s32[1,4]{1,0:T(1,128)S(1)} %copy-done.6, bf16[16,128,128]{2,1,0:T(8,128)(2,1)S(1)} %all-to-all-done.1.arrived, ...), custom_call_target="tpu_custom_call" | custom-call | flops 15000000512 | bytes 8000000 | tf_op jit(solution)/shard_map/fit_and_subtract/pallas_call | solution.py:530
  52.7 5.8 %all-to-all-start.2 = ((bf16[32,72,128]{2,1,0:T(8,128)(2,1)}), bf16[32,72,128]{2,1,0:T(8,128)(2,1)S(1)}, u32[]{:S(2)}, u32[]{:S(2)}) async-start(bf16[32,72,128]{2,1,0:T(8,128)(2,1)} %get-tuple-element.17.payload), calls=%async_computation.2 | async-start | bytes 1179648 | tf_op jit(solution)/shard_map/all_to_all | solution.py:835
  58.6 1.2 %sum_variance.1 = (f32[32,32,128]{2,1,0:T(8,128)S(1)}, bf16[1,32,32,128]{3,2,1,0:T(8,128)(2,1)S(1)}, bf16[32,32,128]{2,1,0:T(8,128)(2,1)S(1)}) custom-call(s32[1]{0:T(128)} %bitcast.1.me, s32[4,8,2]{2,1,0:T(8,128)S(1)} %copy.35.earlier.table, bf16[16,128,128]{2,1,0:T(8,128)(2,1)S(1)} %all-to-all-done.3.parts, bf16[32,128,128]{2,1,0:T(8,128)(2,1)S(1)} %copy-done.1), custom_call_target="tpu_custom_call" | custom-call | bytes 4000000 | tf_op jit(solution)/shard_map/sum_variance/pallas_call | solution.py:670
  59.8 1.4 %collective-permute-start.3 = (bf16[32,32,128]{2,1,0:T(8,128)(2,1)S(1)}, bf16[32,32,128]{2,1,0:T(8,128)(2,1)S(1)}, u32[]{:S(2)}, u32[]{:S(2)}) collective-permute-start(bf16[32,32,128]{2,1,0:T(8,128)(2,1)S(1)} %bitcast.22), channel_id=1, source_target_pairs={{0,2},{2,0},{1,3},{3,1},{4,6},{6,4},{5,7},{7,5},{8,10},{10,8},{9,1... | collective-permute-start | bytes 786440 | tf_op jit(solution)/shard_map/ppermute | solution.py:843
  61.2 13.8 %all-to-all-done.2.parts = bf16[32,72,128]{2,1,0:T(8,128)(2,1)S(1)} async-done(((bf16[32,72,128]{2,1,0:T(8,128)(2,1)}), bf16[32,72,128]{2,1,0:T(8,128)(2,1)S(1)}, u32[]{:S(2)}, u32[]{:S(2)}) %all-to-all-start.2) | async-done | bytes 589856 | tf_op jit(solution)/shard_map/all_to_all | solution.py:835
  75.0 1.5 %combine.1.refs_0_ = bf16[32,32,128]{2,1,0:T(8,128)(2,1)S(1)} custom-call(s32[1]{0:T(128)} %bitcast.1.me, s32[4,8,2]{2,1,0:T(8,128)S(1)} %copy.35.earlier.table, bf16[32,72,128]{2,1,0:T(8,128)(2,1)S(1)} %all-to-all-done.2.parts, f32[32,32,128]{2,1,0:T(8,128)S(1)} %get-tuple-element.19.own_var, bf16[32,32,128]{2,1,0:T(8,128)(2,1)S(1)} %get-tuple-element.20.var_template, ...), custom_call_target="tpu_custom_call" | custom-call | tf_op jit(solution)/shard_map/combine/pallas_call | solution.py:717
  76.4 1.3 %collective-permute-start.4 = (bf16[32,32,128]{2,1,0:T(8,128)(2,1)S(1)}, bf16[32,32,128]{2,1,0:T(8,128)(2,1)S(1)}, u32[]{:S(2)}, u32[]{:S(2)}) collective-permute-start(bf16[32,32,128]{2,1,0:T(8,128)(2,1)S(1)} %combine.1.refs_0_), channel_id=1, source_target_pairs={{0,2},{1,3},{2,0},{3,1},{4,6},{5,7},{6,4},{7,5},{8,10},{9,11},{10,... | collective-permute-start | bytes 786440 | tf_op jit(solution)/shard_map/ppermute | solution.py:848
  78.5 5.4 %collective-permute-done.4.refs_2_ = bf16[32,32,128]{2,1,0:T(8,128)(2,1)S(1)} collective-permute-done((bf16[32,32,128]{2,1,0:T(8,128)(2,1)S(1)}, bf16[32,32,128]{2,1,0:T(8,128)(2,1)S(1)}, u32[]{:S(2)}, u32[]{:S(2)}) %collective-permute-start.4) | collective-permute-done | bytes 262176 | tf_op jit(solution)/shard_map/ppermute | solution.py:848
  83.9 1.4 %collective-permute-start.5 = (bf16[32,32,128]{2,1,0:T(8,128)(2,1)S(1)}, bf16[32,32,128]{2,1,0:T(8,128)(2,1)S(1)}, u32[]{:S(2)}, u32[]{:S(2)}) collective-permute-start(bf16[32,32,128]{2,1,0:T(8,128)(2,1)S(1)} %collective-permute-done.4.refs_2_), channel_id=1, source_target_pairs={{0,1},{1,0},{2,3},{3,2},{4,5},{5,4},{6,7},{7,6},{8,9},{9,8},{10,11... | collective-permute-start | bytes 786440 | tf_op jit(solution)/shard_map/ppermute | solution.py:848
  85.3 3.1 %score.1 = f32[256,1024]{1,0:T(8,128)} custom-call(s32[16]{0:T(128)S(1)} %copy-done.7, bf16[32,72,128]{2,1,0:T(8,128)(2,1)} %get-tuple-element.17.payload, f32[1,256]{1,0:T(1,128)S(1)} %pad.26.down, f32[1,256]{1,0:T(1,128)S(1)} %pad_maximum_fusion.1.over), custom_call_target="tpu_custom_call" | custom-call | flops 2000000000 | bytes 2000000 | tf_op jit(solution)/shard_map/score/pallas_call | solution.py:615
  88.4 1.7 %join_parts.2.refs_1_ = f32[32,128,128]{2,1,0:T(8,128)} custom-call(s32[3]{0:T(128)S(1)} %pad_add_fusion.places, bf16[32,32,128]{2,1,0:T(8,128)(2,1)S(1)} %combine.1.refs_0_, bf16[32,32,128]{2,1,0:T(8,128)(2,1)S(1)} %collective-permute-done.6.refs_1_, bf16[32,32,128]{2,1,0:T(8,128)(2,1)S(1)} %collective-permute-done.4.refs_2_), custom_call_target="tpu_custom_call" | custom-call | bytes 9000000 | tf_op jit(solution)/shard_map/join_parts/pallas_call | solution.py:751
  (52 shorter events, 3.2 us)
Async XLA Ops:
  2.0 11.6 %all-to-all-start = ((s32[8,1,2]{2,1,0:T(1,128)}), s32[8,1,2]{2,1,0:T(1,128)S(1)}, u32[]{:S(2)}, u32[]{:S(2)}) async-start(s32[8,1,2]{2,1,0:T(1,128)} %get-tuple-element.13), calls=%async_computation | async-start | bytes 8192 | tf_op jit(solution)/shard_map/all_to_all | solution.py:796
  8.4 1.2 %copy-start = (bf16[32,128,128]{2,1,0:T(8,128)(2,1)S(1)}, bf16[32,128,128]{2,1,0:T(8,128)(2,1)}, u32[]{:S(2)}) copy-start(bf16[32,128,128]{2,1,0:T(8,128)(2,1)} %template.1) | copy-start | bytes 3145732
  9.6 9.2 %copy-start.9 = (bf16[40,21]{0,1:T(8,128)(2,1)S(1)}, bf16[40,21]{0,1:T(8,128)(2,1)}, u32[]{:S(2)}) copy-start(bf16[40,21]{0,1:T(8,128)(2,1)} %param.21) | copy-start | bytes 5044
  9.6 9.4 %copy-start.8 = (bf16[40,21]{0,1:T(8,128)(2,1)S(1)}, bf16[40,21]{0,1:T(8,128)(2,1)}, u32[]{:S(2)}) copy-start(bf16[40,21]{0,1:T(8,128)(2,1)} %param.20) | copy-start | bytes 5044
  9.7 16.6 %copy-start.2 = (bf16[1,256,1024]{2,1,0:T(8,128)(2,1)S(1)}, bf16[1,256,1024]{2,1,0:T(8,128)(2,1)}, u32[]{:S(2)}) copy-start(bf16[1,256,1024]{2,1,0:T(8,128)(2,1)} %param.14) | copy-start | bytes 1572868
  9.7 16.6 %copy-start.3 = (bf16[1,256,1024]{2,1,0:T(8,128)(2,1)S(1)}, bf16[1,256,1024]{2,1,0:T(8,128)(2,1)}, u32[]{:S(2)}) copy-start(bf16[1,256,1024]{2,1,0:T(8,128)(2,1)} %param.15) | copy-start | bytes 1572868
  9.7 16.6 %copy-start.4 = (s32[16]{0:T(128)S(1)}, s32[16]{0:T(128)}, u32[]{:S(2)}) copy-start(s32[16]{0:T(128)} %get-tuple-element.15.sender) | copy-start | bytes 196
  15.2 22.7 %copy-start.5 = (s32[1,4]{1,0:T(1,128)S(1)}, s32[1,4]{1,0:T(1,128)}, u32[]{:S(2)}) copy-start(s32[1,4]{1,0:T(1,128)} %rows_at.1) | copy-start | bytes 52
  15.2 22.7 %copy-start.6 = (s32[1,4]{1,0:T(1,128)S(1)}, s32[1,4]{1,0:T(1,128)}, u32[]{:S(2)}) copy-start(s32[1,4]{1,0:T(1,128)} %cols_at.1) | copy-start | bytes 52
  15.2 22.7 %copy-start.7 = (s32[16]{0:T(128)S(1)}, s32[16]{0:T(128)}, u32[]{:S(2)}) copy-start(s32[16]{0:T(128)} %get-tuple-element.14.slot_of) | copy-start | bytes 196
  15.2 14.6 %all-to-all-start.1 = ((bf16[16,128,128]{2,1,0:T(8,128)(2,1)}), bf16[16,128,128]{2,1,0:T(8,128)(2,1)S(1)}, u32[]{:S(2)}, u32[]{:S(2)}) async-start(bf16[16,128,128]{2,1,0:T(8,128)(2,1)} %pick_blocks.1.earlier), calls=%async_computation.1 | async-start | bytes 1048576 | tf_op jit(solution)/shard_map/all_to_all | solution.py:802
  19.4 4.0 %collective-permute-start = (s32[8,1,2]{2,1,0:T(1,128)S(1)}, s32[8,1,2]{2,1,0:T(1,128)S(1)}, u32[]{:S(2)}, u32[]{:S(2)}) collective-permute-start(s32[8,1,2]{2,1,0:T(1,128)S(1)} %hold.1), channel_id=1, source_target_pairs={{0,1},{1,0},{2,3},{3,2},{4,5},{5,4},{6,7},{7,6},{8,9},{9,8},{10,11... | collective-permute-start | bytes 200 | tf_op jit(solution)/shard_map/ppermute | solution.py:45
  21.6 2.8 %collective-permute-start.1 = (s32[8,1,2]{2,1,0:T(1,128)S(1)}, s32[8,1,2]{2,1,0:T(1,128)S(1)}, u32[]{:S(2)}, u32[]{:S(2)}) collective-permute-start(s32[8,1,2]{2,1,0:T(1,128)S(1)} %hold.1), channel_id=1, source_target_pairs={{0,2},{1,3},{2,0},{3,1},{4,6},{5,7},{6,4},{7,5},{8,10},{9,11},{10,... | collective-permute-start | bytes 200 | tf_op jit(solution)/shard_map/ppermute | solution.py:45
  22.8 3.3 %collective-permute-start.2 = (s32[8,1,2]{2,1,0:T(1,128)S(1)}, s32[8,1,2]{2,1,0:T(1,128)S(1)}, u32[]{:S(2)}, u32[]{:S(2)}) collective-permute-start(s32[8,1,2]{2,1,0:T(1,128)S(1)} %hold.1), channel_id=1, source_target_pairs={{0,3},{1,2},{2,1},{3,0},{4,7},{5,6},{6,5},{7,4},{8,11},{9,10},{10,... | collective-permute-start | bytes 200 | tf_op jit(solution)/shard_map/ppermute | solution.py:45
  29.8 23.0 %all-to-all-start.3 = ((bf16[16,128,128]{2,1,0:T(8,128)(2,1)}), bf16[16,128,128]{2,1,0:T(8,128)(2,1)S(1)}, u32[]{:S(2)}, u32[]{:S(2)}) async-start(bf16[16,128,128]{2,1,0:T(8,128)(2,1)} %prepare.1), calls=%async_computation.3 | async-start | bytes 1048576 | tf_op jit(solution)/shard_map/all_to_all | solution.py:814
  37.9 20.6 %copy-start.1 = (bf16[32,128,128]{2,1,0:T(8,128)(2,1)S(1)}, bf16[32,128,128]{2,1,0:T(8,128)(2,1)}, u32[]{:S(2)}) copy-start(bf16[32,128,128]{2,1,0:T(8,128)(2,1)} %template_var.1) | copy-start | bytes 3145732
  52.7 22.2 %all-to-all-start.2 = ((bf16[32,72,128]{2,1,0:T(8,128)(2,1)}), bf16[32,72,128]{2,1,0:T(8,128)(2,1)S(1)}, u32[]{:S(2)}, u32[]{:S(2)}) async-start(bf16[32,72,128]{2,1,0:T(8,128)(2,1)} %get-tuple-element.17.payload), calls=%async_computation.2 | async-start | bytes 1179648 | tf_op jit(solution)/shard_map/all_to_all | solution.py:835
  58.5 19.2 %copy-start.10 = (f32[1,21]{1,0:T(1,128)S(1)}, f32[1,21]{1,0:T(1,128)}, u32[]{:S(2)}) copy-start(f32[1,21]{1,0:T(1,128)} %param.23) | copy-start | bytes 256
  58.5 19.3 %copy-start.11 = (f32[1,21]{1,0:T(1,128)S(1)}, f32[1,21]{1,0:T(1,128)}, u32[]{:S(2)}) copy-start(f32[1,21]{1,0:T(1,128)} %param.22) | copy-start | bytes 256
  59.8 15.2 %collective-permute-start.3 = (bf16[32,32,128]{2,1,0:T(8,128)(2,1)S(1)}, bf16[32,32,128]{2,1,0:T(8,128)(2,1)S(1)}, u32[]{:S(2)}, u32[]{:S(2)}) collective-permute-start(bf16[32,32,128]{2,1,0:T(8,128)(2,1)S(1)} %bitcast.22), channel_id=1, source_target_pairs={{0,2},{2,0},{1,3},{3,1},{4,6},{6,4},{5,7},{7,5},{8,10},{10,8},{9,1... | collective-permute-start | bytes 786440 | tf_op jit(solution)/shard_map/ppermute | solution.py:843
  76.4 7.4 %collective-permute-start.4 = (bf16[32,32,128]{2,1,0:T(8,128)(2,1)S(1)}, bf16[32,32,128]{2,1,0:T(8,128)(2,1)S(1)}, u32[]{:S(2)}, u32[]{:S(2)}) collective-permute-start(bf16[32,32,128]{2,1,0:T(8,128)(2,1)S(1)} %combine.1.refs_0_), channel_id=1, source_target_pairs={{0,2},{1,3},{2,0},{3,1},{4,6},{5,7},{6,4},{7,5},{8,10},{9,11},{10,... | collective-permute-start | bytes 786440 | tf_op jit(solution)/shard_map/ppermute | solution.py:848
  78.0 10.4 %collective-permute-start.6 = (bf16[32,32,128]{2,1,0:T(8,128)(2,1)S(1)}, bf16[32,32,128]{2,1,0:T(8,128)(2,1)S(1)}, u32[]{:S(2)}, u32[]{:S(2)}) collective-permute-start(bf16[32,32,128]{2,1,0:T(8,128)(2,1)S(1)} %combine.1.refs_0_), channel_id=1, source_target_pairs={{0,1},{1,0},{2,3},{3,2},{4,5},{5,4},{6,7},{7,6},{8,9},{9,8},{10,11... | collective-permute-start | bytes 786440 | tf_op jit(solution)/shard_map/ppermute | solution.py:848
  83.9 6.3 %collective-permute-start.5 = (bf16[32,32,128]{2,1,0:T(8,128)(2,1)S(1)}, bf16[32,32,128]{2,1,0:T(8,128)(2,1)S(1)}, u32[]{:S(2)}, u32[]{:S(2)}) collective-permute-start(bf16[32,32,128]{2,1,0:T(8,128)(2,1)S(1)} %collective-permute-done.4.refs_2_), channel_id=1, source_target_pairs={{0,1},{1,0},{2,3},{3,2},{4,5},{5,4},{6,7},{7,6},{8,9},{9,8},{10,11... | collective-permute-start | bytes 786440 | tf_op jit(solution)/shard_map/ppermute | solution.py:848

commit v10 on v9

--- a/solution.py
+++ b/solution.py
@@ -401,22 +401,29 @@
                 ] = made[2 * q + a - b]
 
     step = side - taps + 1
-    for q in range(pairs):
+    joint = 4
+    for q in range(0, pairs, joint):
+        last = min(q + joint, pairs)
         lhs = jnp.concatenate(
             [
                 jnp.concatenate(
-                    [frames[c, a, q : q + rows_half, :].astype(bf16) for a in range(2)], axis=1
+                    [
+                        frames[c, a, p : p + rows_half, :].astype(bf16)
+                        for p in range(q, last)
+                        for a in range(2)
+                    ],
+                    axis=1,
                 )
                 for c in range(wins)
             ],
             axis=0,
         )
         out = jnp.dot(
-            lhs, bands[q * 2 * side : (q + 1) * 2 * side, :], preferred_element_type=f32
+            lhs, bands[q * 2 * side : last * 2 * side, :], preferred_element_type=f32
         )
         if q:
             out = out + total[...]
-        if q < pairs - 1:
+        if last < pairs:
             total[...] = out
     for c in range(wins):
         rows = out[c * rows_half : (c + 1) * rows_half]
@@ -526,7 +533,7 @@
     half = up(high // 2 + pairs, 8)
     tall = up(taps // 2, 8) + max(high - side + span, 2 * half)
     wins = -(-wide // (side - taps + 1))
-    group = next(g for g in (8, 4, 2, 1) if count % g == 0)
+    group = next(g for g in (20, 8, 4, 2, 1) if count % g == 0)
     return pl.pallas_call(
         functools.partial(fit_body, order=order, capacity=capacity, count=count, taps=taps),
         out_shape=(
@@ -686,7 +693,8 @@
     )(me, table, parts, template_var)
 
 
-def combine_body(me, table, parts, own_var, var_template, *rest, part, capacity):
+def combine_body(me, table, earlier, parts, own_var, var_template, *rest, part, capacity):
+    del earlier
     others = rest[:-3]
     out, total, gain = rest[-3:]
     total[...] = jnp.zeros(total.shape, f32)
@@ -712,12 +720,13 @@
         out[t] = (total[t] * lax.rsqrt(jnp.maximum(variance, 1.0))).astype(bf16)
 
 
-def combine(me, table, parts, own_var, var_template, others, capacity):
+def combine(me, table, earlier, parts, own_var, var_template, others, capacity):
     tract, part, side = own_var.shape
     return pl.pallas_call(
         functools.partial(combine_body, part=part, capacity=capacity),
         out_shape=jax.ShapeDtypeStruct((tract, part, side), bf16),
-        in_specs=[smem(), smem()] + [vmem()] * (3 + len(others)),
+        in_specs=[smem(), smem(), pl.BlockSpec(memory_space=pl.ANY)]
+        + [vmem()] * (3 + len(others)),
         out_specs=vmem(),
         scratch_shapes=[
             pltpu.VMEM((tract + 1, part, side), f32),
@@ -725,7 +734,7 @@
         ],
         compiler_params=pltpu.CompilerParams(vmem_limit_bytes=16 * mib),
         name="combine",
-    )(me, table, parts, own_var, var_template, *others)
+    )(me, table, earlier, parts, own_var, var_template, *others)
 
 
 def join_body(places, *refs, part, count):
@@ -842,7 +851,7 @@
         pairs = [(f, (f + g) % fars) for f in range(fars)]
         others.append(lax.ppermute(other_var[g - 1], "far", pairs))
     scored = score(slot_of, payload, down, over_rev, high, wide, taps, order, capacity)
-    mine = combine(me[None], table, diff_back, own_var, var_template, others, capacity)
+    mine = combine(me[None], table, scored, diff_back, own_var, var_template, others, capacity)
 
     def swap(value, distance):
         return lax.ppermute(value, exposure_axes, [(e, e ^ distance) for e in range(exps)])

time: 91.5 us -> 89.5 us (0.978)
  waiting for transfers between devices: 27.6 us -> 24.7 us
  local copies, waits for them, and re-layouts: 2.31 us -> 3.53 us
    all_to_all x1, waiting for transfers between devices: 13.8 us -> 10.4 us  [local(): lax.all_to_all(payload, ('det',) + exposure_axes, split_axis=0, concat_ax...]
    unnamed x25 -> x27, local copies, waits for them, and re-layouts: 1.38 us -> 2.61 us
where the time goes in v10:
time: 89.5 us; the launch traced here: 89 us
  starting transfers between devices  32.2 us (36%)
  Pallas kernels  27.4 us (31%)
  waiting for transfers between devices  24.7 us (28%)
  local copies, waits for them, and re-layouts  3.53 us (4%)
    pallas_call x1, Pallas kernels, fit_and_subtract(): pl.pallas_call(functools.partial(fit_body, order=order, capacity=capacity...  14.6 us
    all_to_all x1, waiting for transfers between devices, local(): lax.all_to_all(payload, ('det',) + exposure_axes, split_axis=0, concat_ax...  10.4 us
    all_to_all x1, starting transfers between devices, local(): lax.all_to_all(var_late, ('det', 'near'), split_axis=0, concat_axis=0, ti...  8.11 us
    all_to_all x1, starting transfers between devices, local(): lax.all_to_all(request, 'det', split_axis=0, concat_axis=0, tiled=True)  6.37 us
    all_to_all x1, starting transfers between devices, local(): lax.all_to_all(payload, ('det',) + exposure_axes, split_axis=0, concat_ax...  5.8 us
    ppermute x3, waiting for transfers between devices, swap(): lax.ppermute(value, exposure_axes, [(e, e ^ distance) for e in range(exps)])  5.66 us
    all_to_all x1, waiting for transfers between devices, local(): lax.all_to_all(request, 'det', split_axis=0, concat_axis=0, tiled=True)  3.89 us
    ppermute x3, starting transfers between devices, from_exposure(): return lax.ppermute(value, exposure_axes, pairs)  3.7 us
  transfers between devices with their start and end apart: 11, of which 6 were waited for; matrix products, arithmetic and copies ran while one was open for 1% of the time, Pallas kernels for 25%

profile of v10, /device:TPU:1, one launch (start us, length us, event | category | flops | bytes accessed | tf_op | source)
XLA Modules:
  0.0 89.0 jit_solution(18419282960086145589)
XLA Ops:
  0.6 1.4 %route_tables.1 = (s32[16]{0:T(128)}, s32[16]{0:T(128)}, s32[8,1,2]{2,1,0:T(1,128)}) custom-call(s32[1,16]{1,0:T(1,128)} %src.1, s32[1,16]{1,0:T(1,128)} %blk.1), custom_call_target="tpu_custom_call" | custom-call | tf_op jit(solution)/shard_map/route_tables/pallas_call | solution.py:70
  2.0 6.4 %all-to-all-start = ((s32[8,1,2]{2,1,0:T(1,128)}), s32[8,1,2]{2,1,0:T(1,128)S(1)}, u32[]{:S(2)}, u32[]{:S(2)}) async-start(s32[8,1,2]{2,1,0:T(1,128)} %get-tuple-element.13), calls=%async_computation | async-start | bytes 8192 | tf_op jit(solution)/shard_map/all_to_all | solution.py:805
  8.4 1.2 %copy-done.1 = bf16[32,128,128]{2,1,0:T(8,128)(2,1)S(1)} copy-done((bf16[32,128,128]{2,1,0:T(8,128)(2,1)S(1)}, bf16[32,128,128]{2,1,0:T(8,128)(2,1)}, u32[]{:S(2)}) %copy-start.1) | copy-done | bytes 1048600
  9.8 3.9 %all-to-all-done.asked = s32[8,1,2]{2,1,0:T(1,128)S(1)} async-done(((s32[8,1,2]{2,1,0:T(1,128)}), s32[8,1,2]{2,1,0:T(1,128)S(1)}, u32[]{:S(2)}, u32[]{:S(2)}) %all-to-all-start) | async-done | bytes 96 | tf_op jit(solution)/shard_map/all_to_all | solution.py:805
  13.6 1.5 %pick_blocks.1.earlier = bf16[16,128,128]{2,1,0:T(8,128)(2,1)} custom-call(s32[8,1,2]{2,1,0:T(1,128)S(1)} %all-to-all-done.asked, bf16[32,128,128]{2,1,0:T(8,128)(2,1)S(1)} %fetch.1.template), custom_call_target="tpu_custom_call" | custom-call | tf_op jit(solution)/shard_map/pick_blocks/pallas_call | solution.py:114
  15.2 3.6 %all-to-all-start.1 = ((bf16[16,128,128]{2,1,0:T(8,128)(2,1)}), bf16[16,128,128]{2,1,0:T(8,128)(2,1)S(1)}, u32[]{:S(2)}, u32[]{:S(2)}) async-start(bf16[16,128,128]{2,1,0:T(8,128)(2,1)} %pick_blocks.1.earlier), calls=%async_computation.1 | async-start | bytes 1048576 | tf_op jit(solution)/shard_map/all_to_all | solution.py:811
  19.5 3.2 %collective-permute-start.2 = (s32[8,1,2]{2,1,0:T(1,128)S(1)}, s32[8,1,2]{2,1,0:T(1,128)S(1)}, u32[]{:S(2)}, u32[]{:S(2)}) collective-permute-start(s32[8,1,2]{2,1,0:T(1,128)S(1)} %hold.1), channel_id=1, source_target_pairs={{0,3},{1,2},{2,1},{3,0},{4,7},{5,6},{6,5},{7,4},{8,11},{9,10},{10,... | collective-permute-start | bytes 200 | tf_op jit(solution)/shard_map/ppermute | solution.py:45
  23.2 1.1 %collective-permute-done.2 = s32[8,1,2]{2,1,0:T(1,128)S(1)} collective-permute-done((s32[8,1,2]{2,1,0:T(1,128)S(1)}, s32[8,1,2]{2,1,0:T(1,128)S(1)}, u32[]{:S(2)}, u32[]{:S(2)}) %collective-permute-start.2) | collective-permute-done | bytes 96 | tf_op jit(solution)/shard_map/ppermute | solution.py:45
  24.4 1.0 %collective-permute-done.1 = s32[8,1,2]{2,1,0:T(1,128)S(1)} collective-permute-done((s32[8,1,2]{2,1,0:T(1,128)S(1)}, s32[8,1,2]{2,1,0:T(1,128)S(1)}, u32[]{:S(2)}, u32[]{:S(2)}) %collective-permute-start.1) | collective-permute-done | bytes 96 | tf_op jit(solution)/shard_map/ppermute | solution.py:45
  25.7 1.5 %prepare.1 = bf16[16,128,128]{2,1,0:T(8,128)(2,1)} custom-call(s32[16]{0:T(128)S(1)} %copy-done.5, bf16[256,1024]{1,0:T(8,128)(2,1)S(1)} %bitcast.21, bf16[256,1024]{1,0:T(8,128)(2,1)S(1)} %bitcast.19, s32[4,8,2]{2,1,0:T(8,128)S(1)} %copy.35.earlier.table), custom_call_target="tpu_custom_call" | custom-call | bytes 6000000 | tf_op jit(solution)/shard_map/prepare/pallas_call | solution.py:175
  27.2 2.6 %all-to-all-done.1.arrived = bf16[16,128,128]{2,1,0:T(8,128)(2,1)S(1)} async-done(((bf16[16,128,128]{2,1,0:T(8,128)(2,1)}), bf16[16,128,128]{2,1,0:T(8,128)(2,1)S(1)}, u32[]{:S(2)}, u32[]{:S(2)}) %all-to-all-start.1) | async-done | bytes 524320 | tf_op jit(solution)/shard_map/all_to_all | solution.py:811
  29.8 8.1 %all-to-all-start.3 = ((bf16[16,128,128]{2,1,0:T(8,128)(2,1)}), bf16[16,128,128]{2,1,0:T(8,128)(2,1)S(1)}, u32[]{:S(2)}, u32[]{:S(2)}) async-start(bf16[16,128,128]{2,1,0:T(8,128)(2,1)} %prepare.1), calls=%async_computation.3 | async-start | bytes 1048576 | tf_op jit(solution)/shard_map/all_to_all | solution.py:823
  38.0 14.6 %fit_and_subtract.1 = (f32[1,128]{1,0:T(1,128)}, bf16[32,72,128]{2,1,0:T(8,128)(2,1)}) custom-call(s32[16]{0:T(128)S(1)} %copy-done.8, s32[16]{0:T(128)S(1)} %copy-done.5, s32[1,4]{1,0:T(1,128)S(1)} %copy-done.6, s32[1,4]{1,0:T(1,128)S(1)} %copy-done.7, bf16[16,128,128]{2,1,0:T(8,128)(2,1)S(1)} %all-to-all-done.1.arrived, ...), custom_call_target="tpu_custom_call" | custom-call | flops 15000000512 | bytes 8000000 | tf_op jit(solution)/shard_map/fit_and_subtract/pallas_call | solution.py:537
  52.6 5.8 %all-to-all-start.2 = ((bf16[32,72,128]{2,1,0:T(8,128)(2,1)}), bf16[32,72,128]{2,1,0:T(8,128)(2,1)S(1)}, u32[]{:S(2)}, u32[]{:S(2)}) async-start(bf16[32,72,128]{2,1,0:T(8,128)(2,1)} %get-tuple-element.17.payload), calls=%async_computation.2 | async-start | bytes 1179648 | tf_op jit(solution)/shard_map/all_to_all | solution.py:844
  58.6 1.2 %sum_variance.1 = (f32[32,32,128]{2,1,0:T(8,128)S(1)}, bf16[1,32,32,128]{3,2,1,0:T(8,128)(2,1)S(1)}, bf16[32,32,128]{2,1,0:T(8,128)(2,1)S(1)}) custom-call(s32[1]{0:T(128)} %bitcast.1.me, s32[4,8,2]{2,1,0:T(8,128)S(1)} %copy.35.earlier.table, bf16[16,128,128]{2,1,0:T(8,128)(2,1)S(1)} %all-to-all-done.3.parts, bf16[32,128,128]{2,1,0:T(8,128)(2,1)S(1)} %copy-done.2), custom_call_target="tpu_custom_call" | custom-call | bytes 4000000 | tf_op jit(solution)/shard_map/sum_variance/pallas_call | solution.py:677
  59.8 1.5 %collective-permute-start.3 = (bf16[32,32,128]{2,1,0:T(8,128)(2,1)S(1)}, bf16[32,32,128]{2,1,0:T(8,128)(2,1)S(1)}, u32[]{:S(2)}, u32[]{:S(2)}) collective-permute-start(bf16[32,32,128]{2,1,0:T(8,128)(2,1)S(1)} %bitcast.23), channel_id=1, source_target_pairs={{0,2},{2,0},{1,3},{3,1},{4,6},{6,4},{5,7},{7,5},{8,10},{10,8},{9,1... | collective-permute-start | bytes 786440 | tf_op jit(solution)/shard_map/ppermute | solution.py:852
  61.3 3.1 %score.1.earlier = f32[256,1024]{1,0:T(8,128)} custom-call(s32[16]{0:T(128)S(1)} %copy-done.8, bf16[32,72,128]{2,1,0:T(8,128)(2,1)} %get-tuple-element.17.payload, f32[1,256]{1,0:T(1,128)S(1)} %pad.26.down, f32[1,256]{1,0:T(1,128)S(1)} %pad_maximum_fusion.1.over), custom_call_target="tpu_custom_call" | custom-call | flops 2000000000 | bytes 2000000 | tf_op jit(solution)/shard_map/score/pallas_call | solution.py:622
  64.4 10.4 %all-to-all-done.2.parts = bf16[32,72,128]{2,1,0:T(8,128)(2,1)S(1)} async-done(((bf16[32,72,128]{2,1,0:T(8,128)(2,1)}), bf16[32,72,128]{2,1,0:T(8,128)(2,1)S(1)}, u32[]{:S(2)}, u32[]{:S(2)}) %all-to-all-start.2) | async-done | bytes 589856 | tf_op jit(solution)/shard_map/all_to_all | solution.py:844
  74.8 1.2 %copy-done = f32[256,1024]{1,0:T(8,128)S(1)} copy-done((f32[256,1024]{1,0:T(8,128)S(1)}, f32[256,1024]{1,0:T(8,128)}, u32[]{:S(2)}) %copy-start) | copy-done | bytes 1048600
  76.1 1.4 %combine.1.refs_0_ = bf16[32,32,128]{2,1,0:T(8,128)(2,1)S(1)} custom-call(s32[1]{0:T(128)} %bitcast.1.me, s32[4,8,2]{2,1,0:T(8,128)S(1)} %copy.35.earlier.table, f32[256,1024]{1,0:T(8,128)S(1)} %copy-done, bf16[32,72,128]{2,1,0:T(8,128)(2,1)S(1)} %all-to-all-done.2.parts, f32[32,32,128]{2,1,0:T(8,128)S(1)} %get-tuple-element.19.own_var, ...), custom_call_target="tpu_custom_call" | custom-call | tf_op jit(solution)/shard_map/combine/pallas_call | solution.py:725
  77.5 1.3 %collective-permute-start.4 = (bf16[32,32,128]{2,1,0:T(8,128)(2,1)S(1)}, bf16[32,32,128]{2,1,0:T(8,128)(2,1)S(1)}, u32[]{:S(2)}, u32[]{:S(2)}) collective-permute-start(bf16[32,32,128]{2,1,0:T(8,128)(2,1)S(1)} %combine.1.refs_0_), channel_id=1, source_target_pairs={{0,2},{1,3},{2,0},{3,1},{4,6},{5,7},{6,4},{7,5},{8,10},{9,11},{10,... | collective-permute-start | bytes 786440 | tf_op jit(solution)/shard_map/ppermute | solution.py:857
  79.2 5.7 %collective-permute-done.4.refs_2_ = bf16[32,32,128]{2,1,0:T(8,128)(2,1)S(1)} collective-permute-done((bf16[32,32,128]{2,1,0:T(8,128)(2,1)S(1)}, bf16[32,32,128]{2,1,0:T(8,128)(2,1)S(1)}, u32[]{:S(2)}, u32[]{:S(2)}) %collective-permute-start.4) | collective-permute-done | bytes 262176 | tf_op jit(solution)/shard_map/ppermute | solution.py:857
  84.9 1.4 %collective-permute-start.5 = (bf16[32,32,128]{2,1,0:T(8,128)(2,1)S(1)}, bf16[32,32,128]{2,1,0:T(8,128)(2,1)S(1)}, u32[]{:S(2)}, u32[]{:S(2)}) collective-permute-start(bf16[32,32,128]{2,1,0:T(8,128)(2,1)S(1)} %collective-permute-done.4.refs_2_), channel_id=1, source_target_pairs={{0,1},{1,0},{2,3},{3,2},{4,5},{5,4},{6,7},{7,6},{8,9},{9,8},{10,11... | collective-permute-start | bytes 786440 | tf_op jit(solution)/shard_map/ppermute | solution.py:857
  86.4 1.7 %join_parts.2.refs_1_ = f32[32,128,128]{2,1,0:T(8,128)} custom-call(s32[3]{0:T(128)S(1)} %pad_add_fusion.places, bf16[32,32,128]{2,1,0:T(8,128)(2,1)S(1)} %combine.1.refs_0_, bf16[32,32,128]{2,1,0:T(8,128)(2,1)S(1)} %collective-permute-done.6.refs_1_, bf16[32,32,128]{2,1,0:T(8,128)(2,1)S(1)} %collective-permute-done.4.refs_2_), custom_call_target="tpu_custom_call" | custom-call | bytes 9000000 | tf_op jit(solution)/shard_map/join_parts/pallas_call | solution.py:760
  (54 shorter events, 3.2 us)
Async XLA Ops:
  2.0 11.6 %all-to-all-start = ((s32[8,1,2]{2,1,0:T(1,128)}), s32[8,1,2]{2,1,0:T(1,128)S(1)}, u32[]{:S(2)}, u32[]{:S(2)}) async-start(s32[8,1,2]{2,1,0:T(1,128)} %get-tuple-element.13), calls=%async_computation | async-start | bytes 8192 | tf_op jit(solution)/shard_map/all_to_all | solution.py:805
  8.4 1.2 %copy-start.1 = (bf16[32,128,128]{2,1,0:T(8,128)(2,1)S(1)}, bf16[32,128,128]{2,1,0:T(8,128)(2,1)}, u32[]{:S(2)}) copy-start(bf16[32,128,128]{2,1,0:T(8,128)(2,1)} %template.1) | copy-start | bytes 3145732
  9.6 9.2 %copy-start.9 = (bf16[40,21]{0,1:T(8,128)(2,1)S(1)}, bf16[40,21]{0,1:T(8,128)(2,1)}, u32[]{:S(2)}) copy-start(bf16[40,21]{0,1:T(8,128)(2,1)} %param.20) | copy-start | bytes 5044
  9.6 9.3 %copy-start.10 = (bf16[40,21]{0,1:T(8,128)(2,1)S(1)}, bf16[40,21]{0,1:T(8,128)(2,1)}, u32[]{:S(2)}) copy-start(bf16[40,21]{0,1:T(8,128)(2,1)} %param.21) | copy-start | bytes 5044
  9.7 15.9 %copy-start.3 = (bf16[1,256,1024]{2,1,0:T(8,128)(2,1)S(1)}, bf16[1,256,1024]{2,1,0:T(8,128)(2,1)}, u32[]{:S(2)}) copy-start(bf16[1,256,1024]{2,1,0:T(8,128)(2,1)} %param.14) | copy-start | bytes 1572868
  9.7 15.9 %copy-start.4 = (bf16[1,256,1024]{2,1,0:T(8,128)(2,1)S(1)}, bf16[1,256,1024]{2,1,0:T(8,128)(2,1)}, u32[]{:S(2)}) copy-start(bf16[1,256,1024]{2,1,0:T(8,128)(2,1)} %param.15) | copy-start | bytes 1572868
  9.7 15.9 %copy-start.5 = (s32[16]{0:T(128)S(1)}, s32[16]{0:T(128)}, u32[]{:S(2)}) copy-start(s32[16]{0:T(128)} %get-tuple-element.15.sender) | copy-start | bytes 196
  15.2 22.7 %copy-start.6 = (s32[1,4]{1,0:T(1,128)S(1)}, s32[1,4]{1,0:T(1,128)}, u32[]{:S(2)}) copy-start(s32[1,4]{1,0:T(1,128)} %rows_at.1) | copy-start | bytes 52
  15.2 22.7 %copy-start.7 = (s32[1,4]{1,0:T(1,128)S(1)}, s32[1,4]{1,0:T(1,128)}, u32[]{:S(2)}) copy-start(s32[1,4]{1,0:T(1,128)} %cols_at.1) | copy-start | bytes 52
  15.2 22.7 %copy-start.8 = (s32[16]{0:T(128)S(1)}, s32[16]{0:T(128)}, u32[]{:S(2)}) copy-start(s32[16]{0:T(128)} %get-tuple-element.14.slot_of) | copy-start | bytes 196
  15.2 14.6 %all-to-all-start.1 = ((bf16[16,128,128]{2,1,0:T(8,128)(2,1)}), bf16[16,128,128]{2,1,0:T(8,128)(2,1)S(1)}, u32[]{:S(2)}, u32[]{:S(2)}) async-start(bf16[16,128,128]{2,1,0:T(8,128)(2,1)} %pick_blocks.1.earlier), calls=%async_computation.1 | async-start | bytes 1048576 | tf_op jit(solution)/shard_map/all_to_all | solution.py:811
  19.5 4.8 %collective-permute-start.2 = (s32[8,1,2]{2,1,0:T(1,128)S(1)}, s32[8,1,2]{2,1,0:T(1,128)S(1)}, u32[]{:S(2)}, u32[]{:S(2)}) collective-permute-start(s32[8,1,2]{2,1,0:T(1,128)S(1)} %hold.1), channel_id=1, source_target_pairs={{0,3},{1,2},{2,1},{3,0},{4,7},{5,6},{6,5},{7,4},{8,11},{9,10},{10,... | collective-permute-start | bytes 200 | tf_op jit(solution)/shard_map/ppermute | solution.py:45
  22.7 2.7 %collective-permute-start.1 = (s32[8,1,2]{2,1,0:T(1,128)S(1)}, s32[8,1,2]{2,1,0:T(1,128)S(1)}, u32[]{:S(2)}, u32[]{:S(2)}) collective-permute-start(s32[8,1,2]{2,1,0:T(1,128)S(1)} %hold.1), channel_id=1, source_target_pairs={{0,2},{1,3},{2,0},{3,1},{4,6},{5,7},{6,4},{7,5},{8,10},{9,11},{10,... | collective-permute-start | bytes 200 | tf_op jit(solution)/shard_map/ppermute | solution.py:45
  22.9 2.5 %collective-permute-start = (s32[8,1,2]{2,1,0:T(1,128)S(1)}, s32[8,1,2]{2,1,0:T(1,128)S(1)}, u32[]{:S(2)}, u32[]{:S(2)}) collective-permute-start(s32[8,1,2]{2,1,0:T(1,128)S(1)} %hold.1), channel_id=1, source_target_pairs={{0,1},{1,0},{2,3},{3,2},{4,5},{5,4},{6,7},{7,6},{8,9},{9,8},{10,11... | collective-permute-start | bytes 200 | tf_op jit(solution)/shard_map/ppermute | solution.py:45
  29.8 22.8 %all-to-all-start.3 = ((bf16[16,128,128]{2,1,0:T(8,128)(2,1)}), bf16[16,128,128]{2,1,0:T(8,128)(2,1)S(1)}, u32[]{:S(2)}, u32[]{:S(2)}) async-start(bf16[16,128,128]{2,1,0:T(8,128)(2,1)} %prepare.1), calls=%async_computation.3 | async-start | bytes 1048576 | tf_op jit(solution)/shard_map/all_to_all | solution.py:823
  37.9 20.5 %copy-start.11 = (f32[1,21]{1,0:T(1,128)S(1)}, f32[1,21]{1,0:T(1,128)}, u32[]{:S(2)}) copy-start(f32[1,21]{1,0:T(1,128)} %param.23) | copy-start | bytes 256
  37.9 20.6 %copy-start.12 = (f32[1,21]{1,0:T(1,128)S(1)}, f32[1,21]{1,0:T(1,128)}, u32[]{:S(2)}) copy-start(f32[1,21]{1,0:T(1,128)} %param.22) | copy-start | bytes 256
  37.9 20.6 %copy-start.2 = (bf16[32,128,128]{2,1,0:T(8,128)(2,1)S(1)}, bf16[32,128,128]{2,1,0:T(8,128)(2,1)}, u32[]{:S(2)}) copy-start(bf16[32,128,128]{2,1,0:T(8,128)(2,1)} %template_var.1) | copy-start | bytes 3145732
  52.6 22.3 %all-to-all-start.2 = ((bf16[32,72,128]{2,1,0:T(8,128)(2,1)}), bf16[32,72,128]{2,1,0:T(8,128)(2,1)S(1)}, u32[]{:S(2)}, u32[]{:S(2)}) async-start(bf16[32,72,128]{2,1,0:T(8,128)(2,1)} %get-tuple-element.17.payload), calls=%async_computation.2 | async-start | bytes 1179648 | tf_op jit(solution)/shard_map/all_to_all | solution.py:844
  59.8 15.1 %collective-permute-start.3 = (bf16[32,32,128]{2,1,0:T(8,128)(2,1)S(1)}, bf16[32,32,128]{2,1,0:T(8,128)(2,1)S(1)}, u32[]{:S(2)}, u32[]{:S(2)}) collective-permute-start(bf16[32,32,128]{2,1,0:T(8,128)(2,1)S(1)} %bitcast.23), channel_id=1, source_target_pairs={{0,2},{2,0},{1,3},{3,1},{4,6},{6,4},{5,7},{7,5},{8,10},{10,8},{9,1... | collective-permute-start | bytes 786440 | tf_op jit(solution)/shard_map/ppermute | solution.py:852
  74.8 1.2 %copy-start = (f32[256,1024]{1,0:T(8,128)S(1)}, f32[256,1024]{1,0:T(8,128)}, u32[]{:S(2)}) copy-start(f32[256,1024]{1,0:T(8,128)} %score.1.earlier) | copy-start | bytes 3145732
  77.5 7.4 %collective-permute-start.4 = (bf16[32,32,128]{2,1,0:T(8,128)(2,1)S(1)}, bf16[32,32,128]{2,1,0:T(8,128)(2,1)S(1)}, u32[]{:S(2)}, u32[]{:S(2)}) collective-permute-start(bf16[32,32,128]{2,1,0:T(8,128)(2,1)S(1)} %combine.1.refs_0_), channel_id=1, source_target_pairs={{0,2},{1,3},{2,0},{3,1},{4,6},{5,7},{6,4},{7,5},{8,10},{9,11},{10,... | collective-permute-start | bytes 786440 | tf_op jit(solution)/shard_map/ppermute | solution.py:857
  78.8 7.6 %collective-permute-start.6 = (bf16[32,32,128]{2,1,0:T(8,128)(2,1)S(1)}, bf16[32,32,128]{2,1,0:T(8,128)(2,1)S(1)}, u32[]{:S(2)}, u32[]{:S(2)}) collective-permute-start(bf16[32,32,128]{2,1,0:T(8,128)(2,1)S(1)} %combine.1.refs_0_), channel_id=1, source_target_pairs={{0,1},{1,0},{2,3},{3,2},{4,5},{5,4},{6,7},{7,6},{8,9},{9,8},{10,11... | collective-permute-start | bytes 786440 | tf_op jit(solution)/shard_map/ppermute | solution.py:857
  84.9 3.2 %collective-permute-start.5 = (bf16[32,32,128]{2,1,0:T(8,128)(2,1)S(1)}, bf16[32,32,128]{2,1,0:T(8,128)(2,1)S(1)}, u32[]{:S(2)}, u32[]{:S(2)}) collective-permute-start(bf16[32,32,128]{2,1,0:T(8,128)(2,1)S(1)} %collective-permute-done.4.refs_2_), channel_id=1, source_target_pairs={{0,1},{1,0},{2,3},{3,2},{4,5},{5,4},{6,7},{7,6},{8,9},{9,8},{10,11... | collective-permute-start | bytes 786440 | tf_op jit(solution)/shard_map/ppermute | solution.py:857

commit v11 on v10

--- a/solution.py
+++ b/solution.py
@@ -401,7 +401,7 @@
                 ] = made[2 * q + a - b]
 
     step = side - taps + 1
-    joint = 4
+    joint = pairs
     for q in range(0, pairs, joint):
         last = min(q + joint, pairs)
         lhs = jnp.concatenate(
@@ -580,7 +580,10 @@
     return top, (value - top.astype(f32)).astype(bf16)
 
 
-def score_body(slot_of, payload, down, over, out, padded, sideways, *, order, taps, capacity):
+def score_body(
+    slot_of, payload, down, over, out, token, padded, sideways, *, order, taps, capacity
+):
+    token[...] = jnp.zeros(token.shape, f32)
     side = payload.shape[2]
     part = side // len(order)
     high, wide = out.shape
@@ -621,9 +624,12 @@
     span = up(side + taps - 1, 16)
     return pl.pallas_call(
         functools.partial(score_body, order=order, taps=taps, capacity=capacity),
-        out_shape=jax.ShapeDtypeStruct((high, wide), f32),
+        out_shape=(
+            jax.ShapeDtypeStruct((high, wide), f32),
+            jax.ShapeDtypeStruct((8, 128), f32),
+        ),
         in_specs=[smem()] + [vmem()] * 3,
-        out_specs=vmem(),
+        out_specs=(vmem(), vmem()),
         scratch_shapes=[
             pltpu.VMEM((high, wide + side), f32),
             pltpu.VMEM((high - side + span, wide), f32),
@@ -850,8 +856,10 @@
     for g in range(1, fars):
         pairs = [(f, (f + g) % fars) for f in range(fars)]
         others.append(lax.ppermute(other_var[g - 1], "far", pairs))
-    scored = score(slot_of, payload, down, over_rev, high, wide, taps, order, capacity)
-    mine = combine(me[None], table, scored, diff_back, own_var, var_template, others, capacity)
+    scored, token = score(
+        slot_of, payload, down, over_rev, high, wide, taps, order, capacity
+    )
+    mine = combine(me[None], table, token, diff_back, own_var, var_template, others, capacity)
 
     def swap(value, distance):
         return lax.ppermute(value, exposure_axes, [(e, e ^ distance) for e in range(exps)])

time: 89.5 us -> 88.3 us (0.987)
  local copies, waits for them, and re-layouts: 3.53 us -> 2.31 us
    unnamed x27 -> x25, local copies, waits for them, and re-layouts: 2.61 us -> 1.38 us
where the time goes in v11:
time: 88.3 us; the launch traced here: 87.7 us
  starting transfers between devices  32.2 us (36%)
  Pallas kernels  27.4 us (31%)
  waiting for transfers between devices  24.7 us (28%)
  local copies, waits for them, and re-layouts  2.31 us (3%)
    pallas_call x1, Pallas kernels, fit_and_subtract(): pl.pallas_call(functools.partial(fit_body, order=order, capacity=capacity...  14.6 us
    all_to_all x1, waiting for transfers between devices, local(): lax.all_to_all(payload, ('det',) + exposure_axes, split_axis=0, concat_ax...  10.4 us
    all_to_all x1, starting transfers between devices, local(): lax.all_to_all(var_late, ('det', 'near'), split_axis=0, concat_axis=0, ti...  8.11 us
    all_to_all x1, starting transfers between devices, local(): lax.all_to_all(request, 'det', split_axis=0, concat_axis=0, tiled=True)  6.37 us
    all_to_all x1, starting transfers between devices, local(): lax.all_to_all(payload, ('det',) + exposure_axes, split_axis=0, concat_ax...  5.79 us
    ppermute x3, waiting for transfers between devices, swap(): lax.ppermute(value, exposure_axes, [(e, e ^ distance) for e in range(exps)])  5.66 us
    all_to_all x1, waiting for transfers between devices, local(): lax.all_to_all(request, 'det', split_axis=0, concat_axis=0, tiled=True)  3.89 us
    ppermute x3, starting transfers between devices, from_exposure(): return lax.ppermute(value, exposure_axes, pairs)  3.7 us
  transfers between devices with their start and end apart: 11, of which 6 were waited for; matrix products, arithmetic and copies ran while one was open for 1% of the time, Pallas kernels for 25%

profile of v11, /device:TPU:1, one launch (start us, length us, event | category | flops | bytes accessed | tf_op | source)
XLA Modules:
  0.0 87.7 jit_solution(15656945426324010082)
XLA Ops:
  0.6 1.4 %route_tables.1 = (s32[16]{0:T(128)}, s32[16]{0:T(128)}, s32[8,1,2]{2,1,0:T(1,128)}) custom-call(s32[1,16]{1,0:T(1,128)} %src.1, s32[1,16]{1,0:T(1,128)} %blk.1), custom_call_target="tpu_custom_call" | custom-call | tf_op jit(solution)/shard_map/route_tables/pallas_call | solution.py:70
  2.0 6.4 %all-to-all-start = ((s32[8,1,2]{2,1,0:T(1,128)}), s32[8,1,2]{2,1,0:T(1,128)S(1)}, u32[]{:S(2)}, u32[]{:S(2)}) async-start(s32[8,1,2]{2,1,0:T(1,128)} %get-tuple-element.15), calls=%async_computation | async-start | bytes 8192 | tf_op jit(solution)/shard_map/all_to_all | solution.py:811
  8.4 1.2 %copy-done = bf16[32,128,128]{2,1,0:T(8,128)(2,1)S(1)} copy-done((bf16[32,128,128]{2,1,0:T(8,128)(2,1)S(1)}, bf16[32,128,128]{2,1,0:T(8,128)(2,1)}, u32[]{:S(2)}) %copy-start) | copy-done | bytes 1048600
  9.8 3.9 %all-to-all-done.asked = s32[8,1,2]{2,1,0:T(1,128)S(1)} async-done(((s32[8,1,2]{2,1,0:T(1,128)}), s32[8,1,2]{2,1,0:T(1,128)S(1)}, u32[]{:S(2)}, u32[]{:S(2)}) %all-to-all-start) | async-done | bytes 96 | tf_op jit(solution)/shard_map/all_to_all | solution.py:811
  13.6 1.5 %pick_blocks.1.earlier = bf16[16,128,128]{2,1,0:T(8,128)(2,1)} custom-call(s32[8,1,2]{2,1,0:T(1,128)S(1)} %all-to-all-done.asked, bf16[32,128,128]{2,1,0:T(8,128)(2,1)S(1)} %fetch.1.template), custom_call_target="tpu_custom_call" | custom-call | tf_op jit(solution)/shard_map/pick_blocks/pallas_call | solution.py:114
  15.2 3.6 %all-to-all-start.1 = ((bf16[16,128,128]{2,1,0:T(8,128)(2,1)}), bf16[16,128,128]{2,1,0:T(8,128)(2,1)S(1)}, u32[]{:S(2)}, u32[]{:S(2)}) async-start(bf16[16,128,128]{2,1,0:T(8,128)(2,1)} %pick_blocks.1.earlier), calls=%async_computation.1 | async-start | bytes 1048576 | tf_op jit(solution)/shard_map/all_to_all | solution.py:817
  19.5 3.2 %collective-permute-start.2 = (s32[8,1,2]{2,1,0:T(1,128)S(1)}, s32[8,1,2]{2,1,0:T(1,128)S(1)}, u32[]{:S(2)}, u32[]{:S(2)}) collective-permute-start(s32[8,1,2]{2,1,0:T(1,128)S(1)} %hold.1), channel_id=1, source_target_pairs={{0,3},{1,2},{2,1},{3,0},{4,7},{5,6},{6,5},{7,4},{8,11},{9,10},{10,... | collective-permute-start | bytes 200 | tf_op jit(solution)/shard_map/ppermute | solution.py:45
  23.2 1.1 %collective-permute-done.2 = s32[8,1,2]{2,1,0:T(1,128)S(1)} collective-permute-done((s32[8,1,2]{2,1,0:T(1,128)S(1)}, s32[8,1,2]{2,1,0:T(1,128)S(1)}, u32[]{:S(2)}, u32[]{:S(2)}) %collective-permute-start.2) | collective-permute-done | bytes 96 | tf_op jit(solution)/shard_map/ppermute | solution.py:45
  24.4 1.0 %collective-permute-done.1 = s32[8,1,2]{2,1,0:T(1,128)S(1)} collective-permute-done((s32[8,1,2]{2,1,0:T(1,128)S(1)}, s32[8,1,2]{2,1,0:T(1,128)S(1)}, u32[]{:S(2)}, u32[]{:S(2)}) %collective-permute-start.1) | collective-permute-done | bytes 96 | tf_op jit(solution)/shard_map/ppermute | solution.py:45
  25.7 1.5 %prepare.1 = bf16[16,128,128]{2,1,0:T(8,128)(2,1)} custom-call(s32[16]{0:T(128)S(1)} %copy-done.4, bf16[256,1024]{1,0:T(8,128)(2,1)S(1)} %bitcast.20, bf16[256,1024]{1,0:T(8,128)(2,1)S(1)} %bitcast.18, s32[4,8,2]{2,1,0:T(8,128)S(1)} %copy.35.earlier.table), custom_call_target="tpu_custom_call" | custom-call | bytes 6000000 | tf_op jit(solution)/shard_map/prepare/pallas_call | solution.py:175
  27.2 2.6 %all-to-all-done.1.arrived = bf16[16,128,128]{2,1,0:T(8,128)(2,1)S(1)} async-done(((bf16[16,128,128]{2,1,0:T(8,128)(2,1)}), bf16[16,128,128]{2,1,0:T(8,128)(2,1)S(1)}, u32[]{:S(2)}, u32[]{:S(2)}) %all-to-all-start.1) | async-done | bytes 524320 | tf_op jit(solution)/shard_map/all_to_all | solution.py:817
  29.8 8.1 %all-to-all-start.3 = ((bf16[16,128,128]{2,1,0:T(8,128)(2,1)}), bf16[16,128,128]{2,1,0:T(8,128)(2,1)S(1)}, u32[]{:S(2)}, u32[]{:S(2)}) async-start(bf16[16,128,128]{2,1,0:T(8,128)(2,1)} %prepare.1), calls=%async_computation.3 | async-start | bytes 1048576 | tf_op jit(solution)/shard_map/all_to_all | solution.py:829
  38.0 14.6 %fit_and_subtract.1 = (f32[1,128]{1,0:T(1,128)}, bf16[32,72,128]{2,1,0:T(8,128)(2,1)}) custom-call(s32[16]{0:T(128)S(1)} %copy-done.7, s32[16]{0:T(128)S(1)} %copy-done.4, s32[1,4]{1,0:T(1,128)S(1)} %copy-done.5, s32[1,4]{1,0:T(1,128)S(1)} %copy-done.6, bf16[16,128,128]{2,1,0:T(8,128)(2,1)S(1)} %all-to-all-done.1.arrived, ...), custom_call_target="tpu_custom_call" | custom-call | flops 15000000512 | bytes 8000000 | tf_op jit(solution)/shard_map/fit_and_subtract/pallas_call | solution.py:537
  52.6 5.8 %all-to-all-start.2 = ((bf16[32,72,128]{2,1,0:T(8,128)(2,1)}), bf16[32,72,128]{2,1,0:T(8,128)(2,1)S(1)}, u32[]{:S(2)}, u32[]{:S(2)}) async-start(bf16[32,72,128]{2,1,0:T(8,128)(2,1)} %get-tuple-element.19.payload), calls=%async_computation.2 | async-start | bytes 1179648 | tf_op jit(solution)/shard_map/all_to_all | solution.py:850
  58.6 1.2 %sum_variance.1 = (f32[32,32,128]{2,1,0:T(8,128)S(1)}, bf16[1,32,32,128]{3,2,1,0:T(8,128)(2,1)S(1)}, bf16[32,32,128]{2,1,0:T(8,128)(2,1)S(1)}) custom-call(s32[1]{0:T(128)} %bitcast.1.me, s32[4,8,2]{2,1,0:T(8,128)S(1)} %copy.35.earlier.table, bf16[16,128,128]{2,1,0:T(8,128)(2,1)S(1)} %all-to-all-done.3.parts, bf16[32,128,128]{2,1,0:T(8,128)(2,1)S(1)} %copy-done.1), custom_call_target="tpu_custom_call" | custom-call | bytes 4000000 | tf_op jit(solution)/shard_map/sum_variance/pallas_call | solution.py:683
  59.8 1.5 %collective-permute-start.3 = (bf16[32,32,128]{2,1,0:T(8,128)(2,1)S(1)}, bf16[32,32,128]{2,1,0:T(8,128)(2,1)S(1)}, u32[]{:S(2)}, u32[]{:S(2)}) collective-permute-start(bf16[32,32,128]{2,1,0:T(8,128)(2,1)S(1)} %bitcast.22), channel_id=1, source_target_pairs={{0,2},{2,0},{1,3},{3,1},{4,6},{6,4},{5,7},{7,5},{8,10},{10,8},{9,1... | collective-permute-start | bytes 786440 | tf_op jit(solution)/shard_map/ppermute | solution.py:858
  61.3 3.1 %score.1 = (f32[256,1024]{1,0:T(8,128)}, f32[8,128]{1,0:T(8,128)S(1)}) custom-call(s32[16]{0:T(128)S(1)} %copy-done.7, bf16[32,72,128]{2,1,0:T(8,128)(2,1)} %get-tuple-element.19.payload, f32[1,256]{1,0:T(1,128)S(1)} %pad.26.down, f32[1,256]{1,0:T(1,128)S(1)} %pad_maximum_fusion.1.over), custom_call_target="tpu_custom_call" | custom-call | flops 2000000000 | bytes 2000000 | tf_op jit(solution)/shard_map/score/pallas_call | solution.py:625
  64.4 10.4 %all-to-all-done.2.parts = bf16[32,72,128]{2,1,0:T(8,128)(2,1)S(1)} async-done(((bf16[32,72,128]{2,1,0:T(8,128)(2,1)}), bf16[32,72,128]{2,1,0:T(8,128)(2,1)S(1)}, u32[]{:S(2)}, u32[]{:S(2)}) %all-to-all-start.2) | async-done | bytes 589856 | tf_op jit(solution)/shard_map/all_to_all | solution.py:850
  74.8 1.4 %combine.1.refs_0_ = bf16[32,32,128]{2,1,0:T(8,128)(2,1)S(1)} custom-call(s32[1]{0:T(128)} %bitcast.1.me, s32[4,8,2]{2,1,0:T(8,128)S(1)} %copy.35.earlier.table, f32[8,128]{1,0:T(8,128)S(1)} %get-tuple-element.20.earlier, bf16[32,72,128]{2,1,0:T(8,128)(2,1)S(1)} %all-to-all-done.2.parts, f32[32,32,128]{2,1,0:T(8,128)S(1)} %get-tuple-element.22.own_var, ...), custom_call_target="tpu_custom_call" | custom-call | tf_op jit(solution)/shard_map/combine/pallas_call | solution.py:731
  76.3 1.3 %collective-permute-start.4 = (bf16[32,32,128]{2,1,0:T(8,128)(2,1)S(1)}, bf16[32,32,128]{2,1,0:T(8,128)(2,1)S(1)}, u32[]{:S(2)}, u32[]{:S(2)}) collective-permute-start(bf16[32,32,128]{2,1,0:T(8,128)(2,1)S(1)} %combine.1.refs_0_), channel_id=1, source_target_pairs={{0,2},{1,3},{2,0},{3,1},{4,6},{5,7},{6,4},{7,5},{8,10},{9,11},{10,... | collective-permute-start | bytes 786440 | tf_op jit(solution)/shard_map/ppermute | solution.py:865
  78.0 5.7 %collective-permute-done.4.refs_2_ = bf16[32,32,128]{2,1,0:T(8,128)(2,1)S(1)} collective-permute-done((bf16[32,32,128]{2,1,0:T(8,128)(2,1)S(1)}, bf16[32,32,128]{2,1,0:T(8,128)(2,1)S(1)}, u32[]{:S(2)}, u32[]{:S(2)}) %collective-permute-start.4) | collective-permute-done | bytes 262176 | tf_op jit(solution)/shard_map/ppermute | solution.py:865
  83.7 1.4 %collective-permute-start.5 = (bf16[32,32,128]{2,1,0:T(8,128)(2,1)S(1)}, bf16[32,32,128]{2,1,0:T(8,128)(2,1)S(1)}, u32[]{:S(2)}, u32[]{:S(2)}) collective-permute-start(bf16[32,32,128]{2,1,0:T(8,128)(2,1)S(1)} %collective-permute-done.4.refs_2_), channel_id=1, source_target_pairs={{0,1},{1,0},{2,3},{3,2},{4,5},{5,4},{6,7},{7,6},{8,9},{9,8},{10,11... | collective-permute-start | bytes 786440 | tf_op jit(solution)/shard_map/ppermute | solution.py:865
  85.1 1.7 %join_parts.2.refs_1_ = f32[32,128,128]{2,1,0:T(8,128)} custom-call(s32[3]{0:T(128)S(1)} %pad_add_fusion.places, bf16[32,32,128]{2,1,0:T(8,128)(2,1)S(1)} %combine.1.refs_0_, bf16[32,32,128]{2,1,0:T(8,128)(2,1)S(1)} %collective-permute-done.6.refs_1_, bf16[32,32,128]{2,1,0:T(8,128)(2,1)S(1)} %collective-permute-done.4.refs_2_), custom_call_target="tpu_custom_call" | custom-call | bytes 9000000 | tf_op jit(solution)/shard_map/join_parts/pallas_call | solution.py:766
  86.9 0.8 join_parts.3
  (52 shorter events, 2.4 us)
Async XLA Ops:
  2.0 11.6 %all-to-all-start = ((s32[8,1,2]{2,1,0:T(1,128)}), s32[8,1,2]{2,1,0:T(1,128)S(1)}, u32[]{:S(2)}, u32[]{:S(2)}) async-start(s32[8,1,2]{2,1,0:T(1,128)} %get-tuple-element.15), calls=%async_computation | async-start | bytes 8192 | tf_op jit(solution)/shard_map/all_to_all | solution.py:811
  8.4 1.2 %copy-start = (bf16[32,128,128]{2,1,0:T(8,128)(2,1)S(1)}, bf16[32,128,128]{2,1,0:T(8,128)(2,1)}, u32[]{:S(2)}) copy-start(bf16[32,128,128]{2,1,0:T(8,128)(2,1)} %template.1) | copy-start | bytes 3145732
  9.6 9.2 %copy-start.8 = (bf16[40,21]{0,1:T(8,128)(2,1)S(1)}, bf16[40,21]{0,1:T(8,128)(2,1)}, u32[]{:S(2)}) copy-start(bf16[40,21]{0,1:T(8,128)(2,1)} %param.20) | copy-start | bytes 5044
  9.6 9.3 %copy-start.9 = (bf16[40,21]{0,1:T(8,128)(2,1)S(1)}, bf16[40,21]{0,1:T(8,128)(2,1)}, u32[]{:S(2)}) copy-start(bf16[40,21]{0,1:T(8,128)(2,1)} %param.21) | copy-start | bytes 5044
  9.7 15.9 %copy-start.2 = (bf16[1,256,1024]{2,1,0:T(8,128)(2,1)S(1)}, bf16[1,256,1024]{2,1,0:T(8,128)(2,1)}, u32[]{:S(2)}) copy-start(bf16[1,256,1024]{2,1,0:T(8,128)(2,1)} %param.14) | copy-start | bytes 1572868
  9.7 15.9 %copy-start.3 = (bf16[1,256,1024]{2,1,0:T(8,128)(2,1)S(1)}, bf16[1,256,1024]{2,1,0:T(8,128)(2,1)}, u32[]{:S(2)}) copy-start(bf16[1,256,1024]{2,1,0:T(8,128)(2,1)} %param.15) | copy-start | bytes 1572868
  9.7 15.9 %copy-start.4 = (s32[16]{0:T(128)S(1)}, s32[16]{0:T(128)}, u32[]{:S(2)}) copy-start(s32[16]{0:T(128)} %get-tuple-element.17.sender) | copy-start | bytes 196
  15.2 22.7 %copy-start.5 = (s32[1,4]{1,0:T(1,128)S(1)}, s32[1,4]{1,0:T(1,128)}, u32[]{:S(2)}) copy-start(s32[1,4]{1,0:T(1,128)} %rows_at.1) | copy-start | bytes 52
  15.2 22.7 %copy-start.6 = (s32[1,4]{1,0:T(1,128)S(1)}, s32[1,4]{1,0:T(1,128)}, u32[]{:S(2)}) copy-start(s32[1,4]{1,0:T(1,128)} %cols_at.1) | copy-start | bytes 52
  15.2 22.7 %copy-start.7 = (s32[16]{0:T(128)S(1)}, s32[16]{0:T(128)}, u32[]{:S(2)}) copy-start(s32[16]{0:T(128)} %get-tuple-element.16.slot_of) | copy-start | bytes 196
  15.2 14.6 %all-to-all-start.1 = ((bf16[16,128,128]{2,1,0:T(8,128)(2,1)}), bf16[16,128,128]{2,1,0:T(8,128)(2,1)S(1)}, u32[]{:S(2)}, u32[]{:S(2)}) async-start(bf16[16,128,128]{2,1,0:T(8,128)(2,1)} %pick_blocks.1.earlier), calls=%async_computation.1 | async-start | bytes 1048576 | tf_op jit(solution)/shard_map/all_to_all | solution.py:817
  19.5 4.8 %collective-permute-start.2 = (s32[8,1,2]{2,1,0:T(1,128)S(1)}, s32[8,1,2]{2,1,0:T(1,128)S(1)}, u32[]{:S(2)}, u32[]{:S(2)}) collective-permute-start(s32[8,1,2]{2,1,0:T(1,128)S(1)} %hold.1), channel_id=1, source_target_pairs={{0,3},{1,2},{2,1},{3,0},{4,7},{5,6},{6,5},{7,4},{8,11},{9,10},{10,... | collective-permute-start | bytes 200 | tf_op jit(solution)/shard_map/ppermute | solution.py:45
  22.7 2.7 %collective-permute-start.1 = (s32[8,1,2]{2,1,0:T(1,128)S(1)}, s32[8,1,2]{2,1,0:T(1,128)S(1)}, u32[]{:S(2)}, u32[]{:S(2)}) collective-permute-start(s32[8,1,2]{2,1,0:T(1,128)S(1)} %hold.1), channel_id=1, source_target_pairs={{0,2},{1,3},{2,0},{3,1},{4,6},{5,7},{6,4},{7,5},{8,10},{9,11},{10,... | collective-permute-start | bytes 200 | tf_op jit(solution)/shard_map/ppermute | solution.py:45
  22.9 2.5 %collective-permute-start = (s32[8,1,2]{2,1,0:T(1,128)S(1)}, s32[8,1,2]{2,1,0:T(1,128)S(1)}, u32[]{:S(2)}, u32[]{:S(2)}) collective-permute-start(s32[8,1,2]{2,1,0:T(1,128)S(1)} %hold.1), channel_id=1, source_target_pairs={{0,1},{1,0},{2,3},{3,2},{4,5},{5,4},{6,7},{7,6},{8,9},{9,8},{10,11... | collective-permute-start | bytes 200 | tf_op jit(solution)/shard_map/ppermute | solution.py:45
  29.8 22.8 %all-to-all-start.3 = ((bf16[16,128,128]{2,1,0:T(8,128)(2,1)}), bf16[16,128,128]{2,1,0:T(8,128)(2,1)S(1)}, u32[]{:S(2)}, u32[]{:S(2)}) async-start(bf16[16,128,128]{2,1,0:T(8,128)(2,1)} %prepare.1), calls=%async_computation.3 | async-start | bytes 1048576 | tf_op jit(solution)/shard_map/all_to_all | solution.py:829
  37.9 20.5 %copy-start.10 = (f32[1,21]{1,0:T(1,128)S(1)}, f32[1,21]{1,0:T(1,128)}, u32[]{:S(2)}) copy-start(f32[1,21]{1,0:T(1,128)} %param.23) | copy-start | bytes 256
  37.9 20.6 %copy-start.11 = (f32[1,21]{1,0:T(1,128)S(1)}, f32[1,21]{1,0:T(1,128)}, u32[]{:S(2)}) copy-start(f32[1,21]{1,0:T(1,128)} %param.22) | copy-start | bytes 256
  37.9 20.6 %copy-start.1 = (bf16[32,128,128]{2,1,0:T(8,128)(2,1)S(1)}, bf16[32,128,128]{2,1,0:T(8,128)(2,1)}, u32[]{:S(2)}) copy-start(bf16[32,128,128]{2,1,0:T(8,128)(2,1)} %template_var.1) | copy-start | bytes 3145732
  52.6 22.3 %all-to-all-start.2 = ((bf16[32,72,128]{2,1,0:T(8,128)(2,1)}), bf16[32,72,128]{2,1,0:T(8,128)(2,1)S(1)}, u32[]{:S(2)}, u32[]{:S(2)}) async-start(bf16[32,72,128]{2,1,0:T(8,128)(2,1)} %get-tuple-element.19.payload), calls=%async_computation.2 | async-start | bytes 1179648 | tf_op jit(solution)/shard_map/all_to_all | solution.py:850
  59.8 15.1 %collective-permute-start.3 = (bf16[32,32,128]{2,1,0:T(8,128)(2,1)S(1)}, bf16[32,32,128]{2,1,0:T(8,128)(2,1)S(1)}, u32[]{:S(2)}, u32[]{:S(2)}) collective-permute-start(bf16[32,32,128]{2,1,0:T(8,128)(2,1)S(1)} %bitcast.22), channel_id=1, source_target_pairs={{0,2},{2,0},{1,3},{3,1},{4,6},{6,4},{5,7},{7,5},{8,10},{10,8},{9,1... | collective-permute-start | bytes 786440 | tf_op jit(solution)/shard_map/ppermute | solution.py:858
  76.3 7.4 %collective-permute-start.4 = (bf16[32,32,128]{2,1,0:T(8,128)(2,1)S(1)}, bf16[32,32,128]{2,1,0:T(8,128)(2,1)S(1)}, u32[]{:S(2)}, u32[]{:S(2)}) collective-permute-start(bf16[32,32,128]{2,1,0:T(8,128)(2,1)S(1)} %combine.1.refs_0_), channel_id=1, source_target_pairs={{0,2},{1,3},{2,0},{3,1},{4,6},{5,7},{6,4},{7,5},{8,10},{9,11},{10,... | collective-permute-start | bytes 786440 | tf_op jit(solution)/shard_map/ppermute | solution.py:865
  77.6 7.6 %collective-permute-start.6 = (bf16[32,32,128]{2,1,0:T(8,128)(2,1)S(1)}, bf16[32,32,128]{2,1,0:T(8,128)(2,1)S(1)}, u32[]{:S(2)}, u32[]{:S(2)}) collective-permute-start(bf16[32,32,128]{2,1,0:T(8,128)(2,1)S(1)} %combine.1.refs_0_), channel_id=1, source_target_pairs={{0,1},{1,0},{2,3},{3,2},{4,5},{5,4},{6,7},{7,6},{8,9},{9,8},{10,11... | collective-permute-start | bytes 786440 | tf_op jit(solution)/shard_map/ppermute | solution.py:865
  83.7 3.2 %collective-permute-start.5 = (bf16[32,32,128]{2,1,0:T(8,128)(2,1)S(1)}, bf16[32,32,128]{2,1,0:T(8,128)(2,1)S(1)}, u32[]{:S(2)}, u32[]{:S(2)}) collective-permute-start(bf16[32,32,128]{2,1,0:T(8,128)(2,1)S(1)} %collective-permute-done.4.refs_2_), channel_id=1, source_target_pairs={{0,1},{1,0},{2,3},{3,2},{4,5},{5,4},{6,7},{7,6},{8,9},{9,8},{10,11... | collective-permute-start | bytes 786440 | tf_op jit(solution)/shard_map/ppermute | solution.py:865

commit v12 on v11

--- a/solution.py
+++ b/solution.py
@@ -251,19 +251,23 @@
         design[place, :] = root * cut_image(science, top, left)
     design[lines_all * pitch :, :] = jnp.zeros((design.shape[0] - lines_all * pitch, side), f32)
 
+    step = side - taps + 1
+    for c in range(windows.shape[0]):
+        left = first_col + c * step
+        window[...] = frame[first_row : first_row + window.shape[0], left : left + side]
+        for parity in range(2):
+            place = pl.ds(parity, windows.shape[2], stride=2)
+            windows[c, parity] = window[place, :]
+
     group = vert.shape[0]
-    step = side - taps + 1
-    starts = list(range(0, count, group))
-    for turn, k in enumerate(starts):
-        for c in range(turn, windows.shape[0], len(starts)):
-            left = first_col + c * step
-            window[...] = frame[first_row : first_row + window.shape[0], left : left + side]
-            for parity in range(2):
-                place = pl.ds(parity, windows.shape[2], stride=2)
-                windows[c, parity] = window[place, :]
+
+    def passes(turn, carry):
+        k = pl.multiple_of(turn * group, group)
+        col_rows = col[pl.ds(k, group), :]
+        row_rows = row_rev[pl.ds(k, group), :]
         filters = []
         for a in range(group):
-            line = jnp.broadcast_to(col[k + a : k + a + 1, :], (side, side))
+            line = jnp.broadcast_to(col_rows[a : a + 1, :], (side, side))
             line = pltpu.roll(line, 0, 1, stride=1, stride_axis=0)
             first = jnp.where(lane >= sub, line, 0.0).astype(bf16)
             second = jnp.where(lane < sub, line, 0.0).astype(bf16)
@@ -276,13 +280,16 @@
             for a in range(group):
                 vert[a, s * side : (s + 1) * side, :] = out[a * side : (a + 1) * side]
         for a in range(group):
-            line = jnp.broadcast_to(row_rev[k + a : k + a + 1, :], (side, side))
+            line = jnp.broadcast_to(row_rows[a : a + 1, :], (side, side))
             line = pltpu.roll(line, 0, 1, stride=1, stride_axis=0)
             first = jnp.where(lane <= sub, line, 0.0).astype(bf16)
             second = jnp.where(lane > sub, line, 0.0).astype(bf16)
             band = jnp.concatenate([first, second], axis=0)
             out = jnp.dot(vert[a], band, preferred_element_type=f32)
             design[pl.ds(k + a, lines_all, stride=pitch), :] = out * roots[...]
+        return carry
+
+    lax.fori_loop(0, count // group, passes, 0)
 
     lines = 16
     sets = 4
@@ -401,7 +408,7 @@
                 ] = made[2 * q + a - b]
 
     step = side - taps + 1
-    joint = pairs
+    joint = 4
     for q in range(0, pairs, joint):
         last = min(q + joint, pairs)
         lhs = jnp.concatenate(
@@ -533,7 +540,7 @@
     half = up(high // 2 + pairs, 8)
     tall = up(taps // 2, 8) + max(high - side + span, 2 * half)
     wins = -(-wide // (side - taps + 1))
-    group = next(g for g in (20, 8, 4, 2, 1) if count % g == 0)
+    group = next(g for g in (8, 4, 2, 1) if count % g == 0)
     return pl.pallas_call(
         functools.partial(fit_body, order=order, capacity=capacity, count=count, taps=taps),
         out_shape=(

time: 88.3 us -> 89.7 us (1.016)
  Pallas kernels: 27.4 us -> 28.9 us
    pallas_call x1, Pallas kernels: 14.6 us -> 16.1 us  [fit_and_subtract(): pl.pallas_call(functools.partial(fit_body, order=order, capacity=capacity...]
  transfers between devices with their start and end apart: 11 -> 11, of which waited for: 6 -> 6; matrix products, arithmetic and copies ran while one was open for 1% -> 1% of each run, Pallas kernels for 25% -> 27%
where the time goes in v12:
time: 89.7 us; the launch traced here: 89.2 us
  starting transfers between devices  32.2 us (36%)
  Pallas kernels  28.9 us (32%)
  waiting for transfers between devices  24.7 us (28%)
  local copies, waits for them, and re-layouts  2.31 us (3%)
    pallas_call x1, Pallas kernels, fit_and_subtract(): pl.pallas_call(functools.partial(fit_body, order=order, capacity=capacity...  16.1 us
    all_to_all x1, waiting for transfers between devices, local(): lax.all_to_all(payload, ('det',) + exposure_axes, split_axis=0, concat_ax...  10.4 us
    all_to_all x1, starting transfers between devices, local(): lax.all_to_all(var_late, ('det', 'near'), split_axis=0, concat_axis=0, ti...  8.11 us
    all_to_all x1, starting transfers between devices, local(): lax.all_to_all(request, 'det', split_axis=0, concat_axis=0, tiled=True)  6.37 us
    all_to_all x1, starting transfers between devices, local(): lax.all_to_all(payload, ('det',) + exposure_axes, split_axis=0, concat_ax...  5.79 us
    ppermute x3, waiting for transfers between devices, swap(): lax.ppermute(value, exposure_axes, [(e, e ^ distance) for e in range(exps)])  5.66 us
    all_to_all x1, waiting for transfers between devices, local(): lax.all_to_all(request, 'det', split_axis=0, concat_axis=0, tiled=True)  3.89 us
    ppermute x3, starting transfers between devices, from_exposure(): return lax.ppermute(value, exposure_axes, pairs)  3.7 us
  transfers between devices with their start and end apart: 11, of which 6 were waited for; matrix products, arithmetic and copies ran while one was open for 1% of the time, Pallas kernels for 27%

profile of v12, /device:TPU:1, one launch (start us, length us, event | category | flops | bytes accessed | tf_op | source)
XLA Modules:
  0.0 89.2 jit_solution(4758657348595020924)
XLA Ops:
  0.6 1.4 %route_tables.1 = (s32[16]{0:T(128)}, s32[16]{0:T(128)}, s32[8,1,2]{2,1,0:T(1,128)}) custom-call(s32[1,16]{1,0:T(1,128)} %src.1, s32[1,16]{1,0:T(1,128)} %blk.1), custom_call_target="tpu_custom_call" | custom-call | tf_op jit(solution)/shard_map/route_tables/pallas_call | solution.py:70
  2.0 6.4 %all-to-all-start = ((s32[8,1,2]{2,1,0:T(1,128)}), s32[8,1,2]{2,1,0:T(1,128)S(1)}, u32[]{:S(2)}, u32[]{:S(2)}) async-start(s32[8,1,2]{2,1,0:T(1,128)} %get-tuple-element.15), calls=%async_computation | async-start | bytes 8192 | tf_op jit(solution)/shard_map/all_to_all | solution.py:818
  8.4 1.2 %copy-done = bf16[32,128,128]{2,1,0:T(8,128)(2,1)S(1)} copy-done((bf16[32,128,128]{2,1,0:T(8,128)(2,1)S(1)}, bf16[32,128,128]{2,1,0:T(8,128)(2,1)}, u32[]{:S(2)}) %copy-start) | copy-done | bytes 1048600
  9.8 3.9 %all-to-all-done.asked = s32[8,1,2]{2,1,0:T(1,128)S(1)} async-done(((s32[8,1,2]{2,1,0:T(1,128)}), s32[8,1,2]{2,1,0:T(1,128)S(1)}, u32[]{:S(2)}, u32[]{:S(2)}) %all-to-all-start) | async-done | bytes 96 | tf_op jit(solution)/shard_map/all_to_all | solution.py:818
  13.6 1.5 %pick_blocks.1.earlier = bf16[16,128,128]{2,1,0:T(8,128)(2,1)} custom-call(s32[8,1,2]{2,1,0:T(1,128)S(1)} %all-to-all-done.asked, bf16[32,128,128]{2,1,0:T(8,128)(2,1)S(1)} %fetch.1.template), custom_call_target="tpu_custom_call" | custom-call | tf_op jit(solution)/shard_map/pick_blocks/pallas_call | solution.py:114
  15.2 3.6 %all-to-all-start.1 = ((bf16[16,128,128]{2,1,0:T(8,128)(2,1)}), bf16[16,128,128]{2,1,0:T(8,128)(2,1)S(1)}, u32[]{:S(2)}, u32[]{:S(2)}) async-start(bf16[16,128,128]{2,1,0:T(8,128)(2,1)} %pick_blocks.1.earlier), calls=%async_computation.1 | async-start | bytes 1048576 | tf_op jit(solution)/shard_map/all_to_all | solution.py:824
  19.5 3.2 %collective-permute-start.2 = (s32[8,1,2]{2,1,0:T(1,128)S(1)}, s32[8,1,2]{2,1,0:T(1,128)S(1)}, u32[]{:S(2)}, u32[]{:S(2)}) collective-permute-start(s32[8,1,2]{2,1,0:T(1,128)S(1)} %hold.1), channel_id=1, source_target_pairs={{0,3},{1,2},{2,1},{3,0},{4,7},{5,6},{6,5},{7,4},{8,11},{9,10},{10,... | collective-permute-start | bytes 200 | tf_op jit(solution)/shard_map/ppermute | solution.py:45
  23.2 1.1 %collective-permute-done.2 = s32[8,1,2]{2,1,0:T(1,128)S(1)} collective-permute-done((s32[8,1,2]{2,1,0:T(1,128)S(1)}, s32[8,1,2]{2,1,0:T(1,128)S(1)}, u32[]{:S(2)}, u32[]{:S(2)}) %collective-permute-start.2) | collective-permute-done | bytes 96 | tf_op jit(solution)/shard_map/ppermute | solution.py:45
  24.4 1.0 %collective-permute-done.1 = s32[8,1,2]{2,1,0:T(1,128)S(1)} collective-permute-done((s32[8,1,2]{2,1,0:T(1,128)S(1)}, s32[8,1,2]{2,1,0:T(1,128)S(1)}, u32[]{:S(2)}, u32[]{:S(2)}) %collective-permute-start.1) | collective-permute-done | bytes 96 | tf_op jit(solution)/shard_map/ppermute | solution.py:45
  25.7 1.5 %prepare.1 = bf16[16,128,128]{2,1,0:T(8,128)(2,1)} custom-call(s32[16]{0:T(128)S(1)} %copy-done.4, bf16[256,1024]{1,0:T(8,128)(2,1)S(1)} %bitcast.20, bf16[256,1024]{1,0:T(8,128)(2,1)S(1)} %bitcast.18, s32[4,8,2]{2,1,0:T(8,128)S(1)} %copy.35.earlier.table), custom_call_target="tpu_custom_call" | custom-call | bytes 6000000 | tf_op jit(solution)/shard_map/prepare/pallas_call | solution.py:175
  27.2 2.6 %all-to-all-done.1.arrived = bf16[16,128,128]{2,1,0:T(8,128)(2,1)S(1)} async-done(((bf16[16,128,128]{2,1,0:T(8,128)(2,1)}), bf16[16,128,128]{2,1,0:T(8,128)(2,1)S(1)}, u32[]{:S(2)}, u32[]{:S(2)}) %all-to-all-start.1) | async-done | bytes 524320 | tf_op jit(solution)/shard_map/all_to_all | solution.py:824
  29.8 8.1 %all-to-all-start.3 = ((bf16[16,128,128]{2,1,0:T(8,128)(2,1)}), bf16[16,128,128]{2,1,0:T(8,128)(2,1)S(1)}, u32[]{:S(2)}, u32[]{:S(2)}) async-start(bf16[16,128,128]{2,1,0:T(8,128)(2,1)} %prepare.1), calls=%async_computation.3 | async-start | bytes 1048576 | tf_op jit(solution)/shard_map/all_to_all | solution.py:836
  38.0 16.1 %fit_and_subtract.1 = (f32[1,128]{1,0:T(1,128)}, bf16[32,72,128]{2,1,0:T(8,128)(2,1)}) custom-call(s32[16]{0:T(128)S(1)} %copy-done.7, s32[16]{0:T(128)S(1)} %copy-done.4, s32[1,4]{1,0:T(1,128)S(1)} %copy-done.5, s32[1,4]{1,0:T(1,128)S(1)} %copy-done.6, bf16[16,128,128]{2,1,0:T(8,128)(2,1)S(1)} %all-to-all-done.1.arrived, ...), custom_call_target="tpu_custom_call" | custom-call | flops 15000000512 | bytes 8000000 | tf_op jit(solution)/shard_map/fit_and_subtract/pallas_call | solution.py:544
  54.0 5.8 %all-to-all-start.2 = ((bf16[32,72,128]{2,1,0:T(8,128)(2,1)}), bf16[32,72,128]{2,1,0:T(8,128)(2,1)S(1)}, u32[]{:S(2)}, u32[]{:S(2)}) async-start(bf16[32,72,128]{2,1,0:T(8,128)(2,1)} %get-tuple-element.19.payload), calls=%async_computation.2 | async-start | bytes 1179648 | tf_op jit(solution)/shard_map/all_to_all | solution.py:857
  60.0 1.2 %sum_variance.1 = (f32[32,32,128]{2,1,0:T(8,128)S(1)}, bf16[1,32,32,128]{3,2,1,0:T(8,128)(2,1)S(1)}, bf16[32,32,128]{2,1,0:T(8,128)(2,1)S(1)}) custom-call(s32[1]{0:T(128)} %bitcast.1.me, s32[4,8,2]{2,1,0:T(8,128)S(1)} %copy.35.earlier.table, bf16[16,128,128]{2,1,0:T(8,128)(2,1)S(1)} %all-to-all-done.3.parts, bf16[32,128,128]{2,1,0:T(8,128)(2,1)S(1)} %copy-done.1), custom_call_target="tpu_custom_call" | custom-call | bytes 4000000 | tf_op jit(solution)/shard_map/sum_variance/pallas_call | solution.py:690
  61.2 1.5 %collective-permute-start.3 = (bf16[32,32,128]{2,1,0:T(8,128)(2,1)S(1)}, bf16[32,32,128]{2,1,0:T(8,128)(2,1)S(1)}, u32[]{:S(2)}, u32[]{:S(2)}) collective-permute-start(bf16[32,32,128]{2,1,0:T(8,128)(2,1)S(1)} %bitcast.22), channel_id=1, source_target_pairs={{0,2},{2,0},{1,3},{3,1},{4,6},{6,4},{5,7},{7,5},{8,10},{10,8},{9,1... | collective-permute-start | bytes 786440 | tf_op jit(solution)/shard_map/ppermute | solution.py:865
  62.8 3.1 %score.1 = (f32[256,1024]{1,0:T(8,128)}, f32[8,128]{1,0:T(8,128)S(1)}) custom-call(s32[16]{0:T(128)S(1)} %copy-done.7, bf16[32,72,128]{2,1,0:T(8,128)(2,1)} %get-tuple-element.19.payload, f32[1,256]{1,0:T(1,128)S(1)} %pad.26.down, f32[1,256]{1,0:T(1,128)S(1)} %pad_maximum_fusion.1.over), custom_call_target="tpu_custom_call" | custom-call | flops 2000000000 | bytes 2000000 | tf_op jit(solution)/shard_map/score/pallas_call | solution.py:632
  65.9 10.4 %all-to-all-done.2.parts = bf16[32,72,128]{2,1,0:T(8,128)(2,1)S(1)} async-done(((bf16[32,72,128]{2,1,0:T(8,128)(2,1)}), bf16[32,72,128]{2,1,0:T(8,128)(2,1)S(1)}, u32[]{:S(2)}, u32[]{:S(2)}) %all-to-all-start.2) | async-done | bytes 589856 | tf_op jit(solution)/shard_map/all_to_all | solution.py:857
  76.3 1.4 %combine.1.refs_0_ = bf16[32,32,128]{2,1,0:T(8,128)(2,1)S(1)} custom-call(s32[1]{0:T(128)} %bitcast.1.me, s32[4,8,2]{2,1,0:T(8,128)S(1)} %copy.35.earlier.table, f32[8,128]{1,0:T(8,128)S(1)} %get-tuple-element.20.earlier, bf16[32,72,128]{2,1,0:T(8,128)(2,1)S(1)} %all-to-all-done.2.parts, f32[32,32,128]{2,1,0:T(8,128)S(1)} %get-tuple-element.22.own_var, ...), custom_call_target="tpu_custom_call" | custom-call | tf_op jit(solution)/shard_map/combine/pallas_call | solution.py:738
  77.7 1.3 %collective-permute-start.4 = (bf16[32,32,128]{2,1,0:T(8,128)(2,1)S(1)}, bf16[32,32,128]{2,1,0:T(8,128)(2,1)S(1)}, u32[]{:S(2)}, u32[]{:S(2)}) collective-permute-start(bf16[32,32,128]{2,1,0:T(8,128)(2,1)S(1)} %combine.1.refs_0_), channel_id=1, source_target_pairs={{0,2},{1,3},{2,0},{3,1},{4,6},{5,7},{6,4},{7,5},{8,10},{9,11},{10,... | collective-permute-start | bytes 786440 | tf_op jit(solution)/shard_map/ppermute | solution.py:872
  79.5 5.7 %collective-permute-done.4.refs_2_ = bf16[32,32,128]{2,1,0:T(8,128)(2,1)S(1)} collective-permute-done((bf16[32,32,128]{2,1,0:T(8,128)(2,1)S(1)}, bf16[32,32,128]{2,1,0:T(8,128)(2,1)S(1)}, u32[]{:S(2)}, u32[]{:S(2)}) %collective-permute-start.4) | collective-permute-done | bytes 262176 | tf_op jit(solution)/shard_map/ppermute | solution.py:872
  85.1 1.4 %collective-permute-start.5 = (bf16[32,32,128]{2,1,0:T(8,128)(2,1)S(1)}, bf16[32,32,128]{2,1,0:T(8,128)(2,1)S(1)}, u32[]{:S(2)}, u32[]{:S(2)}) collective-permute-start(bf16[32,32,128]{2,1,0:T(8,128)(2,1)S(1)} %collective-permute-done.4.refs_2_), channel_id=1, source_target_pairs={{0,1},{1,0},{2,3},{3,2},{4,5},{5,4},{6,7},{7,6},{8,9},{9,8},{10,11... | collective-permute-start | bytes 786440 | tf_op jit(solution)/shard_map/ppermute | solution.py:872
  86.6 1.7 %join_parts.2.refs_1_ = f32[32,128,128]{2,1,0:T(8,128)} custom-call(s32[3]{0:T(128)S(1)} %pad_add_fusion.places, bf16[32,32,128]{2,1,0:T(8,128)(2,1)S(1)} %combine.1.refs_0_, bf16[32,32,128]{2,1,0:T(8,128)(2,1)S(1)} %collective-permute-done.6.refs_1_, bf16[32,32,128]{2,1,0:T(8,128)(2,1)S(1)} %collective-permute-done.4.refs_2_), custom_call_target="tpu_custom_call" | custom-call | bytes 9000000 | tf_op jit(solution)/shard_map/join_parts/pallas_call | solution.py:773
  88.3 0.8 join_parts.3
  (52 shorter events, 2.4 us)
Async XLA Ops:
  2.0 11.6 %all-to-all-start = ((s32[8,1,2]{2,1,0:T(1,128)}), s32[8,1,2]{2,1,0:T(1,128)S(1)}, u32[]{:S(2)}, u32[]{:S(2)}) async-start(s32[8,1,2]{2,1,0:T(1,128)} %get-tuple-element.15), calls=%async_computation | async-start | bytes 8192 | tf_op jit(solution)/shard_map/all_to_all | solution.py:818
  8.4 1.2 %copy-start = (bf16[32,128,128]{2,1,0:T(8,128)(2,1)S(1)}, bf16[32,128,128]{2,1,0:T(8,128)(2,1)}, u32[]{:S(2)}) copy-start(bf16[32,128,128]{2,1,0:T(8,128)(2,1)} %template.1) | copy-start | bytes 3145732
  9.6 9.2 %copy-start.8 = (bf16[40,21]{0,1:T(8,128)(2,1)S(1)}, bf16[40,21]{0,1:T(8,128)(2,1)}, u32[]{:S(2)}) copy-start(bf16[40,21]{0,1:T(8,128)(2,1)} %param.20) | copy-start | bytes 5044
  9.6 9.3 %copy-start.9 = (bf16[40,21]{0,1:T(8,128)(2,1)S(1)}, bf16[40,21]{0,1:T(8,128)(2,1)}, u32[]{:S(2)}) copy-start(bf16[40,21]{0,1:T(8,128)(2,1)} %param.21) | copy-start | bytes 5044
  9.7 15.9 %copy-start.2 = (bf16[1,256,1024]{2,1,0:T(8,128)(2,1)S(1)}, bf16[1,256,1024]{2,1,0:T(8,128)(2,1)}, u32[]{:S(2)}) copy-start(bf16[1,256,1024]{2,1,0:T(8,128)(2,1)} %param.14) | copy-start | bytes 1572868
  9.7 15.9 %copy-start.3 = (bf16[1,256,1024]{2,1,0:T(8,128)(2,1)S(1)}, bf16[1,256,1024]{2,1,0:T(8,128)(2,1)}, u32[]{:S(2)}) copy-start(bf16[1,256,1024]{2,1,0:T(8,128)(2,1)} %param.15) | copy-start | bytes 1572868
  9.7 15.9 %copy-start.4 = (s32[16]{0:T(128)S(1)}, s32[16]{0:T(128)}, u32[]{:S(2)}) copy-start(s32[16]{0:T(128)} %get-tuple-element.17.sender) | copy-start | bytes 196
  15.2 22.7 %copy-start.5 = (s32[1,4]{1,0:T(1,128)S(1)}, s32[1,4]{1,0:T(1,128)}, u32[]{:S(2)}) copy-start(s32[1,4]{1,0:T(1,128)} %rows_at.1) | copy-start | bytes 52
  15.2 22.7 %copy-start.6 = (s32[1,4]{1,0:T(1,128)S(1)}, s32[1,4]{1,0:T(1,128)}, u32[]{:S(2)}) copy-start(s32[1,4]{1,0:T(1,128)} %cols_at.1) | copy-start | bytes 52
  15.2 22.7 %copy-start.7 = (s32[16]{0:T(128)S(1)}, s32[16]{0:T(128)}, u32[]{:S(2)}) copy-start(s32[16]{0:T(128)} %get-tuple-element.16.slot_of) | copy-start | bytes 196
  15.2 14.6 %all-to-all-start.1 = ((bf16[16,128,128]{2,1,0:T(8,128)(2,1)}), bf16[16,128,128]{2,1,0:T(8,128)(2,1)S(1)}, u32[]{:S(2)}, u32[]{:S(2)}) async-start(bf16[16,128,128]{2,1,0:T(8,128)(2,1)} %pick_blocks.1.earlier), calls=%async_computation.1 | async-start | bytes 1048576 | tf_op jit(solution)/shard_map/all_to_all | solution.py:824
  19.5 4.8 %collective-permute-start.2 = (s32[8,1,2]{2,1,0:T(1,128)S(1)}, s32[8,1,2]{2,1,0:T(1,128)S(1)}, u32[]{:S(2)}, u32[]{:S(2)}) collective-permute-start(s32[8,1,2]{2,1,0:T(1,128)S(1)} %hold.1), channel_id=1, source_target_pairs={{0,3},{1,2},{2,1},{3,0},{4,7},{5,6},{6,5},{7,4},{8,11},{9,10},{10,... | collective-permute-start | bytes 200 | tf_op jit(solution)/shard_map/ppermute | solution.py:45
  22.7 2.7 %collective-permute-start.1 = (s32[8,1,2]{2,1,0:T(1,128)S(1)}, s32[8,1,2]{2,1,0:T(1,128)S(1)}, u32[]{:S(2)}, u32[]{:S(2)}) collective-permute-start(s32[8,1,2]{2,1,0:T(1,128)S(1)} %hold.1), channel_id=1, source_target_pairs={{0,2},{1,3},{2,0},{3,1},{4,6},{5,7},{6,4},{7,5},{8,10},{9,11},{10,... | collective-permute-start | bytes 200 | tf_op jit(solution)/shard_map/ppermute | solution.py:45
  22.9 2.5 %collective-permute-start = (s32[8,1,2]{2,1,0:T(1,128)S(1)}, s32[8,1,2]{2,1,0:T(1,128)S(1)}, u32[]{:S(2)}, u32[]{:S(2)}) collective-permute-start(s32[8,1,2]{2,1,0:T(1,128)S(1)} %hold.1), channel_id=1, source_target_pairs={{0,1},{1,0},{2,3},{3,2},{4,5},{5,4},{6,7},{7,6},{8,9},{9,8},{10,11... | collective-permute-start | bytes 200 | tf_op jit(solution)/shard_map/ppermute | solution.py:45
  29.8 24.2 %all-to-all-start.3 = ((bf16[16,128,128]{2,1,0:T(8,128)(2,1)}), bf16[16,128,128]{2,1,0:T(8,128)(2,1)S(1)}, u32[]{:S(2)}, u32[]{:S(2)}) async-start(bf16[16,128,128]{2,1,0:T(8,128)(2,1)} %prepare.1), calls=%async_computation.3 | async-start | bytes 1048576 | tf_op jit(solution)/shard_map/all_to_all | solution.py:836
  37.9 21.9 %copy-start.10 = (f32[1,21]{1,0:T(1,128)S(1)}, f32[1,21]{1,0:T(1,128)}, u32[]{:S(2)}) copy-start(f32[1,21]{1,0:T(1,128)} %param.23) | copy-start | bytes 256
  37.9 22.0 %copy-start.11 = (f32[1,21]{1,0:T(1,128)S(1)}, f32[1,21]{1,0:T(1,128)}, u32[]{:S(2)}) copy-start(f32[1,21]{1,0:T(1,128)} %param.22) | copy-start | bytes 256
  37.9 22.1 %copy-start.1 = (bf16[32,128,128]{2,1,0:T(8,128)(2,1)S(1)}, bf16[32,128,128]{2,1,0:T(8,128)(2,1)}, u32[]{:S(2)}) copy-start(bf16[32,128,128]{2,1,0:T(8,128)(2,1)} %template_var.1) | copy-start | bytes 3145732
  54.0 22.3 %all-to-all-start.2 = ((bf16[32,72,128]{2,1,0:T(8,128)(2,1)}), bf16[32,72,128]{2,1,0:T(8,128)(2,1)S(1)}, u32[]{:S(2)}, u32[]{:S(2)}) async-start(bf16[32,72,128]{2,1,0:T(8,128)(2,1)} %get-tuple-element.19.payload), calls=%async_computation.2 | async-start | bytes 1179648 | tf_op jit(solution)/shard_map/all_to_all | solution.py:857
  61.2 15.1 %collective-permute-start.3 = (bf16[32,32,128]{2,1,0:T(8,128)(2,1)S(1)}, bf16[32,32,128]{2,1,0:T(8,128)(2,1)S(1)}, u32[]{:S(2)}, u32[]{:S(2)}) collective-permute-start(bf16[32,32,128]{2,1,0:T(8,128)(2,1)S(1)} %bitcast.22), channel_id=1, source_target_pairs={{0,2},{2,0},{1,3},{3,1},{4,6},{6,4},{5,7},{7,5},{8,10},{10,8},{9,1... | collective-permute-start | bytes 786440 | tf_op jit(solution)/shard_map/ppermute | solution.py:865
  77.7 7.4 %collective-permute-start.4 = (bf16[32,32,128]{2,1,0:T(8,128)(2,1)S(1)}, bf16[32,32,128]{2,1,0:T(8,128)(2,1)S(1)}, u32[]{:S(2)}, u32[]{:S(2)}) collective-permute-start(bf16[32,32,128]{2,1,0:T(8,128)(2,1)S(1)} %combine.1.refs_0_), channel_id=1, source_target_pairs={{0,2},{1,3},{2,0},{3,1},{4,6},{5,7},{6,4},{7,5},{8,10},{9,11},{10,... | collective-permute-start | bytes 786440 | tf_op jit(solution)/shard_map/ppermute | solution.py:872
  79.0 7.6 %collective-permute-start.6 = (bf16[32,32,128]{2,1,0:T(8,128)(2,1)S(1)}, bf16[32,32,128]{2,1,0:T(8,128)(2,1)S(1)}, u32[]{:S(2)}, u32[]{:S(2)}) collective-permute-start(bf16[32,32,128]{2,1,0:T(8,128)(2,1)S(1)} %combine.1.refs_0_), channel_id=1, source_target_pairs={{0,1},{1,0},{2,3},{3,2},{4,5},{5,4},{6,7},{7,6},{8,9},{9,8},{10,11... | collective-permute-start | bytes 786440 | tf_op jit(solution)/shard_map/ppermute | solution.py:872
  85.1 3.2 %collective-permute-start.5 = (bf16[32,32,128]{2,1,0:T(8,128)(2,1)S(1)}, bf16[32,32,128]{2,1,0:T(8,128)(2,1)S(1)}, u32[]{:S(2)}, u32[]{:S(2)}) collective-permute-start(bf16[32,32,128]{2,1,0:T(8,128)(2,1)S(1)} %collective-permute-done.4.refs_2_), channel_id=1, source_target_pairs={{0,1},{1,0},{2,3},{3,2},{4,5},{5,4},{6,7},{7,6},{8,9},{9,8},{10,11... | collective-permute-start | bytes 786440 | tf_op jit(solution)/shard_map/ppermute | solution.py:872

commit v13 on v11

--- a/solution.py
+++ b/solution.py
@@ -306,7 +306,7 @@
         lines_all // (lines * sets),
         gram_step,
         jnp.zeros((sets * padded_k, sets * padded_k), f32),
-        unroll=2,
+        unroll=4,
     )
     part = jnp.zeros((padded_k, padded_k), f32)
     for g in range(sets):
@@ -401,7 +401,7 @@
                 ] = made[2 * q + a - b]
 
     step = side - taps + 1
-    joint = pairs
+    joint = 4
     for q in range(0, pairs, joint):
         last = min(q + joint, pairs)
         lhs = jnp.concatenate(
@@ -558,7 +558,7 @@
             pltpu.VMEM((pairs * 2 * side, 2 * side), bf16),
             pltpu.VMEM((wins * high // 2, 2 * side), f32),
         ],
-        compiler_params=pltpu.CompilerParams(vmem_limit_bytes=30 * mib),
+        compiler_params=pltpu.CompilerParams(vmem_limit_bytes=34 * mib),
         cost_estimate=cost(15_000_000_000, 8_000_000),
         name="fit_and_subtract",
     )(

time: 88.3 us -> 87.9 us (level)
  no operation moved by 1% of the time
where the time goes in v13:
time: 87.9 us; the launch traced here: 87.4 us
  starting transfers between devices  32.2 us (37%)
  Pallas kernels  27.1 us (31%)
  waiting for transfers between devices  24.7 us (28%)
  local copies, waits for them, and re-layouts  2.31 us (3%)
    pallas_call x1, Pallas kernels, fit_and_subtract(): pl.pallas_call(functools.partial(fit_body, order=order, capacity=capacity...  14.2 us
    all_to_all x1, waiting for transfers between devices, local(): lax.all_to_all(payload, ('det',) + exposure_axes, split_axis=0, concat_ax...  10.4 us
    all_to_all x1, starting transfers between devices, local(): lax.all_to_all(var_late, ('det', 'near'), split_axis=0, concat_axis=0, ti...  8.11 us
    all_to_all x1, starting transfers between devices, local(): lax.all_to_all(request, 'det', split_axis=0, concat_axis=0, tiled=True)  6.37 us
    all_to_all x1, starting transfers between devices, local(): lax.all_to_all(payload, ('det',) + exposure_axes, split_axis=0, concat_ax...  5.8 us
    ppermute x3, waiting for transfers between devices, swap(): lax.ppermute(value, exposure_axes, [(e, e ^ distance) for e in range(exps)])  5.66 us
    all_to_all x1, waiting for transfers between devices, local(): lax.all_to_all(request, 'det', split_axis=0, concat_axis=0, tiled=True)  3.89 us
    ppermute x3, starting transfers between devices, from_exposure(): return lax.ppermute(value, exposure_axes, pairs)  3.7 us
  transfers between devices with their start and end apart: 11, of which 6 were waited for; matrix products, arithmetic and copies ran while one was open for 1% of the time, Pallas kernels for 25%

profile of v13, /device:TPU:1, one launch (start us, length us, event | category | flops | bytes accessed | tf_op | source)
XLA Modules:
  0.0 87.4 jit_solution(1370902291700935983)
XLA Ops:
  0.6 1.4 %route_tables.1 = (s32[16]{0:T(128)}, s32[16]{0:T(128)}, s32[8,1,2]{2,1,0:T(1,128)}) custom-call(s32[1,16]{1,0:T(1,128)} %src.1, s32[1,16]{1,0:T(1,128)} %blk.1), custom_call_target="tpu_custom_call" | custom-call | tf_op jit(solution)/shard_map/route_tables/pallas_call | solution.py:70
  2.0 6.4 %all-to-all-start = ((s32[8,1,2]{2,1,0:T(1,128)}), s32[8,1,2]{2,1,0:T(1,128)S(1)}, u32[]{:S(2)}, u32[]{:S(2)}) async-start(s32[8,1,2]{2,1,0:T(1,128)} %get-tuple-element.15), calls=%async_computation | async-start | bytes 8192 | tf_op jit(solution)/shard_map/all_to_all | solution.py:811
  8.4 1.2 %copy-done = bf16[32,128,128]{2,1,0:T(8,128)(2,1)S(1)} copy-done((bf16[32,128,128]{2,1,0:T(8,128)(2,1)S(1)}, bf16[32,128,128]{2,1,0:T(8,128)(2,1)}, u32[]{:S(2)}) %copy-start) | copy-done | bytes 1048600
  9.8 3.9 %all-to-all-done.asked = s32[8,1,2]{2,1,0:T(1,128)S(1)} async-done(((s32[8,1,2]{2,1,0:T(1,128)}), s32[8,1,2]{2,1,0:T(1,128)S(1)}, u32[]{:S(2)}, u32[]{:S(2)}) %all-to-all-start) | async-done | bytes 96 | tf_op jit(solution)/shard_map/all_to_all | solution.py:811
  13.6 1.5 %pick_blocks.1.earlier = bf16[16,128,128]{2,1,0:T(8,128)(2,1)} custom-call(s32[8,1,2]{2,1,0:T(1,128)S(1)} %all-to-all-done.asked, bf16[32,128,128]{2,1,0:T(8,128)(2,1)S(1)} %fetch.1.template), custom_call_target="tpu_custom_call" | custom-call | tf_op jit(solution)/shard_map/pick_blocks/pallas_call | solution.py:114
  15.2 3.6 %all-to-all-start.1 = ((bf16[16,128,128]{2,1,0:T(8,128)(2,1)}), bf16[16,128,128]{2,1,0:T(8,128)(2,1)S(1)}, u32[]{:S(2)}, u32[]{:S(2)}) async-start(bf16[16,128,128]{2,1,0:T(8,128)(2,1)} %pick_blocks.1.earlier), calls=%async_computation.1 | async-start | bytes 1048576 | tf_op jit(solution)/shard_map/all_to_all | solution.py:817
  19.5 3.2 %collective-permute-start.2 = (s32[8,1,2]{2,1,0:T(1,128)S(1)}, s32[8,1,2]{2,1,0:T(1,128)S(1)}, u32[]{:S(2)}, u32[]{:S(2)}) collective-permute-start(s32[8,1,2]{2,1,0:T(1,128)S(1)} %hold.1), channel_id=1, source_target_pairs={{0,3},{1,2},{2,1},{3,0},{4,7},{5,6},{6,5},{7,4},{8,11},{9,10},{10,... | collective-permute-start | bytes 200 | tf_op jit(solution)/shard_map/ppermute | solution.py:45
  23.2 1.1 %collective-permute-done.2 = s32[8,1,2]{2,1,0:T(1,128)S(1)} collective-permute-done((s32[8,1,2]{2,1,0:T(1,128)S(1)}, s32[8,1,2]{2,1,0:T(1,128)S(1)}, u32[]{:S(2)}, u32[]{:S(2)}) %collective-permute-start.2) | collective-permute-done | bytes 96 | tf_op jit(solution)/shard_map/ppermute | solution.py:45
  24.4 1.0 %collective-permute-done.1 = s32[8,1,2]{2,1,0:T(1,128)S(1)} collective-permute-done((s32[8,1,2]{2,1,0:T(1,128)S(1)}, s32[8,1,2]{2,1,0:T(1,128)S(1)}, u32[]{:S(2)}, u32[]{:S(2)}) %collective-permute-start.1) | collective-permute-done | bytes 96 | tf_op jit(solution)/shard_map/ppermute | solution.py:45
  25.7 1.5 %prepare.1 = bf16[16,128,128]{2,1,0:T(8,128)(2,1)} custom-call(s32[16]{0:T(128)S(1)} %copy-done.4, bf16[256,1024]{1,0:T(8,128)(2,1)S(1)} %bitcast.20, bf16[256,1024]{1,0:T(8,128)(2,1)S(1)} %bitcast.18, s32[4,8,2]{2,1,0:T(8,128)S(1)} %copy.35.earlier.table), custom_call_target="tpu_custom_call" | custom-call | bytes 6000000 | tf_op jit(solution)/shard_map/prepare/pallas_call | solution.py:175
  27.2 2.6 %all-to-all-done.1.arrived = bf16[16,128,128]{2,1,0:T(8,128)(2,1)S(1)} async-done(((bf16[16,128,128]{2,1,0:T(8,128)(2,1)}), bf16[16,128,128]{2,1,0:T(8,128)(2,1)S(1)}, u32[]{:S(2)}, u32[]{:S(2)}) %all-to-all-start.1) | async-done | bytes 524320 | tf_op jit(solution)/shard_map/all_to_all | solution.py:817
  29.8 8.1 %all-to-all-start.3 = ((bf16[16,128,128]{2,1,0:T(8,128)(2,1)}), bf16[16,128,128]{2,1,0:T(8,128)(2,1)S(1)}, u32[]{:S(2)}, u32[]{:S(2)}) async-start(bf16[16,128,128]{2,1,0:T(8,128)(2,1)} %prepare.1), calls=%async_computation.3 | async-start | bytes 1048576 | tf_op jit(solution)/shard_map/all_to_all | solution.py:829
  38.0 14.2 %fit_and_subtract.1 = (f32[1,128]{1,0:T(1,128)}, bf16[32,72,128]{2,1,0:T(8,128)(2,1)}) custom-call(s32[16]{0:T(128)S(1)} %copy-done.7, s32[16]{0:T(128)S(1)} %copy-done.4, s32[1,4]{1,0:T(1,128)S(1)} %copy-done.5, s32[1,4]{1,0:T(1,128)S(1)} %copy-done.6, bf16[16,128,128]{2,1,0:T(8,128)(2,1)S(1)} %all-to-all-done.1.arrived, ...), custom_call_target="tpu_custom_call" | custom-call | flops 15000000512 | bytes 8000000 | tf_op jit(solution)/shard_map/fit_and_subtract/pallas_call | solution.py:537
  52.2 5.8 %all-to-all-start.2 = ((bf16[32,72,128]{2,1,0:T(8,128)(2,1)}), bf16[32,72,128]{2,1,0:T(8,128)(2,1)S(1)}, u32[]{:S(2)}, u32[]{:S(2)}) async-start(bf16[32,72,128]{2,1,0:T(8,128)(2,1)} %get-tuple-element.19.payload), calls=%async_computation.2 | async-start | bytes 1179648 | tf_op jit(solution)/shard_map/all_to_all | solution.py:850
  58.2 1.2 %sum_variance.1 = (f32[32,32,128]{2,1,0:T(8,128)S(1)}, bf16[1,32,32,128]{3,2,1,0:T(8,128)(2,1)S(1)}, bf16[32,32,128]{2,1,0:T(8,128)(2,1)S(1)}) custom-call(s32[1]{0:T(128)} %bitcast.1.me, s32[4,8,2]{2,1,0:T(8,128)S(1)} %copy.35.earlier.table, bf16[16,128,128]{2,1,0:T(8,128)(2,1)S(1)} %all-to-all-done.3.parts, bf16[32,128,128]{2,1,0:T(8,128)(2,1)S(1)} %copy-done.1), custom_call_target="tpu_custom_call" | custom-call | bytes 4000000 | tf_op jit(solution)/shard_map/sum_variance/pallas_call | solution.py:683
  59.4 1.5 %collective-permute-start.3 = (bf16[32,32,128]{2,1,0:T(8,128)(2,1)S(1)}, bf16[32,32,128]{2,1,0:T(8,128)(2,1)S(1)}, u32[]{:S(2)}, u32[]{:S(2)}) collective-permute-start(bf16[32,32,128]{2,1,0:T(8,128)(2,1)S(1)} %bitcast.22), channel_id=1, source_target_pairs={{0,2},{2,0},{1,3},{3,1},{4,6},{6,4},{5,7},{7,5},{8,10},{10,8},{9,1... | collective-permute-start | bytes 786440 | tf_op jit(solution)/shard_map/ppermute | solution.py:858
  61.0 3.1 %score.1 = (f32[256,1024]{1,0:T(8,128)}, f32[8,128]{1,0:T(8,128)S(1)}) custom-call(s32[16]{0:T(128)S(1)} %copy-done.7, bf16[32,72,128]{2,1,0:T(8,128)(2,1)} %get-tuple-element.19.payload, f32[1,256]{1,0:T(1,128)S(1)} %pad.26.down, f32[1,256]{1,0:T(1,128)S(1)} %pad_maximum_fusion.1.over), custom_call_target="tpu_custom_call" | custom-call | flops 2000000000 | bytes 2000000 | tf_op jit(solution)/shard_map/score/pallas_call | solution.py:625
  64.1 10.4 %all-to-all-done.2.parts = bf16[32,72,128]{2,1,0:T(8,128)(2,1)S(1)} async-done(((bf16[32,72,128]{2,1,0:T(8,128)(2,1)}), bf16[32,72,128]{2,1,0:T(8,128)(2,1)S(1)}, u32[]{:S(2)}, u32[]{:S(2)}) %all-to-all-start.2) | async-done | bytes 589856 | tf_op jit(solution)/shard_map/all_to_all | solution.py:850
  74.5 1.4 %combine.1.refs_0_ = bf16[32,32,128]{2,1,0:T(8,128)(2,1)S(1)} custom-call(s32[1]{0:T(128)} %bitcast.1.me, s32[4,8,2]{2,1,0:T(8,128)S(1)} %copy.35.earlier.table, f32[8,128]{1,0:T(8,128)S(1)} %get-tuple-element.20.earlier, bf16[32,72,128]{2,1,0:T(8,128)(2,1)S(1)} %all-to-all-done.2.parts, f32[32,32,128]{2,1,0:T(8,128)S(1)} %get-tuple-element.22.own_var, ...), custom_call_target="tpu_custom_call" | custom-call | tf_op jit(solution)/shard_map/combine/pallas_call | solution.py:731
  75.9 1.3 %collective-permute-start.4 = (bf16[32,32,128]{2,1,0:T(8,128)(2,1)S(1)}, bf16[32,32,128]{2,1,0:T(8,128)(2,1)S(1)}, u32[]{:S(2)}, u32[]{:S(2)}) collective-permute-start(bf16[32,32,128]{2,1,0:T(8,128)(2,1)S(1)} %combine.1.refs_0_), channel_id=1, source_target_pairs={{0,2},{1,3},{2,0},{3,1},{4,6},{5,7},{6,4},{7,5},{8,10},{9,11},{10,... | collective-permute-start | bytes 786440 | tf_op jit(solution)/shard_map/ppermute | solution.py:865
  77.6 5.7 %collective-permute-done.4.refs_2_ = bf16[32,32,128]{2,1,0:T(8,128)(2,1)S(1)} collective-permute-done((bf16[32,32,128]{2,1,0:T(8,128)(2,1)S(1)}, bf16[32,32,128]{2,1,0:T(8,128)(2,1)S(1)}, u32[]{:S(2)}, u32[]{:S(2)}) %collective-permute-start.4) | collective-permute-done | bytes 262176 | tf_op jit(solution)/shard_map/ppermute | solution.py:865
  83.3 1.4 %collective-permute-start.5 = (bf16[32,32,128]{2,1,0:T(8,128)(2,1)S(1)}, bf16[32,32,128]{2,1,0:T(8,128)(2,1)S(1)}, u32[]{:S(2)}, u32[]{:S(2)}) collective-permute-start(bf16[32,32,128]{2,1,0:T(8,128)(2,1)S(1)} %collective-permute-done.4.refs_2_), channel_id=1, source_target_pairs={{0,1},{1,0},{2,3},{3,2},{4,5},{5,4},{6,7},{7,6},{8,9},{9,8},{10,11... | collective-permute-start | bytes 786440 | tf_op jit(solution)/shard_map/ppermute | solution.py:865
  84.8 1.7 %join_parts.2.refs_1_ = f32[32,128,128]{2,1,0:T(8,128)} custom-call(s32[3]{0:T(128)S(1)} %pad_add_fusion.places, bf16[32,32,128]{2,1,0:T(8,128)(2,1)S(1)} %combine.1.refs_0_, bf16[32,32,128]{2,1,0:T(8,128)(2,1)S(1)} %collective-permute-done.6.refs_1_, bf16[32,32,128]{2,1,0:T(8,128)(2,1)S(1)} %collective-permute-done.4.refs_2_), custom_call_target="tpu_custom_call" | custom-call | bytes 9000000 | tf_op jit(solution)/shard_map/join_parts/pallas_call | solution.py:766
  86.5 0.8 join_parts.3
  (52 shorter events, 2.4 us)
Async XLA Ops:
  2.0 11.6 %all-to-all-start = ((s32[8,1,2]{2,1,0:T(1,128)}), s32[8,1,2]{2,1,0:T(1,128)S(1)}, u32[]{:S(2)}, u32[]{:S(2)}) async-start(s32[8,1,2]{2,1,0:T(1,128)} %get-tuple-element.15), calls=%async_computation | async-start | bytes 8192 | tf_op jit(solution)/shard_map/all_to_all | solution.py:811
  8.4 1.2 %copy-start = (bf16[32,128,128]{2,1,0:T(8,128)(2,1)S(1)}, bf16[32,128,128]{2,1,0:T(8,128)(2,1)}, u32[]{:S(2)}) copy-start(bf16[32,128,128]{2,1,0:T(8,128)(2,1)} %template.1) | copy-start | bytes 3145732
  9.6 9.2 %copy-start.8 = (bf16[40,21]{0,1:T(8,128)(2,1)S(1)}, bf16[40,21]{0,1:T(8,128)(2,1)}, u32[]{:S(2)}) copy-start(bf16[40,21]{0,1:T(8,128)(2,1)} %param.20) | copy-start | bytes 5044
  9.6 9.3 %copy-start.9 = (bf16[40,21]{0,1:T(8,128)(2,1)S(1)}, bf16[40,21]{0,1:T(8,128)(2,1)}, u32[]{:S(2)}) copy-start(bf16[40,21]{0,1:T(8,128)(2,1)} %param.21) | copy-start | bytes 5044
  9.7 15.9 %copy-start.2 = (bf16[1,256,1024]{2,1,0:T(8,128)(2,1)S(1)}, bf16[1,256,1024]{2,1,0:T(8,128)(2,1)}, u32[]{:S(2)}) copy-start(bf16[1,256,1024]{2,1,0:T(8,128)(2,1)} %param.14) | copy-start | bytes 1572868
  9.7 15.9 %copy-start.3 = (bf16[1,256,1024]{2,1,0:T(8,128)(2,1)S(1)}, bf16[1,256,1024]{2,1,0:T(8,128)(2,1)}, u32[]{:S(2)}) copy-start(bf16[1,256,1024]{2,1,0:T(8,128)(2,1)} %param.15) | copy-start | bytes 1572868
  9.7 15.9 %copy-start.4 = (s32[16]{0:T(128)S(1)}, s32[16]{0:T(128)}, u32[]{:S(2)}) copy-start(s32[16]{0:T(128)} %get-tuple-element.17.sender) | copy-start | bytes 196
  15.2 22.7 %copy-start.5 = (s32[1,4]{1,0:T(1,128)S(1)}, s32[1,4]{1,0:T(1,128)}, u32[]{:S(2)}) copy-start(s32[1,4]{1,0:T(1,128)} %rows_at.1) | copy-start | bytes 52
  15.2 22.7 %copy-start.6 = (s32[1,4]{1,0:T(1,128)S(1)}, s32[1,4]{1,0:T(1,128)}, u32[]{:S(2)}) copy-start(s32[1,4]{1,0:T(1,128)} %cols_at.1) | copy-start | bytes 52
  15.2 22.7 %copy-start.7 = (s32[16]{0:T(128)S(1)}, s32[16]{0:T(128)}, u32[]{:S(2)}) copy-start(s32[16]{0:T(128)} %get-tuple-element.16.slot_of) | copy-start | bytes 196
  15.2 14.6 %all-to-all-start.1 = ((bf16[16,128,128]{2,1,0:T(8,128)(2,1)}), bf16[16,128,128]{2,1,0:T(8,128)(2,1)S(1)}, u32[]{:S(2)}, u32[]{:S(2)}) async-start(bf16[16,128,128]{2,1,0:T(8,128)(2,1)} %pick_blocks.1.earlier), calls=%async_computation.1 | async-start | bytes 1048576 | tf_op jit(solution)/shard_map/all_to_all | solution.py:817
  19.5 4.8 %collective-permute-start.2 = (s32[8,1,2]{2,1,0:T(1,128)S(1)}, s32[8,1,2]{2,1,0:T(1,128)S(1)}, u32[]{:S(2)}, u32[]{:S(2)}) collective-permute-start(s32[8,1,2]{2,1,0:T(1,128)S(1)} %hold.1), channel_id=1, source_target_pairs={{0,3},{1,2},{2,1},{3,0},{4,7},{5,6},{6,5},{7,4},{8,11},{9,10},{10,... | collective-permute-start | bytes 200 | tf_op jit(solution)/shard_map/ppermute | solution.py:45
  22.7 2.7 %collective-permute-start.1 = (s32[8,1,2]{2,1,0:T(1,128)S(1)}, s32[8,1,2]{2,1,0:T(1,128)S(1)}, u32[]{:S(2)}, u32[]{:S(2)}) collective-permute-start(s32[8,1,2]{2,1,0:T(1,128)S(1)} %hold.1), channel_id=1, source_target_pairs={{0,2},{1,3},{2,0},{3,1},{4,6},{5,7},{6,4},{7,5},{8,10},{9,11},{10,... | collective-permute-start | bytes 200 | tf_op jit(solution)/shard_map/ppermute | solution.py:45
  22.9 2.5 %collective-permute-start = (s32[8,1,2]{2,1,0:T(1,128)S(1)}, s32[8,1,2]{2,1,0:T(1,128)S(1)}, u32[]{:S(2)}, u32[]{:S(2)}) collective-permute-start(s32[8,1,2]{2,1,0:T(1,128)S(1)} %hold.1), channel_id=1, source_target_pairs={{0,1},{1,0},{2,3},{3,2},{4,5},{5,4},{6,7},{7,6},{8,9},{9,8},{10,11... | collective-permute-start | bytes 200 | tf_op jit(solution)/shard_map/ppermute | solution.py:45
  29.8 22.4 %all-to-all-start.3 = ((bf16[16,128,128]{2,1,0:T(8,128)(2,1)}), bf16[16,128,128]{2,1,0:T(8,128)(2,1)S(1)}, u32[]{:S(2)}, u32[]{:S(2)}) async-start(bf16[16,128,128]{2,1,0:T(8,128)(2,1)} %prepare.1), calls=%async_computation.3 | async-start | bytes 1048576 | tf_op jit(solution)/shard_map/all_to_all | solution.py:829
  37.9 20.1 %copy-start.10 = (f32[1,21]{1,0:T(1,128)S(1)}, f32[1,21]{1,0:T(1,128)}, u32[]{:S(2)}) copy-start(f32[1,21]{1,0:T(1,128)} %param.23) | copy-start | bytes 256
  37.9 20.2 %copy-start.11 = (f32[1,21]{1,0:T(1,128)S(1)}, f32[1,21]{1,0:T(1,128)}, u32[]{:S(2)}) copy-start(f32[1,21]{1,0:T(1,128)} %param.22) | copy-start | bytes 256
  37.9 20.2 %copy-start.1 = (bf16[32,128,128]{2,1,0:T(8,128)(2,1)S(1)}, bf16[32,128,128]{2,1,0:T(8,128)(2,1)}, u32[]{:S(2)}) copy-start(bf16[32,128,128]{2,1,0:T(8,128)(2,1)} %template_var.1) | copy-start | bytes 3145732
  52.2 22.3 %all-to-all-start.2 = ((bf16[32,72,128]{2,1,0:T(8,128)(2,1)}), bf16[32,72,128]{2,1,0:T(8,128)(2,1)S(1)}, u32[]{:S(2)}, u32[]{:S(2)}) async-start(bf16[32,72,128]{2,1,0:T(8,128)(2,1)} %get-tuple-element.19.payload), calls=%async_computation.2 | async-start | bytes 1179648 | tf_op jit(solution)/shard_map/all_to_all | solution.py:850
  59.4 15.1 %collective-permute-start.3 = (bf16[32,32,128]{2,1,0:T(8,128)(2,1)S(1)}, bf16[32,32,128]{2,1,0:T(8,128)(2,1)S(1)}, u32[]{:S(2)}, u32[]{:S(2)}) collective-permute-start(bf16[32,32,128]{2,1,0:T(8,128)(2,1)S(1)} %bitcast.22), channel_id=1, source_target_pairs={{0,2},{2,0},{1,3},{3,1},{4,6},{6,4},{5,7},{7,5},{8,10},{10,8},{9,1... | collective-permute-start | bytes 786440 | tf_op jit(solution)/shard_map/ppermute | solution.py:858
  75.9 7.4 %collective-permute-start.4 = (bf16[32,32,128]{2,1,0:T(8,128)(2,1)S(1)}, bf16[32,32,128]{2,1,0:T(8,128)(2,1)S(1)}, u32[]{:S(2)}, u32[]{:S(2)}) collective-permute-start(bf16[32,32,128]{2,1,0:T(8,128)(2,1)S(1)} %combine.1.refs_0_), channel_id=1, source_target_pairs={{0,2},{1,3},{2,0},{3,1},{4,6},{5,7},{6,4},{7,5},{8,10},{9,11},{10,... | collective-permute-start | bytes 786440 | tf_op jit(solution)/shard_map/ppermute | solution.py:865
  77.2 7.6 %collective-permute-start.6 = (bf16[32,32,128]{2,1,0:T(8,128)(2,1)S(1)}, bf16[32,32,128]{2,1,0:T(8,128)(2,1)S(1)}, u32[]{:S(2)}, u32[]{:S(2)}) collective-permute-start(bf16[32,32,128]{2,1,0:T(8,128)(2,1)S(1)} %combine.1.refs_0_), channel_id=1, source_target_pairs={{0,1},{1,0},{2,3},{3,2},{4,5},{5,4},{6,7},{7,6},{8,9},{9,8},{10,11... | collective-permute-start | bytes 786440 | tf_op jit(solution)/shard_map/ppermute | solution.py:865
  83.3 3.2 %collective-permute-start.5 = (bf16[32,32,128]{2,1,0:T(8,128)(2,1)S(1)}, bf16[32,32,128]{2,1,0:T(8,128)(2,1)S(1)}, u32[]{:S(2)}, u32[]{:S(2)}) collective-permute-start(bf16[32,32,128]{2,1,0:T(8,128)(2,1)S(1)} %collective-permute-done.4.refs_2_), channel_id=1, source_target_pairs={{0,1},{1,0},{2,3},{3,2},{4,5},{5,4},{6,7},{7,6},{8,9},{9,8},{10,11... | collective-permute-start | bytes 786440 | tf_op jit(solution)/shard_map/ppermute | solution.py:865

commit v14 on v13

--- a/solution.py
+++ b/solution.py
@@ -699,7 +699,9 @@
     )(me, table, parts, template_var)
 
 
-def combine_body(me, table, earlier, parts, own_var, var_template, *rest, part, capacity):
+def combine_body(
+    me, table, earlier, parts, own_var, var_template, *rest, part, nears, capacity
+):
     del earlier
     others = rest[:-3]
     out, total, gain = rest[-3:]
@@ -709,11 +711,13 @@
     exps = table.shape[0]
 
     def one(j, carry):
+        place = lax.rem(j, exps)
+        exposure = lax.rem(place, exps // nears) * nears + place // (exps // nears)
         tail = parts[j, capacity * part :, :].astype(f32)
         kernel_sum = tail[0:1] + tail[1:2] + tail[2:3]
         square = jnp.broadcast_to(kernel_sum * kernel_sum, gain.shape[1:])
         for c in range(capacity):
-            block = wanted_block(me, lax.rem(j, exps), table, j // exps, c, tract)
+            block = wanted_block(me, exposure, table, j // exps, c, tract)
             total[block] += parts[j, c * part : (c + 1) * part, :].astype(f32)
             gain[block] += square
         return carry
@@ -726,10 +730,10 @@
         out[t] = (total[t] * lax.rsqrt(jnp.maximum(variance, 1.0))).astype(bf16)
 
 
-def combine(me, table, earlier, parts, own_var, var_template, others, capacity):
+def combine(me, table, earlier, parts, own_var, var_template, others, nears, capacity):
     tract, part, side = own_var.shape
     return pl.pallas_call(
-        functools.partial(combine_body, part=part, capacity=capacity),
+        functools.partial(combine_body, part=part, nears=nears, capacity=capacity),
         out_shape=jax.ShapeDtypeStruct((tract, part, side), bf16),
         in_specs=[smem(), smem(), pl.BlockSpec(memory_space=pl.ANY)]
         + [vmem()] * (3 + len(others)),
@@ -758,7 +762,7 @@
         copy.wait()
 
 
-def join_parts(places, parts, whole, exps):
+def join_parts(places, parts, whole, exps, moved):
     tract, part, side = parts[0].shape
     count = len(parts)
     fresh = whole is None
@@ -774,7 +778,7 @@
         ],
         input_output_aliases={} if fresh else {count + 1: 0},
         compiler_params=pltpu.CompilerParams(vmem_limit_bytes=16 * mib),
-        cost_estimate=cost(0, 3_000_000 * count),
+        cost_estimate=cost(0, moved),
         name="join_parts",
     )(places, *parts, *([] if fresh else [whole]))
 
@@ -797,7 +801,7 @@
     nears = lax.axis_size("near")
     exps = lax.axis_size("far") * nears
     me = (lax.axis_index("far") * nears + lax.axis_index("near")).astype(jnp.int32)
-    order = tuple((e % nears) * (exps // nears) + e // nears for e in range(exps))
+    order = tuple(range(exps))
     tract, side, _ = template.shape
     science_img = science[0]
     variance_img = science_var[0]
@@ -847,7 +851,7 @@
         count,
         taps,
     )
-    diff_back = lax.all_to_all(payload, ("det",) + exposure_axes, split_axis=0, concat_axis=0, tiled=True)
+    diff_back = lax.all_to_all(payload, ("det", "near", "far"), split_axis=0, concat_axis=0, tiled=True)
     own_var, other_var, var_template = sum_variance(
         me[None], table, var_back, template_var, nears, capacity
     )
@@ -859,20 +863,23 @@
     scored, token = score(
         slot_of, payload, down, over_rev, high, wide, taps, order, capacity
     )
-    mine = combine(me[None], table, token, diff_back, own_var, var_template, others, capacity)
+    mine = combine(
+        me[None], table, token, diff_back, own_var, var_template, others, nears, capacity
+    )
 
     def swap(value, distance):
         return lax.ppermute(value, exposure_axes, [(e, e ^ distance) for e in range(exps)])
 
-    def put(parts, whole):
+    def put(parts, whole, moved=3_000_000):
         places = jnp.stack([part_of(there, exps, nears) for there, _ in parts])
-        return join_parts(places, [held for _, held in parts], whole, exps)
+        return join_parts(places, [held for _, held in parts], whole, exps, moved)
 
     if exps == 4:
         far = swap(mine, 2)
         near = swap(mine, 1)
         last = swap(far, 1)
-        whole = put([(me, mine), (me ^ 1, near), (me ^ 2, far)], None)
+        whole = put([(me, mine), (me ^ 1, near)], None, 1_000_000)
+        whole = put([(me ^ 2, far)], whole, 100_000_000)
         significance = put([(me ^ 3, last)], whole)
     else:
         parts = [(me, mine)]

time: 87.9 us -> 89.3 us (1.016)
  waiting for transfers between devices: 24.7 us -> 26.5 us
  starting transfers between devices: 32.2 us -> 30.9 us
    ppermute x3, starting transfers between devices: 3.13 us -> 1.72 us  [swap(): lax.ppermute(value, exposure_axes, [(e, e ^ distance) for e in range(exps)])]
    ppermute x3, waiting for transfers between devices: 5.66 us -> 7.07 us  [swap(): lax.ppermute(value, exposure_axes, [(e, e ^ distance) for e in range(exps)])]
    pallas_call x2 -> x3, Pallas kernels: 2.58 us -> 3.24 us  [join_parts(): pl.pallas_call(functools.partial(join_body, part=part, count=count), out_...]
where the time goes in v14:
time: 89.3 us; the launch traced here: 88.8 us
  starting transfers between devices  30.9 us (35%)
  Pallas kernels  27.9 us (31%)
  waiting for transfers between devices  26.5 us (30%)
  local copies, waits for them, and re-layouts  2.31 us (3%)
    pallas_call x1, Pallas kernels, fit_and_subtract(): pl.pallas_call(functools.partial(fit_body, order=order, capacity=capacity...  14.2 us
    all_to_all x1, waiting for transfers between devices, local(): lax.all_to_all(payload, ('det', 'near', 'far'), split_axis=0, concat_axis...  11 us
    all_to_all x1, starting transfers between devices, local(): lax.all_to_all(var_late, ('det', 'near'), split_axis=0, concat_axis=0, ti...  8.11 us
    ppermute x3, waiting for transfers between devices, swap(): lax.ppermute(value, exposure_axes, [(e, e ^ distance) for e in range(exps)])  7.07 us
    all_to_all x1, starting transfers between devices, local(): lax.all_to_all(request, 'det', split_axis=0, concat_axis=0, tiled=True)  6.37 us
    all_to_all x1, starting transfers between devices, local(): lax.all_to_all(payload, ('det', 'near', 'far'), split_axis=0, concat_axis...  5.78 us
    all_to_all x1, waiting for transfers between devices, local(): lax.all_to_all(request, 'det', split_axis=0, concat_axis=0, tiled=True)  3.89 us
    ppermute x3, starting transfers between devices, from_exposure(): return lax.ppermute(value, exposure_axes, pairs)  3.88 us
  transfers between devices with their start and end apart: 11, of which 6 were waited for; matrix products, arithmetic and copies ran while one was open for 1% of the time, Pallas kernels for 25%

profile of v14, /device:TPU:1, one launch (start us, length us, event | category | flops | bytes accessed | tf_op | source)
XLA Modules:
  0.0 88.8 jit_solution(17472584136974041075)
XLA Ops:
  0.6 1.4 %route_tables.1 = (s32[16]{0:T(128)}, s32[16]{0:T(128)}, s32[8,1,2]{2,1,0:T(1,128)}) custom-call(s32[1,16]{1,0:T(1,128)} %src.1, s32[1,16]{1,0:T(1,128)} %blk.1), custom_call_target="tpu_custom_call" | custom-call | tf_op jit(solution)/shard_map/route_tables/pallas_call | solution.py:70
  2.0 6.4 %all-to-all-start = ((s32[8,1,2]{2,1,0:T(1,128)}), s32[8,1,2]{2,1,0:T(1,128)S(1)}, u32[]{:S(2)}, u32[]{:S(2)}) async-start(s32[8,1,2]{2,1,0:T(1,128)} %get-tuple-element.15), calls=%async_computation | async-start | bytes 8192 | tf_op jit(solution)/shard_map/all_to_all | solution.py:815
  8.4 1.2 %copy-done = bf16[32,128,128]{2,1,0:T(8,128)(2,1)S(1)} copy-done((bf16[32,128,128]{2,1,0:T(8,128)(2,1)S(1)}, bf16[32,128,128]{2,1,0:T(8,128)(2,1)}, u32[]{:S(2)}) %copy-start) | copy-done | bytes 1048600
  9.8 3.9 %all-to-all-done.asked = s32[8,1,2]{2,1,0:T(1,128)S(1)} async-done(((s32[8,1,2]{2,1,0:T(1,128)}), s32[8,1,2]{2,1,0:T(1,128)S(1)}, u32[]{:S(2)}, u32[]{:S(2)}) %all-to-all-start) | async-done | bytes 96 | tf_op jit(solution)/shard_map/all_to_all | solution.py:815
  13.6 1.5 %pick_blocks.1.earlier = bf16[16,128,128]{2,1,0:T(8,128)(2,1)} custom-call(s32[8,1,2]{2,1,0:T(1,128)S(1)} %all-to-all-done.asked, bf16[32,128,128]{2,1,0:T(8,128)(2,1)S(1)} %fetch.1.template), custom_call_target="tpu_custom_call" | custom-call | tf_op jit(solution)/shard_map/pick_blocks/pallas_call | solution.py:114
  15.2 3.6 %all-to-all-start.1 = ((bf16[16,128,128]{2,1,0:T(8,128)(2,1)}), bf16[16,128,128]{2,1,0:T(8,128)(2,1)S(1)}, u32[]{:S(2)}, u32[]{:S(2)}) async-start(bf16[16,128,128]{2,1,0:T(8,128)(2,1)} %pick_blocks.1.earlier), calls=%async_computation.1 | async-start | bytes 1048576 | tf_op jit(solution)/shard_map/all_to_all | solution.py:821
  19.4 2.2 %collective-permute-start = (s32[8,1,2]{2,1,0:T(1,128)S(1)}, s32[8,1,2]{2,1,0:T(1,128)S(1)}, u32[]{:S(2)}, u32[]{:S(2)}) collective-permute-start(s32[8,1,2]{2,1,0:T(1,128)S(1)} %hold.1), channel_id=1, source_target_pairs={{0,1},{1,0},{2,3},{3,2},{4,5},{5,4},{6,7},{7,6},{8,9},{9,8},{10,11... | collective-permute-start | bytes 200 | tf_op jit(solution)/shard_map/ppermute | solution.py:45
  21.6 1.3 %collective-permute-start.1 = (s32[8,1,2]{2,1,0:T(1,128)S(1)}, s32[8,1,2]{2,1,0:T(1,128)S(1)}, u32[]{:S(2)}, u32[]{:S(2)}) collective-permute-start(s32[8,1,2]{2,1,0:T(1,128)S(1)} %hold.1), channel_id=1, source_target_pairs={{0,2},{1,3},{2,0},{3,1},{4,6},{5,7},{6,4},{7,5},{8,10},{9,11},{10,... | collective-permute-start | bytes 200 | tf_op jit(solution)/shard_map/ppermute | solution.py:45
  23.4 0.9 %collective-permute-done.1 = s32[8,1,2]{2,1,0:T(1,128)S(1)} collective-permute-done((s32[8,1,2]{2,1,0:T(1,128)S(1)}, s32[8,1,2]{2,1,0:T(1,128)S(1)}, u32[]{:S(2)}, u32[]{:S(2)}) %collective-permute-start.1) | collective-permute-done | bytes 96 | tf_op jit(solution)/shard_map/ppermute | solution.py:45
  24.4 1.7 %collective-permute-done.2 = s32[8,1,2]{2,1,0:T(1,128)S(1)} collective-permute-done((s32[8,1,2]{2,1,0:T(1,128)S(1)}, s32[8,1,2]{2,1,0:T(1,128)S(1)}, u32[]{:S(2)}, u32[]{:S(2)}) %collective-permute-start.2) | collective-permute-done | bytes 96 | tf_op jit(solution)/shard_map/ppermute | solution.py:45
  26.3 1.5 %prepare.1 = bf16[16,128,128]{2,1,0:T(8,128)(2,1)} custom-call(s32[16]{0:T(128)S(1)} %copy-done.4, bf16[256,1024]{1,0:T(8,128)(2,1)S(1)} %bitcast.20, bf16[256,1024]{1,0:T(8,128)(2,1)S(1)} %bitcast.18, s32[4,8,2]{2,1,0:T(8,128)S(1)} %copy.36.earlier.table), custom_call_target="tpu_custom_call" | custom-call | bytes 6000000 | tf_op jit(solution)/shard_map/prepare/pallas_call | solution.py:175
  27.9 1.9 %all-to-all-done.1.arrived = bf16[16,128,128]{2,1,0:T(8,128)(2,1)S(1)} async-done(((bf16[16,128,128]{2,1,0:T(8,128)(2,1)}), bf16[16,128,128]{2,1,0:T(8,128)(2,1)S(1)}, u32[]{:S(2)}, u32[]{:S(2)}) %all-to-all-start.1) | async-done | bytes 524320 | tf_op jit(solution)/shard_map/all_to_all | solution.py:821
  29.8 8.1 %all-to-all-start.3 = ((bf16[16,128,128]{2,1,0:T(8,128)(2,1)}), bf16[16,128,128]{2,1,0:T(8,128)(2,1)S(1)}, u32[]{:S(2)}, u32[]{:S(2)}) async-start(bf16[16,128,128]{2,1,0:T(8,128)(2,1)} %prepare.1), calls=%async_computation.3 | async-start | bytes 1048576 | tf_op jit(solution)/shard_map/all_to_all | solution.py:833
  38.0 14.2 %fit_and_subtract.1 = (f32[1,128]{1,0:T(1,128)}, bf16[32,72,128]{2,1,0:T(8,128)(2,1)}) custom-call(s32[16]{0:T(128)S(1)} %copy-done.7, s32[16]{0:T(128)S(1)} %copy-done.4, s32[1,4]{1,0:T(1,128)S(1)} %copy-done.5, s32[1,4]{1,0:T(1,128)S(1)} %copy-done.6, bf16[16,128,128]{2,1,0:T(8,128)(2,1)S(1)} %all-to-all-done.1.arrived, ...), custom_call_target="tpu_custom_call" | custom-call | flops 15000000512 | bytes 8000000 | tf_op jit(solution)/shard_map/fit_and_subtract/pallas_call | solution.py:537
  52.2 5.8 %all-to-all-start.2 = ((bf16[32,72,128]{2,1,0:T(8,128)(2,1)}), bf16[32,72,128]{2,1,0:T(8,128)(2,1)S(1)}, u32[]{:S(2)}, u32[]{:S(2)}) async-start(bf16[32,72,128]{2,1,0:T(8,128)(2,1)} %get-tuple-element.19.payload), calls=%async_computation.2 | async-start | bytes 1179648 | tf_op jit(solution)/shard_map/all_to_all | solution.py:854
  58.2 1.2 %sum_variance.1 = (f32[32,32,128]{2,1,0:T(8,128)S(1)}, bf16[1,32,32,128]{3,2,1,0:T(8,128)(2,1)S(1)}, bf16[32,32,128]{2,1,0:T(8,128)(2,1)S(1)}) custom-call(s32[1]{0:T(128)} %bitcast.1.me, s32[4,8,2]{2,1,0:T(8,128)S(1)} %copy.36.earlier.table, bf16[16,128,128]{2,1,0:T(8,128)(2,1)S(1)} %all-to-all-done.3.parts, bf16[32,128,128]{2,1,0:T(8,128)(2,1)S(1)} %copy-done.1), custom_call_target="tpu_custom_call" | custom-call | bytes 4000000 | tf_op jit(solution)/shard_map/sum_variance/pallas_call | solution.py:683
  59.4 1.5 %collective-permute-start.3 = (bf16[32,32,128]{2,1,0:T(8,128)(2,1)S(1)}, bf16[32,32,128]{2,1,0:T(8,128)(2,1)S(1)}, u32[]{:S(2)}, u32[]{:S(2)}) collective-permute-start(bf16[32,32,128]{2,1,0:T(8,128)(2,1)S(1)} %bitcast.22), channel_id=1, source_target_pairs={{0,2},{2,0},{1,3},{3,1},{4,6},{6,4},{5,7},{7,5},{8,10},{10,8},{9,1... | collective-permute-start | bytes 786440 | tf_op jit(solution)/shard_map/ppermute | solution.py:862
  61.0 3.1 %score.1 = (f32[256,1024]{1,0:T(8,128)}, f32[8,128]{1,0:T(8,128)S(1)}) custom-call(s32[16]{0:T(128)S(1)} %copy-done.7, bf16[32,72,128]{2,1,0:T(8,128)(2,1)} %get-tuple-element.19.payload, f32[1,256]{1,0:T(1,128)S(1)} %pad.26.down, f32[1,256]{1,0:T(1,128)S(1)} %pad_maximum_fusion.1.over), custom_call_target="tpu_custom_call" | custom-call | flops 2000000000 | bytes 2000000 | tf_op jit(solution)/shard_map/score/pallas_call | solution.py:625
  64.1 11.0 %all-to-all-done.2.parts = bf16[32,72,128]{2,1,0:T(8,128)(2,1)S(1)} async-done(((bf16[32,72,128]{2,1,0:T(8,128)(2,1)}), bf16[32,72,128]{2,1,0:T(8,128)(2,1)S(1)}, u32[]{:S(2)}, u32[]{:S(2)}) %all-to-all-start.2) | async-done | bytes 589856 | tf_op jit(solution)/shard_map/all_to_all | solution.py:854
  75.1 1.5 %combine.1.refs_0_ = bf16[32,32,128]{2,1,0:T(8,128)(2,1)S(1)} custom-call(s32[1]{0:T(128)} %bitcast.1.me, s32[4,8,2]{2,1,0:T(8,128)S(1)} %copy.36.earlier.table, f32[8,128]{1,0:T(8,128)S(1)} %get-tuple-element.20.earlier, bf16[32,72,128]{2,1,0:T(8,128)(2,1)S(1)} %all-to-all-done.2.parts, f32[32,32,128]{2,1,0:T(8,128)S(1)} %get-tuple-element.22.own_var, ...), custom_call_target="tpu_custom_call" | custom-call | tf_op jit(solution)/shard_map/combine/pallas_call | solution.py:735
  76.7 1.2 %collective-permute-start.6 = (bf16[32,32,128]{2,1,0:T(8,128)(2,1)S(1)}, bf16[32,32,128]{2,1,0:T(8,128)(2,1)S(1)}, u32[]{:S(2)}, u32[]{:S(2)}) collective-permute-start(bf16[32,32,128]{2,1,0:T(8,128)(2,1)S(1)} %combine.1.refs_0_), channel_id=1, source_target_pairs={{0,1},{1,0},{2,3},{3,2},{4,5},{5,4},{6,7},{7,6},{8,9},{9,8},{10,11... | collective-permute-start | bytes 786440 | tf_op jit(solution)/shard_map/ppermute | solution.py:871
  77.9 7.1 %collective-permute-done.4.refs_0_ = bf16[32,32,128]{2,1,0:T(8,128)(2,1)S(1)} collective-permute-done((bf16[32,32,128]{2,1,0:T(8,128)(2,1)S(1)}, bf16[32,32,128]{2,1,0:T(8,128)(2,1)S(1)}, u32[]{:S(2)}, u32[]{:S(2)}) %collective-permute-start.4) | collective-permute-done | bytes 262176 | tf_op jit(solution)/shard_map/ppermute | solution.py:871
  85.5 1.6 %join_parts.3.refs_1_ = f32[32,128,128]{2,1,0:T(8,128)} custom-call(s32[2]{0:T(128)S(1)} %pad_add_fusion.places, bf16[32,32,128]{2,1,0:T(8,128)(2,1)S(1)} %combine.1.refs_0_, bf16[32,32,128]{2,1,0:T(8,128)(2,1)S(1)} %collective-permute-done.6.refs_1_), custom_call_target="tpu_custom_call" | custom-call | bytes 1000000 | tf_op jit(solution)/shard_map/join_parts/pallas_call | solution.py:770
  87.1 0.8 join_parts.4.refs_1_
  (53 shorter events, 3.3 us)
Async XLA Ops:
  2.0 11.6 %all-to-all-start = ((s32[8,1,2]{2,1,0:T(1,128)}), s32[8,1,2]{2,1,0:T(1,128)S(1)}, u32[]{:S(2)}, u32[]{:S(2)}) async-start(s32[8,1,2]{2,1,0:T(1,128)} %get-tuple-element.15), calls=%async_computation | async-start | bytes 8192 | tf_op jit(solution)/shard_map/all_to_all | solution.py:815
  8.4 1.2 %copy-start = (bf16[32,128,128]{2,1,0:T(8,128)(2,1)S(1)}, bf16[32,128,128]{2,1,0:T(8,128)(2,1)}, u32[]{:S(2)}) copy-start(bf16[32,128,128]{2,1,0:T(8,128)(2,1)} %template.1) | copy-start | bytes 3145732
  9.6 9.2 %copy-start.9 = (bf16[40,21]{0,1:T(8,128)(2,1)S(1)}, bf16[40,21]{0,1:T(8,128)(2,1)}, u32[]{:S(2)}) copy-start(bf16[40,21]{0,1:T(8,128)(2,1)} %param.21) | copy-start | bytes 5044
  9.6 9.4 %copy-start.8 = (bf16[40,21]{0,1:T(8,128)(2,1)S(1)}, bf16[40,21]{0,1:T(8,128)(2,1)}, u32[]{:S(2)}) copy-start(bf16[40,21]{0,1:T(8,128)(2,1)} %param.20) | copy-start | bytes 5044
  9.7 16.6 %copy-start.2 = (bf16[1,256,1024]{2,1,0:T(8,128)(2,1)S(1)}, bf16[1,256,1024]{2,1,0:T(8,128)(2,1)}, u32[]{:S(2)}) copy-start(bf16[1,256,1024]{2,1,0:T(8,128)(2,1)} %param.14) | copy-start | bytes 1572868
  9.7 16.6 %copy-start.3 = (bf16[1,256,1024]{2,1,0:T(8,128)(2,1)S(1)}, bf16[1,256,1024]{2,1,0:T(8,128)(2,1)}, u32[]{:S(2)}) copy-start(bf16[1,256,1024]{2,1,0:T(8,128)(2,1)} %param.15) | copy-start | bytes 1572868
  9.7 16.6 %copy-start.4 = (s32[16]{0:T(128)S(1)}, s32[16]{0:T(128)}, u32[]{:S(2)}) copy-start(s32[16]{0:T(128)} %get-tuple-element.17.sender) | copy-start | bytes 196
  15.2 22.7 %copy-start.5 = (s32[1,4]{1,0:T(1,128)S(1)}, s32[1,4]{1,0:T(1,128)}, u32[]{:S(2)}) copy-start(s32[1,4]{1,0:T(1,128)} %rows_at.1) | copy-start | bytes 52
  15.2 22.7 %copy-start.6 = (s32[1,4]{1,0:T(1,128)S(1)}, s32[1,4]{1,0:T(1,128)}, u32[]{:S(2)}) copy-start(s32[1,4]{1,0:T(1,128)} %cols_at.1) | copy-start | bytes 52
  15.2 22.7 %copy-start.7 = (s32[16]{0:T(128)S(1)}, s32[16]{0:T(128)}, u32[]{:S(2)}) copy-start(s32[16]{0:T(128)} %get-tuple-element.16.slot_of) | copy-start | bytes 196
  15.2 14.6 %all-to-all-start.1 = ((bf16[16,128,128]{2,1,0:T(8,128)(2,1)}), bf16[16,128,128]{2,1,0:T(8,128)(2,1)S(1)}, u32[]{:S(2)}, u32[]{:S(2)}) async-start(bf16[16,128,128]{2,1,0:T(8,128)(2,1)} %pick_blocks.1.earlier), calls=%async_computation.1 | async-start | bytes 1048576 | tf_op jit(solution)/shard_map/all_to_all | solution.py:821
  19.4 4.0 %collective-permute-start = (s32[8,1,2]{2,1,0:T(1,128)S(1)}, s32[8,1,2]{2,1,0:T(1,128)S(1)}, u32[]{:S(2)}, u32[]{:S(2)}) collective-permute-start(s32[8,1,2]{2,1,0:T(1,128)S(1)} %hold.1), channel_id=1, source_target_pairs={{0,1},{1,0},{2,3},{3,2},{4,5},{5,4},{6,7},{7,6},{8,9},{9,8},{10,11... | collective-permute-start | bytes 200 | tf_op jit(solution)/shard_map/ppermute | solution.py:45
  21.6 2.8 %collective-permute-start.1 = (s32[8,1,2]{2,1,0:T(1,128)S(1)}, s32[8,1,2]{2,1,0:T(1,128)S(1)}, u32[]{:S(2)}, u32[]{:S(2)}) collective-permute-start(s32[8,1,2]{2,1,0:T(1,128)S(1)} %hold.1), channel_id=1, source_target_pairs={{0,2},{1,3},{2,0},{3,1},{4,6},{5,7},{6,4},{7,5},{8,10},{9,11},{10,... | collective-permute-start | bytes 200 | tf_op jit(solution)/shard_map/ppermute | solution.py:45
  22.8 3.3 %collective-permute-start.2 = (s32[8,1,2]{2,1,0:T(1,128)S(1)}, s32[8,1,2]{2,1,0:T(1,128)S(1)}, u32[]{:S(2)}, u32[]{:S(2)}) collective-permute-start(s32[8,1,2]{2,1,0:T(1,128)S(1)} %hold.1), channel_id=1, source_target_pairs={{0,3},{1,2},{2,1},{3,0},{4,7},{5,6},{6,5},{7,4},{8,11},{9,10},{10,... | collective-permute-start | bytes 200 | tf_op jit(solution)/shard_map/ppermute | solution.py:45
  29.8 22.4 %all-to-all-start.3 = ((bf16[16,128,128]{2,1,0:T(8,128)(2,1)}), bf16[16,128,128]{2,1,0:T(8,128)(2,1)S(1)}, u32[]{:S(2)}, u32[]{:S(2)}) async-start(bf16[16,128,128]{2,1,0:T(8,128)(2,1)} %prepare.1), calls=%async_computation.3 | async-start | bytes 1048576 | tf_op jit(solution)/shard_map/all_to_all | solution.py:833
  37.9 20.1 %copy-start.10 = (f32[1,21]{1,0:T(1,128)S(1)}, f32[1,21]{1,0:T(1,128)}, u32[]{:S(2)}) copy-start(f32[1,21]{1,0:T(1,128)} %param.23) | copy-start | bytes 256
  37.9 20.2 %copy-start.11 = (f32[1,21]{1,0:T(1,128)S(1)}, f32[1,21]{1,0:T(1,128)}, u32[]{:S(2)}) copy-start(f32[1,21]{1,0:T(1,128)} %param.22) | copy-start | bytes 256
  37.9 20.2 %copy-start.1 = (bf16[32,128,128]{2,1,0:T(8,128)(2,1)S(1)}, bf16[32,128,128]{2,1,0:T(8,128)(2,1)}, u32[]{:S(2)}) copy-start(bf16[32,128,128]{2,1,0:T(8,128)(2,1)} %template_var.1) | copy-start | bytes 3145732
  52.2 22.9 %all-to-all-start.2 = ((bf16[32,72,128]{2,1,0:T(8,128)(2,1)}), bf16[32,72,128]{2,1,0:T(8,128)(2,1)S(1)}, u32[]{:S(2)}, u32[]{:S(2)}) async-start(bf16[32,72,128]{2,1,0:T(8,128)(2,1)} %get-tuple-element.19.payload), calls=%async_computation.2 | async-start | bytes 1179648 | tf_op jit(solution)/shard_map/all_to_all | solution.py:854
  59.4 15.7 %collective-permute-start.3 = (bf16[32,32,128]{2,1,0:T(8,128)(2,1)S(1)}, bf16[32,32,128]{2,1,0:T(8,128)(2,1)S(1)}, u32[]{:S(2)}, u32[]{:S(2)}) collective-permute-start(bf16[32,32,128]{2,1,0:T(8,128)(2,1)S(1)} %bitcast.22), channel_id=1, source_target_pairs={{0,2},{2,0},{1,3},{3,1},{4,6},{6,4},{5,7},{7,5},{8,10},{10,8},{9,1... | collective-permute-start | bytes 786440 | tf_op jit(solution)/shard_map/ppermute | solution.py:862
  76.6 8.4 %collective-permute-start.4 = (bf16[32,32,128]{2,1,0:T(8,128)(2,1)S(1)}, bf16[32,32,128]{2,1,0:T(8,128)(2,1)S(1)}, u32[]{:S(2)}, u32[]{:S(2)}) collective-permute-start(bf16[32,32,128]{2,1,0:T(8,128)(2,1)S(1)} %combine.1.refs_0_), channel_id=1, source_target_pairs={{0,2},{1,3},{2,0},{3,1},{4,6},{5,7},{6,4},{7,5},{8,10},{9,11},{10,... | collective-permute-start | bytes 786440 | tf_op jit(solution)/shard_map/ppermute | solution.py:871
  76.7 8.8 %collective-permute-start.6 = (bf16[32,32,128]{2,1,0:T(8,128)(2,1)S(1)}, bf16[32,32,128]{2,1,0:T(8,128)(2,1)S(1)}, u32[]{:S(2)}, u32[]{:S(2)}) collective-permute-start(bf16[32,32,128]{2,1,0:T(8,128)(2,1)S(1)} %combine.1.refs_0_), channel_id=1, source_target_pairs={{0,1},{1,0},{2,3},{3,2},{4,5},{5,4},{6,7},{7,6},{8,9},{9,8},{10,11... | collective-permute-start | bytes 786440 | tf_op jit(solution)/shard_map/ppermute | solution.py:871
  85.0 2.9 %collective-permute-start.5 = (bf16[32,32,128]{2,1,0:T(8,128)(2,1)S(1)}, bf16[32,32,128]{2,1,0:T(8,128)(2,1)S(1)}, u32[]{:S(2)}, u32[]{:S(2)}) collective-permute-start(bf16[32,32,128]{2,1,0:T(8,128)(2,1)S(1)} %collective-permute-done.4.refs_0_), channel_id=1, source_target_pairs={{0,1},{1,0},{2,3},{3,2},{4,5},{5,4},{6,7},{7,6},{8,9},{9,8},{10,11... | collective-permute-start | bytes 786440 | tf_op jit(solution)/shard_map/ppermute | solution.py:871

commit v15 on v13

--- a/solution.py
+++ b/solution.py
@@ -45,14 +45,15 @@
     return lax.ppermute(value, exposure_axes, pairs)
 
 
-def route_body(src, blk, slot_of, sender, request, count, *, peers, capacity):
+def route_body(src, blk, earlier, slot_of, sender, count, *, peers, capacity):
+    del earlier
+
     def clear_count(p, carry):
         count[p] = 0
         return carry
 
     def clear_slot(s, carry):
         sender[s] = 0
-        request[s // capacity, 0, s % capacity] = 0
         return carry
 
     lax.fori_loop(0, peers, clear_count, 0, unroll=peers <= 16)
@@ -63,21 +64,42 @@
         count[owner] = place + 1
         slot_of[b] = owner * capacity + place
         sender[owner * capacity + place] = b
-        request[owner, 0, place] = blk[0, b] + 1
-
-
-def route_tables(routes_src, routes_blk, peers, capacity):
+
+
+def route_tables(routes_src, routes_blk, earlier, peers, capacity):
     return pl.pallas_call(
         functools.partial(route_body, peers=peers, capacity=capacity),
         out_shape=(
             jax.ShapeDtypeStruct((routes_src.shape[1],), jnp.int32),
             jax.ShapeDtypeStruct((peers * capacity,), jnp.int32),
-            jax.ShapeDtypeStruct((peers, 1, capacity), jnp.int32),
         ),
-        in_specs=[smem()] * 2,
-        out_specs=(smem(),) * 3,
+        in_specs=[smem()] * 2 + [pl.BlockSpec(memory_space=pl.ANY)],
+        out_specs=(smem(),) * 2,
         scratch_shapes=[pltpu.SMEM((peers,), jnp.int32)],
         name="route_tables",
+    )(routes_src, routes_blk, earlier)
+
+
+def request_body(src, blk, request, count, *, peers, capacity):
+    for p in range(peers):
+        count[p] = 0
+        for c in range(capacity):
+            request[p, 0, c] = 0
+    for b in range(src.shape[1]):
+        owner = src[0, b]
+        place = count[owner]
+        count[owner] = place + 1
+        request[owner, 0, place] = blk[0, b] + 1
+
+
+def request_table(routes_src, routes_blk, peers, capacity):
+    return pl.pallas_call(
+        functools.partial(request_body, peers=peers, capacity=capacity),
+        out_shape=jax.ShapeDtypeStruct((peers, 1, capacity), jnp.int32),
+        in_specs=[smem()] * 2,
+        out_specs=smem(),
+        scratch_shapes=[pltpu.SMEM((peers,), jnp.int32)],
+        name="request_table",
     )(routes_src, routes_blk)
 
 
@@ -807,9 +829,10 @@
     slots = peers * capacity
     part = side // exps
 
-    slot_of, sender, request = route_tables(routes_src, routes_blk, peers, capacity)
+    request = request_table(routes_src, routes_blk, peers, capacity)
     asked = lax.all_to_all(request, "det", split_axis=0, concat_axis=0, tiled=True)
     picked = pick_blocks(asked, fetch(template), slots, capacity)
+    slot_of, sender = route_tables(routes_src, routes_blk, picked, peers, capacity)
     held = hold(asked, picked)
     tables = [held] + [from_exposure(held, g, exps) for g in range(1, exps)]
     table = jnp.stack(tables).reshape(exps, peers, capacity)

time: 87.9 us -> 87.7 us (level)
  waiting for transfers between devices: 24.7 us -> 22.7 us
  Pallas kernels: 27.1 us -> 28.3 us
    all_to_all x1, waiting for transfers between devices: 2.6 us -> 0.54 us  [local(): lax.all_to_all(picked, 'det', split_axis=0, concat_axis=0, tiled=True)]
    pallas_call x0 -> x1, Pallas kernels: none -> 1.36 us  [request_table(): pl.pallas_call(functools.partial(request_body, peers=peers, capacity=capa...]
  transfers between devices with their start and end apart: 11 -> 11, of which waited for: 6 -> 6; matrix products, arithmetic and copies ran while one was open for 1% -> 1% of each run, Pallas kernels for 25% -> 27%
where the time goes in v15:
time: 87.7 us; the launch traced here: 87.1 us
  starting transfers between devices  32.1 us (37%)
  Pallas kernels  28.3 us (32%)
  waiting for transfers between devices  22.7 us (26%)
  local copies, waits for them, and re-layouts  2.96 us (3%)
    pallas_call x1, Pallas kernels, fit_and_subtract(): pl.pallas_call(functools.partial(fit_body, order=order, capacity=capacity...  14.2 us
    all_to_all x1, waiting for transfers between devices, local(): lax.all_to_all(payload, ('det',) + exposure_axes, split_axis=0, concat_ax...  10.4 us
    all_to_all x1, starting transfers between devices, local(): lax.all_to_all(var_late, ('det', 'near'), split_axis=0, concat_axis=0, ti...  8.11 us
    all_to_all x1, starting transfers between devices, local(): lax.all_to_all(request, 'det', split_axis=0, concat_axis=0, tiled=True)  6.37 us
    all_to_all x1, starting transfers between devices, local(): lax.all_to_all(payload, ('det',) + exposure_axes, split_axis=0, concat_ax...  5.79 us
    ppermute x3, waiting for transfers between devices, swap(): lax.ppermute(value, exposure_axes, [(e, e ^ distance) for e in range(exps)])  5.66 us
    all_to_all x1, waiting for transfers between devices, local(): lax.all_to_all(request, 'det', split_axis=0, concat_axis=0, tiled=True)  3.9 us
    ppermute x3, starting transfers between devices, from_exposure(): return lax.ppermute(value, exposure_axes, pairs)  3.7 us
  transfers between devices with their start and end apart: 11, of which 6 were waited for; matrix products, arithmetic and copies ran while one was open for 1% of the time, Pallas kernels for 27%

profile of v15, /device:TPU:1, one launch (start us, length us, event | category | flops | bytes accessed | tf_op | source)
XLA Modules:
  0.0 87.1 jit_solution(11829419418609843046)
XLA Ops:
  0.6 1.4 %request_table.1 = s32[8,1,2]{2,1,0:T(1,128)} custom-call(s32[1,16]{1,0:T(1,128)} %src.3, s32[1,16]{1,0:T(1,128)} %blk.3), custom_call_target="tpu_custom_call" | custom-call | tf_op jit(solution)/shard_map/request_table/pallas_call | solution.py:96
  2.0 6.4 %all-to-all-start = ((s32[8,1,2]{2,1,0:T(1,128)}), s32[8,1,2]{2,1,0:T(1,128)S(1)}, u32[]{:S(2)}, u32[]{:S(2)}) async-start(s32[8,1,2]{2,1,0:T(1,128)} %request_table.1), calls=%async_computation | async-start | bytes 8192 | tf_op jit(solution)/shard_map/all_to_all | solution.py:833
  8.4 1.2 %copy-done = bf16[32,128,128]{2,1,0:T(8,128)(2,1)S(1)} copy-done((bf16[32,128,128]{2,1,0:T(8,128)(2,1)S(1)}, bf16[32,128,128]{2,1,0:T(8,128)(2,1)}, u32[]{:S(2)}) %copy-start) | copy-done | bytes 1048600
  9.7 3.9 %all-to-all-done.asked = s32[8,1,2]{2,1,0:T(1,128)S(1)} async-done(((s32[8,1,2]{2,1,0:T(1,128)}), s32[8,1,2]{2,1,0:T(1,128)S(1)}, u32[]{:S(2)}, u32[]{:S(2)}) %all-to-all-start) | async-done | bytes 96 | tf_op jit(solution)/shard_map/all_to_all | solution.py:833
  13.6 1.5 %pick_blocks.1.earlier = bf16[16,128,128]{2,1,0:T(8,128)(2,1)} custom-call(s32[8,1,2]{2,1,0:T(1,128)S(1)} %all-to-all-done.asked, bf16[32,128,128]{2,1,0:T(8,128)(2,1)S(1)} %fetch.1.template), custom_call_target="tpu_custom_call" | custom-call | tf_op jit(solution)/shard_map/pick_blocks/pallas_call | solution.py:136
  15.1 3.5 %all-to-all-start.1 = ((bf16[16,128,128]{2,1,0:T(8,128)(2,1)}), bf16[16,128,128]{2,1,0:T(8,128)(2,1)S(1)}, u32[]{:S(2)}, u32[]{:S(2)}) async-start(bf16[16,128,128]{2,1,0:T(8,128)(2,1)} %pick_blocks.1.earlier), calls=%async_computation.1 | async-start | bytes 1048576 | tf_op jit(solution)/shard_map/all_to_all | solution.py:840
  19.2 1.3 %route_tables.1 = (s32[16]{0:T(128)}, s32[16]{0:T(128)}) custom-call(s32[1,16]{1,0:T(1,128)} %src.3, s32[1,16]{1,0:T(1,128)} %blk.3, bf16[16,128,128]{2,1,0:T(8,128)(2,1)} %pick_blocks.1.earlier), custom_call_target="tpu_custom_call" | custom-call | tf_op jit(solution)/shard_map/route_tables/pallas_call | solution.py:70
  20.6 3.2 %collective-permute-start.2 = (s32[8,1,2]{2,1,0:T(1,128)S(1)}, s32[8,1,2]{2,1,0:T(1,128)S(1)}, u32[]{:S(2)}, u32[]{:S(2)}) collective-permute-start(s32[8,1,2]{2,1,0:T(1,128)S(1)} %hold.1), channel_id=1, source_target_pairs={{0,3},{1,2},{2,1},{3,0},{4,7},{5,6},{6,5},{7,4},{8,11},{9,10},{10,... | collective-permute-start | bytes 200 | tf_op jit(solution)/shard_map/ppermute | solution.py:45
  24.3 1.0 %collective-permute-done.2 = s32[8,1,2]{2,1,0:T(1,128)S(1)} collective-permute-done((s32[8,1,2]{2,1,0:T(1,128)S(1)}, s32[8,1,2]{2,1,0:T(1,128)S(1)}, u32[]{:S(2)}, u32[]{:S(2)}) %collective-permute-start.2) | collective-permute-done | bytes 96 | tf_op jit(solution)/shard_map/ppermute | solution.py:45
  25.4 1.2 %collective-permute-done.1 = s32[8,1,2]{2,1,0:T(1,128)S(1)} collective-permute-done((s32[8,1,2]{2,1,0:T(1,128)S(1)}, s32[8,1,2]{2,1,0:T(1,128)S(1)}, u32[]{:S(2)}, u32[]{:S(2)}) %collective-permute-start.1) | collective-permute-done | bytes 96 | tf_op jit(solution)/shard_map/ppermute | solution.py:45
  27.5 1.5 %prepare.1 = bf16[16,128,128]{2,1,0:T(8,128)(2,1)} custom-call(s32[16]{0:T(128)S(1)} %copy-done.4, bf16[256,1024]{1,0:T(8,128)(2,1)S(1)} %bitcast.20, bf16[256,1024]{1,0:T(8,128)(2,1)S(1)} %bitcast.18, s32[4,8,2]{2,1,0:T(8,128)S(1)} %copy.35.earlier.table), custom_call_target="tpu_custom_call" | custom-call | bytes 6000000 | tf_op jit(solution)/shard_map/prepare/pallas_call | solution.py:197
  29.6 8.1 %all-to-all-start.3 = ((bf16[16,128,128]{2,1,0:T(8,128)(2,1)}), bf16[16,128,128]{2,1,0:T(8,128)(2,1)S(1)}, u32[]{:S(2)}, u32[]{:S(2)}) async-start(bf16[16,128,128]{2,1,0:T(8,128)(2,1)} %prepare.1), calls=%async_computation.3 | async-start | bytes 1048576 | tf_op jit(solution)/shard_map/all_to_all | solution.py:852
  37.7 14.2 %fit_and_subtract.1 = (f32[1,128]{1,0:T(1,128)}, bf16[32,72,128]{2,1,0:T(8,128)(2,1)}) custom-call(s32[16]{0:T(128)S(1)} %copy-done.7, s32[16]{0:T(128)S(1)} %copy-done.4, s32[1,4]{1,0:T(1,128)S(1)} %copy-done.5, s32[1,4]{1,0:T(1,128)S(1)} %copy-done.6, bf16[16,128,128]{2,1,0:T(8,128)(2,1)S(1)} %all-to-all-done.1.arrived, ...), custom_call_target="tpu_custom_call" | custom-call | flops 15000000512 | bytes 8000000 | tf_op jit(solution)/shard_map/fit_and_subtract/pallas_call | solution.py:559
  52.0 5.8 %all-to-all-start.2 = ((bf16[32,72,128]{2,1,0:T(8,128)(2,1)}), bf16[32,72,128]{2,1,0:T(8,128)(2,1)S(1)}, u32[]{:S(2)}, u32[]{:S(2)}) async-start(bf16[32,72,128]{2,1,0:T(8,128)(2,1)} %get-tuple-element.17.payload), calls=%async_computation.2 | async-start | bytes 1179648 | tf_op jit(solution)/shard_map/all_to_all | solution.py:873
  58.0 1.2 %sum_variance.1 = (f32[32,32,128]{2,1,0:T(8,128)S(1)}, bf16[1,32,32,128]{3,2,1,0:T(8,128)(2,1)S(1)}, bf16[32,32,128]{2,1,0:T(8,128)(2,1)S(1)}) custom-call(s32[1]{0:T(128)} %bitcast.1.me, s32[4,8,2]{2,1,0:T(8,128)S(1)} %copy.35.earlier.table, bf16[16,128,128]{2,1,0:T(8,128)(2,1)S(1)} %all-to-all-done.3.parts, bf16[32,128,128]{2,1,0:T(8,128)(2,1)S(1)} %copy-done.1), custom_call_target="tpu_custom_call" | custom-call | bytes 4000000 | tf_op jit(solution)/shard_map/sum_variance/pallas_call | solution.py:705
  59.2 1.5 %collective-permute-start.3 = (bf16[32,32,128]{2,1,0:T(8,128)(2,1)S(1)}, bf16[32,32,128]{2,1,0:T(8,128)(2,1)S(1)}, u32[]{:S(2)}, u32[]{:S(2)}) collective-permute-start(bf16[32,32,128]{2,1,0:T(8,128)(2,1)S(1)} %bitcast.22), channel_id=1, source_target_pairs={{0,2},{2,0},{1,3},{3,1},{4,6},{6,4},{5,7},{7,5},{8,10},{10,8},{9,1... | collective-permute-start | bytes 786440 | tf_op jit(solution)/shard_map/ppermute | solution.py:881
  60.7 3.1 %score.1 = (f32[256,1024]{1,0:T(8,128)}, f32[8,128]{1,0:T(8,128)S(1)}) custom-call(s32[16]{0:T(128)S(1)} %copy-done.7, bf16[32,72,128]{2,1,0:T(8,128)(2,1)} %get-tuple-element.17.payload, f32[1,256]{1,0:T(1,128)S(1)} %pad.26.down, f32[1,256]{1,0:T(1,128)S(1)} %pad_maximum_fusion.1.over), custom_call_target="tpu_custom_call" | custom-call | flops 2000000000 | bytes 2000000 | tf_op jit(solution)/shard_map/score/pallas_call | solution.py:647
  63.9 10.4 %all-to-all-done.2.parts = bf16[32,72,128]{2,1,0:T(8,128)(2,1)S(1)} async-done(((bf16[32,72,128]{2,1,0:T(8,128)(2,1)}), bf16[32,72,128]{2,1,0:T(8,128)(2,1)S(1)}, u32[]{:S(2)}, u32[]{:S(2)}) %all-to-all-start.2) | async-done | bytes 589856 | tf_op jit(solution)/shard_map/all_to_all | solution.py:873
  74.2 1.4 %combine.1.refs_0_ = bf16[32,32,128]{2,1,0:T(8,128)(2,1)S(1)} custom-call(s32[1]{0:T(128)} %bitcast.1.me, s32[4,8,2]{2,1,0:T(8,128)S(1)} %copy.35.earlier.table, f32[8,128]{1,0:T(8,128)S(1)} %get-tuple-element.18.earlier, bf16[32,72,128]{2,1,0:T(8,128)(2,1)S(1)} %all-to-all-done.2.parts, f32[32,32,128]{2,1,0:T(8,128)S(1)} %get-tuple-element.20.own_var, ...), custom_call_target="tpu_custom_call" | custom-call | tf_op jit(solution)/shard_map/combine/pallas_call | solution.py:753
  75.7 1.3 %collective-permute-start.4 = (bf16[32,32,128]{2,1,0:T(8,128)(2,1)S(1)}, bf16[32,32,128]{2,1,0:T(8,128)(2,1)S(1)}, u32[]{:S(2)}, u32[]{:S(2)}) collective-permute-start(bf16[32,32,128]{2,1,0:T(8,128)(2,1)S(1)} %combine.1.refs_0_), channel_id=1, source_target_pairs={{0,2},{1,3},{2,0},{3,1},{4,6},{5,7},{6,4},{7,5},{8,10},{9,11},{10,... | collective-permute-start | bytes 786440 | tf_op jit(solution)/shard_map/ppermute | solution.py:888
  77.4 5.7 %collective-permute-done.4.refs_2_ = bf16[32,32,128]{2,1,0:T(8,128)(2,1)S(1)} collective-permute-done((bf16[32,32,128]{2,1,0:T(8,128)(2,1)S(1)}, bf16[32,32,128]{2,1,0:T(8,128)(2,1)S(1)}, u32[]{:S(2)}, u32[]{:S(2)}) %collective-permute-start.4) | collective-permute-done | bytes 262176 | tf_op jit(solution)/shard_map/ppermute | solution.py:888
  83.1 1.4 %collective-permute-start.5 = (bf16[32,32,128]{2,1,0:T(8,128)(2,1)S(1)}, bf16[32,32,128]{2,1,0:T(8,128)(2,1)S(1)}, u32[]{:S(2)}, u32[]{:S(2)}) collective-permute-start(bf16[32,32,128]{2,1,0:T(8,128)(2,1)S(1)} %collective-permute-done.4.refs_2_), channel_id=1, source_target_pairs={{0,1},{1,0},{2,3},{3,2},{4,5},{5,4},{6,7},{7,6},{8,9},{9,8},{10,11... | collective-permute-start | bytes 786440 | tf_op jit(solution)/shard_map/ppermute | solution.py:888
  84.5 1.7 %join_parts.2.refs_1_ = f32[32,128,128]{2,1,0:T(8,128)} custom-call(s32[3]{0:T(128)S(1)} %pad_add_fusion.places, bf16[32,32,128]{2,1,0:T(8,128)(2,1)S(1)} %combine.1.refs_0_, bf16[32,32,128]{2,1,0:T(8,128)(2,1)S(1)} %collective-permute-done.6.refs_1_, bf16[32,32,128]{2,1,0:T(8,128)(2,1)S(1)} %collective-permute-done.4.refs_2_), custom_call_target="tpu_custom_call" | custom-call | bytes 9000000 | tf_op jit(solution)/shard_map/join_parts/pallas_call | solution.py:788
  86.3 0.8 join_parts.3
  (53 shorter events, 3.6 us)
Async XLA Ops:
  2.0 11.6 %all-to-all-start = ((s32[8,1,2]{2,1,0:T(1,128)}), s32[8,1,2]{2,1,0:T(1,128)S(1)}, u32[]{:S(2)}, u32[]{:S(2)}) async-start(s32[8,1,2]{2,1,0:T(1,128)} %request_table.1), calls=%async_computation | async-start | bytes 8192 | tf_op jit(solution)/shard_map/all_to_all | solution.py:833
  8.4 1.2 %copy-start = (bf16[32,128,128]{2,1,0:T(8,128)(2,1)S(1)}, bf16[32,128,128]{2,1,0:T(8,128)(2,1)}, u32[]{:S(2)}) copy-start(bf16[32,128,128]{2,1,0:T(8,128)(2,1)} %template.1) | copy-start | bytes 3145732
  9.6 9.1 %copy-start.8 = (bf16[40,21]{0,1:T(8,128)(2,1)S(1)}, bf16[40,21]{0,1:T(8,128)(2,1)}, u32[]{:S(2)}) copy-start(bf16[40,21]{0,1:T(8,128)(2,1)} %param.20) | copy-start | bytes 5044
  9.6 9.2 %copy-start.9 = (bf16[40,21]{0,1:T(8,128)(2,1)S(1)}, bf16[40,21]{0,1:T(8,128)(2,1)}, u32[]{:S(2)}) copy-start(bf16[40,21]{0,1:T(8,128)(2,1)} %param.21) | copy-start | bytes 5044
  9.7 17.2 %copy-start.2 = (bf16[1,256,1024]{2,1,0:T(8,128)(2,1)S(1)}, bf16[1,256,1024]{2,1,0:T(8,128)(2,1)}, u32[]{:S(2)}) copy-start(bf16[1,256,1024]{2,1,0:T(8,128)(2,1)} %param.14) | copy-start | bytes 1572868
  9.7 17.2 %copy-start.3 = (bf16[1,256,1024]{2,1,0:T(8,128)(2,1)S(1)}, bf16[1,256,1024]{2,1,0:T(8,128)(2,1)}, u32[]{:S(2)}) copy-start(bf16[1,256,1024]{2,1,0:T(8,128)(2,1)} %param.15) | copy-start | bytes 1572868
  15.1 14.4 %all-to-all-start.1 = ((bf16[16,128,128]{2,1,0:T(8,128)(2,1)}), bf16[16,128,128]{2,1,0:T(8,128)(2,1)S(1)}, u32[]{:S(2)}, u32[]{:S(2)}) async-start(bf16[16,128,128]{2,1,0:T(8,128)(2,1)} %pick_blocks.1.earlier), calls=%async_computation.1 | async-start | bytes 1048576 | tf_op jit(solution)/shard_map/all_to_all | solution.py:840
  18.7 19.0 %copy-start.5 = (s32[1,4]{1,0:T(1,128)S(1)}, s32[1,4]{1,0:T(1,128)}, u32[]{:S(2)}) copy-start(s32[1,4]{1,0:T(1,128)} %rows_at.1) | copy-start | bytes 52
  18.7 19.0 %copy-start.6 = (s32[1,4]{1,0:T(1,128)S(1)}, s32[1,4]{1,0:T(1,128)}, u32[]{:S(2)}) copy-start(s32[1,4]{1,0:T(1,128)} %cols_at.1) | copy-start | bytes 52
  20.5 17.2 %copy-start.7 = (s32[16]{0:T(128)S(1)}, s32[16]{0:T(128)}, u32[]{:S(2)}) copy-start(s32[16]{0:T(128)} %get-tuple-element.14.slot_of) | copy-start | bytes 196
  20.6 4.7 %collective-permute-start.2 = (s32[8,1,2]{2,1,0:T(1,128)S(1)}, s32[8,1,2]{2,1,0:T(1,128)S(1)}, u32[]{:S(2)}, u32[]{:S(2)}) collective-permute-start(s32[8,1,2]{2,1,0:T(1,128)S(1)} %hold.1), channel_id=1, source_target_pairs={{0,3},{1,2},{2,1},{3,0},{4,7},{5,6},{6,5},{7,4},{8,11},{9,10},{10,... | collective-permute-start | bytes 200 | tf_op jit(solution)/shard_map/ppermute | solution.py:45
  23.8 2.8 %collective-permute-start.1 = (s32[8,1,2]{2,1,0:T(1,128)S(1)}, s32[8,1,2]{2,1,0:T(1,128)S(1)}, u32[]{:S(2)}, u32[]{:S(2)}) collective-permute-start(s32[8,1,2]{2,1,0:T(1,128)S(1)} %hold.1), channel_id=1, source_target_pairs={{0,2},{1,3},{2,0},{3,1},{4,6},{5,7},{6,4},{7,5},{8,10},{9,11},{10,... | collective-permute-start | bytes 200 | tf_op jit(solution)/shard_map/ppermute | solution.py:45
  24.1 2.6 %collective-permute-start = (s32[8,1,2]{2,1,0:T(1,128)S(1)}, s32[8,1,2]{2,1,0:T(1,128)S(1)}, u32[]{:S(2)}, u32[]{:S(2)}) collective-permute-start(s32[8,1,2]{2,1,0:T(1,128)S(1)} %hold.1), channel_id=1, source_target_pairs={{0,1},{1,0},{2,3},{3,2},{4,5},{5,4},{6,7},{7,6},{8,9},{9,8},{10,11... | collective-permute-start | bytes 200 | tf_op jit(solution)/shard_map/ppermute | solution.py:45
  26.9 0.7 copy-start.4
  29.6 22.4 %all-to-all-start.3 = ((bf16[16,128,128]{2,1,0:T(8,128)(2,1)}), bf16[16,128,128]{2,1,0:T(8,128)(2,1)S(1)}, u32[]{:S(2)}, u32[]{:S(2)}) async-start(bf16[16,128,128]{2,1,0:T(8,128)(2,1)} %prepare.1), calls=%async_computation.3 | async-start | bytes 1048576 | tf_op jit(solution)/shard_map/all_to_all | solution.py:852
  37.7 20.1 %copy-start.10 = (f32[1,21]{1,0:T(1,128)S(1)}, f32[1,21]{1,0:T(1,128)}, u32[]{:S(2)}) copy-start(f32[1,21]{1,0:T(1,128)} %param.23) | copy-start | bytes 256
  37.7 20.2 %copy-start.11 = (f32[1,21]{1,0:T(1,128)S(1)}, f32[1,21]{1,0:T(1,128)}, u32[]{:S(2)}) copy-start(f32[1,21]{1,0:T(1,128)} %param.22) | copy-start | bytes 256
  37.7 20.2 %copy-start.1 = (bf16[32,128,128]{2,1,0:T(8,128)(2,1)S(1)}, bf16[32,128,128]{2,1,0:T(8,128)(2,1)}, u32[]{:S(2)}) copy-start(bf16[32,128,128]{2,1,0:T(8,128)(2,1)} %template_var.1) | copy-start | bytes 3145732
  52.0 22.3 %all-to-all-start.2 = ((bf16[32,72,128]{2,1,0:T(8,128)(2,1)}), bf16[32,72,128]{2,1,0:T(8,128)(2,1)S(1)}, u32[]{:S(2)}, u32[]{:S(2)}) async-start(bf16[32,72,128]{2,1,0:T(8,128)(2,1)} %get-tuple-element.17.payload), calls=%async_computation.2 | async-start | bytes 1179648 | tf_op jit(solution)/shard_map/all_to_all | solution.py:873
  59.2 15.1 %collective-permute-start.3 = (bf16[32,32,128]{2,1,0:T(8,128)(2,1)S(1)}, bf16[32,32,128]{2,1,0:T(8,128)(2,1)S(1)}, u32[]{:S(2)}, u32[]{:S(2)}) collective-permute-start(bf16[32,32,128]{2,1,0:T(8,128)(2,1)S(1)} %bitcast.22), channel_id=1, source_target_pairs={{0,2},{2,0},{1,3},{3,1},{4,6},{6,4},{5,7},{7,5},{8,10},{10,8},{9,1... | collective-permute-start | bytes 786440 | tf_op jit(solution)/shard_map/ppermute | solution.py:881
  75.7 7.4 %collective-permute-start.4 = (bf16[32,32,128]{2,1,0:T(8,128)(2,1)S(1)}, bf16[32,32,128]{2,1,0:T(8,128)(2,1)S(1)}, u32[]{:S(2)}, u32[]{:S(2)}) collective-permute-start(bf16[32,32,128]{2,1,0:T(8,128)(2,1)S(1)} %combine.1.refs_0_), channel_id=1, source_target_pairs={{0,2},{1,3},{2,0},{3,1},{4,6},{5,7},{6,4},{7,5},{8,10},{9,11},{10,... | collective-permute-start | bytes 786440 | tf_op jit(solution)/shard_map/ppermute | solution.py:888
  77.0 7.6 %collective-permute-start.6 = (bf16[32,32,128]{2,1,0:T(8,128)(2,1)S(1)}, bf16[32,32,128]{2,1,0:T(8,128)(2,1)S(1)}, u32[]{:S(2)}, u32[]{:S(2)}) collective-permute-start(bf16[32,32,128]{2,1,0:T(8,128)(2,1)S(1)} %combine.1.refs_0_), channel_id=1, source_target_pairs={{0,1},{1,0},{2,3},{3,2},{4,5},{5,4},{6,7},{7,6},{8,9},{9,8},{10,11... | collective-permute-start | bytes 786440 | tf_op jit(solution)/shard_map/ppermute | solution.py:888
  83.1 3.2 %collective-permute-start.5 = (bf16[32,32,128]{2,1,0:T(8,128)(2,1)S(1)}, bf16[32,32,128]{2,1,0:T(8,128)(2,1)S(1)}, u32[]{:S(2)}, u32[]{:S(2)}) collective-permute-start(bf16[32,32,128]{2,1,0:T(8,128)(2,1)S(1)} %collective-permute-done.4.refs_2_), channel_id=1, source_target_pairs={{0,1},{1,0},{2,3},{3,2},{4,5},{5,4},{6,7},{7,6},{8,9},{9,8},{10,11... | collective-permute-start | bytes 786440 | tf_op jit(solution)/shard_map/ppermute | solution.py:888
